TPU v7x, 32 devices: a whole 2x2x4 slice. The times are simulated.
32 devices in a mesh: group: 4 (over z), dev: 8 (over y, x, core).
Axes of the slice: x: 2, y: 2, z: 4, core: 2. Of those that a mesh axis runs over, the one named last changes fastest.
Arguments:
- corpus_tokens: bfloat16 [4096, 1024], P(('group', 'dev')), may hold values from -6 to 6
- norm_gain: float32 [1024], replicated, may hold values from 0.1 to 1.9
- wi_weight: bfloat16 [1024, 5248], P('dev'), may hold values from -0.1875 to 0.1875
- wo_weight: bfloat16 [2624, 1024], P('dev'), may hold values from -0.125 to 0.125
- final_gain: float32 [1024], replicated, may hold values from 0.1 to 1.9
- proj_weight: bfloat16 [1024, 128], replicated, may hold values from -0.1875 to 0.1875
- query_vectors: bfloat16 [64, 32, 128], P(('group', 'dev')), may hold values from -6 to 6
- doc_lengths: int32 [4, 4], P('group'), may hold values from 1 to 512, 1024 in all within a row
- candidates: int32 [64, 100], P(('group', 'dev')), may hold values from 0 to 15
Outputs:
- doc_vectors: bfloat16 [4096, 128], P(('group', 'dev'))
- scores: float32 [64, 100], P(('group', 'dev'))
Inputs may be any that keep to these rules, and one draw needn't show every extreme that they name: `doc_lengths`: each row sums to 1024; its largest length is exactly 512. `candidates`: document k of group g has id g * 4 + k; ids may repeat within a row.
All inputs are finite; a program needn't handle non-finite values.
Results may differ from a plain program's by a relative error of at most 0.0062.
Values may be sent and summed in bfloat16 or wider, within the bound.
No kernel may reach another device: no remote copies, remote signals or barrier semaphores. Data moves between devices by JAX's collectives and lax.ppermute only.
A program may use at most 128 MiB of HBM per device.

v0:
```python
import math

import jax
import jax.numpy as jnp
from jax import lax
from jax.sharding import PartitionSpec as P


def layer_norm(values, gain_row):
    values = values.astype(jnp.float32)
    center = jnp.mean(values, axis=-1, keepdims=True)
    spread = jnp.mean(jnp.square(values - center), axis=-1, keepdims=True)
    return (values - center) * lax.rsqrt(spread + 1e-05) * gain_row


def owner_of(places, doc_ends):
    return jnp.sum((places[:, None] >= doc_ends[None, :]).astype(jnp.int32), axis=1)


def raise_row(running, row_index, values):
    current = lax.dynamic_index_in_dim(running, row_index, 0, keepdims=False)
    return lax.dynamic_update_index_in_dim(running, jnp.maximum(current, values), row_index, 0)


def token_maxima(query_rows, vectors, owners, doc_count):
    total_rows = query_rows.shape[0]
    query_block = math.gcd(total_rows, 512)
    vector_rows = vectors.shape[0]
    vector_block = math.gcd(vector_rows, 512)
    stacked_vectors = vectors.reshape(vector_rows // vector_block, vector_block, vectors.shape[1])
    stacked_owners = owners.reshape(vector_rows // vector_block, vector_block)
    lowest = jnp.array(-jnp.inf, jnp.bfloat16)

    def one_block(query_part):

        def advance(running, element):
            vector_part, owner_part = element
            similar = jnp.einsum(
                "tk,qk->tq", vector_part, query_part, preferred_element_type=jnp.float32
            ).astype(jnp.bfloat16)
            first_doc = owner_part[0]
            last_doc = owner_part[-1]

            def inside_one(state):
                return raise_row(state, first_doc, jnp.max(similar, axis=0))

            def across_several(state):

                def per_doc(doc_index, inner):
                    masked = jnp.where((owner_part == doc_index)[:, None], similar, lowest)
                    return raise_row(inner, doc_index, jnp.max(masked, axis=0))

                return lax.fori_loop(first_doc, last_doc + 1, per_doc, state)

            return (lax.cond(first_doc == last_doc, inside_one, across_several, running), None)

        start_value = jnp.full((doc_count, query_block), -jnp.inf, jnp.bfloat16)
        outcome, _ = lax.scan(advance, start_value, (stacked_vectors, stacked_owners))
        return outcome

    blocks = lax.map(
        one_block, query_rows.reshape(total_rows // query_block, query_block, query_rows.shape[1])
    )
    return jnp.transpose(blocks, (1, 0, 2)).reshape(doc_count, total_rows)


def body(
    corpus_tokens,
    norm_gain,
    wi_weight,
    wo_weight,
    final_gain,
    proj_weight,
    query_vectors,
    doc_lengths,
    candidates,
):
    local_rows = corpus_tokens.shape[0]
    normed = layer_norm(corpus_tokens, norm_gain).astype(jnp.bfloat16)
    columns = normed
    lifted = jnp.dot(
        columns,
        lax.all_gather(wi_weight, "dev", axis=0, tiled=True),
        preferred_element_type=jnp.float32,
    )
    hidden_width = wi_weight.shape[1] // 2
    hidden = (
        jax.nn.gelu(lifted[:, :hidden_width], approximate=False) * lifted[:, hidden_width:]
    ).astype(jnp.bfloat16)
    columns = hidden
    down_sum = jnp.dot(
        columns,
        lax.all_gather(wo_weight, "dev", axis=0, tiled=True),
        preferred_element_type=jnp.float32,
    )
    mixed_sum = corpus_tokens.astype(jnp.float32) + down_sum
    normed_out = layer_norm(mixed_sum, final_gain).astype(jnp.bfloat16)
    projected = jnp.dot(normed_out, proj_weight, preferred_element_type=jnp.float32)
    inverse = lax.rsqrt(jnp.sum(projected * projected, axis=-1, keepdims=True) + 1e-06)
    vectors = (projected * inverse).astype(jnp.bfloat16)
    doc_count = doc_lengths.shape[1]
    doc_ends = jnp.cumsum(doc_lengths[0])
    groups = lax.axis_size("group")
    devices = lax.axis_size("dev")
    per_query, query_len, vector_dim = query_vectors.shape
    every_query = lax.all_gather(query_vectors, ("group", "dev"), axis=0, tiled=True)
    places = lax.axis_index("dev") * local_rows + jnp.arange(local_rows, dtype=jnp.int32)
    partial_max = token_maxima(
        every_query.reshape(-1, vector_dim), vectors, owner_of(places, doc_ends), doc_count
    )
    group_max = lax.pmax(partial_max, "dev")
    arranged = group_max.reshape(doc_count, groups, devices, per_query * query_len)
    mine = lax.dynamic_index_in_dim(arranged, lax.axis_index("dev"), axis=2, keepdims=False)
    totals = (
        jnp.sum(mine.astype(jnp.float32).reshape(doc_count, groups, per_query, query_len), axis=-1)
        / query_len
    )
    outgoing = jnp.transpose(totals, (1, 2, 0))
    incoming = lax.all_to_all(outgoing, "group", split_axis=0, concat_axis=0, tiled=True)
    score_table = jnp.transpose(incoming, (1, 0, 2)).reshape(per_query, groups * doc_count)
    labels = jnp.arange(groups * doc_count, dtype=jnp.int32)
    picked = (candidates[:, :, None] == labels[None, None, :]).astype(jnp.float32)
    scores = jnp.sum(picked * score_table[:, None, :], axis=-1)
    return (vectors, scores)


def solution(mesh):
    placed = (
        P(("group", "dev"), None),
        P(),
        P("dev", None),
        P("dev", None),
        P(),
        P(),
        P(("group", "dev"), None, None),
        P("group", None),
        P(("group", "dev"), None),
    )
    return jax.shard_map(
        body,
        mesh=mesh,
        in_specs=placed,
        out_specs=(P(("group", "dev"), None), P(("group", "dev"), None)),
        check_vma=False,
    )
```

profile of v0, /device:TPU:0, one launch (start us, length us, event | category | flops | bytes accessed | tf_op | source)
XLA Modules:
  0.0 212.1 jit_solution(10959462327773286862)
XLA Ops:
  11.2 47.9 %all_gather.11 = bf16[64,32,128]{2,1,0:T(8,128)(2,1)} all-gather(bf16[2,32,128]{2,1,0:T(8,128)(2,1)S(1)} %copy-done.3), channel_id=1, replica_groups=mesh['group'=4,'dev'=8] {'group','dev'}, dimensions={0}, use_global_device_ids=true | all-gather | bytes 540672 | tf_op jit(solution)/shard_map/all_gather | solution.py:106
  59.1 20.6 %all-gather.3.cloned.1.call-done = bf16[1024,5248]{1,0:T(8,128)(2,1)} async-done(((bf16[128,5248]{1,0:T(8,128)(2,1)}), bf16[1024,5248]{1,0:T(8,128)(2,1)}) %all-gather.3.cloned.1.call-update) | async-done | bytes 10747920 | tf_op jit(solution)/shard_map/all_gather | solution.py:83
  79.7 5.7 %fusion.53 = f32[128,5248]{1,0:T(8,128)S(1)} fusion(bf16[1024,5248]{1,0:T(8,128)(2,1)} %all-gather.3.cloned.1.call-done, bf16[128,1024]{1,0:T(8,128)(2,1)S(1)} %copy-done.1, f32[1024]{0:T(1024)S(1)} %copy-done.2, f32[128]{0:T(128)S(1)} %add_rsqrt_fusion.2, f32[128]{0:T(128)S(1)} %broadcast_multiply_fusion.1), kind=kOutput, calls=%fused_computation.72 | convolution fusion | flops 1376387072 | bytes 13702144 | tf_op jit(solution)/shard_map/dot_general | solution.py:81
  85.5 37.3 %all-gather.5.cloned.1.call-done = bf16[2624,1024]{1,0:T(8,128)(2,1)} async-done(((bf16[328,1024]{1,0:T(8,128)(2,1)}), bf16[2624,1024]{1,0:T(8,128)(2,1)}) %all-gather.5.cloned.1.call-update) | async-done | bytes 5373968 | tf_op jit(solution)/shard_map/all_gather | solution.py:93
  122.8 6.3 %fusion.92 = (f32[128]{0:T(128)S(1)}, f32[128,1024]{1,0:T(8,128)S(1)}) fusion(bf16[2624,1024]{1,0:T(8,128)(2,1)} %all-gather.5.cloned.1.call-done, f32[128,5248]{1,0:T(8,128)S(1)} %fusion.53, bf16[128,1024]{1,0:T(8,128)(2,1)S(1)} %copy-done.1), kind=kOutput, calls=%fused_computation.123 | convolution fusion | flops 710426496 | bytes 8913408 | tf_op jit(solution)/shard_map/dot_general | solution.py:91
  129.8 34.8 %while.26 = (s32[]{:T(128)}, bf16[4,4,512]{2,1,0:T(4,128)(2,1)S(1)}, pred[]{:T(512)}, bf16[4,512,128]{2,1,0:T(8,128)(2,1)}, bf16[1,128,128]{2,1,0:T(8,128)(2,1)S...) while((s32[]{:T(128)}, bf16[4,4,512]{2,1,0:T(4,128)(2,1)S(1)}, pred[]{:T(512)}, ...), condition=%wide.region_14.15_spmd, body=%wide.region_7.14_spmd.sunk | while | flops 16975496 | bytes 712321 | solution.py:61
  129.8 1.1 fusion.102
  132.1 5.7 %conditional.2 = (bf16[1,4,512]{2,1,0:T(4,128)(2,1)}) conditional(s32[]{:T(128)} %convert_element_type.88, (s32[1,128]{1,0:T(1,128)S(1)}, bf16[128,512]{0,1:T(8,128)(2,1)S(1)}, s32[]{:T(128)S(1)}, bf16[4,512]{1,0:T(4,128)(2,1)}) %tuple.83, (s32[]{:T(128)S(1)}, bf16[4,512]{1,0:T(4,128)(2,1)}, bf16[128,512]{0,1:T(8,128)(2,1)S(1)}) %tuple.84), branch_computations={%region_8.11_spmd, %region_12.13_spmd} | conditional | flops 132742 | bytes 400359 | solution.py:55
  133.6 4.3 %while.25 = (s32[]{:T(128)}, bf16[4,512]{1,0:T(4,128)(2,1)}, s32[]{:T(128)}, s32[128]{0:T(128)S(1)}, bf16[128,512]{1,0:T(8,128)(2,1)S(1)}, /*index=5*/s32[]{:T(128)}, s32[]{:T(128)}, s32[]{:T(128)}) while((s32[]{:T(128)}, bf16[4,512]{1,0:T(4,128)(2,1)}, s32[]{:T(128)}, s32[128]{0:T(128)S(1)}, bf16[128,512]{1,0:T(8,128)(2,1)S(1)}, ...), condition=%wide.region_11.10_spmd, body=%wide.region_9.9_spmd.sunk | while | flops 132741 | bytes 138115 | solution.py:53
  133.7 0.7 reshape_maximum_fusion.2
  134.4 1.3 dynamic_update_slice.18
  136.5 1.3 dynamic_update_slice.18
  138.5 1.1 fusion.102
  140.8 5.7 %conditional.2 = (bf16[1,4,512]{2,1,0:T(4,128)(2,1)}) conditional(s32[]{:T(128)} %convert_element_type.88, (s32[1,128]{1,0:T(1,128)S(1)}, bf16[128,512]{0,1:T(8,128)(2,1)S(1)}, s32[]{:T(128)S(1)}, bf16[4,512]{1,0:T(4,128)(2,1)}) %tuple.83, (s32[]{:T(128)S(1)}, bf16[4,512]{1,0:T(4,128)(2,1)}, bf16[128,512]{0,1:T(8,128)(2,1)S(1)}) %tuple.84), branch_computations={%region_8.11_spmd, %region_12.13_spmd} | conditional | flops 132742 | bytes 400359 | solution.py:55
  142.3 4.3 %while.25 = (s32[]{:T(128)}, bf16[4,512]{1,0:T(4,128)(2,1)}, s32[]{:T(128)}, s32[128]{0:T(128)S(1)}, bf16[128,512]{1,0:T(8,128)(2,1)S(1)}, /*index=5*/s32[]{:T(128)}, s32[]{:T(128)}, s32[]{:T(128)}) while((s32[]{:T(128)}, bf16[4,512]{1,0:T(4,128)(2,1)}, s32[]{:T(128)}, s32[128]{0:T(128)S(1)}, bf16[128,512]{1,0:T(8,128)(2,1)S(1)}, ...), condition=%wide.region_11.10_spmd, body=%wide.region_9.9_spmd.sunk | while | flops 132741 | bytes 138115 | solution.py:53
  143.1 1.3 dynamic_update_slice.18
  145.2 1.3 dynamic_update_slice.18
  147.2 1.1 fusion.102
  149.5 5.7 %conditional.2 = (bf16[1,4,512]{2,1,0:T(4,128)(2,1)}) conditional(s32[]{:T(128)} %convert_element_type.88, (s32[1,128]{1,0:T(1,128)S(1)}, bf16[128,512]{0,1:T(8,128)(2,1)S(1)}, s32[]{:T(128)S(1)}, bf16[4,512]{1,0:T(4,128)(2,1)}) %tuple.83, (s32[]{:T(128)S(1)}, bf16[4,512]{1,0:T(4,128)(2,1)}, bf16[128,512]{0,1:T(8,128)(2,1)S(1)}) %tuple.84), branch_computations={%region_8.11_spmd, %region_12.13_spmd} | conditional | flops 132742 | bytes 400359 | solution.py:55
  151.0 4.3 %while.25 = (s32[]{:T(128)}, bf16[4,512]{1,0:T(4,128)(2,1)}, s32[]{:T(128)}, s32[128]{0:T(128)S(1)}, bf16[128,512]{1,0:T(8,128)(2,1)S(1)}, /*index=5*/s32[]{:T(128)}, s32[]{:T(128)}, s32[]{:T(128)}) while((s32[]{:T(128)}, bf16[4,512]{1,0:T(4,128)(2,1)}, s32[]{:T(128)}, s32[128]{0:T(128)S(1)}, bf16[128,512]{1,0:T(8,128)(2,1)S(1)}, ...), condition=%wide.region_11.10_spmd, body=%wide.region_9.9_spmd.sunk | while | flops 132741 | bytes 138115 | solution.py:53
  151.8 1.3 dynamic_update_slice.18
  153.9 1.3 dynamic_update_slice.18
  155.9 1.1 fusion.102
  158.2 5.7 %conditional.2 = (bf16[1,4,512]{2,1,0:T(4,128)(2,1)}) conditional(s32[]{:T(128)} %convert_element_type.88, (s32[1,128]{1,0:T(1,128)S(1)}, bf16[128,512]{0,1:T(8,128)(2,1)S(1)}, s32[]{:T(128)S(1)}, bf16[4,512]{1,0:T(4,128)(2,1)}) %tuple.83, (s32[]{:T(128)S(1)}, bf16[4,512]{1,0:T(4,128)(2,1)}, bf16[128,512]{0,1:T(8,128)(2,1)S(1)}) %tuple.84), branch_computations={%region_8.11_spmd, %region_12.13_spmd} | conditional | flops 132742 | bytes 400359 | solution.py:55
  159.7 4.3 %while.25 = (s32[]{:T(128)}, bf16[4,512]{1,0:T(4,128)(2,1)}, s32[]{:T(128)}, s32[128]{0:T(128)S(1)}, bf16[128,512]{1,0:T(8,128)(2,1)S(1)}, /*index=5*/s32[]{:T(128)}, s32[]{:T(128)}, s32[]{:T(128)}) while((s32[]{:T(128)}, bf16[4,512]{1,0:T(4,128)(2,1)}, s32[]{:T(128)}, s32[128]{0:T(128)S(1)}, bf16[128,512]{1,0:T(8,128)(2,1)S(1)}, ...), condition=%wide.region_11.10_spmd, body=%wide.region_9.9_spmd.sunk | while | flops 132741 | bytes 138115 | solution.py:53
  160.5 1.3 dynamic_update_slice.18
  162.6 1.3 dynamic_update_slice.18
  164.7 23.5 %pmax.7 = bf16[4,4,8,64]{3,2,0,1:T(8,128)(2,1)S(1)} all-reduce(bf16[4,4,8,64]{3,2,0,1:T(8,128)(2,1)S(1)} %reshape.99), channel_id=1, replica_groups=mesh['group'=4,'dev'=8] {'dev'}, use_global_device_ids=true, to_apply=%region_15.16 | all-reduce | flops 8192 | bytes 32768 | tf_op jit(solution)/shard_map/pmax | solution.py:111
  188.5 0.7 copy.24
  189.2 9.8 %all-to-all-start = ((f32[4,2,4]{2,1,0:T(2,128)}), f32[4,2,4]{2,1,0:T(2,128)S(1)}, u32[]{:S(2)}, u32[]{:S(2)}) async-start(f32[4,2,4]{2,1,0:T(2,128)} %copy.24), calls=%async_computation | async-start | bytes 8192 | tf_op jit(solution)/shard_map/all_to_all | solution.py:119
  199.0 0.7 copy.26
  199.7 4.8 %all-to-all-done = f32[4,2,4]{2,1,0:T(2,128)S(1)} async-done(((f32[4,2,4]{2,1,0:T(2,128)}), f32[4,2,4]{2,1,0:T(2,128)S(1)}, u32[]{:S(2)}, u32[]{:S(2)}) %all-to-all-start) | async-done | bytes 160 | tf_op jit(solution)/shard_map/all_to_all | solution.py:119
  (86 shorter events, 20.8 us)
Async XLA Ops:
  7.2 122.2 %copy-start = (bf16[1024,128]{1,0:T(8,128)(2,1)S(1)}, bf16[1024,128]{1,0:T(8,128)(2,1)}, u32[]{:S(2)}) copy-start(bf16[1024,128]{1,0:T(8,128)(2,1)} %param.20) | copy-start | bytes 786436
  7.2 1.5 copy-start.6
  7.2 3.7 %copy-start.1 = (bf16[128,1024]{1,0:T(8,128)(2,1)S(1)}, bf16[128,1024]{1,0:T(8,128)(2,1)}, u32[]{:S(2)}) copy-start(bf16[128,1024]{1,0:T(8,128)(2,1)} %param.15) | copy-start | bytes 786436
  7.2 4.0 %copy-start.3 = (bf16[2,32,128]{2,1,0:T(8,128)(2,1)S(1)}, bf16[2,32,128]{2,1,0:T(8,128)(2,1)}, u32[]{:S(2)}) copy-start(bf16[2,32,128]{2,1,0:T(8,128)(2,1)} %param.21) | copy-start | bytes 49156
  7.2 72.5 %copy-start.2 = (f32[1024]{0:T(1024)S(1)}, f32[1024]{0:T(1024)}, u32[]{:S(2)}) copy-start(f32[1024]{0:T(1024)} %param.16) | copy-start | bytes 12292
  7.2 72.5 %all-gather.3.cloned.1.call-start = ((), (), s32[]{:S(2)}) async-start(), calls=%async_computation.1 | async-start | bytes 12091392 | tf_op jit(solution)/shard_map/all_gather | solution.py:83
  8.0 114.8 %all-gather.5.cloned.1.call-start = ((), (), s32[]{:S(2)}) async-start(), calls=%async_computation.2 | async-start | bytes 6045696 | tf_op jit(solution)/shard_map/all_gather | solution.py:93
  85.4 43.9 %copy-start.4 = (f32[1024]{0:T(1024)S(1)}, f32[1024]{0:T(1024)}, u32[]{:S(2)}) copy-start(f32[1024]{0:T(1024)} %param.19) | copy-start | bytes 12292
  129.8 74.8 %copy-start.5 = (s32[2,100]{1,0:T(2,128)S(1)}, s32[2,100]{1,0:T(2,128)}, u32[]{:S(2)}) copy-start(s32[2,100]{1,0:T(2,128)} %param.23) | copy-start | bytes 2404
  189.2 15.4 %all-to-all-start = ((f32[4,2,4]{2,1,0:T(2,128)}), f32[4,2,4]{2,1,0:T(2,128)S(1)}, u32[]{:S(2)}, u32[]{:S(2)}) async-start(f32[4,2,4]{2,1,0:T(2,128)} %copy.24), calls=%async_computation | async-start | bytes 8192 | tf_op jit(solution)/shard_map/all_to_all | solution.py:119
Sparse Core Ops, SparseCore 0:
  9.9 69.7 all-gather.2
  81.6 41.1 all-gather.4
where the time goes:
time: 211 us; the launch traced here: 212 us
  blocking collectives  71.4 us (34%)
  waiting for transfers between devices  64.1 us (30%)
  local copies, waits for them, and re-layouts  23.4 us (11%)
  matrix products  16.8 us (8%)
  between operations  15.5 us (7%)
  starting transfers between devices  9.86 us (5%)
  other arithmetic  8.15 us (4%)
  loops' own time  2.93 us (1%)
    all_gather x1, blocking collectives, body(): lax.all_gather(query_vectors, ('group', 'dev'), axis=0, tiled=True)  47.9 us
    all_gather x1, waiting for transfers between devices, body(): lax.all_gather(wo_weight, 'dev', axis=0, tiled=True)  37.3 us
    pmax x1, blocking collectives, body(): group_max = lax.pmax(partial_max, 'dev')  23.5 us
    all_gather x1, waiting for transfers between devices, body(): lax.all_gather(wi_weight, 'dev', axis=0, tiled=True)  20.6 us
    dynamic_update_slice x8, local copies, waits for them, and re-layouts, raise_row(): lax.dynamic_update_index_in_dim(running, jnp.maximum(current, values), ro...  10.4 us
    all_to_all x1, starting transfers between devices, body(): lax.all_to_all(outgoing, 'group', split_axis=0, concat_axis=0, tiled=True)  9.79 us
    dot_general x1, matrix products, body(): jnp.dot(columns, lax.all_gather(wo_weight, 'dev', axis=0, tiled=True), pr...  6.33 us
    dot_general x1, matrix products, body(): jnp.dot(columns, lax.all_gather(wi_weight, 'dev', axis=0, tiled=True), pr...  5.72 us
  transfers between devices with their start and end apart: 3, of which 3 were waited for; matrix products, arithmetic and copies ran while one was open for 4% of the time, Pallas kernels for 0%

commit v1 on v0

v1 whole, which is shorter than its diff:
```python
import functools

import jax
import jax.numpy as jnp
from jax import lax
from jax.experimental import pallas as pl
from jax.experimental.pallas import tpu as pltpu
from jax.sharding import PartitionSpec as P

VMEM_LIMIT = 48 * 1024 * 1024


def norm_rows(values, gain_row):
    center = jnp.mean(values, axis=-1, keepdims=True)
    shifted = values - center
    spread = jnp.mean(shifted * shifted, axis=-1, keepdims=True)
    return (shifted * lax.rsqrt(spread + 1e-05) * gain_row).astype(jnp.bfloat16)


def dot_nt(left, right):
    return lax.dot_general(
        left, right, (((1,), (1,)), ((), ())), preferred_element_type=jnp.float32
    )


def split_kernel(chips, place_ref, wi_ref, *refs):
    pieces, turned = refs[:chips], refs[chips]
    columns = wi_ref.shape[1]
    width = columns // 2
    part = width // chips
    chip = place_ref[0]
    for start in range(0, columns, 128):
        turned[start : start + 128, :] = wi_ref[:, start : start + 128].T
    for step in range(chips):
        target = chip ^ step
        for half in range(2):
            first = pl.multiple_of(half * width + target * part, 16)
            pieces[step][half] = turned[pl.ds(first, part), :]


def ffn_kernel(chips, pieces, place_ref, gain_ref, wo_ref, *refs):
    tokens, refs = refs[:chips], refs[chips:]
    if pieces:
        mine, other, outs = refs[:pieces], refs[pieces : 2 * pieces], refs[2 * pieces : -2]
    else:
        outs, refs = refs[2:], refs[:2]
    gelu_w, gate_w = refs[-2:]
    chip, core = place_ref[0], place_ref[1]
    for step in range(pieces):
        source = (chip ^ step) * 2
        for block, at in ((mine[step], source + core), (other[step], source + 1 - core)):
            columns = pl.ds(pl.multiple_of(at * 128, 128), 128)
            gelu_w[:, columns] = block[0]
            gate_w[:, columns] = block[1]
    for step in list(range(1, chips)) + [0]:
        normed = norm_rows(tokens[step][...].astype(jnp.float32), gain_ref[...])
        first = dot_nt(normed, gelu_w[...])
        second = dot_nt(normed, gate_w[...])
        hidden = (0.5 * first * (1.0 + lax.erf(first * 0.7071067811865476)) * second).astype(jnp.bfloat16)
        outs[step][...] = jnp.dot(hidden, wo_ref[...], preferred_element_type=jnp.float32).astype(
            outs[step].dtype
        )


def finish_kernel(chips, tokens_ref, gain_ref, proj_ref, own_ref, *refs):
    mixed = tokens_ref[...].astype(jnp.float32) + own_ref[...]
    for step in range(chips - 1):
        mixed = mixed + refs[step][...].astype(jnp.float32)
    final = norm_rows(mixed, gain_ref[...])
    projected = jnp.dot(final, proj_ref[...], preferred_element_type=jnp.float32)
    total = jnp.sum(projected * projected, axis=-1, keepdims=True)
    refs[chips - 1][...] = (projected * lax.rsqrt(total + 1e-06)).astype(jnp.bfloat16)


def score_kernel(devices, docs, query_len, place_ref, ends_ref, query_ref, *refs):
    blocks, out_ref = refs[:devices], refs[devices]
    me = place_ref[0]
    rows = blocks[0].shape[0]
    query_rows = query_ref.shape[0]
    queries = query_rows // query_len
    best = [jnp.full((1, query_rows), -jnp.inf, jnp.float32) for _ in range(docs)]
    for step in range(devices):
        similar = dot_nt(blocks[step][...], query_ref[...])
        spot = (me ^ step) * rows + lax.broadcasted_iota(jnp.int32, similar.shape, 0)
        low = jnp.int32(0)
        for doc in range(docs):
            high = ends_ref[doc]
            inside = (spot >= low) & (spot < high)
            masked = jnp.where(inside, similar, -jnp.inf)
            best[doc] = jnp.maximum(best[doc], jnp.max(masked, axis=0, keepdims=True))
            low = high
    maxima = jnp.concatenate(best, axis=0).astype(jnp.bfloat16)
    row = lax.broadcasted_iota(jnp.int32, (query_rows, queries), 0) // query_len
    column = lax.broadcasted_iota(jnp.int32, (query_rows, queries), 1)
    member = (row == column).astype(jnp.bfloat16)
    out_ref[...] = jnp.dot(maxima, member, preferred_element_type=jnp.float32) / query_len


def body(
    corpus_tokens,
    norm_gain,
    wi_weight,
    wo_weight,
    final_gain,
    proj_weight,
    query_vectors,
    doc_lengths,
    candidates,
):
    groups = lax.axis_size("group")
    devices = lax.axis_size("dev")
    chips = devices // 2
    rows, width = corpus_tokens.shape
    part = wo_weight.shape[0] * 2
    me = lax.axis_index("dev").astype(jnp.int32)
    place = jnp.stack([me // 2, me % 2])
    smem = pl.BlockSpec(memory_space=pltpu.SMEM)
    vmem = pl.BlockSpec(memory_space=pltpu.VMEM)
    params = pltpu.CompilerParams(vmem_limit_bytes=VMEM_LIMIT)

    def swap(values, mask, axis="dev"):
        size = devices if axis == "dev" else groups
        return lax.ppermute(values, axis, [(i, i ^ mask) for i in range(size)])

    tokens = [corpus_tokens] + [swap(corpus_tokens, 2 * step) for step in range(1, chips)]
    if wi_weight.shape[0] == 128 and part % 16 == 0:
        pieces = pl.pallas_call(
            functools.partial(split_kernel, chips),
            out_shape=[jax.ShapeDtypeStruct((2, part, 128), jnp.bfloat16)] * chips,
            in_specs=[smem, vmem],
            out_specs=[vmem] * chips,
            scratch_shapes=[pltpu.VMEM((wi_weight.shape[1], 128), jnp.bfloat16)],
            compiler_params=params,
        )(place, wi_weight)
        mine = [pieces[0]] + [swap(pieces[step], 2 * step) for step in range(1, chips)]
        other = [swap(piece, 1) for piece in mine]
        weights = mine + other
        scratch = [pltpu.VMEM((part, width), jnp.bfloat16)] * 2
    else:
        whole = lax.all_gather(wi_weight, "dev", axis=0, tiled=True).reshape(width, 2, chips, part)
        columns = lax.dynamic_index_in_dim(whole, me // 2, 2, keepdims=False)
        weights = [columns[:, half].T for half in range(2)]
        scratch = []
    wo_other = swap(wo_weight, 1)
    even = (me % 2) == 0
    wo_part = jnp.concatenate(
        [jnp.where(even, wo_weight, wo_other), jnp.where(even, wo_other, wo_weight)], axis=0
    )
    query_own = query_vectors
    queries = [query_own] + [swap(query_own, mask, "group") for mask in range(1, groups)]
    query_rows = jnp.concatenate([each.reshape(-1, each.shape[-1]) for each in queries], axis=0)

    partial = pl.pallas_call(
        functools.partial(ffn_kernel, chips, len(weights) // 2 if scratch else 0),
        out_shape=[
            jax.ShapeDtypeStruct((rows, width), jnp.float32 if step == 0 else jnp.bfloat16)
            for step in range(chips)
        ],
        in_specs=[smem, vmem, vmem] + [vmem] * (chips + len(weights)),
        out_specs=[vmem] * chips,
        scratch_shapes=scratch,
        compiler_params=params,
    )(place, norm_gain.reshape(1, -1), wo_part, *tokens, *weights)
    arrived = [swap(partial[step], 2 * step) for step in range(1, chips)]
    vectors = pl.pallas_call(
        functools.partial(finish_kernel, chips),
        out_shape=jax.ShapeDtypeStruct((rows, proj_weight.shape[1]), jnp.bfloat16),
        in_specs=[vmem] * (4 + chips - 1),
        out_specs=vmem,
        compiler_params=params,
    )(corpus_tokens, final_gain.reshape(1, -1), proj_weight, partial[0], *arrived)

    blocks = [vectors] + [swap(vectors, mask) for mask in range(1, devices)]
    docs = doc_lengths.shape[1]
    per_query, query_len, _ = query_vectors.shape
    table = pl.pallas_call(
        functools.partial(score_kernel, devices, docs, query_len),
        out_shape=jax.ShapeDtypeStruct((docs, groups * per_query), jnp.float32),
        in_specs=[smem, smem, vmem] + [vmem] * devices,
        out_specs=vmem,
        compiler_params=params,
    )(me.reshape(1), jnp.cumsum(doc_lengths[0]), query_rows, *blocks)
    sent = [table[:, mask * per_query : (mask + 1) * per_query] for mask in range(groups)]
    got = [sent[0]] + [swap(sent[mask], mask, "group") for mask in range(1, groups)]
    home = lax.axis_index("group").astype(jnp.int32)
    scores = jnp.zeros(candidates.shape, jnp.float32)
    for mask in range(groups):
        for doc in range(docs):
            wanted = (home ^ mask) * docs + doc
            scores = jnp.where(candidates == wanted, got[mask][doc][:, None], scores)
    return (vectors, scores)


def solution(mesh):
    placed = (
        P(("group", "dev"), None),
        P(),
        P("dev", None),
        P("dev", None),
        P(),
        P(),
        P(("group", "dev"), None, None),
        P("group", None),
        P(("group", "dev"), None),
    )
    return jax.shard_map(
        body,
        mesh=mesh,
        in_specs=placed,
        out_specs=(P(("group", "dev"), None), P(("group", "dev"), None)),
        check_vma=False,
    )
```

time: 211 us -> 86.9 us (0.41)
  blocking collectives: 71.4 us -> 0 us
  waiting for transfers between devices: 64.1 us -> 42.1 us
  local copies, waits for them, and re-layouts: 23.4 us -> 2.22 us
  starting transfers between devices: 9.86 us -> 27.7 us
  matrix products: 16.8 us -> 0 us
  between operations: 15.5 us -> 0.77 us
  Pallas kernels: 0 us -> 10.3 us
  other arithmetic: 8.15 us -> 3.57 us
  loops' own time: 2.93 us -> 0 us
    all_gather x2 -> x0, waiting for transfers between devices: 57.9 us -> none  [the longest x1 37.3 us: body(): lax.all_gather(wo_weight, 'dev', axis=0, tiled=True)]
    all_gather x1 -> x0, blocking collectives: 47.9 us -> none  [body(): lax.all_gather(query_vectors, ('group', 'dev'), axis=0, tiled=True)]
    ppermute x0 -> x27, waiting for transfers between devices: none -> 42.1 us  [swap(): return lax.ppermute(values, axis, [(i, i ^ mask) for i in range(size)])]
    ppermute x0 -> x27, starting transfers between devices: none -> 27.7 us  [swap(): return lax.ppermute(values, axis, [(i, i ^ mask) for i in range(size)])]
    pmax x1 -> x0, blocking collectives: 23.5 us -> none  [body(): group_max = lax.pmax(partial_max, 'dev')]
    dot_general x7 -> x0, matrix products: 16.8 us -> none  [the longest x1 6.33 us: body(): jnp.dot(columns, lax.all_gather(wo_weight, 'dev', axis=0, tiled=True), pr...]
    dynamic_update_slice x12 -> x0, local copies, waits for them, and re-layouts: 13.2 us -> none  [the longest x8 10.4 us: raise_row(): lax.dynamic_update_index_in_dim(running, jnp.maximum(current, values), ro...]
    pallas_call x0 -> x4, Pallas kernels: none -> 10.3 us  [the longest x1 6.73 us: body(): pl.pallas_call(functools.partial(ffn_kernel, chips, len(weights) // 2 if...]
  transfers between devices with their start and end apart: 3 -> 27, of which waited for: 3 -> 13; matrix products, arithmetic and copies ran while one was open for 4% -> 3% of each run, Pallas kernels for 0% -> 1%
where the time goes in v1:
time: 86.9 us; the launch traced here: 86.6 us
  waiting for transfers between devices  42.1 us (48%)
  starting transfers between devices  27.7 us (32%)
  Pallas kernels  10.3 us (12%)
  other arithmetic  3.57 us (4%)
  local copies, waits for them, and re-layouts  2.22 us (3%)
    ppermute x27, waiting for transfers between devices, swap(): return lax.ppermute(values, axis, [(i, i ^ mask) for i in range(size)])  42.1 us
    ppermute x27, starting transfers between devices, swap(): return lax.ppermute(values, axis, [(i, i ^ mask) for i in range(size)])  27.7 us
    pallas_call x1, Pallas kernels, body(): pl.pallas_call(functools.partial(ffn_kernel, chips, len(weights) // 2 if...  6.73 us
    unnamed x18, local copies, waits for them, and re-layouts  2.13 us
  transfers between devices with their start and end apart: 27, of which 13 were waited for; matrix products, arithmetic and copies ran while one was open for 3% of the time, Pallas kernels for 1%

profile of v1, /device:TPU:0, one launch (start us, length us, event | category | flops | bytes accessed | tf_op | source)
XLA Modules:
  0.0 86.6 jit_solution(15565400204034844285)
XLA Ops:
  1.1 2.6 %collective-permute-start.1 = (bf16[128,1024]{1,0:T(8,128)(2,1)}, bf16[128,1024]{1,0:T(8,128)(2,1)S(1)}, u32[]{:S(2)}, u32[]{:S(2)}) collective-permute-start(bf16[128,1024]{1,0:T(8,128)(2,1)} %tokens_ref.1), channel_id=1, source_target_pairs={{0,2},{1,3},{2,0},{3,1},{4,6},{5,7},{6,4},{7,5},{8,10},{9,11},{10,... | collective-permute-start | bytes 786440 | tf_op jit(solution)/shard_map/ppermute | solution.py:123
  3.8 1.3 %copy-done = bf16[128,5248]{1,0:T(8,128)(2,1)S(1)} copy-done((bf16[128,5248]{1,0:T(8,128)(2,1)S(1)}, bf16[128,5248]{1,0:T(8,128)(2,1)}, u32[]{:S(2)}) %copy-start) | copy-done | bytes 1343512
  5.1 1.0 %shard_map.104 = (bf16[2,656,128]{2,1,0:T(8,128)(2,1)S(1)}, bf16[2,656,128]{2,1,0:T(8,128)(2,1)S(1)}, bf16[2,656,128]{2,1,0:T(8,128)(2,1)S(1)}, bf16[2,656,128]{2,1,0:T(8,128)(2,1)S(1)}) custom-call(s32[2]{0:T(128)S(1)} %pad_add_fusion.place_ref, bf16[128,5248]{1,0:T(8,128)(2,1)S(1)} %copy-done), custom_call_target="tpu_custom_call" | custom-call | tf_op jit(solution)/shard_map/pallas_call | solution.py:127
  6.2 1.6 %collective-permute-start.6 = (bf16[2,656,128]{2,1,0:T(8,128)(2,1)S(1)}, bf16[2,656,128]{2,1,0:T(8,128)(2,1)S(1)}, u32[]{:S(2)}, u32[]{:S(2)}) collective-permute-start(bf16[2,656,128]{2,1,0:T(8,128)(2,1)S(1)} %get-tuple-element.13), channel_id=1, source_target_pairs={{0,6},{1,7},{2,4},{3,5},{4,2},{5,3},{6,0},{7,1},{8,14},{9,15},{10,... | collective-permute-start | bytes 1007624 | tf_op jit(solution)/shard_map/ppermute | solution.py:123
  7.7 1.5 %collective-permute-start.4 = (bf16[2,656,128]{2,1,0:T(8,128)(2,1)S(1)}, bf16[2,656,128]{2,1,0:T(8,128)(2,1)S(1)}, u32[]{:S(2)}, u32[]{:S(2)}) collective-permute-start(bf16[2,656,128]{2,1,0:T(8,128)(2,1)S(1)} %get-tuple-element.11), channel_id=1, source_target_pairs={{0,2},{1,3},{2,0},{3,1},{4,6},{5,7},{6,4},{7,5},{8,10},{9,11},{10,... | collective-permute-start | bytes 1007624 | tf_op jit(solution)/shard_map/ppermute | solution.py:123
  9.7 1.4 %collective-permute-done.1.refs_1_ = bf16[128,1024]{1,0:T(8,128)(2,1)S(1)} collective-permute-done((bf16[128,1024]{1,0:T(8,128)(2,1)}, bf16[128,1024]{1,0:T(8,128)(2,1)S(1)}, u32[]{:S(2)}, u32[]{:S(2)}) %collective-permute-start.1) | collective-permute-done | bytes 262176 | tf_op jit(solution)/shard_map/ppermute | solution.py:123
  11.1 2.0 %collective-permute-start.2 = (bf16[128,1024]{1,0:T(8,128)(2,1)S(1)}, bf16[128,1024]{1,0:T(8,128)(2,1)S(1)}, u32[]{:S(2)}, u32[]{:S(2)}) collective-permute-start(bf16[128,1024]{1,0:T(8,128)(2,1)S(1)} %copy-done.1), channel_id=1, source_target_pairs={{0,4},{1,5},{2,6},{3,7},{4,0},{5,1},{6,2},{7,3},{8,12},{9,13},{10,... | collective-permute-start | bytes 786440 | tf_op jit(solution)/shard_map/ppermute | solution.py:123
  13.1 18.3 %collective-permute-done.2.refs_2_ = bf16[128,1024]{1,0:T(8,128)(2,1)S(1)} collective-permute-done((bf16[128,1024]{1,0:T(8,128)(2,1)S(1)}, bf16[128,1024]{1,0:T(8,128)(2,1)S(1)}, u32[]{:S(2)}, u32[]{:S(2)}) %collective-permute-start.2) | collective-permute-done | bytes 262176 | tf_op jit(solution)/shard_map/ppermute | solution.py:123
  32.8 1.4 %broadcast_select_fusion.1 = (bf16[328,1024]{1,0:T(8,128)(2,1)S(1)}, bf16[328,1024]{1,0:T(8,128)(2,1)S(1)}) fusion(bf16[328,1024]{1,0:T(8,128)(2,1)} %param.12, bf16[328,1024]{1,0:T(8,128)(2,1)} %collective-permute-done, pred[]{:T(512)S(6)} %eq.102), kind=kLoop, calls=%fused_computation.2 | loop fusion | flops 671744 | bytes 2686977 | tf_op jit(solution)/shard_map/jit(_where)/select_n | solution.py:147
  34.2 1.2 %pad_maximum_fusion.wo_ref = bf16[656,1024]{1,0:T(8,128)(2,1)} fusion(bf16[328,1024]{1,0:T(8,128)(2,1)S(1)} %get-tuple-element.19, bf16[328,1024]{1,0:T(8,128)(2,1)S(1)} %get-tuple-element.18), kind=kLoop, calls=%fused_computation | loop fusion | flops 2686976 | bytes 2686976 | tf_op jit(solution)/shard_map/concatenate | solution.py:146
  35.5 4.4 %collective-permute-done.3.refs_3_ = bf16[128,1024]{1,0:T(8,128)(2,1)S(1)} collective-permute-done((bf16[128,1024]{1,0:T(8,128)(2,1)S(1)}, bf16[128,1024]{1,0:T(8,128)(2,1)S(1)}, u32[]{:S(2)}, u32[]{:S(2)}) %collective-permute-start.3) | collective-permute-done | bytes 262176 | tf_op jit(solution)/shard_map/ppermute | solution.py:123
  39.9 6.7 %shard_map.105 = (f32[128,1024]{1,0:T(8,128)S(1)}, bf16[128,1024]{1,0:T(8,128)(2,1)S(1)}, bf16[128,1024]{1,0:T(8,128)(2,1)S(1)}, bf16[128,1024]{1,0:T(8,128)(2,1)S(1)}) custom-call(s32[2]{0:T(128)S(1)} %pad_add_fusion.place_ref, f32[1,1024]{1,0:T(1,128)S(1)} %bitcast.43, bf16[656,1024]{1,0:T(8,128)(2,1)} %pad_maximum_fusion.wo_ref, ...), custom_call_target="tpu_custom_call" | custom-call | tf_op jit(solution)/shard_map/pallas_call | solution.py:153
  46.8 0.9 collective-permute-start.12
  47.6 2.6 %collective-permute-start.13 = (bf16[128,1024]{1,0:T(8,128)(2,1)S(1)}, bf16[128,1024]{1,0:T(8,128)(2,1)S(1)}, u32[]{:S(2)}, u32[]{:S(2)}) collective-permute-start(bf16[128,1024]{1,0:T(8,128)(2,1)S(1)} %get-tuple-element.17), channel_id=1, source_target_pairs={{0,6},{1,7},{2,4},{3,5},{4,2},{5,3},{6,0},{7,1},{8,14},{9,15},{10,... | collective-permute-start | bytes 786440 | tf_op jit(solution)/shard_map/ppermute | solution.py:123
  50.2 5.8 %collective-permute-done.11.refs_0_ = bf16[128,1024]{1,0:T(8,128)(2,1)S(1)} collective-permute-done((bf16[128,1024]{1,0:T(8,128)(2,1)S(1)}, bf16[128,1024]{1,0:T(8,128)(2,1)S(1)}, u32[]{:S(2)}, u32[]{:S(2)}) %collective-permute-start.11) | collective-permute-done | bytes 262176 | tf_op jit(solution)/shard_map/ppermute | solution.py:123
  56.0 3.5 %collective-permute-done.13.refs_2_ = bf16[128,1024]{1,0:T(8,128)(2,1)S(1)} collective-permute-done((bf16[128,1024]{1,0:T(8,128)(2,1)S(1)}, bf16[128,1024]{1,0:T(8,128)(2,1)S(1)}, u32[]{:S(2)}, u32[]{:S(2)}) %collective-permute-start.13) | collective-permute-done | bytes 262176 | tf_op jit(solution)/shard_map/ppermute | solution.py:123
  59.5 1.2 %shard_map.106.refs_0_ = bf16[128,128]{1,0:T(8,128)(2,1)} custom-call(bf16[128,1024]{1,0:T(8,128)(2,1)S(1)} %copy-done.1, f32[1,1024]{1,0:T(1,128)S(1)} %bitcast.44, bf16[1024,128]{1,0:T(8,128)(2,1)S(1)} %copy-done.2, f32[128,1024]{1,0:T(8,128)S(1)} %get-tuple-element.14.own_ref, bf16[128,1024]{1,0:T(8,128)(2,1)S(1)} %collective-permute-done.11.refs_0_, ...), custom_call_target="tpu_custom_call" | custom-call | tf_op jit(solution)/shard_map/pallas_call | solution.py:165
  60.7 1.3 %collective-permute-start.18 = (bf16[128,128]{1,0:T(8,128)(2,1)}, bf16[128,128]{1,0:T(8,128)(2,1)S(1)}, u32[]{:S(2)}, u32[]{:S(2)}) collective-permute-start(bf16[128,128]{1,0:T(8,128)(2,1)} %shard_map.106.refs_0_), channel_id=1, source_target_pairs={{0,2},{1,3},{2,0},{3,1},{4,6},{5,7},{6,4},{7,5},{8,10},{9,11},{10,... | collective-permute-start | bytes 98312 | tf_op jit(solution)/shard_map/ppermute | solution.py:123
  62.0 3.6 %collective-permute-start.16 = (bf16[2,32,128]{2,1,0:T(8,128)(2,1)S(1)}, bf16[2,32,128]{2,1,0:T(8,128)(2,1)S(1)}, u32[]{:S(2)}, u32[]{:S(2)}) collective-permute-start(bf16[2,32,128]{2,1,0:T(8,128)(2,1)S(1)} %copy-done.6), channel_id=1, source_target_pairs={{0,24},{8,16},{16,8},{24,0},{1,25},{9,17},{17,9},{25,1},{2,26},{10... | collective-permute-start | bytes 49160 | tf_op jit(solution)/shard_map/ppermute | solution.py:123
  65.6 0.8 collective-permute-start.15
  66.5 1.0 %collective-permute-done.16 = bf16[2,32,128]{2,1,0:T(8,128)(2,1)S(1)} collective-permute-done((bf16[2,32,128]{2,1,0:T(8,128)(2,1)S(1)}, bf16[2,32,128]{2,1,0:T(8,128)(2,1)S(1)}, u32[]{:S(2)}, u32[]{:S(2)}) %collective-permute-start.16) | collective-permute-done | bytes 16416 | tf_op jit(solution)/shard_map/ppermute | solution.py:123
  67.5 1.9 %collective-permute-done.14 = bf16[2,32,128]{2,1,0:T(8,128)(2,1)S(1)} collective-permute-done((bf16[2,32,128]{2,1,0:T(8,128)(2,1)S(1)}, bf16[2,32,128]{2,1,0:T(8,128)(2,1)S(1)}, u32[]{:S(2)}, u32[]{:S(2)}) %collective-permute-start.14) | collective-permute-done | bytes 16416 | tf_op jit(solution)/shard_map/ppermute | solution.py:123
  70.2 1.3 %collective-permute-start.22 = (bf16[128,128]{1,0:T(8,128)(2,1)}, bf16[128,128]{1,0:T(8,128)(2,1)S(1)}, u32[]{:S(2)}, u32[]{:S(2)}) collective-permute-start(bf16[128,128]{1,0:T(8,128)(2,1)} %shard_map.106.refs_0_), channel_id=1, source_target_pairs={{0,6},{1,7},{2,4},{3,5},{4,2},{5,3},{6,0},{7,1},{8,14},{9,15},{10,... | collective-permute-start | bytes 98312 | tf_op jit(solution)/shard_map/ppermute | solution.py:123
  71.5 2.3 %collective-permute-start.23 = (bf16[128,128]{1,0:T(8,128)(2,1)}, bf16[128,128]{1,0:T(8,128)(2,1)S(1)}, u32[]{:S(2)}, u32[]{:S(2)}) collective-permute-start(bf16[128,128]{1,0:T(8,128)(2,1)} %shard_map.106.refs_0_), channel_id=1, source_target_pairs={{0,7},{1,6},{2,5},{3,4},{4,3},{5,2},{6,1},{7,0},{8,15},{9,14},{10,... | collective-permute-start | bytes 98312 | tf_op jit(solution)/shard_map/ppermute | solution.py:123
  74.1 1.2 %collective-permute-done.22.refs_6_ = bf16[128,128]{1,0:T(8,128)(2,1)S(1)} collective-permute-done((bf16[128,128]{1,0:T(8,128)(2,1)}, bf16[128,128]{1,0:T(8,128)(2,1)S(1)}, u32[]{:S(2)}, u32[]{:S(2)}) %collective-permute-start.22) | collective-permute-done | bytes 32800 | tf_op jit(solution)/shard_map/ppermute | solution.py:123
  76.0 0.8 copy-done.3
  76.7 1.3 %shard_map.107 = f32[4,8]{1,0:T(4,128)S(1)} custom-call(s32[1]{0:T(128)} %bitcast.4.place_ref, s32[4]{0:T(128)S(1)} %bitcast.45, bf16[256,128]{1,0:T(8,128)(2,1)S(1)} %pad_maximum_fusion.1.query_ref, bf16[128,128]{1,0:T(8,128)(2,1)S(1)} %copy-done.3, bf16[128,128]{1,0:T(8,128)(2,1)S(1)} %collective-permute-done.17.refs_1_, ...), custom_call_target="tpu_custom_call" | custom-call | tf_op jit(solution)/shard_map/pallas_call | solution.py:176
  78.1 3.3 %collective-permute-start.24 = (f32[4,2]{1,0:T(4,128)S(1)}, f32[4,2]{1,0:T(4,128)S(1)}, u32[]{:S(2)}, u32[]{:S(2)}) collective-permute-start(f32[4,2]{1,0:T(4,128)S(1)} %get-tuple-element.24), channel_id=1, source_target_pairs={{0,24},{8,16},{16,8},{24,0},{1,25},{9,17},{17,9},{25,1},{2,26},{10... | collective-permute-start | bytes 104 | tf_op jit(solution)/shard_map/ppermute | solution.py:123
  81.5 1.0 %collective-permute-start.26 = (f32[4,2]{1,0:T(4,128)S(1)}, f32[4,2]{1,0:T(4,128)S(1)}, u32[]{:S(2)}, u32[]{:S(2)}) collective-permute-start(f32[4,2]{1,0:T(4,128)S(1)} %get-tuple-element.25), channel_id=1, source_target_pairs={{0,8},{8,0},{16,24},{24,16},{1,9},{9,1},{17,25},{25,17},{2,10},{10... | collective-permute-start | bytes 104 | tf_op jit(solution)/shard_map/ppermute | solution.py:123
  82.5 1.0 %collective-permute-done.24 = f32[4,2]{1,0:T(4,128)S(1)} collective-permute-done((f32[4,2]{1,0:T(4,128)S(1)}, f32[4,2]{1,0:T(4,128)S(1)}, u32[]{:S(2)}, u32[]{:S(2)}) %collective-permute-start.24) | collective-permute-done | bytes 64 | tf_op jit(solution)/shard_map/ppermute | solution.py:123
  83.5 2.4 %collective-permute-done.25 = f32[4,2]{1,0:T(4,128)S(1)} collective-permute-done((f32[4,2]{1,0:T(4,128)S(1)}, f32[4,2]{1,0:T(4,128)S(1)}, u32[]{:S(2)}, u32[]{:S(2)}) %collective-permute-start.25) | collective-permute-done | bytes 64 | tf_op jit(solution)/shard_map/ppermute | solution.py:123
  85.9 0.7 compare_select_fusion.15
  (55 shorter events, 4.9 us)
Async XLA Ops:
  0.6 31.7 %collective-permute-start = (bf16[328,1024]{1,0:T(8,128)(2,1)}, bf16[328,1024]{1,0:T(8,128)(2,1)}, u32[]{:S(2)}, u32[]{:S(2)}) collective-permute-start(bf16[328,1024]{1,0:T(8,128)(2,1)} %param.12), channel_id=1, source_target_pairs={{0,1},{1,0},{2,3},{3,2},{4,5},{5,4},{6,7},{7,6},{8,9},{9,8},{10,11... | collective-permute-start | bytes 2015240 | tf_op jit(solution)/shard_map/ppermute | solution.py:123
  1.1 9.9 %collective-permute-start.1 = (bf16[128,1024]{1,0:T(8,128)(2,1)}, bf16[128,1024]{1,0:T(8,128)(2,1)S(1)}, u32[]{:S(2)}, u32[]{:S(2)}) collective-permute-start(bf16[128,1024]{1,0:T(8,128)(2,1)} %tokens_ref.1), channel_id=1, source_target_pairs={{0,2},{1,3},{2,0},{3,1},{4,6},{5,7},{6,4},{7,5},{8,10},{9,11},{10,... | collective-permute-start | bytes 786440 | tf_op jit(solution)/shard_map/ppermute | solution.py:123
  6.2 25.6 %collective-permute-start.6 = (bf16[2,656,128]{2,1,0:T(8,128)(2,1)S(1)}, bf16[2,656,128]{2,1,0:T(8,128)(2,1)S(1)}, u32[]{:S(2)}, u32[]{:S(2)}) collective-permute-start(bf16[2,656,128]{2,1,0:T(8,128)(2,1)S(1)} %get-tuple-element.13), channel_id=1, source_target_pairs={{0,6},{1,7},{2,4},{3,5},{4,2},{5,3},{6,0},{7,1},{8,14},{9,15},{10,... | collective-permute-start | bytes 1007624 | tf_op jit(solution)/shard_map/ppermute | solution.py:123
  7.7 24.1 %collective-permute-start.4 = (bf16[2,656,128]{2,1,0:T(8,128)(2,1)S(1)}, bf16[2,656,128]{2,1,0:T(8,128)(2,1)S(1)}, u32[]{:S(2)}, u32[]{:S(2)}) collective-permute-start(bf16[2,656,128]{2,1,0:T(8,128)(2,1)S(1)} %get-tuple-element.11), channel_id=1, source_target_pairs={{0,2},{1,3},{2,0},{3,1},{4,6},{5,7},{6,4},{7,5},{8,10},{9,11},{10,... | collective-permute-start | bytes 1007624 | tf_op jit(solution)/shard_map/ppermute | solution.py:123
  9.2 23.1 %collective-permute-start.5 = (bf16[2,656,128]{2,1,0:T(8,128)(2,1)S(1)}, bf16[2,656,128]{2,1,0:T(8,128)(2,1)S(1)}, u32[]{:S(2)}, u32[]{:S(2)}) collective-permute-start(bf16[2,656,128]{2,1,0:T(8,128)(2,1)S(1)} %get-tuple-element.12), channel_id=1, source_target_pairs={{0,4},{1,5},{2,6},{3,7},{4,0},{5,1},{6,2},{7,3},{8,12},{9,13},{10,... | collective-permute-start | bytes 1007624 | tf_op jit(solution)/shard_map/ppermute | solution.py:123
  11.1 20.3 %collective-permute-start.2 = (bf16[128,1024]{1,0:T(8,128)(2,1)S(1)}, bf16[128,1024]{1,0:T(8,128)(2,1)S(1)}, u32[]{:S(2)}, u32[]{:S(2)}) collective-permute-start(bf16[128,1024]{1,0:T(8,128)(2,1)S(1)} %copy-done.1), channel_id=1, source_target_pairs={{0,4},{1,5},{2,6},{3,7},{4,0},{5,1},{6,2},{7,3},{8,12},{9,13},{10,... | collective-permute-start | bytes 786440 | tf_op jit(solution)/shard_map/ppermute | solution.py:123
  31.4 8.4 %collective-permute-start.3 = (bf16[128,1024]{1,0:T(8,128)(2,1)S(1)}, bf16[128,1024]{1,0:T(8,128)(2,1)S(1)}, u32[]{:S(2)}, u32[]{:S(2)}) collective-permute-start(bf16[128,1024]{1,0:T(8,128)(2,1)S(1)} %copy-done.1), channel_id=1, source_target_pairs={{0,6},{1,7},{2,4},{3,5},{4,2},{5,3},{6,0},{7,1},{8,14},{9,15},{10,... | collective-permute-start | bytes 786440 | tf_op jit(solution)/shard_map/ppermute | solution.py:123
  31.8 8.1 %collective-permute-start.7 = (bf16[2,656,128]{2,1,0:T(8,128)(2,1)S(1)}, bf16[2,656,128]{2,1,0:T(8,128)(2,1)S(1)}, u32[]{:S(2)}, u32[]{:S(2)}) collective-permute-start(bf16[2,656,128]{2,1,0:T(8,128)(2,1)S(1)} %get-tuple-element.10.refs_4_), channel_id=1, source_target_pairs={{0,1},{1,0},{2,3},{3,2},{4,5},{5,4},{6,7},{7,6},{8,9},{9,8},{10,11... | collective-permute-start | bytes 1007624 | tf_op jit(solution)/shard_map/ppermute | solution.py:123
  31.8 8.1 %collective-permute-start.10 = (bf16[2,656,128]{2,1,0:T(8,128)(2,1)S(1)}, bf16[2,656,128]{2,1,0:T(8,128)(2,1)S(1)}, u32[]{:S(2)}, u32[]{:S(2)}) collective-permute-start(bf16[2,656,128]{2,1,0:T(8,128)(2,1)S(1)} %collective-permute-done.6.refs_7_), channel_id=1, source_target_pairs={{0,1},{1,0},{2,3},{3,2},{4,5},{5,4},{6,7},{7,6},{8,9},{9,8},{10,11... | collective-permute-start | bytes 1007624 | tf_op jit(solution)/shard_map/ppermute | solution.py:123
  32.3 7.6 %collective-permute-start.8 = (bf16[2,656,128]{2,1,0:T(8,128)(2,1)S(1)}, bf16[2,656,128]{2,1,0:T(8,128)(2,1)S(1)}, u32[]{:S(2)}, u32[]{:S(2)}) collective-permute-start(bf16[2,656,128]{2,1,0:T(8,128)(2,1)S(1)} %collective-permute-done.4.refs_5_), channel_id=1, source_target_pairs={{0,1},{1,0},{2,3},{3,2},{4,5},{5,4},{6,7},{7,6},{8,9},{9,8},{10,11... | collective-permute-start | bytes 1007624 | tf_op jit(solution)/shard_map/ppermute | solution.py:123
  32.4 7.5 %collective-permute-start.9 = (bf16[2,656,128]{2,1,0:T(8,128)(2,1)S(1)}, bf16[2,656,128]{2,1,0:T(8,128)(2,1)S(1)}, u32[]{:S(2)}, u32[]{:S(2)}) collective-permute-start(bf16[2,656,128]{2,1,0:T(8,128)(2,1)S(1)} %collective-permute-done.5.refs_6_), channel_id=1, source_target_pairs={{0,1},{1,0},{2,3},{3,2},{4,5},{5,4},{6,7},{7,6},{8,9},{9,8},{10,11... | collective-permute-start | bytes 1007624 | tf_op jit(solution)/shard_map/ppermute | solution.py:123
  39.9 19.6 %copy-start.2 = (bf16[1024,128]{1,0:T(8,128)(2,1)S(1)}, bf16[1024,128]{1,0:T(8,128)(2,1)}, u32[]{:S(2)}) copy-start(bf16[1024,128]{1,0:T(8,128)(2,1)} %proj_ref.1) | copy-start | bytes 786436
  39.9 19.6 %copy-start.5 = (f32[1024]{0:T(1024)S(1)}, f32[1024]{0:T(1024)}, u32[]{:S(2)}) copy-start(f32[1024]{0:T(1024)} %param.13) | copy-start | bytes 12292
  46.6 15.3 %copy-start.6 = (bf16[2,32,128]{2,1,0:T(8,128)(2,1)S(1)}, bf16[2,32,128]{2,1,0:T(8,128)(2,1)}, u32[]{:S(2)}) copy-start(bf16[2,32,128]{2,1,0:T(8,128)(2,1)} %param.15) | copy-start | bytes 49156
  46.7 19.7 %copy-start.8 = (s32[1,4]{1,0:T(1,128)S(1)}, s32[1,4]{1,0:T(1,128)}, u32[]{:S(2)}) copy-start(s32[1,4]{1,0:T(1,128)} %param.16) | copy-start | bytes 52
  46.7 39.3 %copy-start.7 = (s32[2,100]{1,0:T(2,128)S(1)}, s32[2,100]{1,0:T(2,128)}, u32[]{:S(2)}) copy-start(s32[2,100]{1,0:T(2,128)} %param.17) | copy-start | bytes 2404
  46.7 9.3 %collective-permute-start.11 = (bf16[128,1024]{1,0:T(8,128)(2,1)S(1)}, bf16[128,1024]{1,0:T(8,128)(2,1)S(1)}, u32[]{:S(2)}, u32[]{:S(2)}) collective-permute-start(bf16[128,1024]{1,0:T(8,128)(2,1)S(1)} %get-tuple-element.15), channel_id=1, source_target_pairs={{0,2},{1,3},{2,0},{3,1},{4,6},{5,7},{6,4},{7,5},{8,10},{9,11},{10,... | collective-permute-start | bytes 786440 | tf_op jit(solution)/shard_map/ppermute | solution.py:123
  46.8 9.2 %collective-permute-start.12 = (bf16[128,1024]{1,0:T(8,128)(2,1)S(1)}, bf16[128,1024]{1,0:T(8,128)(2,1)S(1)}, u32[]{:S(2)}, u32[]{:S(2)}) collective-permute-start(bf16[128,1024]{1,0:T(8,128)(2,1)S(1)} %get-tuple-element.16), channel_id=1, source_target_pairs={{0,4},{1,5},{2,6},{3,7},{4,0},{5,1},{6,2},{7,3},{8,12},{9,13},{10,... | collective-permute-start | bytes 786440 | tf_op jit(solution)/shard_map/ppermute | solution.py:123
  47.6 11.9 %collective-permute-start.13 = (bf16[128,1024]{1,0:T(8,128)(2,1)S(1)}, bf16[128,1024]{1,0:T(8,128)(2,1)S(1)}, u32[]{:S(2)}, u32[]{:S(2)}) collective-permute-start(bf16[128,1024]{1,0:T(8,128)(2,1)S(1)} %get-tuple-element.17), channel_id=1, source_target_pairs={{0,6},{1,7},{2,4},{3,5},{4,2},{5,3},{6,0},{7,1},{8,14},{9,15},{10,... | collective-permute-start | bytes 786440 | tf_op jit(solution)/shard_map/ppermute | solution.py:123
  60.7 9.5 %collective-permute-start.17 = (bf16[128,128]{1,0:T(8,128)(2,1)}, bf16[128,128]{1,0:T(8,128)(2,1)S(1)}, u32[]{:S(2)}, u32[]{:S(2)}) collective-permute-start(bf16[128,128]{1,0:T(8,128)(2,1)} %shard_map.106.refs_0_), channel_id=1, source_target_pairs={{0,1},{1,0},{2,3},{3,2},{4,5},{5,4},{6,7},{7,6},{8,9},{9,8},{10,11... | collective-permute-start | bytes 98312 | tf_op jit(solution)/shard_map/ppermute | solution.py:123
  60.7 10.8 %collective-permute-start.18 = (bf16[128,128]{1,0:T(8,128)(2,1)}, bf16[128,128]{1,0:T(8,128)(2,1)S(1)}, u32[]{:S(2)}, u32[]{:S(2)}) collective-permute-start(bf16[128,128]{1,0:T(8,128)(2,1)} %shard_map.106.refs_0_), channel_id=1, source_target_pairs={{0,2},{1,3},{2,0},{3,1},{4,6},{5,7},{6,4},{7,5},{8,10},{9,11},{10,... | collective-permute-start | bytes 98312 | tf_op jit(solution)/shard_map/ppermute | solution.py:123
  62.0 5.5 %collective-permute-start.16 = (bf16[2,32,128]{2,1,0:T(8,128)(2,1)S(1)}, bf16[2,32,128]{2,1,0:T(8,128)(2,1)S(1)}, u32[]{:S(2)}, u32[]{:S(2)}) collective-permute-start(bf16[2,32,128]{2,1,0:T(8,128)(2,1)S(1)} %copy-done.6), channel_id=1, source_target_pairs={{0,24},{8,16},{16,8},{24,0},{1,25},{9,17},{17,9},{25,1},{2,26},{10... | collective-permute-start | bytes 49160 | tf_op jit(solution)/shard_map/ppermute | solution.py:123
  65.6 3.8 %collective-permute-start.14 = (bf16[2,32,128]{2,1,0:T(8,128)(2,1)S(1)}, bf16[2,32,128]{2,1,0:T(8,128)(2,1)S(1)}, u32[]{:S(2)}, u32[]{:S(2)}) collective-permute-start(bf16[2,32,128]{2,1,0:T(8,128)(2,1)S(1)} %copy-done.6), channel_id=1, source_target_pairs={{0,8},{8,0},{16,24},{24,16},{1,9},{9,1},{17,25},{25,17},{2,10},{10... | collective-permute-start | bytes 49160 | tf_op jit(solution)/shard_map/ppermute | solution.py:123
  65.6 4.6 %collective-permute-start.15 = (bf16[2,32,128]{2,1,0:T(8,128)(2,1)S(1)}, bf16[2,32,128]{2,1,0:T(8,128)(2,1)S(1)}, u32[]{:S(2)}, u32[]{:S(2)}) collective-permute-start(bf16[2,32,128]{2,1,0:T(8,128)(2,1)S(1)} %copy-done.6), channel_id=1, source_target_pairs={{0,16},{8,24},{16,0},{24,8},{1,17},{9,25},{17,1},{25,9},{2,18},{10... | collective-permute-start | bytes 49160 | tf_op jit(solution)/shard_map/ppermute | solution.py:123
  67.5 6.3 %collective-permute-start.19 = (bf16[128,128]{1,0:T(8,128)(2,1)}, bf16[128,128]{1,0:T(8,128)(2,1)S(1)}, u32[]{:S(2)}, u32[]{:S(2)}) collective-permute-start(bf16[128,128]{1,0:T(8,128)(2,1)} %shard_map.106.refs_0_), channel_id=1, source_target_pairs={{0,3},{1,2},{2,1},{3,0},{4,7},{5,6},{6,5},{7,4},{8,11},{9,10},{10,... | collective-permute-start | bytes 98312 | tf_op jit(solution)/shard_map/ppermute | solution.py:123
  69.4 4.4 %collective-permute-start.20 = (bf16[128,128]{1,0:T(8,128)(2,1)}, bf16[128,128]{1,0:T(8,128)(2,1)S(1)}, u32[]{:S(2)}, u32[]{:S(2)}) collective-permute-start(bf16[128,128]{1,0:T(8,128)(2,1)} %shard_map.106.refs_0_), channel_id=1, source_target_pairs={{0,4},{1,5},{2,6},{3,7},{4,0},{5,1},{6,2},{7,3},{8,12},{9,13},{10,... | collective-permute-start | bytes 98312 | tf_op jit(solution)/shard_map/ppermute | solution.py:123
  70.2 3.9 %collective-permute-start.21 = (bf16[128,128]{1,0:T(8,128)(2,1)}, bf16[128,128]{1,0:T(8,128)(2,1)S(1)}, u32[]{:S(2)}, u32[]{:S(2)}) collective-permute-start(bf16[128,128]{1,0:T(8,128)(2,1)} %shard_map.106.refs_0_), channel_id=1, source_target_pairs={{0,5},{1,4},{2,7},{3,6},{4,1},{5,0},{6,3},{7,2},{8,13},{9,12},{10,... | collective-permute-start | bytes 98312 | tf_op jit(solution)/shard_map/ppermute | solution.py:123
  70.2 5.1 %collective-permute-start.22 = (bf16[128,128]{1,0:T(8,128)(2,1)}, bf16[128,128]{1,0:T(8,128)(2,1)S(1)}, u32[]{:S(2)}, u32[]{:S(2)}) collective-permute-start(bf16[128,128]{1,0:T(8,128)(2,1)} %shard_map.106.refs_0_), channel_id=1, source_target_pairs={{0,6},{1,7},{2,4},{3,5},{4,2},{5,3},{6,0},{7,1},{8,14},{9,15},{10,... | collective-permute-start | bytes 98312 | tf_op jit(solution)/shard_map/ppermute | solution.py:123
  71.5 4.5 %collective-permute-start.23 = (bf16[128,128]{1,0:T(8,128)(2,1)}, bf16[128,128]{1,0:T(8,128)(2,1)S(1)}, u32[]{:S(2)}, u32[]{:S(2)}) collective-permute-start(bf16[128,128]{1,0:T(8,128)(2,1)} %shard_map.106.refs_0_), channel_id=1, source_target_pairs={{0,7},{1,6},{2,5},{3,4},{4,3},{5,2},{6,1},{7,0},{8,15},{9,14},{10,... | collective-permute-start | bytes 98312 | tf_op jit(solution)/shard_map/ppermute | solution.py:123
  78.1 5.4 %collective-permute-start.24 = (f32[4,2]{1,0:T(4,128)S(1)}, f32[4,2]{1,0:T(4,128)S(1)}, u32[]{:S(2)}, u32[]{:S(2)}) collective-permute-start(f32[4,2]{1,0:T(4,128)S(1)} %get-tuple-element.24), channel_id=1, source_target_pairs={{0,24},{8,16},{16,8},{24,0},{1,25},{9,17},{17,9},{25,1},{2,26},{10... | collective-permute-start | bytes 104 | tf_op jit(solution)/shard_map/ppermute | solution.py:123
  81.4 4.5 %collective-permute-start.25 = (f32[4,2]{1,0:T(4,128)S(1)}, f32[4,2]{1,0:T(4,128)S(1)}, u32[]{:S(2)}, u32[]{:S(2)}) collective-permute-start(f32[4,2]{1,0:T(4,128)S(1)} %get-tuple-element.26), channel_id=1, source_target_pairs={{0,16},{8,24},{16,0},{24,8},{1,17},{9,25},{17,1},{25,9},{2,18},{10... | collective-permute-start | bytes 104 | tf_op jit(solution)/shard_map/ppermute | solution.py:123
  81.5 4.4 %collective-permute-start.26 = (f32[4,2]{1,0:T(4,128)S(1)}, f32[4,2]{1,0:T(4,128)S(1)}, u32[]{:S(2)}, u32[]{:S(2)}) collective-permute-start(f32[4,2]{1,0:T(4,128)S(1)} %get-tuple-element.25), channel_id=1, source_target_pairs={{0,8},{8,0},{16,24},{24,16},{1,9},{9,1},{17,25},{25,17},{2,10},{10... | collective-permute-start | bytes 104 | tf_op jit(solution)/shard_map/ppermute | solution.py:123
  (4 other events, 13.7 us)

commit v2 on v1

v2 whole, which is shorter than its diff:
```python
import functools

import jax
import jax.numpy as jnp
from jax import lax
from jax.experimental import pallas as pl
from jax.experimental.pallas import tpu as pltpu
from jax.sharding import PartitionSpec as P

VMEM_LIMIT = 20 * 1024 * 1024


def norm_rows(values, gain_row):
    center = jnp.mean(values, axis=-1, keepdims=True)
    shifted = values - center
    spread = jnp.mean(shifted * shifted, axis=-1, keepdims=True)
    return (shifted * lax.rsqrt(spread + 1e-05) * gain_row).astype(jnp.bfloat16)


def dot_nt(left, right):
    return lax.dot_general(
        left, right, (((1,), (1,)), ((), ())), preferred_element_type=jnp.float32
    )


def split_kernel(chips, place_ref, wi_ref, *refs):
    pieces, turned = refs[:chips], refs[chips]
    columns = wi_ref.shape[1]
    width = columns // 2
    part = width // chips
    chip = place_ref[0]
    for start in range(0, columns, 128):
        turned[start : start + 128, :] = wi_ref[:, start : start + 128].T
    for step in range(chips):
        target = chip ^ step
        for half in range(2):
            first = pl.multiple_of(half * width + target * part, 16)
            pieces[step][half] = turned[pl.ds(first, part), :]


def join_kernel(chips, place_ref, wo_mine, wo_other, *refs):
    mine, other = refs[:chips], refs[chips : 2 * chips]
    gelu_w, gate_w, wo_part = refs[2 * chips :]
    chip, core = place_ref[0], place_ref[1]
    rows = wo_mine.shape[0]
    for first, upper, lower in ((0, wo_mine, wo_other), (1, wo_other, wo_mine)):

        @pl.when(core == first)
        def _(upper=upper, lower=lower):
            wo_part[:rows] = upper[...]
            wo_part[rows:] = lower[...]

    for step in range(chips):
        source = (chip ^ step) * 2
        for block, at in ((mine[step], source + core), (other[step], source + 1 - core)):
            columns = pl.ds(pl.multiple_of(at * 128, 128), 128)
            gelu_w[:, columns] = block[0]
            gate_w[:, columns] = block[1]


def ffn_kernel(gain_ref, gelu_w, gate_w, wo_part, tokens_ref, out_ref):
    normed = norm_rows(tokens_ref[...].astype(jnp.float32), gain_ref[...])
    first = dot_nt(normed, gelu_w[...])
    second = dot_nt(normed, gate_w[...])
    hidden = (0.5 * first * (1.0 + lax.erf(first * 0.7071067811865476)) * second).astype(jnp.bfloat16)
    out_ref[...] = jnp.dot(hidden, wo_part[...], preferred_element_type=jnp.float32).astype(
        out_ref.dtype
    )


def finish_kernel(chips, docs, place_ref, ends_ref, tokens_ref, gain_ref, proj_ref, own_ref, *refs):
    parts, refs = refs[: chips - 1], refs[chips - 1 :]
    queries, (vectors_ref, out_ref) = refs[:-2], refs[-2:]
    mixed = tokens_ref[...].astype(jnp.float32) + own_ref[...]
    for part in parts:
        mixed = mixed + part[...].astype(jnp.float32)
    final = norm_rows(mixed, gain_ref[...])
    projected = jnp.dot(final, proj_ref[...], preferred_element_type=jnp.float32)
    total = jnp.sum(projected * projected, axis=-1, keepdims=True)
    vectors = (projected * lax.rsqrt(total + 1e-06)).astype(jnp.bfloat16)
    vectors_ref[...] = vectors
    group, me = place_ref[0], place_ref[1]
    devices = 2 * chips
    rows = vectors.shape[0]
    block_rows = queries[0].shape[0]
    groups = out_ref.shape[0] // devices
    together = 128 // (block_rows // groups)
    spot = me * rows + lax.broadcasted_iota(jnp.int32, (rows, block_rows), 0)
    inside, low = [], jnp.int32(0)
    for doc in range(docs):
        high = ends_ref[doc]
        inside.append((spot >= low) & (spot < high))
        low = high
    for mask, block in enumerate(queries):
        similar = dot_nt(vectors, block[...])
        best = [
            jnp.max(jnp.where(inside[doc], similar, -jnp.inf), axis=0, keepdims=True)
            for doc in range(docs)
        ]
        best = jnp.concatenate(best, axis=0).astype(jnp.bfloat16)
        for far in range(groups):
            tile = far // together
            out_ref[(group ^ far) * devices + (me ^ mask)] = best[:, tile * 128 : (tile + 1) * 128]


def pick_kernel(query_len, place_ref, cand_ref, best_ref, out_ref):
    group = place_ref[0]
    groups, devices, docs, lanes = best_ref.shape
    own, listed = cand_ref.shape
    together = lanes // (own * query_len)
    scores = [jnp.zeros((1, listed), jnp.float32) for _ in range(own)]
    lane = lax.broadcasted_iota(jnp.int32, (docs, lanes), 1)
    label = lax.broadcasted_iota(jnp.int32, (docs, listed), 0)
    for far in range(groups):
        best = jnp.max(best_ref[far].astype(jnp.float32), axis=0)
        offset = ((group ^ far) % together) * own * query_len
        for query in range(own):
            start = offset + query * query_len
            taken = jnp.where((lane >= start) & (lane < start + query_len), best, 0.0)
            value = jnp.sum(taken, axis=1, keepdims=True) / query_len
            wanted = cand_ref[query : query + 1, :] - far * docs
            scores[query] += jnp.sum(jnp.where(wanted == label, value, 0.0), axis=0, keepdims=True)
    for query in range(own):
        out_ref[query : query + 1, :] = scores[query]


def body(
    corpus_tokens,
    norm_gain,
    wi_weight,
    wo_weight,
    final_gain,
    proj_weight,
    query_vectors,
    doc_lengths,
    candidates,
):
    groups = lax.axis_size("group")
    devices = lax.axis_size("dev")
    chips = devices // 2
    rows, width = corpus_tokens.shape
    part = wo_weight.shape[0] * 2
    me = lax.axis_index("dev").astype(jnp.int32)
    place = jnp.stack([me // 2, me % 2])
    smem = pl.BlockSpec(memory_space=pltpu.SMEM)
    vmem = pl.BlockSpec(memory_space=pltpu.VMEM)
    params = pltpu.CompilerParams(vmem_limit_bytes=VMEM_LIMIT)

    def swap(values, mask, axis="dev"):
        size = devices if axis == "dev" else groups
        return lax.ppermute(values, axis, [(i, i ^ mask) for i in range(size)])

    per_query, query_len, vector_dim = query_vectors.shape
    query_own = query_vectors.reshape(-1, vector_dim)
    wo_other = swap(wo_weight, 1)
    tokens = [corpus_tokens] + [swap(corpus_tokens, 2 * step) for step in range(1, chips)]
    weight_shapes = [
        jax.ShapeDtypeStruct((part, width), jnp.bfloat16),
        jax.ShapeDtypeStruct((part, width), jnp.bfloat16),
        jax.ShapeDtypeStruct((part, wo_weight.shape[1]), jnp.bfloat16),
    ]
    if wi_weight.shape[0] == 128 and part % 16 == 0:
        pieces = pl.pallas_call(
            functools.partial(split_kernel, chips),
            out_shape=[jax.ShapeDtypeStruct((2, part, 128), jnp.bfloat16)] * chips,
            in_specs=[smem, vmem],
            out_specs=[vmem] * chips,
            scratch_shapes=[pltpu.VMEM((wi_weight.shape[1], 128), jnp.bfloat16)],
            compiler_params=params,
        )(place, wi_weight)
        mine = [pieces[0]] + [swap(pieces[step], 2 * step) for step in range(1, chips)]
        mine[1], tokens[1], tokens[2], query_own = lax.optimization_barrier(
            (mine[1], tokens[1], tokens[2], query_own)
        )
        other = [swap(piece, 1) for piece in mine]
        weights = pl.pallas_call(
            functools.partial(join_kernel, chips),
            out_shape=weight_shapes,
            in_specs=[smem] + [vmem] * (2 + 2 * chips),
            out_specs=[vmem] * 3,
            compiler_params=params,
        )(place, wo_weight, wo_other, *mine, *other)
    else:
        whole = lax.all_gather(wi_weight, "dev", axis=0, tiled=True).reshape(width, 2, chips, part)
        columns = lax.dynamic_index_in_dim(whole, me // 2, 2, keepdims=False)
        even = (me % 2) == 0
        wo_part = jnp.concatenate(
            [jnp.where(even, wo_weight, wo_other), jnp.where(even, wo_other, wo_weight)], axis=0
        )
        weights = [columns[:, 0].T, columns[:, 1].T, wo_part]

    line = jnp.concatenate(
        [query_own] + [swap(query_own, mask, "group") for mask in range(1, groups)], axis=0
    )
    plane = jnp.stack([line] + [swap(line, 2 * step) for step in range(1, chips)])
    beside = swap(plane, 1)
    queries = [(plane, beside)[mask % 2][mask // 2] for mask in range(devices)]

    partial = [None] * chips
    for step in list(range(1, chips)) + [0]:
        partial[step] = pl.pallas_call(
            ffn_kernel,
            out_shape=jax.ShapeDtypeStruct((rows, width), jnp.bfloat16 if step else jnp.float32),
            in_specs=[vmem] * 5,
            out_specs=vmem,
            compiler_params=params,
        )(norm_gain.reshape(1, -1), *weights, tokens[step])
    arrived = [swap(partial[step], 2 * step) for step in range(1, chips)]

    docs = doc_lengths.shape[1]
    home = jnp.stack([lax.axis_index("group").astype(jnp.int32), me])
    vectors, best = pl.pallas_call(
        functools.partial(finish_kernel, chips, docs),
        out_shape=[
            jax.ShapeDtypeStruct((rows, proj_weight.shape[1]), jnp.bfloat16),
            jax.ShapeDtypeStruct((groups * devices, docs, 128), jnp.bfloat16),
        ],
        in_specs=[smem, smem] + [vmem] * (4 + chips - 1 + devices),
        out_specs=[vmem, vmem],
        compiler_params=params,
    )(
        home,
        jnp.cumsum(doc_lengths[0]),
        corpus_tokens,
        final_gain.reshape(1, -1),
        proj_weight,
        partial[0],
        *arrived,
        *queries,
    )
    met = lax.all_to_all(best, ("group", "dev"), split_axis=0, concat_axis=0, tiled=True)
    scores = pl.pallas_call(
        functools.partial(pick_kernel, query_len),
        out_shape=jax.ShapeDtypeStruct(candidates.shape, jnp.float32),
        in_specs=[smem, vmem, vmem],
        out_specs=vmem,
        compiler_params=params,
    )(home, candidates, met.reshape(groups, devices, docs, 128))
    return (vectors, scores)


def solution(mesh):
    placed = (
        P(("group", "dev"), None),
        P(),
        P("dev", None),
        P("dev", None),
        P(),
        P(),
        P(("group", "dev"), None, None),
        P("group", None),
        P(("group", "dev"), None),
    )
    return jax.shard_map(
        body,
        mesh=mesh,
        in_specs=placed,
        out_specs=(P(("group", "dev"), None), P(("group", "dev"), None)),
        check_vma=False,
    )
```

time: 86.9 us -> 99.6 us (1.15)
  local copies, waits for them, and re-layouts: 2.22 us -> 19.3 us
  waiting for transfers between devices: 42.1 us -> 27.6 us
  blocking collectives: 0 us -> 12.1 us
  starting transfers between devices: 27.7 us -> 23.1 us
  Pallas kernels: 10.3 us -> 14.8 us
  other arithmetic: 3.57 us -> 1.07 us
    unnamed x18 -> x67, local copies, waits for them, and re-layouts: 2.13 us -> 18.4 us
    ppermute x27 -> x21, waiting for transfers between devices: 42.1 us -> 27.6 us  [swap(): return lax.ppermute(values, axis, [(i, i ^ mask) for i in range(size)])]
    all_to_all x0 -> x1, blocking collectives: none -> 12.1 us  [body(): lax.all_to_all(best, ('group', 'dev'), split_axis=0, concat_axis=0, tiled...]
    ppermute x27 -> x21, starting transfers between devices: 27.7 us -> 23.1 us  [swap(): return lax.ppermute(values, axis, [(i, i ^ mask) for i in range(size)])]
    pallas_call x3 -> x7, Pallas kernels: 9.27 us -> 13.8 us  [the longest x4 8.56 us: body(): pl.pallas_call(ffn_kernel, out_shape=jax.ShapeDtypeStruct((rows, width),...]
    select_n x2 -> x0, other arithmetic: 2.07 us -> none  [the longest x1 1.39 us: body(): jnp.where(even, wo_weight, wo_other)]
    concatenate x2 -> x0, other arithmetic: 1.24 us -> none  [the longest x1 1.24 us: body(): jnp.concatenate([jnp.where(even, wo_weight, wo_other), jnp.where(even, wo...]
  transfers between devices with their start and end apart: 27 -> 21, of which waited for: 13 -> 7; matrix products, arithmetic and copies ran while one was open for 3% -> 2% of each run, Pallas kernels for 1% -> 10%
where the time goes in v2:
time: 99.6 us; the launch traced here: 98.9 us
  waiting for transfers between devices  27.6 us (28%)
  starting transfers between devices  23.1 us (23%)
  local copies, waits for them, and re-layouts  19.3 us (19%)
  Pallas kernels  14.8 us (15%)
  blocking collectives  12.1 us (12%)
  other arithmetic  1.07 us (1%)
    ppermute x21, waiting for transfers between devices, swap(): return lax.ppermute(values, axis, [(i, i ^ mask) for i in range(size)])  27.6 us
    ppermute x21, starting transfers between devices, swap(): return lax.ppermute(values, axis, [(i, i ^ mask) for i in range(size)])  23.1 us
    unnamed x67, local copies, waits for them, and re-layouts  18.4 us
    all_to_all x1, blocking collectives, body(): lax.all_to_all(best, ('group', 'dev'), split_axis=0, concat_axis=0, tiled...  12.1 us
    pallas_call x4, Pallas kernels, body(): pl.pallas_call(ffn_kernel, out_shape=jax.ShapeDtypeStruct((rows, width),...  8.56 us
    pallas_call x1, Pallas kernels, body(): pl.pallas_call(functools.partial(finish_kernel, chips, docs), out_shape=[...  2.63 us
  transfers between devices with their start and end apart: 21, of which 7 were waited for; matrix products, arithmetic and copies ran while one was open for 2% of the time, Pallas kernels for 10%

profile of v2, /device:TPU:0, one launch (start us, length us, event | category | flops | bytes accessed | tf_op | source)
XLA Modules:
  0.0 98.9 jit_solution(11638965360571975369)
XLA Ops:
  0.7 1.3 %copy-done.2 = bf16[128,5248]{1,0:T(8,128)(2,1)S(1)} copy-done((bf16[128,5248]{1,0:T(8,128)(2,1)S(1)}, bf16[128,5248]{1,0:T(8,128)(2,1)}, u32[]{:S(2)}) %copy-start.2) | copy-done | bytes 1343512
  2.1 1.0 %shard_map.104 = (bf16[2,656,128]{2,1,0:T(8,128)(2,1)S(1)}, bf16[2,656,128]{2,1,0:T(8,128)(2,1)S(1)}, bf16[2,656,128]{2,1,0:T(8,128)(2,1)S(1)}, bf16[2,656,128]{2,1,0:T(8,128)(2,1)S(1)}) custom-call(s32[2]{0:T(128)S(1)} %pad_add_fusion.1.place_ref, bf16[128,5248]{1,0:T(8,128)(2,1)S(1)} %copy-done.2), custom_call_target="tpu_custom_call" | custom-call | tf_op jit(solution)/shard_map/pallas_call | solution.py:163
  3.1 3.0 %collective-permute-start.1 = (bf16[2,656,128]{2,1,0:T(8,128)(2,1)S(1)}, bf16[2,656,128]{2,1,0:T(8,128)(2,1)S(1)}, u32[]{:S(2)}, u32[]{:S(2)}) collective-permute-start(bf16[2,656,128]{2,1,0:T(8,128)(2,1)S(1)} %get-tuple-element.16), channel_id=1, source_target_pairs={{0,2},{1,3},{2,0},{3,1},{4,6},{5,7},{6,4},{7,5},{8,10},{9,11},{10,... | collective-permute-start | bytes 1007624 | tf_op jit(solution)/shard_map/ppermute | solution.py:151
  6.2 2.0 %collective-permute-start.3 = (bf16[128,1024]{1,0:T(8,128)(2,1)S(1)}, bf16[128,1024]{1,0:T(8,128)(2,1)S(1)}, u32[]{:S(2)}, u32[]{:S(2)}) collective-permute-start(bf16[128,1024]{1,0:T(8,128)(2,1)S(1)} %copy-done.3), channel_id=1, source_target_pairs={{0,4},{1,5},{2,6},{3,7},{4,0},{5,1},{6,2},{7,3},{8,12},{9,13},{10,... | collective-permute-start | bytes 786440 | tf_op jit(solution)/shard_map/ppermute | solution.py:151
  8.2 11.4 %collective-permute-done.2.tokens_ref = bf16[128,1024]{1,0:T(8,128)(2,1)S(1)} collective-permute-done((bf16[128,1024]{1,0:T(8,128)(2,1)S(1)}, bf16[128,1024]{1,0:T(8,128)(2,1)S(1)}, u32[]{:S(2)}, u32[]{:S(2)}) %collective-permute-start.2) | collective-permute-done | bytes 262176 | tf_op jit(solution)/shard_map/ppermute | solution.py:151
  20.3 2.7 %collective-permute-start.5 = (bf16[2,656,128]{2,1,0:T(8,128)(2,1)S(1)}, bf16[2,656,128]{2,1,0:T(8,128)(2,1)S(1)}, u32[]{:S(2)}, u32[]{:S(2)}) collective-permute-start(bf16[2,656,128]{2,1,0:T(8,128)(2,1)S(1)} %get-tuple-element.19), channel_id=1, source_target_pairs={{0,6},{1,7},{2,4},{3,5},{4,2},{5,3},{6,0},{7,1},{8,14},{9,15},{10,... | collective-permute-start | bytes 1007624 | tf_op jit(solution)/shard_map/ppermute | solution.py:151
  23.7 1.6 %collective-permute-start.14 = (bf16[64,128]{1,0:T(8,128)(2,1)S(1)}, bf16[64,128]{1,0:T(8,128)(2,1)S(1)}, u32[]{:S(2)}, u32[]{:S(2)}) collective-permute-start(bf16[64,128]{1,0:T(8,128)(2,1)S(1)} %bitcast.33), channel_id=1, source_target_pairs={{0,8},{8,0},{16,24},{24,16},{1,9},{9,1},{17,25},{25,17},{2,10},{10... | collective-permute-start | bytes 49160 | tf_op jit(solution)/shard_map/ppermute | solution.py:151
  25.4 2.2 %collective-permute-done.14 = bf16[64,128]{1,0:T(8,128)(2,1)S(1)} collective-permute-done((bf16[64,128]{1,0:T(8,128)(2,1)S(1)}, bf16[64,128]{1,0:T(8,128)(2,1)S(1)}, u32[]{:S(2)}, u32[]{:S(2)}) %collective-permute-start.14) | collective-permute-done | bytes 16416 | tf_op jit(solution)/shard_map/ppermute | solution.py:151
  27.5 2.6 %collective-permute-start.15 = (bf16[64,128]{1,0:T(8,128)(2,1)S(1)}, bf16[64,128]{1,0:T(8,128)(2,1)S(1)}, u32[]{:S(2)}, u32[]{:S(2)}) collective-permute-start(bf16[64,128]{1,0:T(8,128)(2,1)S(1)} %bitcast.35), channel_id=1, source_target_pairs={{0,16},{8,24},{16,0},{24,8},{1,17},{9,25},{17,1},{25,9},{2,18},{10... | collective-permute-start | bytes 49160 | tf_op jit(solution)/shard_map/ppermute | solution.py:151
  30.1 2.0 %collective-permute-done.15 = bf16[64,128]{1,0:T(8,128)(2,1)S(1)} collective-permute-done((bf16[64,128]{1,0:T(8,128)(2,1)S(1)}, bf16[64,128]{1,0:T(8,128)(2,1)S(1)}, u32[]{:S(2)}, u32[]{:S(2)}) %collective-permute-start.15) | collective-permute-done | bytes 16416 | tf_op jit(solution)/shard_map/ppermute | solution.py:151
  32.2 3.7 %collective-permute-start.16 = (bf16[64,128]{1,0:T(8,128)(2,1)S(1)}, bf16[64,128]{1,0:T(8,128)(2,1)S(1)}, u32[]{:S(2)}, u32[]{:S(2)}) collective-permute-start(bf16[64,128]{1,0:T(8,128)(2,1)S(1)} %bitcast.36), channel_id=1, source_target_pairs={{0,24},{8,16},{16,8},{24,0},{1,25},{9,17},{17,9},{25,1},{2,26},{10... | collective-permute-start | bytes 49160 | tf_op jit(solution)/shard_map/ppermute | solution.py:151
  35.8 1.9 %collective-permute-done.16 = bf16[64,128]{1,0:T(8,128)(2,1)S(1)} collective-permute-done((bf16[64,128]{1,0:T(8,128)(2,1)S(1)}, bf16[64,128]{1,0:T(8,128)(2,1)S(1)}, u32[]{:S(2)}, u32[]{:S(2)}) %collective-permute-start.16) | collective-permute-done | bytes 16416 | tf_op jit(solution)/shard_map/ppermute | solution.py:151
  38.0 1.7 %collective-permute-start.18 = (bf16[256,128]{1,0:T(8,128)(2,1)S(1)}, bf16[256,128]{1,0:T(8,128)(2,1)S(1)}, u32[]{:S(2)}, u32[]{:S(2)}) collective-permute-start(bf16[256,128]{1,0:T(8,128)(2,1)S(1)} %constant_dynamic-update-slice_fusion.refs_3_), channel_id=1, source_target_pairs={{0,4},{1,5},{2,6},{3,7},{4,0},{5,1},{6,2},{7,3},{8,12},{9,13},{10,... | collective-permute-start | bytes 196616 | tf_op jit(solution)/shard_map/ppermute | solution.py:151
  41.7 1.3 %collective-permute-done.19.refs_9_ = bf16[256,128]{1,0:T(8,128)(2,1)S(1)} collective-permute-done((bf16[256,128]{1,0:T(8,128)(2,1)S(1)}, bf16[256,128]{1,0:T(8,128)(2,1)S(1)}, u32[]{:S(2)}, u32[]{:S(2)}) %collective-permute-start.19) | collective-permute-done | bytes 65568 | tf_op jit(solution)/shard_map/ppermute | solution.py:151
  44.2 4.1 %collective-permute-done.17.refs_5_ = bf16[256,128]{1,0:T(8,128)(2,1)S(1)} collective-permute-done((bf16[256,128]{1,0:T(8,128)(2,1)S(1)}, bf16[256,128]{1,0:T(8,128)(2,1)S(1)}, u32[]{:S(2)}, u32[]{:S(2)}) %collective-permute-start.17) | collective-permute-done | bytes 65568 | tf_op jit(solution)/shard_map/ppermute | solution.py:151
  53.0 1.1 %copy-done.5 = bf16[328,1024]{1,0:T(8,128)(2,1)S(1)} copy-done((bf16[328,1024]{1,0:T(8,128)(2,1)S(1)}, bf16[328,1024]{1,0:T(8,128)(2,1)}, u32[]{:S(2)}) %copy-start.5) | copy-done | bytes 671768
  54.1 1.1 %copy-done.7 = bf16[328,1024]{1,0:T(8,128)(2,1)S(1)} copy-done((bf16[328,1024]{1,0:T(8,128)(2,1)S(1)}, bf16[328,1024]{1,0:T(8,128)(2,1)}, u32[]{:S(2)}) %copy-start.7) | copy-done | bytes 671768
  55.2 1.0 copy-done.9
  56.2 1.0 copy-done.11
  57.1 1.0 copy-done.13
  60.1 1.0 copy-done.19
  62.0 1.4 %shard_map.105 = (bf16[656,1024]{1,0:T(8,128)(2,1)S(1)}, bf16[656,1024]{1,0:T(8,128)(2,1)S(1)}, bf16[656,1024]{1,0:T(8,128)(2,1)S(1)}) custom-call(s32[2]{0:T(128)S(1)} %pad_add_fusion.1.place_ref, bf16[328,1024]{1,0:T(8,128)(2,1)S(1)} %copy-done.5, bf16[328,1024]{1,0:T(8,128)(2,1)S(1)} %copy-done.7, bf16[2,656,128]{2,1,0:T(8,128)(2,1)S(1)} %get-tuple-element.15.refs_0_, ...), custom_call_target="tpu_custom_call" | custom-call | tf_op jit(solution)/shard_map/pallas_call | solution.py:176
  63.5 2.1 %shard_map.107 = bf16[128,1024]{1,0:T(8,128)(2,1)} custom-call(f32[1,1024]{1,0:T(1,128)S(1)} %bitcast.27, bf16[656,1024]{1,0:T(8,128)(2,1)S(1)} %get-tuple-element.20.gelu_w, bf16[656,1024]{1,0:T(8,128)(2,1)S(1)} %get-tuple-element.21.gate_w, bf16[656,1024]{1,0:T(8,128)(2,1)S(1)} %get-tuple-element.22.wo_part, bf16[128,1024]{1,0:T(8,128)(2,1)S(1)} %copy-done.26), custom_call_target="tpu_custom_call" | custom-call | tf_op jit(solution)/shard_map/pallas_call | solution.py:201
  66.5 2.1 %shard_map.108 = bf16[128,1024]{1,0:T(8,128)(2,1)} custom-call(f32[1,1024]{1,0:T(1,128)S(1)} %bitcast.28, bf16[656,1024]{1,0:T(8,128)(2,1)S(1)} %get-tuple-element.20.gelu_w, bf16[656,1024]{1,0:T(8,128)(2,1)S(1)} %get-tuple-element.21.gate_w, bf16[656,1024]{1,0:T(8,128)(2,1)S(1)} %get-tuple-element.22.wo_part, bf16[128,1024]{1,0:T(8,128)(2,1)S(1)} %copy-done.24), custom_call_target="tpu_custom_call" | custom-call | tf_op jit(solution)/shard_map/pallas_call | solution.py:201
  68.5 1.6 %collective-permute-start.11 = (bf16[128,1024]{1,0:T(8,128)(2,1)}, bf16[128,1024]{1,0:T(8,128)(2,1)}, u32[]{:S(2)}, u32[]{:S(2)}) collective-permute-start(bf16[128,1024]{1,0:T(8,128)(2,1)} %shard_map.108), channel_id=1, source_target_pairs={{0,4},{1,5},{2,6},{3,7},{4,0},{5,1},{6,2},{7,3},{8,12},{9,13},{10,... | collective-permute-start | bytes 786440 | tf_op jit(solution)/shard_map/ppermute | solution.py:151
  70.2 3.0 %shard_map.109 = bf16[128,1024]{1,0:T(8,128)(2,1)} custom-call(f32[1,1024]{1,0:T(1,128)S(1)} %bitcast.29, bf16[656,1024]{1,0:T(8,128)(2,1)S(1)} %get-tuple-element.20.gelu_w, bf16[656,1024]{1,0:T(8,128)(2,1)S(1)} %get-tuple-element.21.gate_w, bf16[656,1024]{1,0:T(8,128)(2,1)S(1)} %get-tuple-element.22.wo_part, ...), custom_call_target="tpu_custom_call" | custom-call | tf_op jit(solution)/shard_map/pallas_call | solution.py:201
  74.4 1.3 %copy-done.1 = bf16[656,1024]{1,0:T(8,128)(2,1)S(1)} copy-done((bf16[656,1024]{1,0:T(8,128)(2,1)S(1)}, bf16[656,1024]{1,0:T(8,128)(2,1)}, u32[]{:S(2)}) %copy-start.1) | copy-done | bytes 1343512
  75.8 1.4 %shard_map.106.own_ref = f32[128,1024]{1,0:T(8,128)S(1)} custom-call(f32[1,1024]{1,0:T(1,128)S(1)} %bitcast.30, bf16[656,1024]{1,0:T(8,128)(2,1)S(1)} %get-tuple-element.20.gelu_w, bf16[656,1024]{1,0:T(8,128)(2,1)S(1)} %get-tuple-element.21.gate_w, bf16[656,1024]{1,0:T(8,128)(2,1)S(1)} %copy-done.1, bf16[128,1024]{1,0:T(8,128)(2,1)S(1)} %copy-done.3), custom_call_target="tpu_custom_call" | custom-call | tf_op jit(solution)/shard_map/pallas_call | solution.py:201
  78.1 4.8 %collective-permute-done.11.refs_1_ = bf16[128,1024]{1,0:T(8,128)(2,1)} collective-permute-done((bf16[128,1024]{1,0:T(8,128)(2,1)}, bf16[128,1024]{1,0:T(8,128)(2,1)}, u32[]{:S(2)}, u32[]{:S(2)}) %collective-permute-start.11) | collective-permute-done | bytes 262176 | tf_op jit(solution)/shard_map/ppermute | solution.py:151
  82.9 2.6 %shard_map.110 = (bf16[128,128]{1,0:T(8,128)(2,1)}, bf16[32,4,128]{2,1,0:T(4,128)(2,1)S(1)}) custom-call(s32[2]{0:T(128)S(1)} %pad_add_fusion.place_ref, s32[4]{0:T(128)S(1)} %bitcast.32, bf16[128,1024]{1,0:T(8,128)(2,1)S(1)} %copy-done.3, f32[1,1024]{1,0:T(1,128)S(1)} %bitcast.31, bf16[1024,128]{1,0:T(8,128)(2,1)S(1)} %copy-done.22, ...), custom_call_target="tpu_custom_call" | custom-call | tf_op jit(solution)/shard_map/pallas_call | solution.py:212
  85.6 12.1 %all_to_all.5 = bf16[32,4,128]{2,1,0:T(4,128)(2,1)S(1)} all-to-all(bf16[32,4,128]{2,1,0:T(4,128)(2,1)S(1)} %get-tuple-element.27), channel_id=1, replica_groups=mesh['group'=4,'dev'=8] {'group','dev'}, dimensions={0} | all-to-all | bytes 65536 | tf_op jit(solution)/shard_map/all_to_all | solution.py:231
  97.7 1.2 %shard_map.111 = f32[2,100]{1,0:T(2,128)} custom-call(s32[2]{0:T(128)S(1)} %pad_add_fusion.place_ref, s32[2,100]{1,0:T(2,128)S(1)} %copy-done.29, bf16[4,8,4,128]{3,2,1,0:T(4,128)(2,1)S(1)} %bitcast.26), custom_call_target="tpu_custom_call" | custom-call | tf_op jit(solution)/shard_map/pallas_call | solution.py:232
  (92 shorter events, 16.0 us)
Async XLA Ops:
  0.6 23.1 %copy-start.30 = (bf16[2,32,128]{2,1,0:T(8,128)(2,1)S(1)}, bf16[2,32,128]{2,1,0:T(8,128)(2,1)}, u32[]{:S(2)}) copy-start(bf16[2,32,128]{2,1,0:T(8,128)(2,1)} %param.15) | copy-start | bytes 49156
  2.1 4.0 %copy-start.3 = (bf16[128,1024]{1,0:T(8,128)(2,1)S(1)}, bf16[128,1024]{1,0:T(8,128)(2,1)}, u32[]{:S(2)}) copy-start(bf16[128,1024]{1,0:T(8,128)(2,1)} %tokens_ref.3) | copy-start | bytes 786436
  2.1 6.1 %copy-start.4 = (bf16[328,1024]{1,0:T(8,128)(2,1)S(1)}, bf16[328,1024]{1,0:T(8,128)(2,1)}, u32[]{:S(2)}) copy-start(bf16[328,1024]{1,0:T(8,128)(2,1)} %wo_mine.1) | copy-start | bytes 2015236
  3.1 20.6 %collective-permute-start.1 = (bf16[2,656,128]{2,1,0:T(8,128)(2,1)S(1)}, bf16[2,656,128]{2,1,0:T(8,128)(2,1)S(1)}, u32[]{:S(2)}, u32[]{:S(2)}) collective-permute-start(bf16[2,656,128]{2,1,0:T(8,128)(2,1)S(1)} %get-tuple-element.16), channel_id=1, source_target_pairs={{0,2},{1,3},{2,0},{3,1},{4,6},{5,7},{6,4},{7,5},{8,10},{9,11},{10,... | collective-permute-start | bytes 1007624 | tf_op jit(solution)/shard_map/ppermute | solution.py:151
  6.1 13.5 %collective-permute-start.2 = (bf16[128,1024]{1,0:T(8,128)(2,1)S(1)}, bf16[128,1024]{1,0:T(8,128)(2,1)S(1)}, u32[]{:S(2)}, u32[]{:S(2)}) collective-permute-start(bf16[128,1024]{1,0:T(8,128)(2,1)S(1)} %copy-done.3), channel_id=1, source_target_pairs={{0,2},{1,3},{2,0},{3,1},{4,6},{5,7},{6,4},{7,5},{8,10},{9,11},{10,... | collective-permute-start | bytes 786440 | tf_op jit(solution)/shard_map/ppermute | solution.py:151
  6.2 16.8 %collective-permute-start.3 = (bf16[128,1024]{1,0:T(8,128)(2,1)S(1)}, bf16[128,1024]{1,0:T(8,128)(2,1)S(1)}, u32[]{:S(2)}, u32[]{:S(2)}) collective-permute-start(bf16[128,1024]{1,0:T(8,128)(2,1)S(1)} %copy-done.3), channel_id=1, source_target_pairs={{0,4},{1,5},{2,6},{3,7},{4,0},{5,1},{6,2},{7,3},{8,12},{9,13},{10,... | collective-permute-start | bytes 786440 | tf_op jit(solution)/shard_map/ppermute | solution.py:151
  8.2 41.8 %collective-permute-start = (bf16[328,1024]{1,0:T(8,128)(2,1)S(1)}, bf16[328,1024]{1,0:T(8,128)(2,1)S(1)}, u32[]{:S(2)}, u32[]{:S(2)}) collective-permute-start(bf16[328,1024]{1,0:T(8,128)(2,1)S(1)} %copy-done.4), channel_id=1, source_target_pairs={{0,1},{1,0},{2,3},{3,2},{4,5},{5,4},{6,7},{7,6},{8,9},{9,8},{10,11... | collective-permute-start | bytes 2015240 | tf_op jit(solution)/shard_map/ppermute | solution.py:151
  8.2 29.9 %collective-permute-start.4 = (bf16[2,656,128]{2,1,0:T(8,128)(2,1)S(1)}, bf16[2,656,128]{2,1,0:T(8,128)(2,1)S(1)}, u32[]{:S(2)}, u32[]{:S(2)}) collective-permute-start(bf16[2,656,128]{2,1,0:T(8,128)(2,1)S(1)} %get-tuple-element.18), channel_id=1, source_target_pairs={{0,4},{1,5},{2,6},{3,7},{4,0},{5,1},{6,2},{7,3},{8,12},{9,13},{10,... | collective-permute-start | bytes 1007624 | tf_op jit(solution)/shard_map/ppermute | solution.py:151
  20.3 19.4 %collective-permute-start.5 = (bf16[2,656,128]{2,1,0:T(8,128)(2,1)S(1)}, bf16[2,656,128]{2,1,0:T(8,128)(2,1)S(1)}, u32[]{:S(2)}, u32[]{:S(2)}) collective-permute-start(bf16[2,656,128]{2,1,0:T(8,128)(2,1)S(1)} %get-tuple-element.19), channel_id=1, source_target_pairs={{0,6},{1,7},{2,4},{3,5},{4,2},{5,3},{6,0},{7,1},{8,14},{9,15},{10,... | collective-permute-start | bytes 1007624 | tf_op jit(solution)/shard_map/ppermute | solution.py:151
  23.7 16.0 %collective-permute-start.6 = (bf16[2,656,128]{2,1,0:T(8,128)(2,1)S(1)}, bf16[2,656,128]{2,1,0:T(8,128)(2,1)S(1)}, u32[]{:S(2)}, u32[]{:S(2)}) collective-permute-start(bf16[2,656,128]{2,1,0:T(8,128)(2,1)S(1)} %get-tuple-element.15.refs_0_), channel_id=1, source_target_pairs={{0,1},{1,0},{2,3},{3,2},{4,5},{5,4},{6,7},{7,6},{8,9},{9,8},{10,11... | collective-permute-start | bytes 1007624 | tf_op jit(solution)/shard_map/ppermute | solution.py:151
  23.7 27.8 %copy-start.8 = (bf16[2,656,128]{2,1,0:T(8,128)(2,1)}, bf16[2,656,128]{2,1,0:T(8,128)(2,1)S(1)}, u32[]{:S(2)}) copy-start(bf16[2,656,128]{2,1,0:T(8,128)(2,1)S(1)} %collective-permute-done.1.refs_1_) | copy-start | bytes 1007620
  23.7 3.8 %collective-permute-start.14 = (bf16[64,128]{1,0:T(8,128)(2,1)S(1)}, bf16[64,128]{1,0:T(8,128)(2,1)S(1)}, u32[]{:S(2)}, u32[]{:S(2)}) collective-permute-start(bf16[64,128]{1,0:T(8,128)(2,1)S(1)} %bitcast.33), channel_id=1, source_target_pairs={{0,8},{8,0},{16,24},{24,16},{1,9},{9,1},{17,25},{25,17},{2,10},{10... | collective-permute-start | bytes 49160 | tf_op jit(solution)/shard_map/ppermute | solution.py:151
  27.5 4.6 %collective-permute-start.15 = (bf16[64,128]{1,0:T(8,128)(2,1)S(1)}, bf16[64,128]{1,0:T(8,128)(2,1)S(1)}, u32[]{:S(2)}, u32[]{:S(2)}) collective-permute-start(bf16[64,128]{1,0:T(8,128)(2,1)S(1)} %bitcast.35), channel_id=1, source_target_pairs={{0,16},{8,24},{16,0},{24,8},{1,17},{9,25},{17,1},{25,9},{2,18},{10... | collective-permute-start | bytes 49160 | tf_op jit(solution)/shard_map/ppermute | solution.py:151
  32.2 5.5 %collective-permute-start.16 = (bf16[64,128]{1,0:T(8,128)(2,1)S(1)}, bf16[64,128]{1,0:T(8,128)(2,1)S(1)}, u32[]{:S(2)}, u32[]{:S(2)}) collective-permute-start(bf16[64,128]{1,0:T(8,128)(2,1)S(1)} %bitcast.36), channel_id=1, source_target_pairs={{0,24},{8,16},{16,8},{24,0},{1,25},{9,17},{17,9},{25,1},{2,26},{10... | collective-permute-start | bytes 49160 | tf_op jit(solution)/shard_map/ppermute | solution.py:151
  37.7 5.3 %collective-permute-start.19 = (bf16[256,128]{1,0:T(8,128)(2,1)S(1)}, bf16[256,128]{1,0:T(8,128)(2,1)S(1)}, u32[]{:S(2)}, u32[]{:S(2)}) collective-permute-start(bf16[256,128]{1,0:T(8,128)(2,1)S(1)} %constant_dynamic-update-slice_fusion.refs_3_), channel_id=1, source_target_pairs={{0,6},{1,7},{2,4},{3,5},{4,2},{5,3},{6,0},{7,1},{8,14},{9,15},{10,... | collective-permute-start | bytes 196616 | tf_op jit(solution)/shard_map/ppermute | solution.py:151
  38.0 5.7 %collective-permute-start.18 = (bf16[256,128]{1,0:T(8,128)(2,1)S(1)}, bf16[256,128]{1,0:T(8,128)(2,1)S(1)}, u32[]{:S(2)}, u32[]{:S(2)}) collective-permute-start(bf16[256,128]{1,0:T(8,128)(2,1)S(1)} %constant_dynamic-update-slice_fusion.refs_3_), channel_id=1, source_target_pairs={{0,4},{1,5},{2,6},{3,7},{4,0},{5,1},{6,2},{7,3},{8,12},{9,13},{10,... | collective-permute-start | bytes 196616 | tf_op jit(solution)/shard_map/ppermute | solution.py:151
  39.7 11.1 %collective-permute-start.7 = (bf16[2,656,128]{2,1,0:T(8,128)(2,1)S(1)}, bf16[2,656,128]{2,1,0:T(8,128)(2,1)S(1)}, u32[]{:S(2)}, u32[]{:S(2)}) collective-permute-start(bf16[2,656,128]{2,1,0:T(8,128)(2,1)S(1)} %collective-permute-done.1.refs_1_), channel_id=1, source_target_pairs={{0,1},{1,0},{2,3},{3,2},{4,5},{5,4},{6,7},{7,6},{8,9},{9,8},{10,11... | collective-permute-start | bytes 1007624 | tf_op jit(solution)/shard_map/ppermute | solution.py:151
  40.5 11.1 %collective-permute-start.8 = (bf16[2,656,128]{2,1,0:T(8,128)(2,1)S(1)}, bf16[2,656,128]{2,1,0:T(8,128)(2,1)S(1)}, u32[]{:S(2)}, u32[]{:S(2)}) collective-permute-start(bf16[2,656,128]{2,1,0:T(8,128)(2,1)S(1)} %collective-permute-done.4.refs_2_), channel_id=1, source_target_pairs={{0,1},{1,0},{2,3},{3,2},{4,5},{5,4},{6,7},{7,6},{8,9},{9,8},{10,11... | collective-permute-start | bytes 1007624 | tf_op jit(solution)/shard_map/ppermute | solution.py:151
  43.0 9.3 %collective-permute-start.9 = (bf16[2,656,128]{2,1,0:T(8,128)(2,1)S(1)}, bf16[2,656,128]{2,1,0:T(8,128)(2,1)S(1)}, u32[]{:S(2)}, u32[]{:S(2)}) collective-permute-start(bf16[2,656,128]{2,1,0:T(8,128)(2,1)S(1)} %collective-permute-done.5.refs_3_), channel_id=1, source_target_pairs={{0,1},{1,0},{2,3},{3,2},{4,5},{5,4},{6,7},{7,6},{8,9},{9,8},{10,11... | collective-permute-start | bytes 1007624 | tf_op jit(solution)/shard_map/ppermute | solution.py:151
  43.7 4.5 %collective-permute-start.17 = (bf16[256,128]{1,0:T(8,128)(2,1)S(1)}, bf16[256,128]{1,0:T(8,128)(2,1)S(1)}, u32[]{:S(2)}, u32[]{:S(2)}) collective-permute-start(bf16[256,128]{1,0:T(8,128)(2,1)S(1)} %constant_dynamic-update-slice_fusion.refs_3_), channel_id=1, source_target_pairs={{0,2},{1,3},{2,0},{3,1},{4,6},{5,7},{6,4},{7,5},{8,10},{9,11},{10,... | collective-permute-start | bytes 196616 | tf_op jit(solution)/shard_map/ppermute | solution.py:151
  48.2 21.9 %collective-permute-start.12 = (bf16[128,1024]{1,0:T(8,128)(2,1)S(1)}, bf16[128,1024]{1,0:T(8,128)(2,1)}, u32[]{:S(2)}, u32[]{:S(2)}) collective-permute-start(bf16[128,1024]{1,0:T(8,128)(2,1)S(1)} %copy-done.3), channel_id=1, source_target_pairs={{0,6},{1,7},{2,4},{3,5},{4,2},{5,3},{6,0},{7,1},{8,14},{9,15},{10,... | collective-permute-start | bytes 786440 | tf_op jit(solution)/shard_map/ppermute | solution.py:151
  50.8 26.3 %collective-permute-start.20 = (bf16[4,256,128]{2,1,0:T(8,128)(2,1)}, bf16[4,256,128]{2,1,0:T(8,128)(2,1)}, u32[]{:S(2)}, u32[]{:S(2)}) collective-permute-start(bf16[4,256,128]{2,1,0:T(8,128)(2,1)} %pad_maximum_fusion), channel_id=1, source_target_pairs={{0,1},{1,0},{2,3},{3,2},{4,5},{5,4},{6,7},{7,6},{8,9},{9,8},{10,11... | collective-permute-start | bytes 786440 | tf_op jit(solution)/shard_map/ppermute | solution.py:151
  62.0 1.4 %copy-start.27 = (f32[1024]{0:T(1024)S(1)}, f32[1024]{0:T(1024)}, u32[]{:S(2)}) copy-start(f32[1024]{0:T(1024)} %param.10) | copy-start | bytes 12292
  63.4 6.7 %copy-start = (bf16[656,1024]{1,0:T(8,128)(2,1)}, bf16[656,1024]{1,0:T(8,128)(2,1)S(1)}, u32[]{:S(2)}) copy-start(bf16[656,1024]{1,0:T(8,128)(2,1)S(1)} %get-tuple-element.22.wo_part) | copy-start | bytes 4030468
  63.5 3.0 %copy-start.24 = (bf16[128,1024]{1,0:T(8,128)(2,1)S(1)}, bf16[128,1024]{1,0:T(8,128)(2,1)}, u32[]{:S(2)}) copy-start(bf16[128,1024]{1,0:T(8,128)(2,1)} %copy-done.23) | copy-start | bytes 786436
  65.6 12.6 %collective-permute-start.10 = (bf16[128,1024]{1,0:T(8,128)(2,1)}, bf16[128,1024]{1,0:T(8,128)(2,1)}, u32[]{:S(2)}, u32[]{:S(2)}) collective-permute-start(bf16[128,1024]{1,0:T(8,128)(2,1)} %shard_map.107), channel_id=1, source_target_pairs={{0,2},{1,3},{2,0},{3,1},{4,6},{5,7},{6,4},{7,5},{8,10},{9,11},{10,... | collective-permute-start | bytes 786440 | tf_op jit(solution)/shard_map/ppermute | solution.py:151
  68.5 5.7 %copy-start.31 = (s32[1,4]{1,0:T(1,128)S(1)}, s32[1,4]{1,0:T(1,128)}, u32[]{:S(2)}) copy-start(s32[1,4]{1,0:T(1,128)} %param.16) | copy-start | bytes 52
  68.5 14.4 %collective-permute-start.11 = (bf16[128,1024]{1,0:T(8,128)(2,1)}, bf16[128,1024]{1,0:T(8,128)(2,1)}, u32[]{:S(2)}, u32[]{:S(2)}) collective-permute-start(bf16[128,1024]{1,0:T(8,128)(2,1)} %shard_map.108), channel_id=1, source_target_pairs={{0,4},{1,5},{2,6},{3,7},{4,0},{5,1},{6,2},{7,3},{8,12},{9,13},{10,... | collective-permute-start | bytes 786440 | tf_op jit(solution)/shard_map/ppermute | solution.py:151
  73.2 9.7 %collective-permute-start.13 = (bf16[128,1024]{1,0:T(8,128)(2,1)}, bf16[128,1024]{1,0:T(8,128)(2,1)}, u32[]{:S(2)}, u32[]{:S(2)}) collective-permute-start(bf16[128,1024]{1,0:T(8,128)(2,1)} %shard_map.109), channel_id=1, source_target_pairs={{0,6},{1,7},{2,4},{3,5},{4,2},{5,3},{6,0},{7,1},{8,14},{9,15},{10,... | collective-permute-start | bytes 786440 | tf_op jit(solution)/shard_map/ppermute | solution.py:151
  75.7 7.2 %copy-start.22 = (bf16[1024,128]{1,0:T(8,128)(2,1)S(1)}, bf16[1024,128]{1,0:T(8,128)(2,1)}, u32[]{:S(2)}) copy-start(bf16[1024,128]{1,0:T(8,128)(2,1)} %proj_ref.1) | copy-start | bytes 786436
  75.8 7.2 %copy-start.28 = (f32[1024]{0:T(1024)S(1)}, f32[1024]{0:T(1024)}, u32[]{:S(2)}) copy-start(f32[1024]{0:T(1024)} %param.13) | copy-start | bytes 12292
  78.1 19.6 %copy-start.29 = (s32[2,100]{1,0:T(2,128)S(1)}, s32[2,100]{1,0:T(2,128)}, u32[]{:S(2)}) copy-start(s32[2,100]{1,0:T(2,128)} %cand_ref.1) | copy-start | bytes 2404
  (21 other events, 19.7 us)

commit v3 on v2

v3 whole, which is shorter than its diff:
```python
import functools

import jax
import jax.numpy as jnp
from jax import lax
from jax.experimental import pallas as pl
from jax.experimental.pallas import tpu as pltpu
from jax.sharding import PartitionSpec as P

VMEM_LIMIT = 20 * 1024 * 1024


def norm_rows(values, gain_row):
    center = jnp.mean(values, axis=-1, keepdims=True)
    shifted = values - center
    spread = jnp.mean(shifted * shifted, axis=-1, keepdims=True)
    return (shifted * lax.rsqrt(spread + 1e-05) * gain_row).astype(jnp.bfloat16)


def dot_nt(left, right):
    return lax.dot_general(
        left, right, (((1,), (1,)), ((), ())), preferred_element_type=jnp.float32
    )


def split_kernel(chips, wi_ref, query_ref, *refs):
    pieces, turned = refs[:chips], refs[chips]
    columns = wi_ref.shape[1]
    width = columns // 2
    part = width // chips
    chip = lax.axis_index("dev") // 2
    for start in range(0, columns, 128):
        turned[start : start + 128, :] = wi_ref[:, start : start + 128].T
    for step in range(chips):
        for half in range(2):
            first = pl.multiple_of(half * width + (chip ^ step) * part, 16)
            pieces[step][half * part : (half + 1) * part] = turned[pl.ds(first, part), :]
        pieces[step][2 * part :] = query_ref[...]


def join_kernel(chips, wo_mine, wo_other, *refs):
    mine, other = refs[:chips], refs[chips : 2 * chips]
    gelu_w, gate_w, wo_part, queries = refs[2 * chips :]
    chip, core = lax.axis_index("dev") // 2, lax.axis_index("dev") % 2
    rows = wo_mine.shape[0]
    for first, upper, lower in ((0, wo_mine, wo_other), (1, wo_other, wo_mine)):

        @pl.when(core == first)
        def _(upper=upper, lower=lower):
            wo_part[:rows] = upper[...]
            wo_part[rows:] = lower[...]

    part = gelu_w.shape[0]
    own = mine[0].shape[0] - 2 * part
    for step in range(chips):
        source = (chip ^ step) * 2
        for block, at in ((mine[step], source + core), (other[step], source + 1 - core)):
            columns = pl.ds(pl.multiple_of(at * 128, 128), 128)
            gelu_w[:, columns] = block[:part]
            gate_w[:, columns] = block[part : 2 * part]
            queries[pl.ds(pl.multiple_of(at * own, own), own), :] = block[2 * part :]


def ffn_kernel(gain_ref, gelu_w, gate_w, wo_part, tokens_ref, out_ref):
    normed = norm_rows(tokens_ref[...].astype(jnp.float32), gain_ref[...])
    first = dot_nt(normed, gelu_w[...])
    second = dot_nt(normed, gate_w[...])
    hidden = (0.5 * first * (1.0 + lax.erf(first * 0.7071067811865476)) * second).astype(jnp.bfloat16)
    out_ref[...] = jnp.dot(hidden, wo_part[...], preferred_element_type=jnp.float32).astype(
        out_ref.dtype
    )


def finish_kernel(chips, lengths_ref, tokens_ref, gain_ref, proj_ref, own_ref, *refs):
    parts, refs = refs[: chips - 1], refs[chips - 1 :]
    queries, (vectors_ref, out_ref) = refs[:-2], refs[-2:]
    mixed = tokens_ref[...].astype(jnp.float32) + own_ref[...]
    for part in parts:
        mixed = mixed + part[...].astype(jnp.float32)
    final = norm_rows(mixed, gain_ref[...])
    projected = jnp.dot(final, proj_ref[...], preferred_element_type=jnp.float32)
    total = jnp.sum(projected * projected, axis=-1, keepdims=True)
    vectors = (projected * lax.rsqrt(total + 1e-06)).astype(jnp.bfloat16)
    vectors_ref[...] = vectors
    group, me = lax.axis_index("group"), lax.axis_index("dev")
    rows = vectors.shape[0]
    docs = out_ref.shape[1]
    spot = me * rows + lax.broadcasted_iota(jnp.int32, (rows, 128), 0)
    inside, low = [], jnp.int32(0)
    for doc in range(docs):
        high = low + lengths_ref[0, doc]
        inside.append((spot >= low) & (spot < high))
        low = high
    for far, block in enumerate(queries):
        for start in range(0, block.shape[0], 128):
            similar = dot_nt(vectors, block[start : start + 128, :])
            best = [
                jnp.max(jnp.where(inside[doc], similar, -jnp.inf), axis=0, keepdims=True)
                for doc in range(docs)
            ]
            best = jnp.concatenate(best, axis=0).astype(jnp.bfloat16)
            target = (group ^ far) * (2 * chips) + start // 64
            out_ref[target] = best
            out_ref[target + 1] = best


def pick_kernel(query_len, cand_ref, best_ref, out_ref):
    groups, _, docs, lanes = best_ref.shape
    own, listed = cand_ref.shape
    offset = (lax.axis_index("dev") % 2) * own * query_len
    scores = [jnp.zeros((1, listed), jnp.float32) for _ in range(own)]
    lane = lax.broadcasted_iota(jnp.int32, (docs, lanes), 1)
    label = lax.broadcasted_iota(jnp.int32, (docs, listed), 0)
    for far in range(groups):
        best = jnp.max(best_ref[far].astype(jnp.float32), axis=0)
        for query in range(own):
            start = offset + query * query_len
            taken = jnp.where((lane >= start) & (lane < start + query_len), best, 0.0)
            value = jnp.sum(taken, axis=1, keepdims=True) / query_len
            wanted = cand_ref[query : query + 1, :] - far * docs
            scores[query] += jnp.sum(jnp.where(wanted == label, value, 0.0), axis=0, keepdims=True)
    for query in range(own):
        out_ref[query : query + 1, :] = scores[query]


def body(
    corpus_tokens,
    norm_gain,
    wi_weight,
    wo_weight,
    final_gain,
    proj_weight,
    query_vectors,
    doc_lengths,
    candidates,
):
    groups = lax.axis_size("group")
    devices = lax.axis_size("dev")
    chips = devices // 2
    rows, width = corpus_tokens.shape
    part = wo_weight.shape[0] * 2
    smem = pl.BlockSpec(memory_space=pltpu.SMEM)
    vmem = pl.BlockSpec(memory_space=pltpu.VMEM)
    params = pltpu.CompilerParams(vmem_limit_bytes=VMEM_LIMIT)

    def swap(values, mask, axis="dev"):
        size = devices if axis == "dev" else groups
        return lax.ppermute(values, axis, [(i, i ^ mask) for i in range(size)])

    per_query, query_len, vector_dim = query_vectors.shape
    query_own = query_vectors.reshape(-1, vector_dim)
    wo_other = swap(wo_weight, 1)
    tokens = [corpus_tokens] + [swap(corpus_tokens, 2 * step) for step in range(1, chips)]
    if wi_weight.shape[0] == 128 and part % 16 == 0:
        piece_shape = jax.ShapeDtypeStruct((2 * part + query_own.shape[0], 128), jnp.bfloat16)
        pieces = pl.pallas_call(
            functools.partial(split_kernel, chips),
            out_shape=[piece_shape] * chips,
            in_specs=[vmem] * 2,
            out_specs=[vmem] * chips,
            scratch_shapes=[pltpu.VMEM((wi_weight.shape[1], 128), jnp.bfloat16)],
            compiler_params=params,
        )(wi_weight, query_own)
        mine = [pieces[0]] + [swap(pieces[step], 2 * step) for step in range(1, chips)]
        mine[1], tokens[1], tokens[2] = lax.optimization_barrier((mine[1], tokens[1], tokens[2]))
        other = [swap(piece, 1) for piece in mine]
        *weights, plane = pl.pallas_call(
            functools.partial(join_kernel, chips),
            out_shape=[
                jax.ShapeDtypeStruct((part, width), jnp.bfloat16),
                jax.ShapeDtypeStruct((part, width), jnp.bfloat16),
                jax.ShapeDtypeStruct((part, wo_weight.shape[1]), jnp.bfloat16),
                jax.ShapeDtypeStruct((devices * query_own.shape[0], vector_dim), jnp.bfloat16),
            ],
            in_specs=[vmem] * (2 + 2 * chips),
            out_specs=[vmem] * 4,
            compiler_params=params,
        )(wo_weight, wo_other, *mine, *other)
    else:
        me = lax.axis_index("dev")
        whole = lax.all_gather(wi_weight, "dev", axis=0, tiled=True).reshape(width, 2, chips, part)
        columns = lax.dynamic_index_in_dim(whole, me // 2, 2, keepdims=False)
        even = (me % 2) == 0
        wo_part = jnp.concatenate(
            [jnp.where(even, wo_weight, wo_other), jnp.where(even, wo_other, wo_weight)], axis=0
        )
        weights = [columns[:, 0].T, columns[:, 1].T, wo_part]
        plane = lax.all_gather(query_own, "dev", axis=0, tiled=True)
    partial = [None] * chips
    for step in list(range(1, chips)) + [0]:
        partial[step] = pl.pallas_call(
            ffn_kernel,
            out_shape=jax.ShapeDtypeStruct((rows, width), jnp.bfloat16 if step else jnp.float32),
            in_specs=[vmem] * 5,
            out_specs=vmem,
            compiler_params=params,
        )(norm_gain.reshape(1, -1), *weights, tokens[step])
    arrived = [swap(partial[step], 2 * step) for step in range(1, chips)]
    queries = [plane] + [swap(plane, mask, "group") for mask in range(1, groups)]

    docs = doc_lengths.shape[1]
    vectors, best = pl.pallas_call(
        functools.partial(finish_kernel, chips),
        out_shape=[
            jax.ShapeDtypeStruct((rows, proj_weight.shape[1]), jnp.bfloat16),
            jax.ShapeDtypeStruct((groups * devices, docs, 128), jnp.bfloat16),
        ],
        in_specs=[smem] + [vmem] * (4 + chips - 1 + groups),
        out_specs=[vmem, vmem],
        compiler_params=params,
    )(
        doc_lengths,
        corpus_tokens,
        final_gain.reshape(1, -1),
        proj_weight,
        partial[0],
        *arrived[::-1],
        *queries,
    )
    met = lax.all_to_all(best, ("group", "dev"), split_axis=0, concat_axis=0, tiled=True)
    scores = pl.pallas_call(
        functools.partial(pick_kernel, query_len),
        out_shape=jax.ShapeDtypeStruct(candidates.shape, jnp.float32),
        in_specs=[vmem, vmem],
        out_specs=vmem,
        compiler_params=params,
    )(candidates, met.reshape(groups, devices, docs, 128))
    return (vectors, scores)


def solution(mesh):
    placed = (
        P(("group", "dev"), None),
        P(),
        P("dev", None),
        P("dev", None),
        P(),
        P(),
        P(("group", "dev"), None, None),
        P("group", None),
        P(("group", "dev"), None),
    )
    return jax.shard_map(
        body,
        mesh=mesh,
        in_specs=placed,
        out_specs=(P(("group", "dev"), None), P(("group", "dev"), None)),
        check_vma=False,
    )
```

time: 99.6 us -> 66.9 us (0.67)
  local copies, waits for them, and re-layouts: 19.3 us -> 2.08 us
  Pallas kernels: 14.8 us -> 9.39 us
  waiting for transfers between devices: 27.6 us -> 22.7 us
  starting transfers between devices: 23.1 us -> 19.3 us
  other arithmetic: 1.07 us -> 0 us
    unnamed x67 -> x18, local copies, waits for them, and re-layouts: 18.4 us -> 2.08 us
    ppermute x21 -> x17, waiting for transfers between devices: 27.6 us -> 22.7 us  [swap(): return lax.ppermute(values, axis, [(i, i ^ mask) for i in range(size)])]
    ppermute x21 -> x17, starting transfers between devices: 23.1 us -> 19.3 us  [swap(): return lax.ppermute(values, axis, [(i, i ^ mask) for i in range(size)])]
    pallas_call x4, Pallas kernels: 8.56 us -> 5.52 us  [body(): pl.pallas_call(ffn_kernel, out_shape=jax.ShapeDtypeStruct((rows, width),...]
    pallas_call x3, Pallas kernels: 5.06 us -> 3.2 us  [the longest x1 1.85 us: body(): pl.pallas_call(functools.partial(finish_kernel, chips), out_shape=[jax.Sh...]
    another operation x4 -> x0, other arithmetic: 1.07 us -> none  [the longest x1 0.74 us: body(): jnp.stack([line] + [swap(line, 2 * step) for step in range(1, chips)])]
  transfers between devices with their start and end apart: 21 -> 17, of which waited for: 7 -> 6; matrix products, arithmetic and copies ran while one was open for 2% -> 0% of each run, Pallas kernels for 10% -> 10%
where the time goes in v3:
time: 66.9 us; the launch traced here: 66.6 us
  waiting for transfers between devices  22.7 us (34%)
  starting transfers between devices  19.3 us (29%)
  blocking collectives  12.4 us (19%)
  Pallas kernels  9.39 us (14%)
  local copies, waits for them, and re-layouts  2.08 us (3%)
  between operations  0.78 us (1%)
    ppermute x17, waiting for transfers between devices, swap(): return lax.ppermute(values, axis, [(i, i ^ mask) for i in range(size)])  22.7 us
    ppermute x17, starting transfers between devices, swap(): return lax.ppermute(values, axis, [(i, i ^ mask) for i in range(size)])  19.3 us
    all_to_all x1, blocking collectives, body(): lax.all_to_all(best, ('group', 'dev'), split_axis=0, concat_axis=0, tiled...  12.4 us
    pallas_call x4, Pallas kernels, body(): pl.pallas_call(ffn_kernel, out_shape=jax.ShapeDtypeStruct((rows, width),...  5.52 us
    unnamed x18, local copies, waits for them, and re-layouts  2.08 us
    pallas_call x1, Pallas kernels, body(): pl.pallas_call(functools.partial(finish_kernel, chips), out_shape=[jax.Sh...  1.85 us
  transfers between devices with their start and end apart: 17, of which 6 were waited for; matrix products, arithmetic and copies ran while one was open for 0% of the time, Pallas kernels for 10%

profile of v3, /device:TPU:0, one launch (start us, length us, event | category | flops | bytes accessed | tf_op | source)
XLA Modules:
  0.0 66.6 jit_solution(1321684537140914925)
XLA Ops:
  0.6 3.0 %collective-permute-start.2 = (bf16[128,1024]{1,0:T(8,128)(2,1)}, bf16[128,1024]{1,0:T(8,128)(2,1)S(1)}, u32[]{:S(2)}, u32[]{:S(2)}) collective-permute-start(bf16[128,1024]{1,0:T(8,128)(2,1)} %tokens_ref.3), channel_id=1, source_target_pairs={{0,2},{1,3},{2,0},{3,1},{4,6},{5,7},{6,4},{7,5},{8,10},{9,11},{10,... | collective-permute-start | bytes 786440 | tf_op jit(solution)/shard_map/ppermute | solution.py:148
  3.6 1.5 %collective-permute-start.3 = (bf16[128,1024]{1,0:T(8,128)(2,1)}, bf16[128,1024]{1,0:T(8,128)(2,1)S(1)}, u32[]{:S(2)}, u32[]{:S(2)}) collective-permute-start(bf16[128,1024]{1,0:T(8,128)(2,1)} %tokens_ref.3), channel_id=1, source_target_pairs={{0,4},{1,5},{2,6},{3,7},{4,0},{5,1},{6,2},{7,3},{8,12},{9,13},{10,... | collective-permute-start | bytes 786440 | tf_op jit(solution)/shard_map/ppermute | solution.py:148
  5.2 1.3 %copy-done = bf16[128,5248]{1,0:T(8,128)(2,1)S(1)} copy-done((bf16[128,5248]{1,0:T(8,128)(2,1)S(1)}, bf16[128,5248]{1,0:T(8,128)(2,1)}, u32[]{:S(2)}) %copy-start) | copy-done | bytes 1343512
  6.5 0.7 %copy-done.5 = bf16[2,32,128]{2,1,0:T(8,128)(2,1)S(1)} copy-done((bf16[2,32,128]{2,1,0:T(8,128)(2,1)S(1)}, bf16[2,32,128]{2,1,0:T(8,128)(2,1)}, u32[]{:S(2)}) %copy-start.5) | copy-done | bytes 16408
  7.2 0.5 shard_map.104
  7.7 0.6 collective-permute-start.1
  8.3 0.1 collective-permute-start.4
  8.4 2.9 %collective-permute-start.5 = (bf16[1376,128]{1,0:T(8,128)(2,1)S(1)}, bf16[1376,128]{1,0:T(8,128)(2,1)S(1)}, u32[]{:S(2)}, u32[]{:S(2)}) collective-permute-start(bf16[1376,128]{1,0:T(8,128)(2,1)S(1)} %get-tuple-element.19), channel_id=1, source_target_pairs={{0,6},{1,7},{2,4},{3,5},{4,2},{5,3},{6,0},{7,1},{8,14},{9,15},{10,... | collective-permute-start | bytes 1056776 | tf_op jit(solution)/shard_map/ppermute | solution.py:148
  11.3 1.8 %collective-permute-done.3.tokens_ref = bf16[128,1024]{1,0:T(8,128)(2,1)S(1)} collective-permute-done((bf16[128,1024]{1,0:T(8,128)(2,1)}, bf16[128,1024]{1,0:T(8,128)(2,1)S(1)}, u32[]{:S(2)}, u32[]{:S(2)}) %collective-permute-start.3) | collective-permute-done | bytes 262176 | tf_op jit(solution)/shard_map/ppermute | solution.py:148
  13.1 5.9 %collective-permute-done.1.refs_1_ = bf16[1376,128]{1,0:T(8,128)(2,1)S(1)} collective-permute-done((bf16[1376,128]{1,0:T(8,128)(2,1)S(1)}, bf16[1376,128]{1,0:T(8,128)(2,1)S(1)}, u32[]{:S(2)}, u32[]{:S(2)}) %collective-permute-start.1) | collective-permute-done | bytes 352288 | tf_op jit(solution)/shard_map/ppermute | solution.py:148
  18.9 7.8 %collective-permute-done.4.refs_2_ = bf16[1376,128]{1,0:T(8,128)(2,1)S(1)} collective-permute-done((bf16[1376,128]{1,0:T(8,128)(2,1)S(1)}, bf16[1376,128]{1,0:T(8,128)(2,1)S(1)}, u32[]{:S(2)}, u32[]{:S(2)}) %collective-permute-start.4) | collective-permute-done | bytes 352288 | tf_op jit(solution)/shard_map/ppermute | solution.py:148
  26.7 0.5 collective-permute-start.9
  27.2 1.5 %collective-permute-start.10 = (bf16[128,1024]{1,0:T(8,128)(2,1)S(1)}, bf16[128,1024]{1,0:T(8,128)(2,1)S(1)}, u32[]{:S(2)}, u32[]{:S(2)}) collective-permute-start(bf16[128,1024]{1,0:T(8,128)(2,1)S(1)} %copy-done.1), channel_id=1, source_target_pairs={{0,6},{1,7},{2,4},{3,5},{4,2},{5,3},{6,0},{7,1},{8,14},{9,15},{10,... | collective-permute-start | bytes 786440 | tf_op jit(solution)/shard_map/ppermute | solution.py:148
  28.7 0.1 collective-permute-done.9.refs_7_
  28.9 0.9 %shard_map.105 = (bf16[656,1024]{1,0:T(8,128)(2,1)S(1)}, bf16[656,1024]{1,0:T(8,128)(2,1)S(1)}, bf16[656,1024]{1,0:T(8,128)(2,1)S(1)}, bf16[512,128]{1,0:T(8,128)(2,1)S(1)}) custom-call(bf16[328,1024]{1,0:T(8,128)(2,1)S(1)} %copy-done.2, bf16[328,1024]{1,0:T(8,128)(2,1)S(1)} %collective-permute-done.wo_other, ...), custom_call_target="tpu_custom_call" | custom-call | tf_op jit(solution)/shard_map/pallas_call | solution.py:167
  29.8 1.4 %shard_map.109 = bf16[128,1024]{1,0:T(8,128)(2,1)S(1)} custom-call(f32[1,1024]{1,0:T(1,128)S(1)} %bitcast.5, bf16[656,1024]{1,0:T(8,128)(2,1)S(1)} %get-tuple-element.20.gelu_w, bf16[656,1024]{1,0:T(8,128)(2,1)S(1)} %get-tuple-element.21.gate_w, bf16[656,1024]{1,0:T(8,128)(2,1)S(1)} %get-tuple-element.22.wo_part, ...), custom_call_target="tpu_custom_call" | custom-call | tf_op jit(solution)/shard_map/pallas_call | solution.py:191
  31.1 1.4 %collective-permute-start.13 = (bf16[128,1024]{1,0:T(8,128)(2,1)S(1)}, bf16[128,1024]{1,0:T(8,128)(2,1)S(1)}, u32[]{:S(2)}, u32[]{:S(2)}) collective-permute-start(bf16[128,1024]{1,0:T(8,128)(2,1)S(1)} %shard_map.109), channel_id=1, source_target_pairs={{0,2},{1,3},{2,0},{3,1},{4,6},{5,7},{6,4},{7,5},{8,10},{9,11},{10,... | collective-permute-start | bytes 786440 | tf_op jit(solution)/shard_map/ppermute | solution.py:148
  32.6 1.4 %shard_map.108 = bf16[128,1024]{1,0:T(8,128)(2,1)S(1)} custom-call(f32[1,1024]{1,0:T(1,128)S(1)} %bitcast.6, bf16[656,1024]{1,0:T(8,128)(2,1)S(1)} %get-tuple-element.20.gelu_w, bf16[656,1024]{1,0:T(8,128)(2,1)S(1)} %get-tuple-element.21.gate_w, bf16[656,1024]{1,0:T(8,128)(2,1)S(1)} %get-tuple-element.22.wo_part, ...), custom_call_target="tpu_custom_call" | custom-call | tf_op jit(solution)/shard_map/pallas_call | solution.py:191
  34.0 1.6 %collective-permute-start.14 = (bf16[512,128]{1,0:T(8,128)(2,1)S(1)}, bf16[512,128]{1,0:T(8,128)(2,1)S(1)}, u32[]{:S(2)}, u32[]{:S(2)}) collective-permute-start(bf16[512,128]{1,0:T(8,128)(2,1)S(1)} %get-tuple-element.25.refs_3_), channel_id=1, source_target_pairs={{0,8},{8,0},{16,24},{24,16},{1,9},{9,1},{17,25},{25,17},{2,10},{10... | collective-permute-start | bytes 393224 | tf_op jit(solution)/shard_map/ppermute | solution.py:148
  35.6 0.7 %collective-permute-start.12 = (bf16[128,1024]{1,0:T(8,128)(2,1)S(1)}, bf16[128,1024]{1,0:T(8,128)(2,1)S(1)}, u32[]{:S(2)}, u32[]{:S(2)}) collective-permute-start(bf16[128,1024]{1,0:T(8,128)(2,1)S(1)} %shard_map.108), channel_id=1, source_target_pairs={{0,4},{1,5},{2,6},{3,7},{4,0},{5,1},{6,2},{7,3},{8,12},{9,13},{10,... | collective-permute-start | bytes 786440 | tf_op jit(solution)/shard_map/ppermute | solution.py:148
  36.3 1.0 %collective-permute-done.10.tokens_ref = bf16[128,1024]{1,0:T(8,128)(2,1)S(1)} collective-permute-done((bf16[128,1024]{1,0:T(8,128)(2,1)S(1)}, bf16[128,1024]{1,0:T(8,128)(2,1)S(1)}, u32[]{:S(2)}, u32[]{:S(2)}) %collective-permute-start.10) | collective-permute-done | bytes 262176 | tf_op jit(solution)/shard_map/ppermute | solution.py:148
  37.3 1.4 %shard_map.107 = bf16[128,1024]{1,0:T(8,128)(2,1)S(1)} custom-call(f32[1,1024]{1,0:T(1,128)S(1)} %bitcast.7, bf16[656,1024]{1,0:T(8,128)(2,1)S(1)} %get-tuple-element.20.gelu_w, bf16[656,1024]{1,0:T(8,128)(2,1)S(1)} %get-tuple-element.21.gate_w, bf16[656,1024]{1,0:T(8,128)(2,1)S(1)} %get-tuple-element.22.wo_part, ...), custom_call_target="tpu_custom_call" | custom-call | tf_op jit(solution)/shard_map/pallas_call | solution.py:191
  38.7 0.0 copy-start.3
  38.7 1.6 %collective-permute-start.11 = (bf16[128,1024]{1,0:T(8,128)(2,1)S(1)}, bf16[128,1024]{1,0:T(8,128)(2,1)S(1)}, u32[]{:S(2)}, u32[]{:S(2)}) collective-permute-start(bf16[128,1024]{1,0:T(8,128)(2,1)S(1)} %shard_map.107), channel_id=1, source_target_pairs={{0,6},{1,7},{2,4},{3,5},{4,2},{5,3},{6,0},{7,1},{8,14},{9,15},{10,... | collective-permute-start | bytes 786440 | tf_op jit(solution)/shard_map/ppermute | solution.py:148
  40.3 2.6 %collective-permute-start.15 = (bf16[512,128]{1,0:T(8,128)(2,1)S(1)}, bf16[512,128]{1,0:T(8,128)(2,1)S(1)}, u32[]{:S(2)}, u32[]{:S(2)}) collective-permute-start(bf16[512,128]{1,0:T(8,128)(2,1)S(1)} %get-tuple-element.25.refs_3_), channel_id=1, source_target_pairs={{0,16},{8,24},{16,0},{24,8},{1,17},{9,25},{17,1},{25,9},{2,18},{10... | collective-permute-start | bytes 393224 | tf_op jit(solution)/shard_map/ppermute | solution.py:148
  42.9 1.4 %collective-permute-start.16 = (bf16[512,128]{1,0:T(8,128)(2,1)S(1)}, bf16[512,128]{1,0:T(8,128)(2,1)S(1)}, u32[]{:S(2)}, u32[]{:S(2)}) collective-permute-start(bf16[512,128]{1,0:T(8,128)(2,1)S(1)} %get-tuple-element.25.refs_3_), channel_id=1, source_target_pairs={{0,24},{8,16},{16,8},{24,0},{1,25},{9,17},{17,9},{25,1},{2,26},{10... | collective-permute-start | bytes 393224 | tf_op jit(solution)/shard_map/ppermute | solution.py:148
  44.2 1.4 %shard_map.106.own_ref = f32[128,1024]{1,0:T(8,128)S(1)} custom-call(f32[1,1024]{1,0:T(1,128)S(1)} %bitcast.8, bf16[656,1024]{1,0:T(8,128)(2,1)S(1)} %get-tuple-element.20.gelu_w, bf16[656,1024]{1,0:T(8,128)(2,1)S(1)} %get-tuple-element.21.gate_w, bf16[656,1024]{1,0:T(8,128)(2,1)S(1)} %get-tuple-element.22.wo_part, bf16[128,1024]{1,0:T(8,128)(2,1)S(1)} %copy-done.1), custom_call_target="tpu_custom_call" | custom-call | tf_op jit(solution)/shard_map/pallas_call | solution.py:191
  45.6 0.0 copy-start.7
  45.6 6.1 %collective-permute-done.15.refs_5_ = bf16[512,128]{1,0:T(8,128)(2,1)S(1)} collective-permute-done((bf16[512,128]{1,0:T(8,128)(2,1)S(1)}, bf16[512,128]{1,0:T(8,128)(2,1)S(1)}, u32[]{:S(2)}, u32[]{:S(2)}) %collective-permute-start.15) | collective-permute-done | bytes 131104 | tf_op jit(solution)/shard_map/ppermute | solution.py:148
  51.7 1.9 %shard_map.110 = (bf16[128,128]{1,0:T(8,128)(2,1)}, bf16[32,4,128]{2,1,0:T(4,128)(2,1)S(1)}) custom-call(s32[1,4]{1,0:T(1,128)S(1)} %copy-done.8, bf16[128,1024]{1,0:T(8,128)(2,1)S(1)} %copy-done.1, f32[1,1024]{1,0:T(1,128)S(1)} %bitcast.10, bf16[1024,128]{1,0:T(8,128)(2,1)S(1)} %copy-done.3, f32[128,1024]{1,0:T(8,128)S(1)} %shard_map.106.own_ref, ...), custom_call_target="tpu_custom_call" | custom-call | tf_op jit(solution)/shard_map/pallas_call | solution.py:202
  53.6 12.4 %all_to_all.5 = bf16[32,4,128]{2,1,0:T(4,128)(2,1)S(1)} all-to-all(bf16[32,4,128]{2,1,0:T(4,128)(2,1)S(1)} %get-tuple-element.27), channel_id=1, replica_groups=mesh['group'=4,'dev'=8] {'group','dev'}, dimensions={0} | all-to-all | bytes 65536 | tf_op jit(solution)/shard_map/all_to_all | solution.py:220
  66.0 0.7 %shard_map.111 = f32[2,100]{1,0:T(2,128)} custom-call(s32[2,100]{1,0:T(2,128)S(1)} %copy-done.7, bf16[4,8,4,128]{3,2,1,0:T(4,128)(2,1)S(1)} %bitcast.4), custom_call_target="tpu_custom_call" | custom-call | tf_op jit(solution)/shard_map/pallas_call | solution.py:221
  (29 shorter events, 0.1 us)
Async XLA Ops:
  0.6 10.6 %collective-permute-start.2 = (bf16[128,1024]{1,0:T(8,128)(2,1)}, bf16[128,1024]{1,0:T(8,128)(2,1)S(1)}, u32[]{:S(2)}, u32[]{:S(2)}) collective-permute-start(bf16[128,1024]{1,0:T(8,128)(2,1)} %tokens_ref.3), channel_id=1, source_target_pairs={{0,2},{1,3},{2,0},{3,1},{4,6},{5,7},{6,4},{7,5},{8,10},{9,11},{10,... | collective-permute-start | bytes 786440 | tf_op jit(solution)/shard_map/ppermute | solution.py:148
  3.6 9.4 %collective-permute-start.3 = (bf16[128,1024]{1,0:T(8,128)(2,1)}, bf16[128,1024]{1,0:T(8,128)(2,1)S(1)}, u32[]{:S(2)}, u32[]{:S(2)}) collective-permute-start(bf16[128,1024]{1,0:T(8,128)(2,1)} %tokens_ref.3), channel_id=1, source_target_pairs={{0,4},{1,5},{2,6},{3,7},{4,0},{5,1},{6,2},{7,3},{8,12},{9,13},{10,... | collective-permute-start | bytes 786440 | tf_op jit(solution)/shard_map/ppermute | solution.py:148
  5.2 1.3 %copy-start = (bf16[128,5248]{1,0:T(8,128)(2,1)S(1)}, bf16[128,5248]{1,0:T(8,128)(2,1)}, u32[]{:S(2)}) copy-start(bf16[128,5248]{1,0:T(8,128)(2,1)} %wi_ref.1) | copy-start | bytes 4030468
  6.5 0.7 %copy-start.5 = (bf16[2,32,128]{2,1,0:T(8,128)(2,1)S(1)}, bf16[2,32,128]{2,1,0:T(8,128)(2,1)}, u32[]{:S(2)}) copy-start(bf16[2,32,128]{2,1,0:T(8,128)(2,1)} %param.15) | copy-start | bytes 49156
  7.2 4.1 %copy-start.2 = (bf16[328,1024]{1,0:T(8,128)(2,1)S(1)}, bf16[328,1024]{1,0:T(8,128)(2,1)}, u32[]{:S(2)}) copy-start(bf16[328,1024]{1,0:T(8,128)(2,1)} %wo_mine.1) | copy-start | bytes 2015236
  7.2 20.0 %copy-start.1 = (bf16[128,1024]{1,0:T(8,128)(2,1)S(1)}, bf16[128,1024]{1,0:T(8,128)(2,1)}, u32[]{:S(2)}) copy-start(bf16[128,1024]{1,0:T(8,128)(2,1)} %tokens_ref.3) | copy-start | bytes 786436
  7.7 11.2 %collective-permute-start.1 = (bf16[1376,128]{1,0:T(8,128)(2,1)S(1)}, bf16[1376,128]{1,0:T(8,128)(2,1)S(1)}, u32[]{:S(2)}, u32[]{:S(2)}) collective-permute-start(bf16[1376,128]{1,0:T(8,128)(2,1)S(1)} %get-tuple-element.16), channel_id=1, source_target_pairs={{0,2},{1,3},{2,0},{3,1},{4,6},{5,7},{6,4},{7,5},{8,10},{9,11},{10,... | collective-permute-start | bytes 1056776 | tf_op jit(solution)/shard_map/ppermute | solution.py:148
  8.3 18.4 %collective-permute-start.4 = (bf16[1376,128]{1,0:T(8,128)(2,1)S(1)}, bf16[1376,128]{1,0:T(8,128)(2,1)S(1)}, u32[]{:S(2)}, u32[]{:S(2)}) collective-permute-start(bf16[1376,128]{1,0:T(8,128)(2,1)S(1)} %get-tuple-element.18), channel_id=1, source_target_pairs={{0,4},{1,5},{2,6},{3,7},{4,0},{5,1},{6,2},{7,3},{8,12},{9,13},{10,... | collective-permute-start | bytes 1056776 | tf_op jit(solution)/shard_map/ppermute | solution.py:148
  8.4 18.4 %collective-permute-start.5 = (bf16[1376,128]{1,0:T(8,128)(2,1)S(1)}, bf16[1376,128]{1,0:T(8,128)(2,1)S(1)}, u32[]{:S(2)}, u32[]{:S(2)}) collective-permute-start(bf16[1376,128]{1,0:T(8,128)(2,1)S(1)} %get-tuple-element.19), channel_id=1, source_target_pairs={{0,6},{1,7},{2,4},{3,5},{4,2},{5,3},{6,0},{7,1},{8,14},{9,15},{10,... | collective-permute-start | bytes 1056776 | tf_op jit(solution)/shard_map/ppermute | solution.py:148
  11.3 17.5 %collective-permute-start = (bf16[328,1024]{1,0:T(8,128)(2,1)S(1)}, bf16[328,1024]{1,0:T(8,128)(2,1)S(1)}, u32[]{:S(2)}, u32[]{:S(2)}) collective-permute-start(bf16[328,1024]{1,0:T(8,128)(2,1)S(1)} %copy-done.2), channel_id=1, source_target_pairs={{0,1},{1,0},{2,3},{3,2},{4,5},{5,4},{6,7},{7,6},{8,9},{9,8},{10,11... | collective-permute-start | bytes 2015240 | tf_op jit(solution)/shard_map/ppermute | solution.py:148
  13.1 16.7 %copy-start.4 = (f32[1024]{0:T(1024)S(1)}, f32[1024]{0:T(1024)}, u32[]{:S(2)}) copy-start(f32[1024]{0:T(1024)} %param.10) | copy-start | bytes 12292
  13.1 14.1 %collective-permute-start.6 = (bf16[1376,128]{1,0:T(8,128)(2,1)S(1)}, bf16[1376,128]{1,0:T(8,128)(2,1)S(1)}, u32[]{:S(2)}, u32[]{:S(2)}) collective-permute-start(bf16[1376,128]{1,0:T(8,128)(2,1)S(1)} %get-tuple-element.15.refs_0_), channel_id=1, source_target_pairs={{0,1},{1,0},{2,3},{3,2},{4,5},{5,4},{6,7},{7,6},{8,9},{9,8},{10,11... | collective-permute-start | bytes 1056776 | tf_op jit(solution)/shard_map/ppermute | solution.py:148
  18.9 9.8 %collective-permute-start.7 = (bf16[1376,128]{1,0:T(8,128)(2,1)S(1)}, bf16[1376,128]{1,0:T(8,128)(2,1)S(1)}, u32[]{:S(2)}, u32[]{:S(2)}) collective-permute-start(bf16[1376,128]{1,0:T(8,128)(2,1)S(1)} %collective-permute-done.1.refs_1_), channel_id=1, source_target_pairs={{0,1},{1,0},{2,3},{3,2},{4,5},{5,4},{6,7},{7,6},{8,9},{9,8},{10,11... | collective-permute-start | bytes 1056776 | tf_op jit(solution)/shard_map/ppermute | solution.py:148
  26.7 2.0 %collective-permute-start.8 = (bf16[1376,128]{1,0:T(8,128)(2,1)S(1)}, bf16[1376,128]{1,0:T(8,128)(2,1)S(1)}, u32[]{:S(2)}, u32[]{:S(2)}) collective-permute-start(bf16[1376,128]{1,0:T(8,128)(2,1)S(1)} %collective-permute-done.4.refs_2_), channel_id=1, source_target_pairs={{0,1},{1,0},{2,3},{3,2},{4,5},{5,4},{6,7},{7,6},{8,9},{9,8},{10,11... | collective-permute-start | bytes 1056776 | tf_op jit(solution)/shard_map/ppermute | solution.py:148
  26.7 2.2 %collective-permute-start.9 = (bf16[1376,128]{1,0:T(8,128)(2,1)S(1)}, bf16[1376,128]{1,0:T(8,128)(2,1)S(1)}, u32[]{:S(2)}, u32[]{:S(2)}) collective-permute-start(bf16[1376,128]{1,0:T(8,128)(2,1)S(1)} %collective-permute-done.5.refs_3_), channel_id=1, source_target_pairs={{0,1},{1,0},{2,3},{3,2},{4,5},{5,4},{6,7},{7,6},{8,9},{9,8},{10,11... | collective-permute-start | bytes 1056776 | tf_op jit(solution)/shard_map/ppermute | solution.py:148
  27.2 10.1 %collective-permute-start.10 = (bf16[128,1024]{1,0:T(8,128)(2,1)S(1)}, bf16[128,1024]{1,0:T(8,128)(2,1)S(1)}, u32[]{:S(2)}, u32[]{:S(2)}) collective-permute-start(bf16[128,1024]{1,0:T(8,128)(2,1)S(1)} %copy-done.1), channel_id=1, source_target_pairs={{0,6},{1,7},{2,4},{3,5},{4,2},{5,3},{6,0},{7,1},{8,14},{9,15},{10,... | collective-permute-start | bytes 786440 | tf_op jit(solution)/shard_map/ppermute | solution.py:148
  31.1 20.5 %collective-permute-start.13 = (bf16[128,1024]{1,0:T(8,128)(2,1)S(1)}, bf16[128,1024]{1,0:T(8,128)(2,1)S(1)}, u32[]{:S(2)}, u32[]{:S(2)}) collective-permute-start(bf16[128,1024]{1,0:T(8,128)(2,1)S(1)} %shard_map.109), channel_id=1, source_target_pairs={{0,2},{1,3},{2,0},{3,1},{4,6},{5,7},{6,4},{7,5},{8,10},{9,11},{10,... | collective-permute-start | bytes 786440 | tf_op jit(solution)/shard_map/ppermute | solution.py:148
  34.0 8.9 %collective-permute-start.14 = (bf16[512,128]{1,0:T(8,128)(2,1)S(1)}, bf16[512,128]{1,0:T(8,128)(2,1)S(1)}, u32[]{:S(2)}, u32[]{:S(2)}) collective-permute-start(bf16[512,128]{1,0:T(8,128)(2,1)S(1)} %get-tuple-element.25.refs_3_), channel_id=1, source_target_pairs={{0,8},{8,0},{16,24},{24,16},{1,9},{9,1},{17,25},{25,17},{2,10},{10... | collective-permute-start | bytes 393224 | tf_op jit(solution)/shard_map/ppermute | solution.py:148
  35.6 16.1 %collective-permute-start.12 = (bf16[128,1024]{1,0:T(8,128)(2,1)S(1)}, bf16[128,1024]{1,0:T(8,128)(2,1)S(1)}, u32[]{:S(2)}, u32[]{:S(2)}) collective-permute-start(bf16[128,1024]{1,0:T(8,128)(2,1)S(1)} %shard_map.108), channel_id=1, source_target_pairs={{0,4},{1,5},{2,6},{3,7},{4,0},{5,1},{6,2},{7,3},{8,12},{9,13},{10,... | collective-permute-start | bytes 786440 | tf_op jit(solution)/shard_map/ppermute | solution.py:148
  38.7 13.0 %copy-start.3 = (bf16[1024,128]{1,0:T(8,128)(2,1)S(1)}, bf16[1024,128]{1,0:T(8,128)(2,1)}, u32[]{:S(2)}) copy-start(bf16[1024,128]{1,0:T(8,128)(2,1)} %proj_ref.1) | copy-start | bytes 786436
  38.7 13.0 %copy-start.6 = (f32[1024]{0:T(1024)S(1)}, f32[1024]{0:T(1024)}, u32[]{:S(2)}) copy-start(f32[1024]{0:T(1024)} %param.13) | copy-start | bytes 12292
  38.7 13.0 %copy-start.8 = (s32[1,4]{1,0:T(1,128)S(1)}, s32[1,4]{1,0:T(1,128)}, u32[]{:S(2)}) copy-start(s32[1,4]{1,0:T(1,128)} %lengths_ref.1) | copy-start | bytes 52
  38.7 13.0 %collective-permute-start.11 = (bf16[128,1024]{1,0:T(8,128)(2,1)S(1)}, bf16[128,1024]{1,0:T(8,128)(2,1)S(1)}, u32[]{:S(2)}, u32[]{:S(2)}) collective-permute-start(bf16[128,1024]{1,0:T(8,128)(2,1)S(1)} %shard_map.107), channel_id=1, source_target_pairs={{0,6},{1,7},{2,4},{3,5},{4,2},{5,3},{6,0},{7,1},{8,14},{9,15},{10,... | collective-permute-start | bytes 786440 | tf_op jit(solution)/shard_map/ppermute | solution.py:148
  40.3 11.4 %collective-permute-start.15 = (bf16[512,128]{1,0:T(8,128)(2,1)S(1)}, bf16[512,128]{1,0:T(8,128)(2,1)S(1)}, u32[]{:S(2)}, u32[]{:S(2)}) collective-permute-start(bf16[512,128]{1,0:T(8,128)(2,1)S(1)} %get-tuple-element.25.refs_3_), channel_id=1, source_target_pairs={{0,16},{8,24},{16,0},{24,8},{1,17},{9,25},{17,1},{25,9},{2,18},{10... | collective-permute-start | bytes 393224 | tf_op jit(solution)/shard_map/ppermute | solution.py:148
  42.9 8.8 %collective-permute-start.16 = (bf16[512,128]{1,0:T(8,128)(2,1)S(1)}, bf16[512,128]{1,0:T(8,128)(2,1)S(1)}, u32[]{:S(2)}, u32[]{:S(2)}) collective-permute-start(bf16[512,128]{1,0:T(8,128)(2,1)S(1)} %get-tuple-element.25.refs_3_), channel_id=1, source_target_pairs={{0,24},{8,16},{16,8},{24,0},{1,25},{9,17},{17,9},{25,1},{2,26},{10... | collective-permute-start | bytes 393224 | tf_op jit(solution)/shard_map/ppermute | solution.py:148
  45.6 20.4 %copy-start.7 = (s32[2,100]{1,0:T(2,128)S(1)}, s32[2,100]{1,0:T(2,128)}, u32[]{:S(2)}) copy-start(s32[2,100]{1,0:T(2,128)} %cand_ref.1) | copy-start | bytes 2404

commit v4 on v3

--- a/solution.py
+++ b/solution.py
@@ -23,8 +23,8 @@
     )
 
 
-def split_kernel(chips, wi_ref, query_ref, *refs):
-    pieces, turned = refs[:chips], refs[chips]
+def split_kernel(chips, groups, wi_ref, *refs):
+    lines, pieces, turned = refs[:groups], refs[groups:-1], refs[-1]
     columns = wi_ref.shape[1]
     width = columns // 2
     part = width // chips
@@ -35,7 +35,9 @@
         for half in range(2):
             first = pl.multiple_of(half * width + (chip ^ step) * part, 16)
             pieces[step][half * part : (half + 1) * part] = turned[pl.ds(first, part), :]
-        pieces[step][2 * part :] = query_ref[...]
+        for far, line in enumerate(lines):
+            rows = line.shape[0]
+            pieces[step][2 * part + far * rows : 2 * part + (far + 1) * rows] = line[...]
 
 
 def join_kernel(chips, wo_mine, wo_other, *refs):
@@ -61,8 +63,9 @@
             queries[pl.ds(pl.multiple_of(at * own, own), own), :] = block[2 * part :]
 
 
-def ffn_kernel(gain_ref, gelu_w, gate_w, wo_part, tokens_ref, out_ref):
-    normed = norm_rows(tokens_ref[...].astype(jnp.float32), gain_ref[...])
+def ffn_kernel(gain_ref, gelu_w, gate_w, wo_part, *refs):
+    tokens, out_ref = jnp.concatenate([ref[...] for ref in refs[:-1]], axis=0), refs[-1]
+    normed = norm_rows(tokens.astype(jnp.float32), gain_ref[...])
     first = dot_nt(normed, gelu_w[...])
     second = dot_nt(normed, gate_w[...])
     hidden = (0.5 * first * (1.0 + lax.erf(first * 0.7071067811865476)) * second).astype(jnp.bfloat16)
@@ -73,7 +76,7 @@
 
 def finish_kernel(chips, lengths_ref, tokens_ref, gain_ref, proj_ref, own_ref, *refs):
     parts, refs = refs[: chips - 1], refs[chips - 1 :]
-    queries, (vectors_ref, out_ref) = refs[:-2], refs[-2:]
+    queries, vectors_ref, out_ref = refs
     mixed = tokens_ref[...].astype(jnp.float32) + own_ref[...]
     for part in parts:
         mixed = mixed + part[...].astype(jnp.float32)
@@ -85,36 +88,36 @@
     group, me = lax.axis_index("group"), lax.axis_index("dev")
     rows = vectors.shape[0]
     docs = out_ref.shape[1]
+    devices = 2 * chips
+    groups = out_ref.shape[0] // devices
     spot = me * rows + lax.broadcasted_iota(jnp.int32, (rows, 128), 0)
     inside, low = [], jnp.int32(0)
     for doc in range(docs):
         high = low + lengths_ref[0, doc]
         inside.append((spot >= low) & (spot < high))
         low = high
-    for far, block in enumerate(queries):
-        for start in range(0, block.shape[0], 128):
-            similar = dot_nt(vectors, block[start : start + 128, :])
-            best = [
-                jnp.max(jnp.where(inside[doc], similar, -jnp.inf), axis=0, keepdims=True)
-                for doc in range(docs)
-            ]
-            best = jnp.concatenate(best, axis=0).astype(jnp.bfloat16)
-            target = (group ^ far) * (2 * chips) + start // 64
-            out_ref[target] = best
-            out_ref[target + 1] = best
+    for start in range(0, queries.shape[0], 128):
+        similar = dot_nt(vectors, queries[start : start + 128, :])
+        best = [
+            jnp.max(jnp.where(inside[doc], similar, -jnp.inf), axis=0, keepdims=True)
+            for doc in range(docs)
+        ]
+        best = jnp.concatenate(best, axis=0).astype(jnp.bfloat16)
+        device, far = divmod(start // 64, groups)
+        out_ref[(group ^ far) * devices + device] = best
+        out_ref[(group ^ (far + 1)) * devices + device] = best
 
 
 def pick_kernel(query_len, cand_ref, best_ref, out_ref):
     groups, _, docs, lanes = best_ref.shape
     own, listed = cand_ref.shape
-    offset = (lax.axis_index("dev") % 2) * own * query_len
     scores = [jnp.zeros((1, listed), jnp.float32) for _ in range(own)]
     lane = lax.broadcasted_iota(jnp.int32, (docs, lanes), 1)
     label = lax.broadcasted_iota(jnp.int32, (docs, listed), 0)
     for far in range(groups):
         best = jnp.max(best_ref[far].astype(jnp.float32), axis=0)
         for query in range(own):
-            start = offset + query * query_len
+            start = ((lax.axis_index("group") ^ far) % 2) * own * query_len + query * query_len
             taken = jnp.where((lane >= start) & (lane < start + query_len), best, 0.0)
             value = jnp.sum(taken, axis=1, keepdims=True) / query_len
             wanted = cand_ref[query : query + 1, :] - far * docs
@@ -149,28 +152,33 @@
 
     per_query, query_len, vector_dim = query_vectors.shape
     query_own = query_vectors.reshape(-1, vector_dim)
-    wo_other = swap(wo_weight, 1)
-    tokens = [corpus_tokens] + [swap(corpus_tokens, 2 * step) for step in range(1, chips)]
-    if wi_weight.shape[0] == 128 and part % 16 == 0:
-        piece_shape = jax.ShapeDtypeStruct((2 * part + query_own.shape[0], 128), jnp.bfloat16)
+    lines = [query_own] + [swap(query_own, mask, "group") for mask in range(1, groups)]
+    line_rows = groups * query_own.shape[0]
+    near = [corpus_tokens] + [swap(corpus_tokens, 2 * step) for step in (1, 2)]
+    if wi_weight.shape[0] == 128 and part % 16 == 0 and chips == 4:
+        piece_shape = jax.ShapeDtypeStruct((2 * part + line_rows, 128), jnp.bfloat16)
         pieces = pl.pallas_call(
-            functools.partial(split_kernel, chips),
+            functools.partial(split_kernel, chips, groups),
             out_shape=[piece_shape] * chips,
-            in_specs=[vmem] * 2,
+            in_specs=[vmem] * (1 + groups),
             out_specs=[vmem] * chips,
             scratch_shapes=[pltpu.VMEM((wi_weight.shape[1], 128), jnp.bfloat16)],
             compiler_params=params,
-        )(wi_weight, query_own)
+        )(wi_weight, *lines)
         mine = [pieces[0]] + [swap(pieces[step], 2 * step) for step in range(1, chips)]
-        mine[1], tokens[1], tokens[2] = lax.optimization_barrier((mine[1], tokens[1], tokens[2]))
+        near[1], near[2], wo_own = lax.optimization_barrier((near[1], near[2], wo_weight))
+        wo_other = swap(wo_own, 1)
+        mine[1], near[1], near[2] = lax.optimization_barrier((mine[1], near[1], near[2]))
+        far = [swap(near[2][: rows // 2], 2), swap(near[1][rows // 2 :], 4)]
+        tokens = [[each] for each in near] + [far]
         other = [swap(piece, 1) for piece in mine]
-        *weights, plane = pl.pallas_call(
+        *weights, queries = pl.pallas_call(
             functools.partial(join_kernel, chips),
             out_shape=[
                 jax.ShapeDtypeStruct((part, width), jnp.bfloat16),
                 jax.ShapeDtypeStruct((part, width), jnp.bfloat16),
                 jax.ShapeDtypeStruct((part, wo_weight.shape[1]), jnp.bfloat16),
-                jax.ShapeDtypeStruct((devices * query_own.shape[0], vector_dim), jnp.bfloat16),
+                jax.ShapeDtypeStruct((devices * line_rows, vector_dim), jnp.bfloat16),
             ],
             in_specs=[vmem] * (2 + 2 * chips),
             out_specs=[vmem] * 4,
@@ -181,22 +189,27 @@
         whole = lax.all_gather(wi_weight, "dev", axis=0, tiled=True).reshape(width, 2, chips, part)
         columns = lax.dynamic_index_in_dim(whole, me // 2, 2, keepdims=False)
         even = (me % 2) == 0
+        wo_other = swap(wo_weight, 1)
         wo_part = jnp.concatenate(
             [jnp.where(even, wo_weight, wo_other), jnp.where(even, wo_other, wo_weight)], axis=0
         )
         weights = [columns[:, 0].T, columns[:, 1].T, wo_part]
-        plane = lax.all_gather(query_own, "dev", axis=0, tiled=True)
-    partial = [None] * chips
+        queries = lax.all_gather(jnp.concatenate(lines, axis=0), "dev", axis=0, tiled=True)
+        tokens = [[each] for each in near]
+        tokens += [[swap(corpus_tokens, 2 * step)] for step in range(3, chips)]
+    partial, arrived = [None] * chips, [None] * chips
     for step in list(range(1, chips)) + [0]:
+        if step == 0:
+            arrived[1], tokens[0][0] = lax.optimization_barrier((arrived[1], tokens[0][0]))
         partial[step] = pl.pallas_call(
             ffn_kernel,
             out_shape=jax.ShapeDtypeStruct((rows, width), jnp.bfloat16 if step else jnp.float32),
-            in_specs=[vmem] * 5,
+            in_specs=[vmem] * (4 + len(tokens[step])),
             out_specs=vmem,
             compiler_params=params,
-        )(norm_gain.reshape(1, -1), *weights, tokens[step])
-    arrived = [swap(partial[step], 2 * step) for step in range(1, chips)]
-    queries = [plane] + [swap(plane, mask, "group") for mask in range(1, groups)]
+        )(norm_gain.reshape(1, -1), *weights, *tokens[step])
+        if step:
+            arrived[step] = swap(partial[step], 2 * step)
 
     docs = doc_lengths.shape[1]
     vectors, best = pl.pallas_call(
@@ -205,7 +218,7 @@
             jax.ShapeDtypeStruct((rows, proj_weight.shape[1]), jnp.bfloat16),
             jax.ShapeDtypeStruct((groups * devices, docs, 128), jnp.bfloat16),
         ],
-        in_specs=[smem] + [vmem] * (4 + chips - 1 + groups),
+        in_specs=[smem] + [vmem] * (4 + chips - 1 + 1),
         out_specs=[vmem, vmem],
         compiler_params=params,
     )(
@@ -214,8 +227,8 @@
         final_gain.reshape(1, -1),
         proj_weight,
         partial[0],
-        *arrived[::-1],
-        *queries,
+        *arrived[:0:-1],
+        queries,
     )
     met = lax.all_to_all(best, ("group", "dev"), split_axis=0, concat_axis=0, tiled=True)
     scores = pl.pallas_call(

time: 66.9 us -> 68.6 us (1.025)
  waiting for transfers between devices: 22.7 us -> 25.7 us
  blocking collectives: 12.4 us -> 10.8 us
    ppermute x17 -> x18, waiting for transfers between devices: 22.7 us -> 25.7 us  [swap(): return lax.ppermute(values, axis, [(i, i ^ mask) for i in range(size)])]
    all_to_all x1, blocking collectives: 12.4 us -> 10.8 us  [body(): lax.all_to_all(best, ('group', 'dev'), split_axis=0, concat_axis=0, tiled...]
    ppermute x17 -> x18, starting transfers between devices: 19.3 us -> 19.4 us  [swap(): return lax.ppermute(values, axis, [(i, i ^ mask) for i in range(size)])]
  transfers between devices with their start and end apart: 17 -> 18, of which waited for: 6 -> 5; matrix products, arithmetic and copies ran while one was open for 0% -> 0% of each run, Pallas kernels for 10% -> 10%
where the time goes in v4:
time: 68.6 us; the launch traced here: 68.4 us
  waiting for transfers between devices  25.7 us (37%)
  starting transfers between devices  19.4 us (28%)
  blocking collectives  10.8 us (16%)
  Pallas kernels  9.64 us (14%)
  local copies, waits for them, and re-layouts  2.11 us (3%)
  between operations  0.79 us (1%)
    ppermute x18, waiting for transfers between devices, swap(): return lax.ppermute(values, axis, [(i, i ^ mask) for i in range(size)])  25.7 us
    ppermute x18, starting transfers between devices, swap(): return lax.ppermute(values, axis, [(i, i ^ mask) for i in range(size)])  19.4 us
    all_to_all x1, blocking collectives, body(): lax.all_to_all(best, ('group', 'dev'), split_axis=0, concat_axis=0, tiled...  10.8 us
    pallas_call x4, Pallas kernels, body(): pl.pallas_call(ffn_kernel, out_shape=jax.ShapeDtypeStruct((rows, width),...  5.51 us
    unnamed x18, local copies, waits for them, and re-layouts  2.09 us
    pallas_call x1, Pallas kernels, body(): pl.pallas_call(functools.partial(finish_kernel, chips), out_shape=[jax.Sh...  2.06 us
  transfers between devices with their start and end apart: 18, of which 5 were waited for; matrix products, arithmetic and copies ran while one was open for 0% of the time, Pallas kernels for 10%

profile of v4, /device:TPU:0, one launch (start us, length us, event | category | flops | bytes accessed | tf_op | source)
XLA Modules:
  0.0 68.4 jit_solution(1772358705212106257)
XLA Ops:
  0.6 3.1 %collective-permute-start.3 = (bf16[64,128]{1,0:T(8,128)(2,1)}, bf16[64,128]{1,0:T(8,128)(2,1)S(1)}, u32[]{:S(2)}, u32[]{:S(2)}) collective-permute-start(bf16[64,128]{1,0:T(8,128)(2,1)} %bitcast.9), channel_id=1, source_target_pairs={{0,8},{8,0},{16,24},{24,16},{1,9},{9,1},{17,25},{25,17},{2,10},{10... | collective-permute-start | bytes 49160 | tf_op jit(solution)/shard_map/ppermute | solution.py:151
  3.7 2.6 %collective-permute-start.4 = (bf16[64,128]{1,0:T(8,128)(2,1)}, bf16[64,128]{1,0:T(8,128)(2,1)S(1)}, u32[]{:S(2)}, u32[]{:S(2)}) collective-permute-start(bf16[64,128]{1,0:T(8,128)(2,1)} %bitcast.10), channel_id=1, source_target_pairs={{0,16},{8,24},{16,0},{24,8},{1,17},{9,25},{17,1},{25,9},{2,18},{10... | collective-permute-start | bytes 49160 | tf_op jit(solution)/shard_map/ppermute | solution.py:151
  6.3 1.7 %collective-permute-start = (bf16[128,1024]{1,0:T(8,128)(2,1)}, bf16[128,1024]{1,0:T(8,128)(2,1)S(1)}, u32[]{:S(2)}, u32[]{:S(2)}) collective-permute-start(bf16[128,1024]{1,0:T(8,128)(2,1)} %tokens_ref.1), channel_id=1, source_target_pairs={{0,2},{1,3},{2,0},{3,1},{4,6},{5,7},{6,4},{7,5},{8,10},{9,11},{10,... | collective-permute-start | bytes 786440 | tf_op jit(solution)/shard_map/ppermute | solution.py:151
  8.0 1.5 %collective-permute-start.1 = (bf16[128,1024]{1,0:T(8,128)(2,1)}, bf16[128,1024]{1,0:T(8,128)(2,1)S(1)}, u32[]{:S(2)}, u32[]{:S(2)}) collective-permute-start(bf16[128,1024]{1,0:T(8,128)(2,1)} %tokens_ref.1), channel_id=1, source_target_pairs={{0,4},{1,5},{2,6},{3,7},{4,0},{5,1},{6,2},{7,3},{8,12},{9,13},{10,... | collective-permute-start | bytes 786440 | tf_op jit(solution)/shard_map/ppermute | solution.py:151
  9.5 2.5 %collective-permute-done.5.refs_3_ = bf16[64,128]{1,0:T(8,128)(2,1)S(1)} collective-permute-done((bf16[64,128]{1,0:T(8,128)(2,1)}, bf16[64,128]{1,0:T(8,128)(2,1)S(1)}, u32[]{:S(2)}, u32[]{:S(2)}) %collective-permute-start.5) | collective-permute-done | bytes 16416 | tf_op jit(solution)/shard_map/ppermute | solution.py:151
  12.1 1.3 %copy-done = bf16[128,5248]{1,0:T(8,128)(2,1)S(1)} copy-done((bf16[128,5248]{1,0:T(8,128)(2,1)S(1)}, bf16[128,5248]{1,0:T(8,128)(2,1)}, u32[]{:S(2)}) %copy-start) | copy-done | bytes 1343512
  13.4 0.7 %copy-done.5 = bf16[2,32,128]{2,1,0:T(8,128)(2,1)S(1)} copy-done((bf16[2,32,128]{2,1,0:T(8,128)(2,1)S(1)}, bf16[2,32,128]{2,1,0:T(8,128)(2,1)}, u32[]{:S(2)}) %copy-start.5) | copy-done | bytes 16408
  14.1 0.5 shard_map.104
  14.6 1.6 %collective-permute-start.6 = (bf16[1568,128]{1,0:T(8,128)(2,1)S(1)}, bf16[1568,128]{1,0:T(8,128)(2,1)S(1)}, u32[]{:S(2)}, u32[]{:S(2)}) collective-permute-start(bf16[1568,128]{1,0:T(8,128)(2,1)S(1)} %get-tuple-element.22), channel_id=1, source_target_pairs={{0,2},{1,3},{2,0},{3,1},{4,6},{5,7},{6,4},{7,5},{8,10},{9,11},{10,... | collective-permute-start | bytes 1204232 | tf_op jit(solution)/shard_map/ppermute | solution.py:151
  16.2 1.5 %collective-permute-start.7 = (bf16[1568,128]{1,0:T(8,128)(2,1)S(1)}, bf16[1568,128]{1,0:T(8,128)(2,1)S(1)}, u32[]{:S(2)}, u32[]{:S(2)}) collective-permute-start(bf16[1568,128]{1,0:T(8,128)(2,1)S(1)} %get-tuple-element.26), channel_id=1, source_target_pairs={{0,4},{1,5},{2,6},{3,7},{4,0},{5,1},{6,2},{7,3},{8,12},{9,13},{10,... | collective-permute-start | bytes 1204232 | tf_op jit(solution)/shard_map/ppermute | solution.py:151
  17.7 0.5 collective-permute-start.8
  18.2 0.1 collective-permute-start.2
  18.3 0.5 collective-permute-start.9
  18.8 8.2 %collective-permute-done.6.refs_1_ = bf16[1568,128]{1,0:T(8,128)(2,1)S(1)} collective-permute-done((bf16[1568,128]{1,0:T(8,128)(2,1)S(1)}, bf16[1568,128]{1,0:T(8,128)(2,1)S(1)}, u32[]{:S(2)}, u32[]{:S(2)}) %collective-permute-start.6) | collective-permute-done | bytes 401440 | tf_op jit(solution)/shard_map/ppermute | solution.py:151
  26.9 6.9 %collective-permute-done.7.refs_2_ = bf16[1568,128]{1,0:T(8,128)(2,1)S(1)} collective-permute-done((bf16[1568,128]{1,0:T(8,128)(2,1)S(1)}, bf16[1568,128]{1,0:T(8,128)(2,1)S(1)}, u32[]{:S(2)}, u32[]{:S(2)}) %collective-permute-start.7) | collective-permute-done | bytes 401440 | tf_op jit(solution)/shard_map/ppermute | solution.py:151
  33.8 0.5 collective-permute-start.12
  34.4 0.8 %collective-permute-start.14 = (bf16[64,1024]{1,0:T(8,128)(2,1)S(1)}, bf16[64,1024]{1,0:T(8,128)(2,1)S(1)}, u32[]{:S(2)}, u32[]{:S(2)}) collective-permute-start(bf16[64,1024]{1,0:T(8,128)(2,1)S(1)} %slice.6), channel_id=1, source_target_pairs={{0,2},{1,3},{2,0},{3,1},{4,6},{5,7},{6,4},{7,5},{8,10},{9,11},{10,... | collective-permute-start | bytes 393224 | tf_op jit(solution)/shard_map/ppermute | solution.py:151
  35.2 1.3 %collective-permute-start.15 = (bf16[64,1024]{1,0:T(8,128)(2,1)S(1)}, bf16[64,1024]{1,0:T(8,128)(2,1)S(1)}, u32[]{:S(2)}, u32[]{:S(2)}) collective-permute-start(bf16[64,1024]{1,0:T(8,128)(2,1)S(1)} %slice.7), channel_id=1, source_target_pairs={{0,4},{1,5},{2,6},{3,7},{4,0},{5,1},{6,2},{7,3},{8,12},{9,13},{10,... | collective-permute-start | bytes 393224 | tf_op jit(solution)/shard_map/ppermute | solution.py:151
  36.5 0.9 %shard_map.105 = (bf16[656,1024]{1,0:T(8,128)(2,1)S(1)}, bf16[656,1024]{1,0:T(8,128)(2,1)S(1)}, bf16[656,1024]{1,0:T(8,128)(2,1)S(1)}, bf16[2048,128]{1,0:T(8,128)(2,1)S(1)}) custom-call(bf16[328,1024]{1,0:T(8,128)(2,1)S(1)} %copy-done.2, bf16[328,1024]{1,0:T(8,128)(2,1)S(1)} %collective-permute-done.2.wo_other, ...), custom_call_target="tpu_custom_call" | custom-call | tf_op jit(solution)/shard_map/pallas_call | solution.py:175
  37.4 1.4 %shard_map.106 = bf16[128,1024]{1,0:T(8,128)(2,1)S(1)} custom-call(f32[1,1024]{1,0:T(1,128)S(1)} %bitcast.5, bf16[656,1024]{1,0:T(8,128)(2,1)S(1)} %get-tuple-element.28.gelu_w, bf16[656,1024]{1,0:T(8,128)(2,1)S(1)} %get-tuple-element.29.gate_w, bf16[656,1024]{1,0:T(8,128)(2,1)S(1)} %get-tuple-element.30.wo_part, ...), custom_call_target="tpu_custom_call" | custom-call | tf_op jit(solution)/shard_map/pallas_call | solution.py:204
  38.8 1.6 %collective-permute-start.13 = (bf16[128,1024]{1,0:T(8,128)(2,1)S(1)}, bf16[128,1024]{1,0:T(8,128)(2,1)S(1)}, u32[]{:S(2)}, u32[]{:S(2)}) collective-permute-start(bf16[128,1024]{1,0:T(8,128)(2,1)S(1)} %shard_map.106), channel_id=1, source_target_pairs={{0,2},{1,3},{2,0},{3,1},{4,6},{5,7},{6,4},{7,5},{8,10},{9,11},{10,... | collective-permute-start | bytes 786440 | tf_op jit(solution)/shard_map/ppermute | solution.py:151
  40.4 1.4 %shard_map.109 = bf16[128,1024]{1,0:T(8,128)(2,1)S(1)} custom-call(f32[1,1024]{1,0:T(1,128)S(1)} %bitcast.6, bf16[656,1024]{1,0:T(8,128)(2,1)S(1)} %get-tuple-element.28.gelu_w, bf16[656,1024]{1,0:T(8,128)(2,1)S(1)} %get-tuple-element.29.gate_w, bf16[656,1024]{1,0:T(8,128)(2,1)S(1)} %get-tuple-element.30.wo_part, ...), custom_call_target="tpu_custom_call" | custom-call | tf_op jit(solution)/shard_map/pallas_call | solution.py:204
  41.8 0.0 copy-start.1
  41.8 0.6 collective-permute-start.17
  42.4 1.4 %shard_map.108 = bf16[128,1024]{1,0:T(8,128)(2,1)S(1)} custom-call(f32[1,1024]{1,0:T(1,128)S(1)} %bitcast.7, bf16[656,1024]{1,0:T(8,128)(2,1)S(1)} %get-tuple-element.28.gelu_w, bf16[656,1024]{1,0:T(8,128)(2,1)S(1)} %get-tuple-element.29.gate_w, bf16[656,1024]{1,0:T(8,128)(2,1)S(1)} %get-tuple-element.30.wo_part, ...), custom_call_target="tpu_custom_call" | custom-call | tf_op jit(solution)/shard_map/pallas_call | solution.py:204
  43.8 1.5 %collective-permute-start.16 = (bf16[128,1024]{1,0:T(8,128)(2,1)S(1)}, bf16[128,1024]{1,0:T(8,128)(2,1)S(1)}, u32[]{:S(2)}, u32[]{:S(2)}) collective-permute-start(bf16[128,1024]{1,0:T(8,128)(2,1)S(1)} %shard_map.108), channel_id=1, source_target_pairs={{0,6},{1,7},{2,4},{3,5},{4,2},{5,3},{6,0},{7,1},{8,14},{9,15},{10,... | collective-permute-start | bytes 786440 | tf_op jit(solution)/shard_map/ppermute | solution.py:151
  45.3 2.0 %collective-permute-done.13.refs_2_ = bf16[128,1024]{1,0:T(8,128)(2,1)S(1)} collective-permute-done((bf16[128,1024]{1,0:T(8,128)(2,1)S(1)}, bf16[128,1024]{1,0:T(8,128)(2,1)S(1)}, u32[]{:S(2)}, u32[]{:S(2)}) %collective-permute-start.13) | collective-permute-done | bytes 262176 | tf_op jit(solution)/shard_map/ppermute | solution.py:151
  47.3 1.4 %shard_map.107.own_ref = f32[128,1024]{1,0:T(8,128)S(1)} custom-call(f32[1,1024]{1,0:T(1,128)S(1)} %bitcast.8, bf16[656,1024]{1,0:T(8,128)(2,1)S(1)} %get-tuple-element.28.gelu_w, bf16[656,1024]{1,0:T(8,128)(2,1)S(1)} %get-tuple-element.29.gate_w, bf16[656,1024]{1,0:T(8,128)(2,1)S(1)} %get-tuple-element.30.wo_part, bf16[128,1024]{1,0:T(8,128)(2,1)S(1)} %copy-done.1), custom_call_target="tpu_custom_call" | custom-call | tf_op jit(solution)/shard_map/pallas_call | solution.py:204
  48.7 6.1 %collective-permute-done.17.refs_1_ = bf16[128,1024]{1,0:T(8,128)(2,1)S(1)} collective-permute-done((bf16[128,1024]{1,0:T(8,128)(2,1)S(1)}, bf16[128,1024]{1,0:T(8,128)(2,1)S(1)}, u32[]{:S(2)}, u32[]{:S(2)}) %collective-permute-start.17) | collective-permute-done | bytes 262176 | tf_op jit(solution)/shard_map/ppermute | solution.py:151
  54.9 2.1 %shard_map.110 = (bf16[128,128]{1,0:T(8,128)(2,1)}, bf16[32,4,128]{2,1,0:T(4,128)(2,1)S(1)}) custom-call(s32[1,4]{1,0:T(1,128)S(1)} %copy-done.8, bf16[128,1024]{1,0:T(8,128)(2,1)S(1)} %copy-done.1, f32[1,1024]{1,0:T(1,128)S(1)} %bitcast.13, bf16[1024,128]{1,0:T(8,128)(2,1)S(1)} %copy-done.3, f32[128,1024]{1,0:T(8,128)S(1)} %shard_map.107.own_ref, ...), custom_call_target="tpu_custom_call" | custom-call | tf_op jit(solution)/shard_map/pallas_call | solution.py:215
  56.9 10.8 %all_to_all.5 = bf16[32,4,128]{2,1,0:T(4,128)(2,1)S(1)} all-to-all(bf16[32,4,128]{2,1,0:T(4,128)(2,1)S(1)} %get-tuple-element.37), channel_id=1, replica_groups=mesh['group'=4,'dev'=8] {'group','dev'}, dimensions={0} | all-to-all | bytes 65536 | tf_op jit(solution)/shard_map/all_to_all | solution.py:233
  67.7 0.7 shard_map.111
  (33 shorter events, 0.1 us)
Async XLA Ops:
  0.6 8.9 %collective-permute-start.3 = (bf16[64,128]{1,0:T(8,128)(2,1)}, bf16[64,128]{1,0:T(8,128)(2,1)S(1)}, u32[]{:S(2)}, u32[]{:S(2)}) collective-permute-start(bf16[64,128]{1,0:T(8,128)(2,1)} %bitcast.9), channel_id=1, source_target_pairs={{0,8},{8,0},{16,24},{24,16},{1,9},{9,1},{17,25},{25,17},{2,10},{10... | collective-permute-start | bytes 49160 | tf_op jit(solution)/shard_map/ppermute | solution.py:151
  3.7 5.8 %collective-permute-start.4 = (bf16[64,128]{1,0:T(8,128)(2,1)}, bf16[64,128]{1,0:T(8,128)(2,1)S(1)}, u32[]{:S(2)}, u32[]{:S(2)}) collective-permute-start(bf16[64,128]{1,0:T(8,128)(2,1)} %bitcast.10), channel_id=1, source_target_pairs={{0,16},{8,24},{16,0},{24,8},{1,17},{9,25},{17,1},{25,9},{2,18},{10... | collective-permute-start | bytes 49160 | tf_op jit(solution)/shard_map/ppermute | solution.py:151
  6.3 5.7 %collective-permute-start.5 = (bf16[64,128]{1,0:T(8,128)(2,1)}, bf16[64,128]{1,0:T(8,128)(2,1)S(1)}, u32[]{:S(2)}, u32[]{:S(2)}) collective-permute-start(bf16[64,128]{1,0:T(8,128)(2,1)} %bitcast.11), channel_id=1, source_target_pairs={{0,24},{8,16},{16,8},{24,0},{1,25},{9,17},{17,9},{25,1},{2,26},{10... | collective-permute-start | bytes 49160 | tf_op jit(solution)/shard_map/ppermute | solution.py:151
  6.3 11.9 %collective-permute-start = (bf16[128,1024]{1,0:T(8,128)(2,1)}, bf16[128,1024]{1,0:T(8,128)(2,1)S(1)}, u32[]{:S(2)}, u32[]{:S(2)}) collective-permute-start(bf16[128,1024]{1,0:T(8,128)(2,1)} %tokens_ref.1), channel_id=1, source_target_pairs={{0,2},{1,3},{2,0},{3,1},{4,6},{5,7},{6,4},{7,5},{8,10},{9,11},{10,... | collective-permute-start | bytes 786440 | tf_op jit(solution)/shard_map/ppermute | solution.py:151
  8.0 10.2 %collective-permute-start.1 = (bf16[128,1024]{1,0:T(8,128)(2,1)}, bf16[128,1024]{1,0:T(8,128)(2,1)S(1)}, u32[]{:S(2)}, u32[]{:S(2)}) collective-permute-start(bf16[128,1024]{1,0:T(8,128)(2,1)} %tokens_ref.1), channel_id=1, source_target_pairs={{0,4},{1,5},{2,6},{3,7},{4,0},{5,1},{6,2},{7,3},{8,12},{9,13},{10,... | collective-permute-start | bytes 786440 | tf_op jit(solution)/shard_map/ppermute | solution.py:151
  12.1 1.3 %copy-start = (bf16[128,5248]{1,0:T(8,128)(2,1)S(1)}, bf16[128,5248]{1,0:T(8,128)(2,1)}, u32[]{:S(2)}) copy-start(bf16[128,5248]{1,0:T(8,128)(2,1)} %wi_ref.1) | copy-start | bytes 4030468
  13.4 0.7 %copy-start.5 = (bf16[2,32,128]{2,1,0:T(8,128)(2,1)S(1)}, bf16[2,32,128]{2,1,0:T(8,128)(2,1)}, u32[]{:S(2)}) copy-start(bf16[2,32,128]{2,1,0:T(8,128)(2,1)} %param.15) | copy-start | bytes 49156
  14.1 4.1 %copy-start.2 = (bf16[328,1024]{1,0:T(8,128)(2,1)S(1)}, bf16[328,1024]{1,0:T(8,128)(2,1)}, u32[]{:S(2)}) copy-start(bf16[328,1024]{1,0:T(8,128)(2,1)} %wo_mine.1) | copy-start | bytes 2015236
  14.6 12.3 %collective-permute-start.6 = (bf16[1568,128]{1,0:T(8,128)(2,1)S(1)}, bf16[1568,128]{1,0:T(8,128)(2,1)S(1)}, u32[]{:S(2)}, u32[]{:S(2)}) collective-permute-start(bf16[1568,128]{1,0:T(8,128)(2,1)S(1)} %get-tuple-element.22), channel_id=1, source_target_pairs={{0,2},{1,3},{2,0},{3,1},{4,6},{5,7},{6,4},{7,5},{8,10},{9,11},{10,... | collective-permute-start | bytes 1204232 | tf_op jit(solution)/shard_map/ppermute | solution.py:151
  16.2 17.6 %collective-permute-start.7 = (bf16[1568,128]{1,0:T(8,128)(2,1)S(1)}, bf16[1568,128]{1,0:T(8,128)(2,1)S(1)}, u32[]{:S(2)}, u32[]{:S(2)}) collective-permute-start(bf16[1568,128]{1,0:T(8,128)(2,1)S(1)} %get-tuple-element.26), channel_id=1, source_target_pairs={{0,4},{1,5},{2,6},{3,7},{4,0},{5,1},{6,2},{7,3},{8,12},{9,13},{10,... | collective-permute-start | bytes 1204232 | tf_op jit(solution)/shard_map/ppermute | solution.py:151
  17.7 16.1 %collective-permute-start.8 = (bf16[1568,128]{1,0:T(8,128)(2,1)S(1)}, bf16[1568,128]{1,0:T(8,128)(2,1)S(1)}, u32[]{:S(2)}, u32[]{:S(2)}) collective-permute-start(bf16[1568,128]{1,0:T(8,128)(2,1)S(1)} %get-tuple-element.27), channel_id=1, source_target_pairs={{0,6},{1,7},{2,4},{3,5},{4,2},{5,3},{6,0},{7,1},{8,14},{9,15},{10,... | collective-permute-start | bytes 1204232 | tf_op jit(solution)/shard_map/ppermute | solution.py:151
  18.2 18.3 %collective-permute-start.2 = (bf16[328,1024]{1,0:T(8,128)(2,1)S(1)}, bf16[328,1024]{1,0:T(8,128)(2,1)S(1)}, u32[]{:S(2)}, u32[]{:S(2)}) collective-permute-start(bf16[328,1024]{1,0:T(8,128)(2,1)S(1)} %copy-done.2), channel_id=1, source_target_pairs={{0,1},{1,0},{2,3},{3,2},{4,5},{5,4},{6,7},{7,6},{8,9},{9,8},{10,11... | collective-permute-start | bytes 2015240 | tf_op jit(solution)/shard_map/ppermute | solution.py:151
  18.3 16.1 %collective-permute-start.9 = (bf16[1568,128]{1,0:T(8,128)(2,1)S(1)}, bf16[1568,128]{1,0:T(8,128)(2,1)S(1)}, u32[]{:S(2)}, u32[]{:S(2)}) collective-permute-start(bf16[1568,128]{1,0:T(8,128)(2,1)S(1)} %get-tuple-element.21.refs_0_), channel_id=1, source_target_pairs={{0,1},{1,0},{2,3},{3,2},{4,5},{5,4},{6,7},{7,6},{8,9},{9,8},{10,11... | collective-permute-start | bytes 1204232 | tf_op jit(solution)/shard_map/ppermute | solution.py:151
  26.9 8.3 %collective-permute-start.10 = (bf16[1568,128]{1,0:T(8,128)(2,1)S(1)}, bf16[1568,128]{1,0:T(8,128)(2,1)S(1)}, u32[]{:S(2)}, u32[]{:S(2)}) collective-permute-start(bf16[1568,128]{1,0:T(8,128)(2,1)S(1)} %collective-permute-done.6.refs_1_), channel_id=1, source_target_pairs={{0,1},{1,0},{2,3},{3,2},{4,5},{5,4},{6,7},{7,6},{8,9},{9,8},{10,11... | collective-permute-start | bytes 1204232 | tf_op jit(solution)/shard_map/ppermute | solution.py:151
  33.8 2.7 %collective-permute-start.11 = (bf16[1568,128]{1,0:T(8,128)(2,1)S(1)}, bf16[1568,128]{1,0:T(8,128)(2,1)S(1)}, u32[]{:S(2)}, u32[]{:S(2)}) collective-permute-start(bf16[1568,128]{1,0:T(8,128)(2,1)S(1)} %collective-permute-done.7.refs_2_), channel_id=1, source_target_pairs={{0,1},{1,0},{2,3},{3,2},{4,5},{5,4},{6,7},{7,6},{8,9},{9,8},{10,11... | collective-permute-start | bytes 1204232 | tf_op jit(solution)/shard_map/ppermute | solution.py:151
  33.8 2.7 %collective-permute-start.12 = (bf16[1568,128]{1,0:T(8,128)(2,1)S(1)}, bf16[1568,128]{1,0:T(8,128)(2,1)S(1)}, u32[]{:S(2)}, u32[]{:S(2)}) collective-permute-start(bf16[1568,128]{1,0:T(8,128)(2,1)S(1)} %collective-permute-done.8.refs_3_), channel_id=1, source_target_pairs={{0,1},{1,0},{2,3},{3,2},{4,5},{5,4},{6,7},{7,6},{8,9},{9,8},{10,11... | collective-permute-start | bytes 1204232 | tf_op jit(solution)/shard_map/ppermute | solution.py:151
  34.4 3.1 %copy-start.4 = (f32[1024]{0:T(1024)S(1)}, f32[1024]{0:T(1024)}, u32[]{:S(2)}) copy-start(f32[1024]{0:T(1024)} %param.10) | copy-start | bytes 12292
  34.4 8.0 %collective-permute-start.14 = (bf16[64,1024]{1,0:T(8,128)(2,1)S(1)}, bf16[64,1024]{1,0:T(8,128)(2,1)S(1)}, u32[]{:S(2)}, u32[]{:S(2)}) collective-permute-start(bf16[64,1024]{1,0:T(8,128)(2,1)S(1)} %slice.6), channel_id=1, source_target_pairs={{0,2},{1,3},{2,0},{3,1},{4,6},{5,7},{6,4},{7,5},{8,10},{9,11},{10,... | collective-permute-start | bytes 393224 | tf_op jit(solution)/shard_map/ppermute | solution.py:151
  35.2 7.2 %collective-permute-start.15 = (bf16[64,1024]{1,0:T(8,128)(2,1)S(1)}, bf16[64,1024]{1,0:T(8,128)(2,1)S(1)}, u32[]{:S(2)}, u32[]{:S(2)}) collective-permute-start(bf16[64,1024]{1,0:T(8,128)(2,1)S(1)} %slice.7), channel_id=1, source_target_pairs={{0,4},{1,5},{2,6},{3,7},{4,0},{5,1},{6,2},{7,3},{8,12},{9,13},{10,... | collective-permute-start | bytes 393224 | tf_op jit(solution)/shard_map/ppermute | solution.py:151
  38.8 8.5 %collective-permute-start.13 = (bf16[128,1024]{1,0:T(8,128)(2,1)S(1)}, bf16[128,1024]{1,0:T(8,128)(2,1)S(1)}, u32[]{:S(2)}, u32[]{:S(2)}) collective-permute-start(bf16[128,1024]{1,0:T(8,128)(2,1)S(1)} %shard_map.106), channel_id=1, source_target_pairs={{0,2},{1,3},{2,0},{3,1},{4,6},{5,7},{6,4},{7,5},{8,10},{9,11},{10,... | collective-permute-start | bytes 786440 | tf_op jit(solution)/shard_map/ppermute | solution.py:151
  41.8 5.5 %copy-start.1 = (bf16[128,1024]{1,0:T(8,128)(2,1)S(1)}, bf16[128,1024]{1,0:T(8,128)(2,1)}, u32[]{:S(2)}) copy-start(bf16[128,1024]{1,0:T(8,128)(2,1)} %tokens_ref.1) | copy-start | bytes 786436
  41.8 13.0 %collective-permute-start.17 = (bf16[128,1024]{1,0:T(8,128)(2,1)S(1)}, bf16[128,1024]{1,0:T(8,128)(2,1)S(1)}, u32[]{:S(2)}, u32[]{:S(2)}) collective-permute-start(bf16[128,1024]{1,0:T(8,128)(2,1)S(1)} %shard_map.109), channel_id=1, source_target_pairs={{0,4},{1,5},{2,6},{3,7},{4,0},{5,1},{6,2},{7,3},{8,12},{9,13},{10,... | collective-permute-start | bytes 786440 | tf_op jit(solution)/shard_map/ppermute | solution.py:151
  43.8 11.1 %copy-start.3 = (bf16[1024,128]{1,0:T(8,128)(2,1)S(1)}, bf16[1024,128]{1,0:T(8,128)(2,1)}, u32[]{:S(2)}) copy-start(bf16[1024,128]{1,0:T(8,128)(2,1)} %proj_ref.1) | copy-start | bytes 786436
  43.8 11.1 %copy-start.6 = (f32[1024]{0:T(1024)S(1)}, f32[1024]{0:T(1024)}, u32[]{:S(2)}) copy-start(f32[1024]{0:T(1024)} %param.13) | copy-start | bytes 12292
  43.8 11.1 %copy-start.8 = (s32[1,4]{1,0:T(1,128)S(1)}, s32[1,4]{1,0:T(1,128)}, u32[]{:S(2)}) copy-start(s32[1,4]{1,0:T(1,128)} %lengths_ref.1) | copy-start | bytes 52
  43.8 11.0 %collective-permute-start.16 = (bf16[128,1024]{1,0:T(8,128)(2,1)S(1)}, bf16[128,1024]{1,0:T(8,128)(2,1)S(1)}, u32[]{:S(2)}, u32[]{:S(2)}) collective-permute-start(bf16[128,1024]{1,0:T(8,128)(2,1)S(1)} %shard_map.108), channel_id=1, source_target_pairs={{0,6},{1,7},{2,4},{3,5},{4,2},{5,3},{6,0},{7,1},{8,14},{9,15},{10,... | collective-permute-start | bytes 786440 | tf_op jit(solution)/shard_map/ppermute | solution.py:151
  48.7 19.0 %copy-start.7 = (s32[2,100]{1,0:T(2,128)S(1)}, s32[2,100]{1,0:T(2,128)}, u32[]{:S(2)}) copy-start(s32[2,100]{1,0:T(2,128)} %cand_ref.1) | copy-start | bytes 2404

commit v5 on v3

--- a/solution.py
+++ b/solution.py
@@ -32,15 +32,16 @@
     for start in range(0, columns, 128):
         turned[start : start + 128, :] = wi_ref[:, start : start + 128].T
     for step in range(chips):
-        for half in range(2):
+        halves = (0, 1) if step < 3 else (lax.axis_index("group") % 2,)
+        for at, half in enumerate(halves):
             first = pl.multiple_of(half * width + (chip ^ step) * part, 16)
-            pieces[step][half * part : (half + 1) * part] = turned[pl.ds(first, part), :]
-        pieces[step][2 * part :] = query_ref[...]
+            pieces[step][at * part : (at + 1) * part] = turned[pl.ds(first, part), :]
+        pieces[step][len(halves) * part :] = query_ref[...]
 
 
 def join_kernel(chips, wo_mine, wo_other, *refs):
-    mine, other = refs[:chips], refs[chips : 2 * chips]
-    gelu_w, gate_w, wo_part, queries = refs[2 * chips :]
+    mine, other = refs[: chips + 1], refs[chips + 1 : 2 * chips + 2]
+    gelu_w, gate_w, wo_part, queries = refs[2 * chips + 2 :]
     chip, core = lax.axis_index("dev") // 2, lax.axis_index("dev") % 2
     rows = wo_mine.shape[0]
     for first, upper, lower in ((0, wo_mine, wo_other), (1, wo_other, wo_mine)):
@@ -54,15 +55,26 @@
     own = mine[0].shape[0] - 2 * part
     for step in range(chips):
         source = (chip ^ step) * 2
-        for block, at in ((mine[step], source + core), (other[step], source + 1 - core)):
+        for blocks, at in ((mine, source + core), (other, source + 1 - core)):
             columns = pl.ds(pl.multiple_of(at * 128, 128), 128)
-            gelu_w[:, columns] = block[:part]
-            gate_w[:, columns] = block[part : 2 * part]
-            queries[pl.ds(pl.multiple_of(at * own, own), own), :] = block[2 * part :]
-
-
-def ffn_kernel(gain_ref, gelu_w, gate_w, wo_part, tokens_ref, out_ref):
-    normed = norm_rows(tokens_ref[...].astype(jnp.float32), gain_ref[...])
+            if step < 3:
+                gelu_w[:, columns] = blocks[step][:part]
+                gate_w[:, columns] = blocks[step][part : 2 * part]
+            else:
+                for parity in range(2):
+
+                    @pl.when(lax.axis_index("group") % 2 == parity)
+                    def _(parity=parity, blocks=blocks, columns=columns):
+                        gelu_w[:, columns] = blocks[3 + parity][:part]
+                        gate_w[:, columns] = blocks[4 - parity][:part]
+
+            last = 2 * part if step < 3 else part
+            queries[pl.ds(pl.multiple_of(at * own, own), own), :] = blocks[step][last : last + own]
+
+
+def ffn_kernel(gain_ref, gelu_w, gate_w, wo_part, *refs):
+    tokens, out_ref = jnp.concatenate([ref[...] for ref in refs[:-1]], axis=0), refs[-1]
+    normed = norm_rows(tokens.astype(jnp.float32), gain_ref[...])
     first = dot_nt(normed, gelu_w[...])
     second = dot_nt(normed, gate_w[...])
     hidden = (0.5 * first * (1.0 + lax.erf(first * 0.7071067811865476)) * second).astype(jnp.bfloat16)
@@ -150,19 +162,25 @@
     per_query, query_len, vector_dim = query_vectors.shape
     query_own = query_vectors.reshape(-1, vector_dim)
     wo_other = swap(wo_weight, 1)
-    tokens = [corpus_tokens] + [swap(corpus_tokens, 2 * step) for step in range(1, chips)]
-    if wi_weight.shape[0] == 128 and part % 16 == 0:
-        piece_shape = jax.ShapeDtypeStruct((2 * part + query_own.shape[0], 128), jnp.bfloat16)
+    near = [corpus_tokens] + [swap(corpus_tokens, 2 * step) for step in (1, 2)]
+    if wi_weight.shape[0] == 128 and part % 16 == 0 and chips == 4 and groups % 2 == 0:
+        own = query_own.shape[0]
         pieces = pl.pallas_call(
             functools.partial(split_kernel, chips),
-            out_shape=[piece_shape] * chips,
+            out_shape=[
+                jax.ShapeDtypeStruct(((2 if step < 3 else 1) * part + own, 128), jnp.bfloat16)
+                for step in range(chips)
+            ],
             in_specs=[vmem] * 2,
             out_specs=[vmem] * chips,
             scratch_shapes=[pltpu.VMEM((wi_weight.shape[1], 128), jnp.bfloat16)],
             compiler_params=params,
         )(wi_weight, query_own)
         mine = [pieces[0]] + [swap(pieces[step], 2 * step) for step in range(1, chips)]
-        mine[1], tokens[1], tokens[2] = lax.optimization_barrier((mine[1], tokens[1], tokens[2]))
+        mine.append(swap(mine[3], 1, "group"))
+        mine[1], near[1], near[2] = lax.optimization_barrier((mine[1], near[1], near[2]))
+        far = [swap(near[2][: rows // 2], 2), swap(near[1][rows // 2 :], 4)]
+        tokens = [[each] for each in near] + [far]
         other = [swap(piece, 1) for piece in mine]
         *weights, plane = pl.pallas_call(
             functools.partial(join_kernel, chips),
@@ -170,9 +188,9 @@
                 jax.ShapeDtypeStruct((part, width), jnp.bfloat16),
                 jax.ShapeDtypeStruct((part, width), jnp.bfloat16),
                 jax.ShapeDtypeStruct((part, wo_weight.shape[1]), jnp.bfloat16),
-                jax.ShapeDtypeStruct((devices * query_own.shape[0], vector_dim), jnp.bfloat16),
+                jax.ShapeDtypeStruct((devices * own, vector_dim), jnp.bfloat16),
             ],
-            in_specs=[vmem] * (2 + 2 * chips),
+            in_specs=[vmem] * (4 + 2 * chips),
             out_specs=[vmem] * 4,
             compiler_params=params,
         )(wo_weight, wo_other, *mine, *other)
@@ -185,17 +203,22 @@
             [jnp.where(even, wo_weight, wo_other), jnp.where(even, wo_other, wo_weight)], axis=0
         )
         weights = [columns[:, 0].T, columns[:, 1].T, wo_part]
+        tokens = [[each] for each in near]
+        tokens += [[swap(corpus_tokens, 2 * step)] for step in range(3, chips)]
         plane = lax.all_gather(query_own, "dev", axis=0, tiled=True)
-    partial = [None] * chips
+    partial, arrived = [None] * chips, [None] * chips
     for step in list(range(1, chips)) + [0]:
+        if step == 0:
+            arrived[1], tokens[0][0] = lax.optimization_barrier((arrived[1], tokens[0][0]))
         partial[step] = pl.pallas_call(
             ffn_kernel,
             out_shape=jax.ShapeDtypeStruct((rows, width), jnp.bfloat16 if step else jnp.float32),
-            in_specs=[vmem] * 5,
+            in_specs=[vmem] * (4 + len(tokens[step])),
             out_specs=vmem,
             compiler_params=params,
-        )(norm_gain.reshape(1, -1), *weights, tokens[step])
-    arrived = [swap(partial[step], 2 * step) for step in range(1, chips)]
+        )(norm_gain.reshape(1, -1), *weights, *tokens[step])
+        if step:
+            arrived[step] = swap(partial[step], 2 * step)
     queries = [plane] + [swap(plane, mask, "group") for mask in range(1, groups)]
 
     docs = doc_lengths.shape[1]
@@ -214,7 +237,7 @@
         final_gain.reshape(1, -1),
         proj_weight,
         partial[0],
-        *arrived[::-1],
+        *arrived[:0:-1],
         *queries,
     )
     met = lax.all_to_all(best, ("group", "dev"), split_axis=0, concat_axis=0, tiled=True)

time: 66.9 us -> 72.7 us (1.087)
  starting transfers between devices: 19.3 us -> 23.6 us
  waiting for transfers between devices: 22.7 us -> 25.6 us
  blocking collectives: 12.4 us -> 11 us
    ppermute x17 -> x20, starting transfers between devices: 19.3 us -> 23.6 us  [swap(): return lax.ppermute(values, axis, [(i, i ^ mask) for i in range(size)])]
    ppermute x17 -> x20, waiting for transfers between devices: 22.7 us -> 25.6 us  [swap(): return lax.ppermute(values, axis, [(i, i ^ mask) for i in range(size)])]
    all_to_all x1, blocking collectives: 12.4 us -> 11 us  [body(): lax.all_to_all(best, ('group', 'dev'), split_axis=0, concat_axis=0, tiled...]
  transfers between devices with their start and end apart: 17 -> 20, of which waited for: 6 -> 6; matrix products, arithmetic and copies ran while one was open for 0% -> 0% of each run, Pallas kernels for 10% -> 9%
where the time goes in v5:
time: 72.7 us; the launch traced here: 72.4 us
  waiting for transfers between devices  25.6 us (35%)
  starting transfers between devices  23.6 us (32%)
  blocking collectives  11 us (15%)
  Pallas kernels  9.38 us (13%)
  local copies, waits for them, and re-layouts  2.09 us (3%)
  between operations  0.8 us (1%)
    ppermute x20, waiting for transfers between devices, swap(): return lax.ppermute(values, axis, [(i, i ^ mask) for i in range(size)])  25.6 us
    ppermute x20, starting transfers between devices, swap(): return lax.ppermute(values, axis, [(i, i ^ mask) for i in range(size)])  23.6 us
    all_to_all x1, blocking collectives, body(): lax.all_to_all(best, ('group', 'dev'), split_axis=0, concat_axis=0, tiled...  11 us
    pallas_call x4, Pallas kernels, body(): pl.pallas_call(ffn_kernel, out_shape=jax.ShapeDtypeStruct((rows, width),...  5.5 us
    unnamed x18, local copies, waits for them, and re-layouts  2.07 us
    pallas_call x1, Pallas kernels, body(): pl.pallas_call(functools.partial(finish_kernel, chips), out_shape=[jax.Sh...  1.85 us
  transfers between devices with their start and end apart: 20, of which 6 were waited for; matrix products, arithmetic and copies ran while one was open for 0% of the time, Pallas kernels for 9%

profile of v5, /device:TPU:0, one launch (start us, length us, event | category | flops | bytes accessed | tf_op | source)
XLA Modules:
  0.0 72.4 jit_solution(18001846383746753113)
XLA Ops:
  0.6 1.3 %copy-done = bf16[128,5248]{1,0:T(8,128)(2,1)S(1)} copy-done((bf16[128,5248]{1,0:T(8,128)(2,1)S(1)}, bf16[128,5248]{1,0:T(8,128)(2,1)}, u32[]{:S(2)}) %copy-start) | copy-done | bytes 1343512
  2.0 0.7 copy-done.5
  2.7 0.5 shard_map.104
  3.2 4.0 %collective-permute-start.5 = (bf16[720,128]{1,0:T(8,128)(2,1)S(1)}, bf16[720,128]{1,0:T(8,128)(2,1)S(1)}, u32[]{:S(2)}, u32[]{:S(2)}) collective-permute-start(bf16[720,128]{1,0:T(8,128)(2,1)S(1)} %get-tuple-element.21), channel_id=1, source_target_pairs={{0,6},{1,7},{2,4},{3,5},{4,2},{5,3},{6,0},{7,1},{8,14},{9,15},{10,... | collective-permute-start | bytes 552968 | tf_op jit(solution)/shard_map/ppermute | solution.py:160
  7.1 0.5 collective-permute-start.2
  7.7 1.5 %collective-permute-start.1 = (bf16[1376,128]{1,0:T(8,128)(2,1)S(1)}, bf16[1376,128]{1,0:T(8,128)(2,1)S(1)}, u32[]{:S(2)}, u32[]{:S(2)}) collective-permute-start(bf16[1376,128]{1,0:T(8,128)(2,1)S(1)} %get-tuple-element.18), channel_id=1, source_target_pairs={{0,2},{1,3},{2,0},{3,1},{4,6},{5,7},{6,4},{7,5},{8,10},{9,11},{10,... | collective-permute-start | bytes 1056776 | tf_op jit(solution)/shard_map/ppermute | solution.py:160
  9.2 0.5 collective-permute-start.4
  9.7 2.9 %collective-permute-done.5.refs_3_ = bf16[720,128]{1,0:T(8,128)(2,1)S(1)} collective-permute-done((bf16[720,128]{1,0:T(8,128)(2,1)S(1)}, bf16[720,128]{1,0:T(8,128)(2,1)S(1)}, u32[]{:S(2)}, u32[]{:S(2)}) %collective-permute-start.5) | collective-permute-done | bytes 184352 | tf_op jit(solution)/shard_map/ppermute | solution.py:160
  12.6 2.0 %collective-permute-start.3 = (bf16[128,1024]{1,0:T(8,128)(2,1)S(1)}, bf16[128,1024]{1,0:T(8,128)(2,1)S(1)}, u32[]{:S(2)}, u32[]{:S(2)}) collective-permute-start(bf16[128,1024]{1,0:T(8,128)(2,1)S(1)} %copy-done.1), channel_id=1, source_target_pairs={{0,4},{1,5},{2,6},{3,7},{4,0},{5,1},{6,2},{7,3},{8,12},{9,13},{10,... | collective-permute-start | bytes 786440 | tf_op jit(solution)/shard_map/ppermute | solution.py:160
  14.6 4.2 %collective-permute-done.2.refs_0_ = bf16[128,1024]{1,0:T(8,128)(2,1)S(1)} collective-permute-done((bf16[128,1024]{1,0:T(8,128)(2,1)S(1)}, bf16[128,1024]{1,0:T(8,128)(2,1)S(1)}, u32[]{:S(2)}, u32[]{:S(2)}) %collective-permute-start.2) | collective-permute-done | bytes 262176 | tf_op jit(solution)/shard_map/ppermute | solution.py:160
  18.8 6.1 %collective-permute-done.3.refs_0_ = bf16[128,1024]{1,0:T(8,128)(2,1)S(1)} collective-permute-done((bf16[128,1024]{1,0:T(8,128)(2,1)S(1)}, bf16[128,1024]{1,0:T(8,128)(2,1)S(1)}, u32[]{:S(2)}, u32[]{:S(2)}) %collective-permute-start.3) | collective-permute-done | bytes 262176 | tf_op jit(solution)/shard_map/ppermute | solution.py:160
  24.9 1.8 %collective-permute-start.6 = (bf16[720,128]{1,0:T(8,128)(2,1)S(1)}, bf16[720,128]{1,0:T(8,128)(2,1)S(1)}, u32[]{:S(2)}, u32[]{:S(2)}) collective-permute-start(bf16[720,128]{1,0:T(8,128)(2,1)S(1)} %collective-permute-done.5.refs_3_), channel_id=1, source_target_pairs={{0,8},{8,0},{16,24},{24,16},{1,9},{9,1},{17,25},{25,17},{2,10},{10... | collective-permute-start | bytes 552968 | tf_op jit(solution)/shard_map/ppermute | solution.py:160
  26.7 0.5 collective-permute-start.9
  27.3 3.3 %collective-permute-done.6.refs_4_ = bf16[720,128]{1,0:T(8,128)(2,1)S(1)} collective-permute-done((bf16[720,128]{1,0:T(8,128)(2,1)S(1)}, bf16[720,128]{1,0:T(8,128)(2,1)S(1)}, u32[]{:S(2)}, u32[]{:S(2)}) %collective-permute-start.6) | collective-permute-done | bytes 184352 | tf_op jit(solution)/shard_map/ppermute | solution.py:160
  30.7 2.2 %collective-permute-start.13 = (bf16[64,1024]{1,0:T(8,128)(2,1)S(1)}, bf16[64,1024]{1,0:T(8,128)(2,1)S(1)}, u32[]{:S(2)}, u32[]{:S(2)}) collective-permute-start(bf16[64,1024]{1,0:T(8,128)(2,1)S(1)} %slice.6), channel_id=1, source_target_pairs={{0,2},{1,3},{2,0},{3,1},{4,6},{5,7},{6,4},{7,5},{8,10},{9,11},{10,... | collective-permute-start | bytes 393224 | tf_op jit(solution)/shard_map/ppermute | solution.py:160
  32.9 0.9 %shard_map.105 = (bf16[656,1024]{1,0:T(8,128)(2,1)S(1)}, bf16[656,1024]{1,0:T(8,128)(2,1)S(1)}, bf16[656,1024]{1,0:T(8,128)(2,1)S(1)}, bf16[512,128]{1,0:T(8,128)(2,1)S(1)}) custom-call(bf16[328,1024]{1,0:T(8,128)(2,1)S(1)} %copy-done.2, bf16[328,1024]{1,0:T(8,128)(2,1)S(1)} %collective-permute-done.wo_other, ...), custom_call_target="tpu_custom_call" | custom-call | tf_op jit(solution)/shard_map/pallas_call | solution.py:185
  33.8 1.4 %shard_map.106 = bf16[128,1024]{1,0:T(8,128)(2,1)S(1)} custom-call(f32[1,1024]{1,0:T(1,128)S(1)} %bitcast.5, bf16[656,1024]{1,0:T(8,128)(2,1)S(1)} %get-tuple-element.22.gelu_w, bf16[656,1024]{1,0:T(8,128)(2,1)S(1)} %get-tuple-element.23.gate_w, bf16[656,1024]{1,0:T(8,128)(2,1)S(1)} %get-tuple-element.24.wo_part, ...), custom_call_target="tpu_custom_call" | custom-call | tf_op jit(solution)/shard_map/pallas_call | solution.py:213
  35.2 1.4 %collective-permute-start.12 = (bf16[128,1024]{1,0:T(8,128)(2,1)S(1)}, bf16[128,1024]{1,0:T(8,128)(2,1)S(1)}, u32[]{:S(2)}, u32[]{:S(2)}) collective-permute-start(bf16[128,1024]{1,0:T(8,128)(2,1)S(1)} %shard_map.106), channel_id=1, source_target_pairs={{0,2},{1,3},{2,0},{3,1},{4,6},{5,7},{6,4},{7,5},{8,10},{9,11},{10,... | collective-permute-start | bytes 786440 | tf_op jit(solution)/shard_map/ppermute | solution.py:160
  36.5 2.0 %collective-permute-start.14 = (bf16[64,1024]{1,0:T(8,128)(2,1)S(1)}, bf16[64,1024]{1,0:T(8,128)(2,1)S(1)}, u32[]{:S(2)}, u32[]{:S(2)}) collective-permute-start(bf16[64,1024]{1,0:T(8,128)(2,1)S(1)} %slice.7), channel_id=1, source_target_pairs={{0,4},{1,5},{2,6},{3,7},{4,0},{5,1},{6,2},{7,3},{8,12},{9,13},{10,... | collective-permute-start | bytes 393224 | tf_op jit(solution)/shard_map/ppermute | solution.py:160
  38.5 1.4 %shard_map.109 = bf16[128,1024]{1,0:T(8,128)(2,1)S(1)} custom-call(f32[1,1024]{1,0:T(1,128)S(1)} %bitcast.6, bf16[656,1024]{1,0:T(8,128)(2,1)S(1)} %get-tuple-element.22.gelu_w, bf16[656,1024]{1,0:T(8,128)(2,1)S(1)} %get-tuple-element.23.gate_w, bf16[656,1024]{1,0:T(8,128)(2,1)S(1)} %get-tuple-element.24.wo_part, ...), custom_call_target="tpu_custom_call" | custom-call | tf_op jit(solution)/shard_map/pallas_call | solution.py:213
  39.9 0.1 collective-permute-start.16
  40.0 2.4 %collective-permute-done.14.refs_1_ = bf16[64,1024]{1,0:T(8,128)(2,1)S(1)} collective-permute-done((bf16[64,1024]{1,0:T(8,128)(2,1)S(1)}, bf16[64,1024]{1,0:T(8,128)(2,1)S(1)}, u32[]{:S(2)}, u32[]{:S(2)}) %collective-permute-start.14) | collective-permute-done | bytes 131104 | tf_op jit(solution)/shard_map/ppermute | solution.py:160
  42.4 1.4 %shard_map.108 = bf16[128,1024]{1,0:T(8,128)(2,1)S(1)} custom-call(f32[1,1024]{1,0:T(1,128)S(1)} %bitcast.7, bf16[656,1024]{1,0:T(8,128)(2,1)S(1)} %get-tuple-element.22.gelu_w, bf16[656,1024]{1,0:T(8,128)(2,1)S(1)} %get-tuple-element.23.gate_w, bf16[656,1024]{1,0:T(8,128)(2,1)S(1)} %get-tuple-element.24.wo_part, ...), custom_call_target="tpu_custom_call" | custom-call | tf_op jit(solution)/shard_map/pallas_call | solution.py:213
  43.8 2.7 %collective-permute-start.15 = (bf16[128,1024]{1,0:T(8,128)(2,1)S(1)}, bf16[128,1024]{1,0:T(8,128)(2,1)S(1)}, u32[]{:S(2)}, u32[]{:S(2)}) collective-permute-start(bf16[128,1024]{1,0:T(8,128)(2,1)S(1)} %shard_map.108), channel_id=1, source_target_pairs={{0,6},{1,7},{2,4},{3,5},{4,2},{5,3},{6,0},{7,1},{8,14},{9,15},{10,... | collective-permute-start | bytes 786440 | tf_op jit(solution)/shard_map/ppermute | solution.py:160
  46.5 1.6 %collective-permute-start.17 = (bf16[512,128]{1,0:T(8,128)(2,1)S(1)}, bf16[512,128]{1,0:T(8,128)(2,1)S(1)}, u32[]{:S(2)}, u32[]{:S(2)}) collective-permute-start(bf16[512,128]{1,0:T(8,128)(2,1)S(1)} %get-tuple-element.29.refs_3_), channel_id=1, source_target_pairs={{0,8},{8,0},{16,24},{24,16},{1,9},{9,1},{17,25},{25,17},{2,10},{10... | collective-permute-start | bytes 393224 | tf_op jit(solution)/shard_map/ppermute | solution.py:160
  48.1 2.6 %collective-permute-start.18 = (bf16[512,128]{1,0:T(8,128)(2,1)S(1)}, bf16[512,128]{1,0:T(8,128)(2,1)S(1)}, u32[]{:S(2)}, u32[]{:S(2)}) collective-permute-start(bf16[512,128]{1,0:T(8,128)(2,1)S(1)} %get-tuple-element.29.refs_3_), channel_id=1, source_target_pairs={{0,16},{8,24},{16,0},{24,8},{1,17},{9,25},{17,1},{25,9},{2,18},{10... | collective-permute-start | bytes 393224 | tf_op jit(solution)/shard_map/ppermute | solution.py:160
  50.6 0.2 collective-permute-start.19
  50.9 1.4 %shard_map.107.own_ref = f32[128,1024]{1,0:T(8,128)S(1)} custom-call(f32[1,1024]{1,0:T(1,128)S(1)} %bitcast.8, bf16[656,1024]{1,0:T(8,128)(2,1)S(1)} %get-tuple-element.22.gelu_w, bf16[656,1024]{1,0:T(8,128)(2,1)S(1)} %get-tuple-element.23.gate_w, bf16[656,1024]{1,0:T(8,128)(2,1)S(1)} %get-tuple-element.24.wo_part, bf16[128,1024]{1,0:T(8,128)(2,1)S(1)} %copy-done.1), custom_call_target="tpu_custom_call" | custom-call | tf_op jit(solution)/shard_map/pallas_call | solution.py:213
  52.3 6.6 %collective-permute-done.18.refs_5_ = bf16[512,128]{1,0:T(8,128)(2,1)S(1)} collective-permute-done((bf16[512,128]{1,0:T(8,128)(2,1)S(1)}, bf16[512,128]{1,0:T(8,128)(2,1)S(1)}, u32[]{:S(2)}, u32[]{:S(2)}) %collective-permute-start.18) | collective-permute-done | bytes 131104 | tf_op jit(solution)/shard_map/ppermute | solution.py:160
  58.9 1.9 %shard_map.110 = (bf16[128,128]{1,0:T(8,128)(2,1)}, bf16[32,4,128]{2,1,0:T(4,128)(2,1)S(1)}) custom-call(s32[1,4]{1,0:T(1,128)S(1)} %copy-done.8, bf16[128,1024]{1,0:T(8,128)(2,1)S(1)} %copy-done.1, f32[1,1024]{1,0:T(1,128)S(1)} %bitcast.10, bf16[1024,128]{1,0:T(8,128)(2,1)S(1)} %copy-done.3, f32[128,1024]{1,0:T(8,128)S(1)} %shard_map.107.own_ref, ...), custom_call_target="tpu_custom_call" | custom-call | tf_op jit(solution)/shard_map/pallas_call | solution.py:225
  60.8 11.0 %all_to_all.5 = bf16[32,4,128]{2,1,0:T(4,128)(2,1)S(1)} all-to-all(bf16[32,4,128]{2,1,0:T(4,128)(2,1)S(1)} %get-tuple-element.31), channel_id=1, replica_groups=mesh['group'=4,'dev'=8] {'group','dev'}, dimensions={0} | all-to-all | bytes 65536 | tf_op jit(solution)/shard_map/all_to_all | solution.py:243
  71.8 0.7 shard_map.111
  (37 shorter events, 0.2 us)
Async XLA Ops:
  0.6 1.3 %copy-start = (bf16[128,5248]{1,0:T(8,128)(2,1)S(1)}, bf16[128,5248]{1,0:T(8,128)(2,1)}, u32[]{:S(2)}) copy-start(bf16[128,5248]{1,0:T(8,128)(2,1)} %wi_ref.1) | copy-start | bytes 4030468
  2.0 0.7 copy-start.5
  2.7 4.5 %copy-start.1 = (bf16[128,1024]{1,0:T(8,128)(2,1)S(1)}, bf16[128,1024]{1,0:T(8,128)(2,1)}, u32[]{:S(2)}) copy-start(bf16[128,1024]{1,0:T(8,128)(2,1)} %tokens_ref.1) | copy-start | bytes 786436
  2.7 7.0 %copy-start.2 = (bf16[328,1024]{1,0:T(8,128)(2,1)S(1)}, bf16[328,1024]{1,0:T(8,128)(2,1)}, u32[]{:S(2)}) copy-start(bf16[328,1024]{1,0:T(8,128)(2,1)} %wo_mine.1) | copy-start | bytes 2015236
  3.2 9.4 %collective-permute-start.5 = (bf16[720,128]{1,0:T(8,128)(2,1)S(1)}, bf16[720,128]{1,0:T(8,128)(2,1)S(1)}, u32[]{:S(2)}, u32[]{:S(2)}) collective-permute-start(bf16[720,128]{1,0:T(8,128)(2,1)S(1)} %get-tuple-element.21), channel_id=1, source_target_pairs={{0,6},{1,7},{2,4},{3,5},{4,2},{5,3},{6,0},{7,1},{8,14},{9,15},{10,... | collective-permute-start | bytes 552968 | tf_op jit(solution)/shard_map/ppermute | solution.py:160
  7.1 11.6 %collective-permute-start.2 = (bf16[128,1024]{1,0:T(8,128)(2,1)S(1)}, bf16[128,1024]{1,0:T(8,128)(2,1)S(1)}, u32[]{:S(2)}, u32[]{:S(2)}) collective-permute-start(bf16[128,1024]{1,0:T(8,128)(2,1)S(1)} %copy-done.1), channel_id=1, source_target_pairs={{0,2},{1,3},{2,0},{3,1},{4,6},{5,7},{6,4},{7,5},{8,10},{9,11},{10,... | collective-permute-start | bytes 786440 | tf_op jit(solution)/shard_map/ppermute | solution.py:160
  7.7 19.0 %collective-permute-start.1 = (bf16[1376,128]{1,0:T(8,128)(2,1)S(1)}, bf16[1376,128]{1,0:T(8,128)(2,1)S(1)}, u32[]{:S(2)}, u32[]{:S(2)}) collective-permute-start(bf16[1376,128]{1,0:T(8,128)(2,1)S(1)} %get-tuple-element.18), channel_id=1, source_target_pairs={{0,2},{1,3},{2,0},{3,1},{4,6},{5,7},{6,4},{7,5},{8,10},{9,11},{10,... | collective-permute-start | bytes 1056776 | tf_op jit(solution)/shard_map/ppermute | solution.py:160
  9.2 17.6 %collective-permute-start.4 = (bf16[1376,128]{1,0:T(8,128)(2,1)S(1)}, bf16[1376,128]{1,0:T(8,128)(2,1)S(1)}, u32[]{:S(2)}, u32[]{:S(2)}) collective-permute-start(bf16[1376,128]{1,0:T(8,128)(2,1)S(1)} %get-tuple-element.20), channel_id=1, source_target_pairs={{0,4},{1,5},{2,6},{3,7},{4,0},{5,1},{6,2},{7,3},{8,12},{9,13},{10,... | collective-permute-start | bytes 1056776 | tf_op jit(solution)/shard_map/ppermute | solution.py:160
  9.7 23.2 %collective-permute-start = (bf16[328,1024]{1,0:T(8,128)(2,1)S(1)}, bf16[328,1024]{1,0:T(8,128)(2,1)S(1)}, u32[]{:S(2)}, u32[]{:S(2)}) collective-permute-start(bf16[328,1024]{1,0:T(8,128)(2,1)S(1)} %copy-done.2), channel_id=1, source_target_pairs={{0,1},{1,0},{2,3},{3,2},{4,5},{5,4},{6,7},{7,6},{8,9},{9,8},{10,11... | collective-permute-start | bytes 2015240 | tf_op jit(solution)/shard_map/ppermute | solution.py:160
  12.6 12.3 %collective-permute-start.3 = (bf16[128,1024]{1,0:T(8,128)(2,1)S(1)}, bf16[128,1024]{1,0:T(8,128)(2,1)S(1)}, u32[]{:S(2)}, u32[]{:S(2)}) collective-permute-start(bf16[128,1024]{1,0:T(8,128)(2,1)S(1)} %copy-done.1), channel_id=1, source_target_pairs={{0,4},{1,5},{2,6},{3,7},{4,0},{5,1},{6,2},{7,3},{8,12},{9,13},{10,... | collective-permute-start | bytes 786440 | tf_op jit(solution)/shard_map/ppermute | solution.py:160
  18.8 8.4 %collective-permute-start.7 = (bf16[1376,128]{1,0:T(8,128)(2,1)S(1)}, bf16[1376,128]{1,0:T(8,128)(2,1)S(1)}, u32[]{:S(2)}, u32[]{:S(2)}) collective-permute-start(bf16[1376,128]{1,0:T(8,128)(2,1)S(1)} %get-tuple-element.17.refs_0_), channel_id=1, source_target_pairs={{0,1},{1,0},{2,3},{3,2},{4,5},{5,4},{6,7},{7,6},{8,9},{9,8},{10,11... | collective-permute-start | bytes 1056776 | tf_op jit(solution)/shard_map/ppermute | solution.py:160
  24.9 5.7 %collective-permute-start.6 = (bf16[720,128]{1,0:T(8,128)(2,1)S(1)}, bf16[720,128]{1,0:T(8,128)(2,1)S(1)}, u32[]{:S(2)}, u32[]{:S(2)}) collective-permute-start(bf16[720,128]{1,0:T(8,128)(2,1)S(1)} %collective-permute-done.5.refs_3_), channel_id=1, source_target_pairs={{0,8},{8,0},{16,24},{24,16},{1,9},{9,1},{17,25},{25,17},{2,10},{10... | collective-permute-start | bytes 552968 | tf_op jit(solution)/shard_map/ppermute | solution.py:160
  26.7 6.2 %collective-permute-start.8 = (bf16[1376,128]{1,0:T(8,128)(2,1)S(1)}, bf16[1376,128]{1,0:T(8,128)(2,1)S(1)}, u32[]{:S(2)}, u32[]{:S(2)}) collective-permute-start(bf16[1376,128]{1,0:T(8,128)(2,1)S(1)} %collective-permute-done.1.refs_1_), channel_id=1, source_target_pairs={{0,1},{1,0},{2,3},{3,2},{4,5},{5,4},{6,7},{7,6},{8,9},{9,8},{10,11... | collective-permute-start | bytes 1056776 | tf_op jit(solution)/shard_map/ppermute | solution.py:160
  26.7 6.2 %collective-permute-start.9 = (bf16[1376,128]{1,0:T(8,128)(2,1)S(1)}, bf16[1376,128]{1,0:T(8,128)(2,1)S(1)}, u32[]{:S(2)}, u32[]{:S(2)}) collective-permute-start(bf16[1376,128]{1,0:T(8,128)(2,1)S(1)} %collective-permute-done.4.refs_2_), channel_id=1, source_target_pairs={{0,1},{1,0},{2,3},{3,2},{4,5},{5,4},{6,7},{7,6},{8,9},{9,8},{10,11... | collective-permute-start | bytes 1056776 | tf_op jit(solution)/shard_map/ppermute | solution.py:160
  27.2 3.4 %collective-permute-start.10 = (bf16[720,128]{1,0:T(8,128)(2,1)S(1)}, bf16[720,128]{1,0:T(8,128)(2,1)S(1)}, u32[]{:S(2)}, u32[]{:S(2)}) collective-permute-start(bf16[720,128]{1,0:T(8,128)(2,1)S(1)} %collective-permute-done.5.refs_3_), channel_id=1, source_target_pairs={{0,1},{1,0},{2,3},{3,2},{4,5},{5,4},{6,7},{7,6},{8,9},{9,8},{10,11... | collective-permute-start | bytes 552968 | tf_op jit(solution)/shard_map/ppermute | solution.py:160
  30.6 2.3 %collective-permute-start.11 = (bf16[720,128]{1,0:T(8,128)(2,1)S(1)}, bf16[720,128]{1,0:T(8,128)(2,1)S(1)}, u32[]{:S(2)}, u32[]{:S(2)}) collective-permute-start(bf16[720,128]{1,0:T(8,128)(2,1)S(1)} %collective-permute-done.6.refs_4_), channel_id=1, source_target_pairs={{0,1},{1,0},{2,3},{3,2},{4,5},{5,4},{6,7},{7,6},{8,9},{9,8},{10,11... | collective-permute-start | bytes 552968 | tf_op jit(solution)/shard_map/ppermute | solution.py:160
  30.6 3.1 %copy-start.4 = (f32[1024]{0:T(1024)S(1)}, f32[1024]{0:T(1024)}, u32[]{:S(2)}) copy-start(f32[1024]{0:T(1024)} %param.10) | copy-start | bytes 12292
  30.7 9.4 %collective-permute-start.13 = (bf16[64,1024]{1,0:T(8,128)(2,1)S(1)}, bf16[64,1024]{1,0:T(8,128)(2,1)S(1)}, u32[]{:S(2)}, u32[]{:S(2)}) collective-permute-start(bf16[64,1024]{1,0:T(8,128)(2,1)S(1)} %slice.6), channel_id=1, source_target_pairs={{0,2},{1,3},{2,0},{3,1},{4,6},{5,7},{6,4},{7,5},{8,10},{9,11},{10,... | collective-permute-start | bytes 393224 | tf_op jit(solution)/shard_map/ppermute | solution.py:160
  35.2 15.5 %collective-permute-start.12 = (bf16[128,1024]{1,0:T(8,128)(2,1)S(1)}, bf16[128,1024]{1,0:T(8,128)(2,1)S(1)}, u32[]{:S(2)}, u32[]{:S(2)}) collective-permute-start(bf16[128,1024]{1,0:T(8,128)(2,1)S(1)} %shard_map.106), channel_id=1, source_target_pairs={{0,2},{1,3},{2,0},{3,1},{4,6},{5,7},{6,4},{7,5},{8,10},{9,11},{10,... | collective-permute-start | bytes 786440 | tf_op jit(solution)/shard_map/ppermute | solution.py:160
  36.5 5.9 %collective-permute-start.14 = (bf16[64,1024]{1,0:T(8,128)(2,1)S(1)}, bf16[64,1024]{1,0:T(8,128)(2,1)S(1)}, u32[]{:S(2)}, u32[]{:S(2)}) collective-permute-start(bf16[64,1024]{1,0:T(8,128)(2,1)S(1)} %slice.7), channel_id=1, source_target_pairs={{0,4},{1,5},{2,6},{3,7},{4,0},{5,1},{6,2},{7,3},{8,12},{9,13},{10,... | collective-permute-start | bytes 393224 | tf_op jit(solution)/shard_map/ppermute | solution.py:160
  39.9 19.0 %collective-permute-start.16 = (bf16[128,1024]{1,0:T(8,128)(2,1)S(1)}, bf16[128,1024]{1,0:T(8,128)(2,1)S(1)}, u32[]{:S(2)}, u32[]{:S(2)}) collective-permute-start(bf16[128,1024]{1,0:T(8,128)(2,1)S(1)} %shard_map.109), channel_id=1, source_target_pairs={{0,4},{1,5},{2,6},{3,7},{4,0},{5,1},{6,2},{7,3},{8,12},{9,13},{10,... | collective-permute-start | bytes 786440 | tf_op jit(solution)/shard_map/ppermute | solution.py:160
  43.8 15.1 %collective-permute-start.15 = (bf16[128,1024]{1,0:T(8,128)(2,1)S(1)}, bf16[128,1024]{1,0:T(8,128)(2,1)S(1)}, u32[]{:S(2)}, u32[]{:S(2)}) collective-permute-start(bf16[128,1024]{1,0:T(8,128)(2,1)S(1)} %shard_map.108), channel_id=1, source_target_pairs={{0,6},{1,7},{2,4},{3,5},{4,2},{5,3},{6,0},{7,1},{8,14},{9,15},{10,... | collective-permute-start | bytes 786440 | tf_op jit(solution)/shard_map/ppermute | solution.py:160
  46.5 12.4 %copy-start.3 = (bf16[1024,128]{1,0:T(8,128)(2,1)S(1)}, bf16[1024,128]{1,0:T(8,128)(2,1)}, u32[]{:S(2)}) copy-start(bf16[1024,128]{1,0:T(8,128)(2,1)} %proj_ref.1) | copy-start | bytes 786436
  46.5 12.4 %copy-start.6 = (f32[1024]{0:T(1024)S(1)}, f32[1024]{0:T(1024)}, u32[]{:S(2)}) copy-start(f32[1024]{0:T(1024)} %param.13) | copy-start | bytes 12292
  46.5 12.4 %copy-start.8 = (s32[1,4]{1,0:T(1,128)S(1)}, s32[1,4]{1,0:T(1,128)}, u32[]{:S(2)}) copy-start(s32[1,4]{1,0:T(1,128)} %lengths_ref.1) | copy-start | bytes 52
  46.5 5.8 %collective-permute-start.17 = (bf16[512,128]{1,0:T(8,128)(2,1)S(1)}, bf16[512,128]{1,0:T(8,128)(2,1)S(1)}, u32[]{:S(2)}, u32[]{:S(2)}) collective-permute-start(bf16[512,128]{1,0:T(8,128)(2,1)S(1)} %get-tuple-element.29.refs_3_), channel_id=1, source_target_pairs={{0,8},{8,0},{16,24},{24,16},{1,9},{9,1},{17,25},{25,17},{2,10},{10... | collective-permute-start | bytes 393224 | tf_op jit(solution)/shard_map/ppermute | solution.py:160
  48.1 10.8 %collective-permute-start.18 = (bf16[512,128]{1,0:T(8,128)(2,1)S(1)}, bf16[512,128]{1,0:T(8,128)(2,1)S(1)}, u32[]{:S(2)}, u32[]{:S(2)}) collective-permute-start(bf16[512,128]{1,0:T(8,128)(2,1)S(1)} %get-tuple-element.29.refs_3_), channel_id=1, source_target_pairs={{0,16},{8,24},{16,0},{24,8},{1,17},{9,25},{17,1},{25,9},{2,18},{10... | collective-permute-start | bytes 393224 | tf_op jit(solution)/shard_map/ppermute | solution.py:160
  50.6 8.2 %collective-permute-start.19 = (bf16[512,128]{1,0:T(8,128)(2,1)S(1)}, bf16[512,128]{1,0:T(8,128)(2,1)S(1)}, u32[]{:S(2)}, u32[]{:S(2)}) collective-permute-start(bf16[512,128]{1,0:T(8,128)(2,1)S(1)} %get-tuple-element.29.refs_3_), channel_id=1, source_target_pairs={{0,24},{8,16},{16,8},{24,0},{1,25},{9,17},{17,9},{25,1},{2,26},{10... | collective-permute-start | bytes 393224 | tf_op jit(solution)/shard_map/ppermute | solution.py:160
  52.2 19.5 %copy-start.7 = (s32[2,100]{1,0:T(2,128)S(1)}, s32[2,100]{1,0:T(2,128)}, u32[]{:S(2)}) copy-start(s32[2,100]{1,0:T(2,128)} %cand_ref.1) | copy-start | bytes 2404

commit v6 on v5

--- a/solution.py
+++ b/solution.py
@@ -36,12 +36,19 @@
         for at, half in enumerate(halves):
             first = pl.multiple_of(half * width + (chip ^ step) * part, 16)
             pieces[step][at * part : (at + 1) * part] = turned[pl.ds(first, part), :]
-        pieces[step][len(halves) * part :] = query_ref[...]
+        if step == 3:
+            pieces[step][part:] = query_ref[...]
+
+
+def stack_kernel(count, *refs):
+    rows = refs[0].shape[0]
+    for at in range(count):
+        refs[count][at * rows : (at + 1) * rows] = refs[at][...]
 
 
 def join_kernel(chips, wo_mine, wo_other, *refs):
     mine, other = refs[: chips + 1], refs[chips + 1 : 2 * chips + 2]
-    gelu_w, gate_w, wo_part, queries = refs[2 * chips + 2 :]
+    gelu_w, gate_w, wo_part = refs[2 * chips + 2 :]
     chip, core = lax.axis_index("dev") // 2, lax.axis_index("dev") % 2
     rows = wo_mine.shape[0]
     for first, upper, lower in ((0, wo_mine, wo_other), (1, wo_other, wo_mine)):
@@ -52,7 +59,6 @@
             wo_part[rows:] = lower[...]
 
     part = gelu_w.shape[0]
-    own = mine[0].shape[0] - 2 * part
     for step in range(chips):
         source = (chip ^ step) * 2
         for blocks, at in ((mine, source + core), (other, source + 1 - core)):
@@ -67,9 +73,6 @@
                     def _(parity=parity, blocks=blocks, columns=columns):
                         gelu_w[:, columns] = blocks[3 + parity][:part]
                         gate_w[:, columns] = blocks[4 - parity][:part]
-
-            last = 2 * part if step < 3 else part
-            queries[pl.ds(pl.multiple_of(at * own, own), own), :] = blocks[step][last : last + own]
 
 
 def ffn_kernel(gain_ref, gelu_w, gate_w, wo_part, *refs):
@@ -103,30 +106,40 @@
         high = low + lengths_ref[0, doc]
         inside.append((spot >= low) & (spot < high))
         low = high
-    for far, block in enumerate(queries):
-        for start in range(0, block.shape[0], 128):
-            similar = dot_nt(vectors, block[start : start + 128, :])
+    chip, core = me // 2, me % 2
+    for side, block in enumerate(queries):
+        for pair in range(block.shape[0] // 128):
+            similar = dot_nt(vectors, block[pair * 128 : (pair + 1) * 128, :])
             best = [
                 jnp.max(jnp.where(inside[doc], similar, -jnp.inf), axis=0, keepdims=True)
                 for doc in range(docs)
             ]
             best = jnp.concatenate(best, axis=0).astype(jnp.bfloat16)
-            target = (group ^ far) * (2 * chips) + start // 64
-            out_ref[target] = best
-            out_ref[target + 1] = best
+            for row in (2 * pair, 2 * pair + 1):
+                far, mask = row // chips, row % chips
+                out_ref[(group ^ far) * (2 * chips) + (chip ^ mask) * 2 + (core ^ side)] = best
 
 
 def pick_kernel(query_len, cand_ref, best_ref, out_ref):
-    groups, _, docs, lanes = best_ref.shape
+    groups, devices, docs, lanes = best_ref.shape
     own, listed = cand_ref.shape
-    offset = (lax.axis_index("dev") % 2) * own * query_len
     scores = [jnp.zeros((1, listed), jnp.float32) for _ in range(own)]
-    lane = lax.broadcasted_iota(jnp.int32, (docs, lanes), 1)
+    lane = lax.broadcasted_iota(jnp.int32, (docs, lanes // 2), 1)
     label = lax.broadcasted_iota(jnp.int32, (docs, listed), 0)
     for far in range(groups):
-        best = jnp.max(best_ref[far].astype(jnp.float32), axis=0)
+        low = best_ref[far, 0].astype(jnp.float32)
+        high = best_ref[far, 2].astype(jnp.float32)
+        for sender in range(1, devices):
+            if sender // 2 % 2:
+                high = jnp.maximum(high, best_ref[far, sender].astype(jnp.float32))
+            else:
+                low = jnp.maximum(low, best_ref[far, sender].astype(jnp.float32))
+        odd = lax.axis_index("dev") // 2 % 2
+        same = jnp.where(odd == 0, low, high)
+        cross = jnp.where(odd == 0, high, low)
+        best = jnp.maximum(same[:, : lanes // 2], cross[:, lanes // 2 :])
         for query in range(own):
-            start = offset + query * query_len
+            start = query * query_len
             taken = jnp.where((lane >= start) & (lane < start + query_len), best, 0.0)
             value = jnp.sum(taken, axis=1, keepdims=True) / query_len
             wanted = cand_ref[query : query + 1, :] - far * docs
@@ -161,14 +174,23 @@
 
     per_query, query_len, vector_dim = query_vectors.shape
     query_own = query_vectors.reshape(-1, vector_dim)
-    wo_other = swap(wo_weight, 1)
+    def stack(parts):
+        shape = (len(parts) * parts[0].shape[0], parts[0].shape[1])
+        return pl.pallas_call(
+            functools.partial(stack_kernel, len(parts)),
+            out_shape=jax.ShapeDtypeStruct(shape, parts[0].dtype),
+            in_specs=[vmem] * len(parts),
+            out_specs=vmem,
+            compiler_params=params,
+        )(*parts)
+
     near = [corpus_tokens] + [swap(corpus_tokens, 2 * step) for step in (1, 2)]
     if wi_weight.shape[0] == 128 and part % 16 == 0 and chips == 4 and groups % 2 == 0:
         own = query_own.shape[0]
         pieces = pl.pallas_call(
             functools.partial(split_kernel, chips),
             out_shape=[
-                jax.ShapeDtypeStruct(((2 if step < 3 else 1) * part + own, 128), jnp.bfloat16)
+                jax.ShapeDtypeStruct((2 * part if step < 3 else part + own, 128), jnp.bfloat16)
                 for step in range(chips)
             ],
             in_specs=[vmem] * 2,
@@ -178,20 +200,27 @@
         )(wi_weight, query_own)
         mine = [pieces[0]] + [swap(pieces[step], 2 * step) for step in range(1, chips)]
         mine.append(swap(mine[3], 1, "group"))
-        mine[1], near[1], near[2] = lax.optimization_barrier((mine[1], near[1], near[2]))
+        mine[3], query_next = lax.optimization_barrier((mine[3], query_own))
+        plane = stack([query_own, swap(query_next, 2), swap(query_next, 4), mine[3][part:]])
+        mine[1], mine[4], near[1], near[2], plane = lax.optimization_barrier(
+            (mine[1], mine[4], near[1], near[2], plane)
+        )
+        near[1], near[2], wo_next = lax.optimization_barrier((near[1], near[2], wo_weight))
+        wo_other = swap(wo_next, 1)
+        lines = [plane] + [swap(plane, mask, "group") for mask in range(1, groups)]
+        mine[2], *lines = lax.optimization_barrier((mine[2], *lines))
         far = [swap(near[2][: rows // 2], 2), swap(near[1][rows // 2 :], 4)]
         tokens = [[each] for each in near] + [far]
         other = [swap(piece, 1) for piece in mine]
-        *weights, plane = pl.pallas_call(
+        weights = pl.pallas_call(
             functools.partial(join_kernel, chips),
             out_shape=[
                 jax.ShapeDtypeStruct((part, width), jnp.bfloat16),
                 jax.ShapeDtypeStruct((part, width), jnp.bfloat16),
                 jax.ShapeDtypeStruct((part, wo_weight.shape[1]), jnp.bfloat16),
-                jax.ShapeDtypeStruct((devices * own, vector_dim), jnp.bfloat16),
             ],
             in_specs=[vmem] * (4 + 2 * chips),
-            out_specs=[vmem] * 4,
+            out_specs=[vmem] * 3,
             compiler_params=params,
         )(wo_weight, wo_other, *mine, *other)
     else:
@@ -199,17 +228,21 @@
         whole = lax.all_gather(wi_weight, "dev", axis=0, tiled=True).reshape(width, 2, chips, part)
         columns = lax.dynamic_index_in_dim(whole, me // 2, 2, keepdims=False)
         even = (me % 2) == 0
+        wo_other = swap(wo_weight, 1)
         wo_part = jnp.concatenate(
             [jnp.where(even, wo_weight, wo_other), jnp.where(even, wo_other, wo_weight)], axis=0
         )
         weights = [columns[:, 0].T, columns[:, 1].T, wo_part]
         tokens = [[each] for each in near]
         tokens += [[swap(corpus_tokens, 2 * step)] for step in range(3, chips)]
-        plane = lax.all_gather(query_own, "dev", axis=0, tiled=True)
+        plane = stack([query_own] + [swap(query_own, 2 * step) for step in range(1, chips)])
+        lines = [plane] + [swap(plane, mask, "group") for mask in range(1, groups)]
     partial, arrived = [None] * chips, [None] * chips
     for step in list(range(1, chips)) + [0]:
         if step == 0:
-            arrived[1], tokens[0][0] = lax.optimization_barrier((arrived[1], tokens[0][0]))
+            arrived[1], arrived[2], tokens[0][0] = lax.optimization_barrier(
+                (arrived[1], arrived[2], tokens[0][0])
+            )
         partial[step] = pl.pallas_call(
             ffn_kernel,
             out_shape=jax.ShapeDtypeStruct((rows, width), jnp.bfloat16 if step else jnp.float32),
@@ -219,7 +252,8 @@
         )(norm_gain.reshape(1, -1), *weights, *tokens[step])
         if step:
             arrived[step] = swap(partial[step], 2 * step)
-    queries = [plane] + [swap(plane, mask, "group") for mask in range(1, groups)]
+    line = stack(lines)
+    queries = [line, swap(line, 1)]
 
     docs = doc_lengths.shape[1]
     vectors, best = pl.pallas_call(
@@ -228,7 +262,7 @@
             jax.ShapeDtypeStruct((rows, proj_weight.shape[1]), jnp.bfloat16),
             jax.ShapeDtypeStruct((groups * devices, docs, 128), jnp.bfloat16),
         ],
-        in_specs=[smem] + [vmem] * (4 + chips - 1 + groups),
+        in_specs=[smem] + [vmem] * (4 + chips - 1 + 2),
         out_specs=[vmem, vmem],
         compiler_params=params,
     )(

time: 72.7 us -> 81.5 us (1.12)
  waiting for transfers between devices: 25.6 us -> 29.4 us
  blocking collectives: 11 us -> 13.6 us
  starting transfers between devices: 23.6 us -> 25.4 us
    ppermute x20 -> x23, waiting for transfers between devices: 25.6 us -> 29.4 us  [swap(): return lax.ppermute(values, axis, [(i, i ^ mask) for i in range(size)])]
    all_to_all x1, blocking collectives: 11 us -> 13.6 us  [body(): lax.all_to_all(best, ('group', 'dev'), split_axis=0, concat_axis=0, tiled...]
    ppermute x20 -> x23, starting transfers between devices: 23.6 us -> 25.4 us  [swap(): return lax.ppermute(values, axis, [(i, i ^ mask) for i in range(size)])]
  transfers between devices with their start and end apart: 20 -> 23, of which waited for: 6 -> 9; matrix products, arithmetic and copies ran while one was open for 0% -> 0% of each run, Pallas kernels for 9% -> 8%
where the time goes in v6:
time: 81.5 us; the launch traced here: 81.2 us
  waiting for transfers between devices  29.4 us (36%)
  starting transfers between devices  25.4 us (31%)
  blocking collectives  13.6 us (17%)
  Pallas kernels  9.8 us (12%)
  local copies, waits for them, and re-layouts  2.1 us (3%)
  between operations  0.86 us (1%)
    ppermute x23, waiting for transfers between devices, swap(): return lax.ppermute(values, axis, [(i, i ^ mask) for i in range(size)])  29.4 us
    ppermute x23, starting transfers between devices, swap(): return lax.ppermute(values, axis, [(i, i ^ mask) for i in range(size)])  25.4 us
    all_to_all x1, blocking collectives, body(): lax.all_to_all(best, ('group', 'dev'), split_axis=0, concat_axis=0, tiled...  13.6 us
    pallas_call x4, Pallas kernels, body(): pl.pallas_call(ffn_kernel, out_shape=jax.ShapeDtypeStruct((rows, width),...  5.51 us
    pallas_call x1, Pallas kernels, body(): pl.pallas_call(functools.partial(finish_kernel, chips), out_shape=[jax.Sh...  2.17 us
    unnamed x18, local copies, waits for them, and re-layouts  2.08 us
  transfers between devices with their start and end apart: 23, of which 9 were waited for; matrix products, arithmetic and copies ran while one was open for 0% of the time, Pallas kernels for 8%

profile of v6, /device:TPU:0, one launch (start us, length us, event | category | flops | bytes accessed | tf_op | source)
XLA Modules:
  0.0 81.2 jit_solution(14267146635349965335)
XLA Ops:
  0.6 1.3 %copy-done = bf16[128,5248]{1,0:T(8,128)(2,1)S(1)} copy-done((bf16[128,5248]{1,0:T(8,128)(2,1)S(1)}, bf16[128,5248]{1,0:T(8,128)(2,1)}, u32[]{:S(2)}) %copy-start) | copy-done | bytes 1343512
  2.0 0.7 copy-done.4
  3.2 4.0 %collective-permute-start.1 = (bf16[720,128]{1,0:T(8,128)(2,1)S(1)}, bf16[720,128]{1,0:T(8,128)(2,1)S(1)}, u32[]{:S(2)}, u32[]{:S(2)}) collective-permute-start(bf16[720,128]{1,0:T(8,128)(2,1)S(1)} %get-tuple-element.30), channel_id=1, source_target_pairs={{0,6},{1,7},{2,4},{3,5},{4,2},{5,3},{6,0},{7,1},{8,14},{9,15},{10,... | collective-permute-start | bytes 552968 | tf_op jit(solution)/shard_map/ppermute | solution.py:173
  7.1 0.5 collective-permute-start
  7.7 1.5 %collective-permute-start.3 = (bf16[128,1024]{1,0:T(8,128)(2,1)S(1)}, bf16[128,1024]{1,0:T(8,128)(2,1)S(1)}, u32[]{:S(2)}, u32[]{:S(2)}) collective-permute-start(bf16[128,1024]{1,0:T(8,128)(2,1)S(1)} %copy-done.1), channel_id=1, source_target_pairs={{0,2},{1,3},{2,0},{3,1},{4,6},{5,7},{6,4},{7,5},{8,10},{9,11},{10,... | collective-permute-start | bytes 786440 | tf_op jit(solution)/shard_map/ppermute | solution.py:173
  9.2 0.5 collective-permute-start.4
  9.7 2.9 %collective-permute-done.1.refs_3_ = bf16[720,128]{1,0:T(8,128)(2,1)S(1)} collective-permute-done((bf16[720,128]{1,0:T(8,128)(2,1)S(1)}, bf16[720,128]{1,0:T(8,128)(2,1)S(1)}, u32[]{:S(2)}, u32[]{:S(2)}) %collective-permute-start.1) | collective-permute-done | bytes 184352 | tf_op jit(solution)/shard_map/ppermute | solution.py:173
  12.6 2.1 %collective-permute-start.2 = (bf16[720,128]{1,0:T(8,128)(2,1)S(1)}, bf16[720,128]{1,0:T(8,128)(2,1)S(1)}, u32[]{:S(2)}, u32[]{:S(2)}) collective-permute-start(bf16[720,128]{1,0:T(8,128)(2,1)S(1)} %collective-permute-done.1.refs_3_), channel_id=1, source_target_pairs={{0,8},{8,0},{16,24},{24,16},{1,9},{9,1},{17,25},{25,17},{2,10},{10... | collective-permute-start | bytes 552968 | tf_op jit(solution)/shard_map/ppermute | solution.py:173
  14.7 1.5 %collective-permute-start.5 = (bf16[64,128]{1,0:T(8,128)(2,1)S(1)}, bf16[64,128]{1,0:T(8,128)(2,1)S(1)}, u32[]{:S(2)}, u32[]{:S(2)}) collective-permute-start(bf16[64,128]{1,0:T(8,128)(2,1)S(1)} %bitcast.6), channel_id=1, source_target_pairs={{0,2},{1,3},{2,0},{3,1},{4,6},{5,7},{6,4},{7,5},{8,10},{9,11},{10,... | collective-permute-start | bytes 49160 | tf_op jit(solution)/shard_map/ppermute | solution.py:173
  16.2 9.0 %collective-permute-done.5.refs_1_ = bf16[64,128]{1,0:T(8,128)(2,1)S(1)} collective-permute-done((bf16[64,128]{1,0:T(8,128)(2,1)S(1)}, bf16[64,128]{1,0:T(8,128)(2,1)S(1)}, u32[]{:S(2)}, u32[]{:S(2)}) %collective-permute-start.5) | collective-permute-done | bytes 16416 | tf_op jit(solution)/shard_map/ppermute | solution.py:173
  25.5 3.4 %collective-permute-done.6.refs_2_ = bf16[64,128]{1,0:T(8,128)(2,1)S(1)} collective-permute-done((bf16[64,128]{1,0:T(8,128)(2,1)S(1)}, bf16[64,128]{1,0:T(8,128)(2,1)S(1)}, u32[]{:S(2)}, u32[]{:S(2)}) %collective-permute-start.6) | collective-permute-done | bytes 16416 | tf_op jit(solution)/shard_map/ppermute | solution.py:173
  29.9 1.8 %collective-permute-start.9 = (bf16[256,128]{1,0:T(8,128)(2,1)S(1)}, bf16[256,128]{1,0:T(8,128)(2,1)S(1)}, u32[]{:S(2)}, u32[]{:S(2)}) collective-permute-start(bf16[256,128]{1,0:T(8,128)(2,1)S(1)} %shard_map.105.refs_0_), channel_id=1, source_target_pairs={{0,8},{8,0},{16,24},{24,16},{1,9},{9,1},{17,25},{25,17},{2,10},{10... | collective-permute-start | bytes 196616 | tf_op jit(solution)/shard_map/ppermute | solution.py:173
  31.6 2.6 %collective-permute-start.10 = (bf16[256,128]{1,0:T(8,128)(2,1)S(1)}, bf16[256,128]{1,0:T(8,128)(2,1)S(1)}, u32[]{:S(2)}, u32[]{:S(2)}) collective-permute-start(bf16[256,128]{1,0:T(8,128)(2,1)S(1)} %shard_map.105.refs_0_), channel_id=1, source_target_pairs={{0,16},{8,24},{16,0},{24,8},{1,17},{9,25},{17,1},{25,9},{2,18},{10... | collective-permute-start | bytes 196616 | tf_op jit(solution)/shard_map/ppermute | solution.py:173
  34.2 2.3 %collective-permute-done.8.refs_2_ = bf16[1312,128]{1,0:T(8,128)(2,1)S(1)} collective-permute-done((bf16[1312,128]{1,0:T(8,128)(2,1)S(1)}, bf16[1312,128]{1,0:T(8,128)(2,1)S(1)}, u32[]{:S(2)}, u32[]{:S(2)}) %collective-permute-start.8) | collective-permute-done | bytes 335904 | tf_op jit(solution)/shard_map/ppermute | solution.py:173
  36.5 3.6 %collective-permute-start.11 = (bf16[256,128]{1,0:T(8,128)(2,1)S(1)}, bf16[256,128]{1,0:T(8,128)(2,1)S(1)}, u32[]{:S(2)}, u32[]{:S(2)}) collective-permute-start(bf16[256,128]{1,0:T(8,128)(2,1)S(1)} %shard_map.105.refs_0_), channel_id=1, source_target_pairs={{0,24},{8,16},{16,8},{24,0},{1,25},{9,17},{17,9},{25,1},{2,26},{10... | collective-permute-start | bytes 196616 | tf_op jit(solution)/shard_map/ppermute | solution.py:173
  40.1 2.4 %collective-permute-done.11.refs_3_ = bf16[256,128]{1,0:T(8,128)(2,1)S(1)} collective-permute-done((bf16[256,128]{1,0:T(8,128)(2,1)S(1)}, bf16[256,128]{1,0:T(8,128)(2,1)S(1)}, u32[]{:S(2)}, u32[]{:S(2)}) %collective-permute-start.11) | collective-permute-done | bytes 65568 | tf_op jit(solution)/shard_map/ppermute | solution.py:173
  42.6 0.5 collective-permute-start.15
  43.2 1.3 %collective-permute-done.15.refs_8_ = bf16[720,128]{1,0:T(8,128)(2,1)S(1)} collective-permute-done((bf16[720,128]{1,0:T(8,128)(2,1)S(1)}, bf16[720,128]{1,0:T(8,128)(2,1)S(1)}, u32[]{:S(2)}, u32[]{:S(2)}) %collective-permute-start.15) | collective-permute-done | bytes 184352 | tf_op jit(solution)/shard_map/ppermute | solution.py:173
  44.5 1.5 %collective-permute-start.19 = (bf16[64,1024]{1,0:T(8,128)(2,1)S(1)}, bf16[64,1024]{1,0:T(8,128)(2,1)S(1)}, u32[]{:S(2)}, u32[]{:S(2)}) collective-permute-start(bf16[64,1024]{1,0:T(8,128)(2,1)S(1)} %slice.10), channel_id=1, source_target_pairs={{0,2},{1,3},{2,0},{3,1},{4,6},{5,7},{6,4},{7,5},{8,10},{9,11},{10,... | collective-permute-start | bytes 393224 | tf_op jit(solution)/shard_map/ppermute | solution.py:173
  46.5 0.9 %shard_map.106 = (bf16[656,1024]{1,0:T(8,128)(2,1)S(1)}, bf16[656,1024]{1,0:T(8,128)(2,1)S(1)}, bf16[656,1024]{1,0:T(8,128)(2,1)S(1)}) custom-call(bf16[328,1024]{1,0:T(8,128)(2,1)S(1)} %copy-done.2, bf16[328,1024]{1,0:T(8,128)(2,1)S(1)} %collective-permute-done.7.wo_other, bf16[1312,128]{1,0:T(8,128)(2,1)S(1)} %get-tuple-element.36.refs_0_, ...), custom_call_target="tpu_custom_call" | custom-call | tf_op jit(solution)/shard_map/pallas_call | solution.py:215
  47.4 1.4 %shard_map.107 = bf16[128,1024]{1,0:T(8,128)(2,1)S(1)} custom-call(f32[1,1024]{1,0:T(1,128)S(1)} %bitcast.9, bf16[656,1024]{1,0:T(8,128)(2,1)S(1)} %get-tuple-element.42.gelu_w, bf16[656,1024]{1,0:T(8,128)(2,1)S(1)} %get-tuple-element.43.gate_w, bf16[656,1024]{1,0:T(8,128)(2,1)S(1)} %get-tuple-element.44.wo_part, ...), custom_call_target="tpu_custom_call" | custom-call | tf_op jit(solution)/shard_map/pallas_call | solution.py:246
  48.8 1.4 %shard_map.108 = bf16[128,1024]{1,0:T(8,128)(2,1)S(1)} custom-call(f32[1,1024]{1,0:T(1,128)S(1)} %bitcast.10, bf16[656,1024]{1,0:T(8,128)(2,1)S(1)} %get-tuple-element.42.gelu_w, bf16[656,1024]{1,0:T(8,128)(2,1)S(1)} %get-tuple-element.43.gate_w, bf16[656,1024]{1,0:T(8,128)(2,1)S(1)} %get-tuple-element.44.wo_part, ...), custom_call_target="tpu_custom_call" | custom-call | tf_op jit(solution)/shard_map/pallas_call | solution.py:246
  50.2 0.7 collective-permute-start.17
  50.9 1.4 %collective-permute-start.18 = (bf16[128,1024]{1,0:T(8,128)(2,1)S(1)}, bf16[128,1024]{1,0:T(8,128)(2,1)S(1)}, u32[]{:S(2)}, u32[]{:S(2)}) collective-permute-start(bf16[128,1024]{1,0:T(8,128)(2,1)S(1)} %shard_map.108), channel_id=1, source_target_pairs={{0,4},{1,5},{2,6},{3,7},{4,0},{5,1},{6,2},{7,3},{8,12},{9,13},{10,... | collective-permute-start | bytes 786440 | tf_op jit(solution)/shard_map/ppermute | solution.py:173
  52.4 1.4 %shard_map.110 = bf16[128,1024]{1,0:T(8,128)(2,1)S(1)} custom-call(f32[1,1024]{1,0:T(1,128)S(1)} %bitcast.11, bf16[656,1024]{1,0:T(8,128)(2,1)S(1)} %get-tuple-element.42.gelu_w, bf16[656,1024]{1,0:T(8,128)(2,1)S(1)} %get-tuple-element.43.gate_w, bf16[656,1024]{1,0:T(8,128)(2,1)S(1)} %get-tuple-element.44.wo_part, ...), custom_call_target="tpu_custom_call" | custom-call | tf_op jit(solution)/shard_map/pallas_call | solution.py:246
  53.8 1.5 %collective-permute-start.21 = (bf16[128,1024]{1,0:T(8,128)(2,1)S(1)}, bf16[128,1024]{1,0:T(8,128)(2,1)S(1)}, u32[]{:S(2)}, u32[]{:S(2)}) collective-permute-start(bf16[128,1024]{1,0:T(8,128)(2,1)S(1)} %shard_map.110), channel_id=1, source_target_pairs={{0,6},{1,7},{2,4},{3,5},{4,2},{5,3},{6,0},{7,1},{8,14},{9,15},{10,... | collective-permute-start | bytes 786440 | tf_op jit(solution)/shard_map/ppermute | solution.py:173
  55.3 3.6 %collective-permute-done.17.refs_2_ = bf16[128,1024]{1,0:T(8,128)(2,1)S(1)} collective-permute-done((bf16[128,1024]{1,0:T(8,128)(2,1)S(1)}, bf16[128,1024]{1,0:T(8,128)(2,1)S(1)}, u32[]{:S(2)}, u32[]{:S(2)}) %collective-permute-start.17) | collective-permute-done | bytes 262176 | tf_op jit(solution)/shard_map/ppermute | solution.py:173
  58.9 4.1 %collective-permute-done.18.refs_1_ = bf16[128,1024]{1,0:T(8,128)(2,1)S(1)} collective-permute-done((bf16[128,1024]{1,0:T(8,128)(2,1)S(1)}, bf16[128,1024]{1,0:T(8,128)(2,1)S(1)}, u32[]{:S(2)}, u32[]{:S(2)}) %collective-permute-start.18) | collective-permute-done | bytes 262176 | tf_op jit(solution)/shard_map/ppermute | solution.py:173
  63.0 1.4 %shard_map.109.own_ref = f32[128,1024]{1,0:T(8,128)S(1)} custom-call(f32[1,1024]{1,0:T(1,128)S(1)} %bitcast.12, bf16[656,1024]{1,0:T(8,128)(2,1)S(1)} %get-tuple-element.42.gelu_w, bf16[656,1024]{1,0:T(8,128)(2,1)S(1)} %get-tuple-element.43.gate_w, bf16[656,1024]{1,0:T(8,128)(2,1)S(1)} %get-tuple-element.44.wo_part, bf16[128,1024]{1,0:T(8,128)(2,1)S(1)} %copy-done.1), custom_call_target="tpu_custom_call" | custom-call | tf_op jit(solution)/shard_map/pallas_call | solution.py:246
  64.7 2.2 %shard_map.112 = (bf16[128,128]{1,0:T(8,128)(2,1)}, bf16[32,4,128]{2,1,0:T(4,128)(2,1)S(1)}) custom-call(s32[1,4]{1,0:T(1,128)S(1)} %copy-done.8, bf16[128,1024]{1,0:T(8,128)(2,1)S(1)} %copy-done.1, f32[1,1024]{1,0:T(1,128)S(1)} %bitcast.13, bf16[1024,128]{1,0:T(8,128)(2,1)S(1)} %copy-done.3, f32[128,1024]{1,0:T(8,128)S(1)} %shard_map.109.own_ref, ...), custom_call_target="tpu_custom_call" | custom-call | tf_op jit(solution)/shard_map/pallas_call | solution.py:259
  66.8 13.6 %all_to_all.5 = bf16[32,4,128]{2,1,0:T(4,128)(2,1)S(1)} all-to-all(bf16[32,4,128]{2,1,0:T(4,128)(2,1)S(1)} %get-tuple-element.55), channel_id=1, replica_groups=mesh['group'=4,'dev'=8] {'group','dev'}, dimensions={0} | all-to-all | bytes 65536 | tf_op jit(solution)/shard_map/all_to_all | solution.py:277
  80.5 0.7 shard_map.113
  (46 shorter events, 2.6 us)
Async XLA Ops:
  0.6 1.3 %copy-start = (bf16[128,5248]{1,0:T(8,128)(2,1)S(1)}, bf16[128,5248]{1,0:T(8,128)(2,1)}, u32[]{:S(2)}) copy-start(bf16[128,5248]{1,0:T(8,128)(2,1)} %wi_ref.1) | copy-start | bytes 4030468
  2.0 0.7 copy-start.4
  2.7 5.0 %copy-start.1 = (bf16[128,1024]{1,0:T(8,128)(2,1)S(1)}, bf16[128,1024]{1,0:T(8,128)(2,1)}, u32[]{:S(2)}) copy-start(bf16[128,1024]{1,0:T(8,128)(2,1)} %tokens_ref.1) | copy-start | bytes 786436
  2.7 26.6 %copy-start.2 = (bf16[328,1024]{1,0:T(8,128)(2,1)S(1)}, bf16[328,1024]{1,0:T(8,128)(2,1)}, u32[]{:S(2)}) copy-start(bf16[328,1024]{1,0:T(8,128)(2,1)} %wo_mine.1) | copy-start | bytes 2015236
  3.2 9.4 %collective-permute-start.1 = (bf16[720,128]{1,0:T(8,128)(2,1)S(1)}, bf16[720,128]{1,0:T(8,128)(2,1)S(1)}, u32[]{:S(2)}, u32[]{:S(2)}) collective-permute-start(bf16[720,128]{1,0:T(8,128)(2,1)S(1)} %get-tuple-element.30), channel_id=1, source_target_pairs={{0,6},{1,7},{2,4},{3,5},{4,2},{5,3},{6,0},{7,1},{8,14},{9,15},{10,... | collective-permute-start | bytes 552968 | tf_op jit(solution)/shard_map/ppermute | solution.py:173
  7.1 22.1 %collective-permute-start = (bf16[1312,128]{1,0:T(8,128)(2,1)S(1)}, bf16[1312,128]{1,0:T(8,128)(2,1)S(1)}, u32[]{:S(2)}, u32[]{:S(2)}) collective-permute-start(bf16[1312,128]{1,0:T(8,128)(2,1)S(1)} %get-tuple-element.29), channel_id=1, source_target_pairs={{0,2},{1,3},{2,0},{3,1},{4,6},{5,7},{6,4},{7,5},{8,10},{9,11},{10,... | collective-permute-start | bytes 1007624 | tf_op jit(solution)/shard_map/ppermute | solution.py:173
  7.7 21.6 %collective-permute-start.3 = (bf16[128,1024]{1,0:T(8,128)(2,1)S(1)}, bf16[128,1024]{1,0:T(8,128)(2,1)S(1)}, u32[]{:S(2)}, u32[]{:S(2)}) collective-permute-start(bf16[128,1024]{1,0:T(8,128)(2,1)S(1)} %copy-done.1), channel_id=1, source_target_pairs={{0,2},{1,3},{2,0},{3,1},{4,6},{5,7},{6,4},{7,5},{8,10},{9,11},{10,... | collective-permute-start | bytes 786440 | tf_op jit(solution)/shard_map/ppermute | solution.py:173
  9.2 20.1 %collective-permute-start.4 = (bf16[128,1024]{1,0:T(8,128)(2,1)S(1)}, bf16[128,1024]{1,0:T(8,128)(2,1)S(1)}, u32[]{:S(2)}, u32[]{:S(2)}) collective-permute-start(bf16[128,1024]{1,0:T(8,128)(2,1)S(1)} %copy-done.1), channel_id=1, source_target_pairs={{0,4},{1,5},{2,6},{3,7},{4,0},{5,1},{6,2},{7,3},{8,12},{9,13},{10,... | collective-permute-start | bytes 786440 | tf_op jit(solution)/shard_map/ppermute | solution.py:173
  12.6 16.7 %collective-permute-start.2 = (bf16[720,128]{1,0:T(8,128)(2,1)S(1)}, bf16[720,128]{1,0:T(8,128)(2,1)S(1)}, u32[]{:S(2)}, u32[]{:S(2)}) collective-permute-start(bf16[720,128]{1,0:T(8,128)(2,1)S(1)} %collective-permute-done.1.refs_3_), channel_id=1, source_target_pairs={{0,8},{8,0},{16,24},{24,16},{1,9},{9,1},{17,25},{25,17},{2,10},{10... | collective-permute-start | bytes 552968 | tf_op jit(solution)/shard_map/ppermute | solution.py:173
  14.7 10.5 %collective-permute-start.5 = (bf16[64,128]{1,0:T(8,128)(2,1)S(1)}, bf16[64,128]{1,0:T(8,128)(2,1)S(1)}, u32[]{:S(2)}, u32[]{:S(2)}) collective-permute-start(bf16[64,128]{1,0:T(8,128)(2,1)S(1)} %bitcast.6), channel_id=1, source_target_pairs={{0,2},{1,3},{2,0},{3,1},{4,6},{5,7},{6,4},{7,5},{8,10},{9,11},{10,... | collective-permute-start | bytes 49160 | tf_op jit(solution)/shard_map/ppermute | solution.py:173
  25.2 3.7 %collective-permute-start.6 = (bf16[64,128]{1,0:T(8,128)(2,1)S(1)}, bf16[64,128]{1,0:T(8,128)(2,1)S(1)}, u32[]{:S(2)}, u32[]{:S(2)}) collective-permute-start(bf16[64,128]{1,0:T(8,128)(2,1)S(1)} %bitcast.7), channel_id=1, source_target_pairs={{0,4},{1,5},{2,6},{3,7},{4,0},{5,1},{6,2},{7,3},{8,12},{9,13},{10,... | collective-permute-start | bytes 49160 | tf_op jit(solution)/shard_map/ppermute | solution.py:173
  28.9 7.6 %collective-permute-start.8 = (bf16[1312,128]{1,0:T(8,128)(2,1)S(1)}, bf16[1312,128]{1,0:T(8,128)(2,1)S(1)}, u32[]{:S(2)}, u32[]{:S(2)}) collective-permute-start(bf16[1312,128]{1,0:T(8,128)(2,1)S(1)} %get-tuple-element.38), channel_id=1, source_target_pairs={{0,4},{1,5},{2,6},{3,7},{4,0},{5,1},{6,2},{7,3},{8,12},{9,13},{10,... | collective-permute-start | bytes 1007624 | tf_op jit(solution)/shard_map/ppermute | solution.py:173
  29.3 17.2 %collective-permute-start.7 = (bf16[328,1024]{1,0:T(8,128)(2,1)S(1)}, bf16[328,1024]{1,0:T(8,128)(2,1)S(1)}, u32[]{:S(2)}, u32[]{:S(2)}) collective-permute-start(bf16[328,1024]{1,0:T(8,128)(2,1)S(1)} %copy-done.2), channel_id=1, source_target_pairs={{0,1},{1,0},{2,3},{3,2},{4,5},{5,4},{6,7},{7,6},{8,9},{9,8},{10,11... | collective-permute-start | bytes 2015240 | tf_op jit(solution)/shard_map/ppermute | solution.py:173
  29.4 13.7 %collective-permute-start.12 = (bf16[1312,128]{1,0:T(8,128)(2,1)S(1)}, bf16[1312,128]{1,0:T(8,128)(2,1)S(1)}, u32[]{:S(2)}, u32[]{:S(2)}) collective-permute-start(bf16[1312,128]{1,0:T(8,128)(2,1)S(1)} %get-tuple-element.36.refs_0_), channel_id=1, source_target_pairs={{0,1},{1,0},{2,3},{3,2},{4,5},{5,4},{6,7},{7,6},{8,9},{9,8},{10,11... | collective-permute-start | bytes 1007624 | tf_op jit(solution)/shard_map/ppermute | solution.py:173
  29.9 10.3 %collective-permute-start.9 = (bf16[256,128]{1,0:T(8,128)(2,1)S(1)}, bf16[256,128]{1,0:T(8,128)(2,1)S(1)}, u32[]{:S(2)}, u32[]{:S(2)}) collective-permute-start(bf16[256,128]{1,0:T(8,128)(2,1)S(1)} %shard_map.105.refs_0_), channel_id=1, source_target_pairs={{0,8},{8,0},{16,24},{24,16},{1,9},{9,1},{17,25},{25,17},{2,10},{10... | collective-permute-start | bytes 196616 | tf_op jit(solution)/shard_map/ppermute | solution.py:173
  31.6 8.5 %collective-permute-start.10 = (bf16[256,128]{1,0:T(8,128)(2,1)S(1)}, bf16[256,128]{1,0:T(8,128)(2,1)S(1)}, u32[]{:S(2)}, u32[]{:S(2)}) collective-permute-start(bf16[256,128]{1,0:T(8,128)(2,1)S(1)} %shard_map.105.refs_0_), channel_id=1, source_target_pairs={{0,16},{8,24},{16,0},{24,8},{1,17},{9,25},{17,1},{25,9},{2,18},{10... | collective-permute-start | bytes 196616 | tf_op jit(solution)/shard_map/ppermute | solution.py:173
  36.5 6.1 %collective-permute-start.11 = (bf16[256,128]{1,0:T(8,128)(2,1)S(1)}, bf16[256,128]{1,0:T(8,128)(2,1)S(1)}, u32[]{:S(2)}, u32[]{:S(2)}) collective-permute-start(bf16[256,128]{1,0:T(8,128)(2,1)S(1)} %shard_map.105.refs_0_), channel_id=1, source_target_pairs={{0,24},{8,16},{16,8},{24,0},{1,25},{9,17},{17,9},{25,1},{2,26},{10... | collective-permute-start | bytes 196616 | tf_op jit(solution)/shard_map/ppermute | solution.py:173
  40.1 6.4 %collective-permute-start.13 = (bf16[1312,128]{1,0:T(8,128)(2,1)S(1)}, bf16[1312,128]{1,0:T(8,128)(2,1)S(1)}, u32[]{:S(2)}, u32[]{:S(2)}) collective-permute-start(bf16[1312,128]{1,0:T(8,128)(2,1)S(1)} %collective-permute-done.refs_1_), channel_id=1, source_target_pairs={{0,1},{1,0},{2,3},{3,2},{4,5},{5,4},{6,7},{7,6},{8,9},{9,8},{10,11... | collective-permute-start | bytes 1007624 | tf_op jit(solution)/shard_map/ppermute | solution.py:173
  42.6 3.9 %collective-permute-start.14 = (bf16[1312,128]{1,0:T(8,128)(2,1)S(1)}, bf16[1312,128]{1,0:T(8,128)(2,1)S(1)}, u32[]{:S(2)}, u32[]{:S(2)}) collective-permute-start(bf16[1312,128]{1,0:T(8,128)(2,1)S(1)} %collective-permute-done.8.refs_2_), channel_id=1, source_target_pairs={{0,1},{1,0},{2,3},{3,2},{4,5},{5,4},{6,7},{7,6},{8,9},{9,8},{10,11... | collective-permute-start | bytes 1007624 | tf_op jit(solution)/shard_map/ppermute | solution.py:173
  42.6 1.9 %collective-permute-start.15 = (bf16[720,128]{1,0:T(8,128)(2,1)S(1)}, bf16[720,128]{1,0:T(8,128)(2,1)S(1)}, u32[]{:S(2)}, u32[]{:S(2)}) collective-permute-start(bf16[720,128]{1,0:T(8,128)(2,1)S(1)} %collective-permute-done.1.refs_3_), channel_id=1, source_target_pairs={{0,1},{1,0},{2,3},{3,2},{4,5},{5,4},{6,7},{7,6},{8,9},{9,8},{10,11... | collective-permute-start | bytes 552968 | tf_op jit(solution)/shard_map/ppermute | solution.py:173
  43.1 2.9 %collective-permute-start.16 = (bf16[720,128]{1,0:T(8,128)(2,1)S(1)}, bf16[720,128]{1,0:T(8,128)(2,1)S(1)}, u32[]{:S(2)}, u32[]{:S(2)}) collective-permute-start(bf16[720,128]{1,0:T(8,128)(2,1)S(1)} %collective-permute-done.2.refs_4_), channel_id=1, source_target_pairs={{0,1},{1,0},{2,3},{3,2},{4,5},{5,4},{6,7},{7,6},{8,9},{9,8},{10,11... | collective-permute-start | bytes 552968 | tf_op jit(solution)/shard_map/ppermute | solution.py:173
  43.1 4.3 %copy-start.5 = (f32[1024]{0:T(1024)S(1)}, f32[1024]{0:T(1024)}, u32[]{:S(2)}) copy-start(f32[1024]{0:T(1024)} %param.10) | copy-start | bytes 12292
  44.5 7.9 %collective-permute-start.19 = (bf16[64,1024]{1,0:T(8,128)(2,1)S(1)}, bf16[64,1024]{1,0:T(8,128)(2,1)S(1)}, u32[]{:S(2)}, u32[]{:S(2)}) collective-permute-start(bf16[64,1024]{1,0:T(8,128)(2,1)S(1)} %slice.10), channel_id=1, source_target_pairs={{0,2},{1,3},{2,0},{3,1},{4,6},{5,7},{6,4},{7,5},{8,10},{9,11},{10,... | collective-permute-start | bytes 393224 | tf_op jit(solution)/shard_map/ppermute | solution.py:173
  46.0 6.4 %collective-permute-start.20 = (bf16[64,1024]{1,0:T(8,128)(2,1)S(1)}, bf16[64,1024]{1,0:T(8,128)(2,1)S(1)}, u32[]{:S(2)}, u32[]{:S(2)}) collective-permute-start(bf16[64,1024]{1,0:T(8,128)(2,1)S(1)} %slice.11), channel_id=1, source_target_pairs={{0,4},{1,5},{2,6},{3,7},{4,0},{5,1},{6,2},{7,3},{8,12},{9,13},{10,... | collective-permute-start | bytes 393224 | tf_op jit(solution)/shard_map/ppermute | solution.py:173
  50.2 8.8 %collective-permute-start.17 = (bf16[128,1024]{1,0:T(8,128)(2,1)S(1)}, bf16[128,1024]{1,0:T(8,128)(2,1)S(1)}, u32[]{:S(2)}, u32[]{:S(2)}) collective-permute-start(bf16[128,1024]{1,0:T(8,128)(2,1)S(1)} %shard_map.107), channel_id=1, source_target_pairs={{0,2},{1,3},{2,0},{3,1},{4,6},{5,7},{6,4},{7,5},{8,10},{9,11},{10,... | collective-permute-start | bytes 786440 | tf_op jit(solution)/shard_map/ppermute | solution.py:173
  50.9 12.1 %collective-permute-start.18 = (bf16[128,1024]{1,0:T(8,128)(2,1)S(1)}, bf16[128,1024]{1,0:T(8,128)(2,1)S(1)}, u32[]{:S(2)}, u32[]{:S(2)}) collective-permute-start(bf16[128,1024]{1,0:T(8,128)(2,1)S(1)} %shard_map.108), channel_id=1, source_target_pairs={{0,4},{1,5},{2,6},{3,7},{4,0},{5,1},{6,2},{7,3},{8,12},{9,13},{10,... | collective-permute-start | bytes 786440 | tf_op jit(solution)/shard_map/ppermute | solution.py:173
  52.3 12.1 %collective-permute-start.22 = (bf16[1024,128]{1,0:T(8,128)(2,1)S(1)}, bf16[1024,128]{1,0:T(8,128)(2,1)S(1)}, u32[]{:S(2)}, u32[]{:S(2)}) collective-permute-start(bf16[1024,128]{1,0:T(8,128)(2,1)S(1)} %shard_map.111.refs_3_), channel_id=1, source_target_pairs={{0,1},{1,0},{2,3},{3,2},{4,5},{5,4},{6,7},{7,6},{8,9},{9,8},{10,11... | collective-permute-start | bytes 786440 | tf_op jit(solution)/shard_map/ppermute | solution.py:173
  53.8 10.8 %copy-start.3 = (bf16[1024,128]{1,0:T(8,128)(2,1)S(1)}, bf16[1024,128]{1,0:T(8,128)(2,1)}, u32[]{:S(2)}) copy-start(bf16[1024,128]{1,0:T(8,128)(2,1)} %proj_ref.1) | copy-start | bytes 786436
  53.8 10.8 %copy-start.6 = (f32[1024]{0:T(1024)S(1)}, f32[1024]{0:T(1024)}, u32[]{:S(2)}) copy-start(f32[1024]{0:T(1024)} %param.13) | copy-start | bytes 12292
  53.8 10.8 %copy-start.8 = (s32[1,4]{1,0:T(1,128)S(1)}, s32[1,4]{1,0:T(1,128)}, u32[]{:S(2)}) copy-start(s32[1,4]{1,0:T(1,128)} %lengths_ref.1) | copy-start | bytes 52
  53.8 10.8 %collective-permute-start.21 = (bf16[128,1024]{1,0:T(8,128)(2,1)S(1)}, bf16[128,1024]{1,0:T(8,128)(2,1)S(1)}, u32[]{:S(2)}, u32[]{:S(2)}) collective-permute-start(bf16[128,1024]{1,0:T(8,128)(2,1)S(1)} %shard_map.110), channel_id=1, source_target_pairs={{0,6},{1,7},{2,4},{3,5},{4,2},{5,3},{6,0},{7,1},{8,14},{9,15},{10,... | collective-permute-start | bytes 786440 | tf_op jit(solution)/shard_map/ppermute | solution.py:173
  64.4 16.1 %copy-start.7 = (s32[2,100]{1,0:T(2,128)S(1)}, s32[2,100]{1,0:T(2,128)}, u32[]{:S(2)}) copy-start(s32[2,100]{1,0:T(2,128)} %cand_ref.1) | copy-start | bytes 2404

commit v7 on v5

--- a/solution.py
+++ b/solution.py
@@ -84,8 +84,7 @@
 
 
 def finish_kernel(chips, lengths_ref, tokens_ref, gain_ref, proj_ref, own_ref, *refs):
-    parts, refs = refs[: chips - 1], refs[chips - 1 :]
-    queries, (vectors_ref, out_ref) = refs[:-2], refs[-2:]
+    parts, (vectors_ref, sent_ref) = refs[: chips - 1], refs[chips - 1 :]
     mixed = tokens_ref[...].astype(jnp.float32) + own_ref[...]
     for part in parts:
         mixed = mixed + part[...].astype(jnp.float32)
@@ -94,42 +93,51 @@
     total = jnp.sum(projected * projected, axis=-1, keepdims=True)
     vectors = (projected * lax.rsqrt(total + 1e-06)).astype(jnp.bfloat16)
     vectors_ref[...] = vectors
-    group, me = lax.axis_index("group"), lax.axis_index("dev")
     rows = vectors.shape[0]
-    docs = out_ref.shape[1]
-    spot = me * rows + lax.broadcasted_iota(jnp.int32, (rows, 128), 0)
-    inside, low = [], jnp.int32(0)
-    for doc in range(docs):
-        high = low + lengths_ref[0, doc]
-        inside.append((spot >= low) & (spot < high))
-        low = high
-    for far, block in enumerate(queries):
-        for start in range(0, block.shape[0], 128):
-            similar = dot_nt(vectors, block[start : start + 128, :])
+    sent_ref[:rows] = vectors
+    spot = lax.axis_index("dev") * rows + lax.broadcasted_iota(jnp.int32, (16, rows), 1)
+    owner, end = jnp.zeros((16, rows), jnp.float32), jnp.int32(0)
+    for doc in range(lengths_ref.shape[1]):
+        end = end + lengths_ref[0, doc]
+        owner = owner + (spot >= end).astype(jnp.float32)
+    sent_ref[rows:] = owner.astype(jnp.bfloat16)
+
+
+def score_kernel(groups, query_ref, *refs):
+    blocks, out_ref = refs[:groups], refs[groups]
+    group = lax.axis_index("group")
+    docs = out_ref.shape[2]
+    rows = query_ref.shape[1]
+    for far, block in enumerate(blocks):
+        vectors = block[:rows]
+        owner = jnp.broadcast_to(block[rows : rows + 1].astype(jnp.float32), (rows, rows)).T
+        for tile in range(query_ref.shape[0] // 128):
+            similar = dot_nt(vectors, query_ref[tile * 128 : (tile + 1) * 128, :])
             best = [
-                jnp.max(jnp.where(inside[doc], similar, -jnp.inf), axis=0, keepdims=True)
+                jnp.max(jnp.where(owner == doc, similar, -jnp.inf), axis=0, keepdims=True)
                 for doc in range(docs)
             ]
             best = jnp.concatenate(best, axis=0).astype(jnp.bfloat16)
-            target = (group ^ far) * (2 * chips) + start // 64
-            out_ref[target] = best
-            out_ref[target + 1] = best
+            out_ref[2 * tile, group ^ far] = best
+            out_ref[2 * tile + 1, group ^ far] = best
 
 
 def pick_kernel(query_len, cand_ref, best_ref, out_ref):
-    groups, _, docs, lanes = best_ref.shape
+    devices, groups, docs, lanes = best_ref.shape
     own, listed = cand_ref.shape
     offset = (lax.axis_index("dev") % 2) * own * query_len
     scores = [jnp.zeros((1, listed), jnp.float32) for _ in range(own)]
     lane = lax.broadcasted_iota(jnp.int32, (docs, lanes), 1)
     label = lax.broadcasted_iota(jnp.int32, (docs, listed), 0)
-    for far in range(groups):
-        best = jnp.max(best_ref[far].astype(jnp.float32), axis=0)
+    for group in range(groups):
+        best = best_ref[0, group].astype(jnp.float32)
+        for sender in range(1, devices):
+            best = jnp.maximum(best, best_ref[sender, group].astype(jnp.float32))
         for query in range(own):
             start = offset + query * query_len
             taken = jnp.where((lane >= start) & (lane < start + query_len), best, 0.0)
             value = jnp.sum(taken, axis=1, keepdims=True) / query_len
-            wanted = cand_ref[query : query + 1, :] - far * docs
+            wanted = cand_ref[query : query + 1, :] - group * docs
             scores[query] += jnp.sum(jnp.where(wanted == label, value, 0.0), axis=0, keepdims=True)
     for query in range(own):
         out_ref[query : query + 1, :] = scores[query]
@@ -161,7 +169,6 @@
 
     per_query, query_len, vector_dim = query_vectors.shape
     query_own = query_vectors.reshape(-1, vector_dim)
-    wo_other = swap(wo_weight, 1)
     near = [corpus_tokens] + [swap(corpus_tokens, 2 * step) for step in (1, 2)]
     if wi_weight.shape[0] == 128 and part % 16 == 0 and chips == 4 and groups % 2 == 0:
         own = query_own.shape[0]
@@ -178,7 +185,9 @@
         )(wi_weight, query_own)
         mine = [pieces[0]] + [swap(pieces[step], 2 * step) for step in range(1, chips)]
         mine.append(swap(mine[3], 1, "group"))
-        mine[1], near[1], near[2] = lax.optimization_barrier((mine[1], near[1], near[2]))
+        mine[1], mine[4], near[1], near[2] = lax.optimization_barrier((mine[1], mine[4], near[1], near[2]))
+        near[1], near[2], wo_next = lax.optimization_barrier((near[1], near[2], wo_weight))
+        wo_other = swap(wo_next, 1)
         far = [swap(near[2][: rows // 2], 2), swap(near[1][rows // 2 :], 4)]
         tokens = [[each] for each in near] + [far]
         other = [swap(piece, 1) for piece in mine]
@@ -199,6 +208,7 @@
         whole = lax.all_gather(wi_weight, "dev", axis=0, tiled=True).reshape(width, 2, chips, part)
         columns = lax.dynamic_index_in_dim(whole, me // 2, 2, keepdims=False)
         even = (me % 2) == 0
+        wo_other = swap(wo_weight, 1)
         wo_part = jnp.concatenate(
             [jnp.where(even, wo_weight, wo_other), jnp.where(even, wo_other, wo_weight)], axis=0
         )
@@ -219,16 +229,14 @@
         )(norm_gain.reshape(1, -1), *weights, *tokens[step])
         if step:
             arrived[step] = swap(partial[step], 2 * step)
-    queries = [plane] + [swap(plane, mask, "group") for mask in range(1, groups)]
-
-    docs = doc_lengths.shape[1]
-    vectors, best = pl.pallas_call(
+
+    vectors, sent = pl.pallas_call(
         functools.partial(finish_kernel, chips),
         out_shape=[
-            jax.ShapeDtypeStruct((rows, proj_weight.shape[1]), jnp.bfloat16),
-            jax.ShapeDtypeStruct((groups * devices, docs, 128), jnp.bfloat16),
+            jax.ShapeDtypeStruct((rows, vector_dim), jnp.bfloat16),
+            jax.ShapeDtypeStruct((rows + 16, vector_dim), jnp.bfloat16),
         ],
-        in_specs=[smem] + [vmem] * (4 + chips - 1 + groups),
+        in_specs=[smem] + [vmem] * (4 + chips - 1),
         out_specs=[vmem, vmem],
         compiler_params=params,
     )(
@@ -238,16 +246,24 @@
         proj_weight,
         partial[0],
         *arrived[:0:-1],
-        *queries,
-    )
-    met = lax.all_to_all(best, ("group", "dev"), split_axis=0, concat_axis=0, tiled=True)
+    )
+    blocks = [sent] + [swap(sent, mask, "group") for mask in range(1, groups)]
+    docs = doc_lengths.shape[1]
+    best = pl.pallas_call(
+        functools.partial(score_kernel, groups),
+        out_shape=jax.ShapeDtypeStruct((devices, groups, docs, 128), jnp.bfloat16),
+        in_specs=[vmem] * (1 + groups),
+        out_specs=vmem,
+        compiler_params=params,
+    )(plane, *blocks)
+    met = lax.all_to_all(best, "dev", split_axis=0, concat_axis=0, tiled=True)
     scores = pl.pallas_call(
         functools.partial(pick_kernel, query_len),
         out_shape=jax.ShapeDtypeStruct(candidates.shape, jnp.float32),
         in_specs=[vmem, vmem],
         out_specs=vmem,
         compiler_params=params,
-    )(candidates, met.reshape(groups, devices, docs, 128))
+    )(candidates, met)
     return (vectors, scores)
 
 

time: 72.7 us -> 70.3 us (0.967)
  blocking collectives: 11 us -> 8.4 us
  starting transfers between devices: 23.6 us -> 21.5 us
  waiting for transfers between devices: 25.6 us -> 27.4 us
    all_to_all x1, blocking collectives: 11 us -> 8.4 us  [body(): met = lax.all_to_all(best, 'dev', split_axis=0, concat_axis=0, tiled=True)]
    ppermute x20, starting transfers between devices: 23.6 us -> 21.5 us  [swap(): return lax.ppermute(values, axis, [(i, i ^ mask) for i in range(size)])]
    ppermute x20, waiting for transfers between devices: 25.6 us -> 27.4 us  [swap(): return lax.ppermute(values, axis, [(i, i ^ mask) for i in range(size)])]
  transfers between devices with their start and end apart: 20 -> 20, of which waited for: 6 -> 8; matrix products, arithmetic and copies ran while one was open for 0% -> 0% of each run, Pallas kernels for 9% -> 9%
where the time goes in v7:
time: 70.3 us; the launch traced here: 70.1 us
  waiting for transfers between devices  27.4 us (39%)
  starting transfers between devices  21.5 us (31%)
  Pallas kernels  9.91 us (14%)
  blocking collectives  8.4 us (12%)
  local copies, waits for them, and re-layouts  2.1 us (3%)
  between operations  0.8 us (1%)
    ppermute x20, waiting for transfers between devices, swap(): return lax.ppermute(values, axis, [(i, i ^ mask) for i in range(size)])  27.4 us
    ppermute x20, starting transfers between devices, swap(): return lax.ppermute(values, axis, [(i, i ^ mask) for i in range(size)])  21.5 us
    all_to_all x1, blocking collectives, body(): met = lax.all_to_all(best, 'dev', split_axis=0, concat_axis=0, tiled=True)  8.4 us
    pallas_call x4, Pallas kernels, body(): pl.pallas_call(ffn_kernel, out_shape=jax.ShapeDtypeStruct((rows, width),...  5.51 us
    unnamed x18, local copies, waits for them, and re-layouts  2.08 us
    pallas_call x1, Pallas kernels, body(): pl.pallas_call(functools.partial(finish_kernel, chips), out_shape=[jax.Sh...  1.75 us
  transfers between devices with their start and end apart: 20, of which 8 were waited for; matrix products, arithmetic and copies ran while one was open for 0% of the time, Pallas kernels for 9%

profile of v7, /device:TPU:0, one launch (start us, length us, event | category | flops | bytes accessed | tf_op | source)
XLA Modules:
  0.0 70.1 jit_solution(17352568644434573842)
XLA Ops:
  0.6 1.3 %copy-done = bf16[128,5248]{1,0:T(8,128)(2,1)S(1)} copy-done((bf16[128,5248]{1,0:T(8,128)(2,1)S(1)}, bf16[128,5248]{1,0:T(8,128)(2,1)}, u32[]{:S(2)}) %copy-start) | copy-done | bytes 1343512
  2.0 0.7 %copy-done.5 = bf16[2,32,128]{2,1,0:T(8,128)(2,1)S(1)} copy-done((bf16[2,32,128]{2,1,0:T(8,128)(2,1)S(1)}, bf16[2,32,128]{2,1,0:T(8,128)(2,1)}, u32[]{:S(2)}) %copy-start.5) | copy-done | bytes 16408
  2.7 0.5 shard_map.104
  3.2 4.0 %collective-permute-start.1 = (bf16[720,128]{1,0:T(8,128)(2,1)S(1)}, bf16[720,128]{1,0:T(8,128)(2,1)S(1)}, u32[]{:S(2)}, u32[]{:S(2)}) collective-permute-start(bf16[720,128]{1,0:T(8,128)(2,1)S(1)} %get-tuple-element.22), channel_id=1, source_target_pairs={{0,6},{1,7},{2,4},{3,5},{4,2},{5,3},{6,0},{7,1},{8,14},{9,15},{10,... | collective-permute-start | bytes 552968 | tf_op jit(solution)/shard_map/ppermute | solution.py:168
  7.1 0.5 collective-permute-start
  7.7 1.5 %collective-permute-start.3 = (bf16[128,1024]{1,0:T(8,128)(2,1)S(1)}, bf16[128,1024]{1,0:T(8,128)(2,1)S(1)}, u32[]{:S(2)}, u32[]{:S(2)}) collective-permute-start(bf16[128,1024]{1,0:T(8,128)(2,1)S(1)} %copy-done.1), channel_id=1, source_target_pairs={{0,2},{1,3},{2,0},{3,1},{4,6},{5,7},{6,4},{7,5},{8,10},{9,11},{10,... | collective-permute-start | bytes 786440 | tf_op jit(solution)/shard_map/ppermute | solution.py:168
  9.2 0.5 collective-permute-start.4
  9.7 2.9 %collective-permute-done.1.refs_3_ = bf16[720,128]{1,0:T(8,128)(2,1)S(1)} collective-permute-done((bf16[720,128]{1,0:T(8,128)(2,1)S(1)}, bf16[720,128]{1,0:T(8,128)(2,1)S(1)}, u32[]{:S(2)}, u32[]{:S(2)}) %collective-permute-start.1) | collective-permute-done | bytes 184352 | tf_op jit(solution)/shard_map/ppermute | solution.py:168
  12.6 2.1 %collective-permute-start.2 = (bf16[720,128]{1,0:T(8,128)(2,1)S(1)}, bf16[720,128]{1,0:T(8,128)(2,1)S(1)}, u32[]{:S(2)}, u32[]{:S(2)}) collective-permute-start(bf16[720,128]{1,0:T(8,128)(2,1)S(1)} %collective-permute-done.1.refs_3_), channel_id=1, source_target_pairs={{0,8},{8,0},{16,24},{24,16},{1,9},{9,1},{17,25},{25,17},{2,10},{10... | collective-permute-start | bytes 552968 | tf_op jit(solution)/shard_map/ppermute | solution.py:168
  14.7 1.5 %collective-permute-start.6 = (bf16[1376,128]{1,0:T(8,128)(2,1)S(1)}, bf16[1376,128]{1,0:T(8,128)(2,1)S(1)}, u32[]{:S(2)}, u32[]{:S(2)}) collective-permute-start(bf16[1376,128]{1,0:T(8,128)(2,1)S(1)} %get-tuple-element.28), channel_id=1, source_target_pairs={{0,4},{1,5},{2,6},{3,7},{4,0},{5,1},{6,2},{7,3},{8,12},{9,13},{10,... | collective-permute-start | bytes 1056776 | tf_op jit(solution)/shard_map/ppermute | solution.py:168
  16.2 9.0 %collective-permute-done.3.refs_0_ = bf16[128,1024]{1,0:T(8,128)(2,1)S(1)} collective-permute-done((bf16[128,1024]{1,0:T(8,128)(2,1)S(1)}, bf16[128,1024]{1,0:T(8,128)(2,1)S(1)}, u32[]{:S(2)}, u32[]{:S(2)}) %collective-permute-start.3) | collective-permute-done | bytes 262176 | tf_op jit(solution)/shard_map/ppermute | solution.py:168
  25.3 0.5 collective-permute-start.7
  26.4 1.5 %collective-permute-done.7.refs_5_ = bf16[1376,128]{1,0:T(8,128)(2,1)S(1)} collective-permute-done((bf16[1376,128]{1,0:T(8,128)(2,1)S(1)}, bf16[1376,128]{1,0:T(8,128)(2,1)S(1)}, u32[]{:S(2)}, u32[]{:S(2)}) %collective-permute-start.7) | collective-permute-done | bytes 352288 | tf_op jit(solution)/shard_map/ppermute | solution.py:168
  28.1 1.1 %collective-permute-done.10.refs_8_ = bf16[720,128]{1,0:T(8,128)(2,1)S(1)} collective-permute-done((bf16[720,128]{1,0:T(8,128)(2,1)S(1)}, bf16[720,128]{1,0:T(8,128)(2,1)S(1)}, u32[]{:S(2)}, u32[]{:S(2)}) %collective-permute-start.10) | collective-permute-done | bytes 184352 | tf_op jit(solution)/shard_map/ppermute | solution.py:168
  29.2 1.5 %collective-permute-start.13 = (bf16[64,1024]{1,0:T(8,128)(2,1)S(1)}, bf16[64,1024]{1,0:T(8,128)(2,1)S(1)}, u32[]{:S(2)}, u32[]{:S(2)}) collective-permute-start(bf16[64,1024]{1,0:T(8,128)(2,1)S(1)} %slice.6), channel_id=1, source_target_pairs={{0,2},{1,3},{2,0},{3,1},{4,6},{5,7},{6,4},{7,5},{8,10},{9,11},{10,... | collective-permute-start | bytes 393224 | tf_op jit(solution)/shard_map/ppermute | solution.py:168
  31.2 0.9 %shard_map.105 = (bf16[656,1024]{1,0:T(8,128)(2,1)S(1)}, bf16[656,1024]{1,0:T(8,128)(2,1)S(1)}, bf16[656,1024]{1,0:T(8,128)(2,1)S(1)}, bf16[512,128]{1,0:T(8,128)(2,1)S(1)}) custom-call(bf16[328,1024]{1,0:T(8,128)(2,1)S(1)} %copy-done.2, bf16[328,1024]{1,0:T(8,128)(2,1)S(1)} %collective-permute-done.5.wo_other, ...), custom_call_target="tpu_custom_call" | custom-call | tf_op jit(solution)/shard_map/pallas_call | solution.py:194
  32.1 1.4 %shard_map.106 = bf16[128,1024]{1,0:T(8,128)(2,1)S(1)} custom-call(f32[1,1024]{1,0:T(1,128)S(1)} %bitcast.3, bf16[656,1024]{1,0:T(8,128)(2,1)S(1)} %get-tuple-element.30.gelu_w, bf16[656,1024]{1,0:T(8,128)(2,1)S(1)} %get-tuple-element.31.gate_w, bf16[656,1024]{1,0:T(8,128)(2,1)S(1)} %get-tuple-element.32.wo_part, ...), custom_call_target="tpu_custom_call" | custom-call | tf_op jit(solution)/shard_map/pallas_call | solution.py:223
  33.9 1.4 %shard_map.109 = bf16[128,1024]{1,0:T(8,128)(2,1)S(1)} custom-call(f32[1,1024]{1,0:T(1,128)S(1)} %bitcast.4, bf16[656,1024]{1,0:T(8,128)(2,1)S(1)} %get-tuple-element.30.gelu_w, bf16[656,1024]{1,0:T(8,128)(2,1)S(1)} %get-tuple-element.31.gate_w, bf16[656,1024]{1,0:T(8,128)(2,1)S(1)} %get-tuple-element.32.wo_part, ...), custom_call_target="tpu_custom_call" | custom-call | tf_op jit(solution)/shard_map/pallas_call | solution.py:223
  35.3 1.8 %collective-permute-start.16 = (bf16[128,1024]{1,0:T(8,128)(2,1)S(1)}, bf16[128,1024]{1,0:T(8,128)(2,1)S(1)}, u32[]{:S(2)}, u32[]{:S(2)}) collective-permute-start(bf16[128,1024]{1,0:T(8,128)(2,1)S(1)} %shard_map.109), channel_id=1, source_target_pairs={{0,4},{1,5},{2,6},{3,7},{4,0},{5,1},{6,2},{7,3},{8,12},{9,13},{10,... | collective-permute-start | bytes 786440 | tf_op jit(solution)/shard_map/ppermute | solution.py:168
  37.0 1.4 %shard_map.108 = bf16[128,1024]{1,0:T(8,128)(2,1)S(1)} custom-call(f32[1,1024]{1,0:T(1,128)S(1)} %bitcast.5, bf16[656,1024]{1,0:T(8,128)(2,1)S(1)} %get-tuple-element.30.gelu_w, bf16[656,1024]{1,0:T(8,128)(2,1)S(1)} %get-tuple-element.31.gate_w, bf16[656,1024]{1,0:T(8,128)(2,1)S(1)} %get-tuple-element.32.wo_part, ...), custom_call_target="tpu_custom_call" | custom-call | tf_op jit(solution)/shard_map/pallas_call | solution.py:223
  38.5 1.5 %collective-permute-start.15 = (bf16[128,1024]{1,0:T(8,128)(2,1)S(1)}, bf16[128,1024]{1,0:T(8,128)(2,1)S(1)}, u32[]{:S(2)}, u32[]{:S(2)}) collective-permute-start(bf16[128,1024]{1,0:T(8,128)(2,1)S(1)} %shard_map.108), channel_id=1, source_target_pairs={{0,6},{1,7},{2,4},{3,5},{4,2},{5,3},{6,0},{7,1},{8,14},{9,15},{10,... | collective-permute-start | bytes 786440 | tf_op jit(solution)/shard_map/ppermute | solution.py:168
  40.0 2.5 %collective-permute-done.12.refs_2_ = bf16[128,1024]{1,0:T(8,128)(2,1)S(1)} collective-permute-done((bf16[128,1024]{1,0:T(8,128)(2,1)S(1)}, bf16[128,1024]{1,0:T(8,128)(2,1)S(1)}, u32[]{:S(2)}, u32[]{:S(2)}) %collective-permute-start.12) | collective-permute-done | bytes 262176 | tf_op jit(solution)/shard_map/ppermute | solution.py:168
  42.5 1.4 %shard_map.107.own_ref = f32[128,1024]{1,0:T(8,128)S(1)} custom-call(f32[1,1024]{1,0:T(1,128)S(1)} %bitcast.6, bf16[656,1024]{1,0:T(8,128)(2,1)S(1)} %get-tuple-element.30.gelu_w, bf16[656,1024]{1,0:T(8,128)(2,1)S(1)} %get-tuple-element.31.gate_w, bf16[656,1024]{1,0:T(8,128)(2,1)S(1)} %get-tuple-element.32.wo_part, bf16[128,1024]{1,0:T(8,128)(2,1)S(1)} %copy-done.1), custom_call_target="tpu_custom_call" | custom-call | tf_op jit(solution)/shard_map/pallas_call | solution.py:223
  43.9 4.8 %collective-permute-done.16.refs_1_ = bf16[128,1024]{1,0:T(8,128)(2,1)S(1)} collective-permute-done((bf16[128,1024]{1,0:T(8,128)(2,1)S(1)}, bf16[128,1024]{1,0:T(8,128)(2,1)S(1)}, u32[]{:S(2)}, u32[]{:S(2)}) %collective-permute-start.16) | collective-permute-done | bytes 262176 | tf_op jit(solution)/shard_map/ppermute | solution.py:168
  48.7 1.8 %shard_map.110 = (bf16[128,128]{1,0:T(8,128)(2,1)}, bf16[144,128]{1,0:T(8,128)(2,1)S(1)}) custom-call(s32[1,4]{1,0:T(1,128)S(1)} %copy-done.8, bf16[128,1024]{1,0:T(8,128)(2,1)S(1)} %copy-done.1, f32[1,1024]{1,0:T(1,128)S(1)} %bitcast.8, bf16[1024,128]{1,0:T(8,128)(2,1)S(1)} %copy-done.3, f32[128,1024]{1,0:T(8,128)S(1)} %shard_map.107.own_ref, ...), custom_call_target="tpu_custom_call" | custom-call | tf_op jit(solution)/shard_map/pallas_call | solution.py:233
  50.4 1.6 %collective-permute-start.17 = (bf16[144,128]{1,0:T(8,128)(2,1)S(1)}, bf16[144,128]{1,0:T(8,128)(2,1)S(1)}, u32[]{:S(2)}, u32[]{:S(2)}) collective-permute-start(bf16[144,128]{1,0:T(8,128)(2,1)S(1)} %get-tuple-element.39.refs_0_), channel_id=1, source_target_pairs={{0,8},{8,0},{16,24},{24,16},{1,9},{9,1},{17,25},{25,17},{2,10},{10... | collective-permute-start | bytes 110600 | tf_op jit(solution)/shard_map/ppermute | solution.py:168
  52.0 2.6 %collective-permute-start.18 = (bf16[144,128]{1,0:T(8,128)(2,1)S(1)}, bf16[144,128]{1,0:T(8,128)(2,1)S(1)}, u32[]{:S(2)}, u32[]{:S(2)}) collective-permute-start(bf16[144,128]{1,0:T(8,128)(2,1)S(1)} %get-tuple-element.39.refs_0_), channel_id=1, source_target_pairs={{0,16},{8,24},{16,0},{24,8},{1,17},{9,25},{17,1},{25,9},{2,18},{10... | collective-permute-start | bytes 110600 | tf_op jit(solution)/shard_map/ppermute | solution.py:168
  54.8 2.8 %collective-permute-done.18.refs_2_ = bf16[144,128]{1,0:T(8,128)(2,1)S(1)} collective-permute-done((bf16[144,128]{1,0:T(8,128)(2,1)S(1)}, bf16[144,128]{1,0:T(8,128)(2,1)S(1)}, u32[]{:S(2)}, u32[]{:S(2)}) %collective-permute-start.18) | collective-permute-done | bytes 36896 | tf_op jit(solution)/shard_map/ppermute | solution.py:168
  57.6 2.8 %collective-permute-done.19.refs_3_ = bf16[144,128]{1,0:T(8,128)(2,1)S(1)} collective-permute-done((bf16[144,128]{1,0:T(8,128)(2,1)S(1)}, bf16[144,128]{1,0:T(8,128)(2,1)S(1)}, u32[]{:S(2)}, u32[]{:S(2)}) %collective-permute-start.19) | collective-permute-done | bytes 36896 | tf_op jit(solution)/shard_map/ppermute | solution.py:168
  60.4 0.6 shard_map.111
  61.0 8.4 %all_to_all.5.best_ref = bf16[8,4,4,128]{3,2,1,0:T(4,128)(2,1)S(1)} all-to-all(bf16[8,4,4,128]{3,2,1,0:T(4,128)(2,1)S(1)} %shard_map.111), channel_id=1, replica_groups=mesh['group'=4,'dev'=8] {'dev'}, dimensions={0} | all-to-all | bytes 65536 | tf_op jit(solution)/shard_map/all_to_all | solution.py:259
  69.4 0.7 shard_map.112
  (38 shorter events, 2.0 us)
Async XLA Ops:
  0.6 1.3 %copy-start = (bf16[128,5248]{1,0:T(8,128)(2,1)S(1)}, bf16[128,5248]{1,0:T(8,128)(2,1)}, u32[]{:S(2)}) copy-start(bf16[128,5248]{1,0:T(8,128)(2,1)} %wi_ref.1) | copy-start | bytes 4030468
  2.0 0.7 %copy-start.5 = (bf16[2,32,128]{2,1,0:T(8,128)(2,1)S(1)}, bf16[2,32,128]{2,1,0:T(8,128)(2,1)}, u32[]{:S(2)}) copy-start(bf16[2,32,128]{2,1,0:T(8,128)(2,1)} %param.15) | copy-start | bytes 49156
  2.7 5.0 %copy-start.1 = (bf16[128,1024]{1,0:T(8,128)(2,1)S(1)}, bf16[128,1024]{1,0:T(8,128)(2,1)}, u32[]{:S(2)}) copy-start(bf16[128,1024]{1,0:T(8,128)(2,1)} %tokens_ref.1) | copy-start | bytes 786436
  2.7 22.5 %copy-start.2 = (bf16[328,1024]{1,0:T(8,128)(2,1)S(1)}, bf16[328,1024]{1,0:T(8,128)(2,1)}, u32[]{:S(2)}) copy-start(bf16[328,1024]{1,0:T(8,128)(2,1)} %wo_mine.1) | copy-start | bytes 2015236
  3.2 9.4 %collective-permute-start.1 = (bf16[720,128]{1,0:T(8,128)(2,1)S(1)}, bf16[720,128]{1,0:T(8,128)(2,1)S(1)}, u32[]{:S(2)}, u32[]{:S(2)}) collective-permute-start(bf16[720,128]{1,0:T(8,128)(2,1)S(1)} %get-tuple-element.22), channel_id=1, source_target_pairs={{0,6},{1,7},{2,4},{3,5},{4,2},{5,3},{6,0},{7,1},{8,14},{9,15},{10,... | collective-permute-start | bytes 552968 | tf_op jit(solution)/shard_map/ppermute | solution.py:168
  7.1 18.1 %collective-permute-start = (bf16[1376,128]{1,0:T(8,128)(2,1)S(1)}, bf16[1376,128]{1,0:T(8,128)(2,1)S(1)}, u32[]{:S(2)}, u32[]{:S(2)}) collective-permute-start(bf16[1376,128]{1,0:T(8,128)(2,1)S(1)} %get-tuple-element.21), channel_id=1, source_target_pairs={{0,2},{1,3},{2,0},{3,1},{4,6},{5,7},{6,4},{7,5},{8,10},{9,11},{10,... | collective-permute-start | bytes 1056776 | tf_op jit(solution)/shard_map/ppermute | solution.py:168
  7.7 17.5 %collective-permute-start.3 = (bf16[128,1024]{1,0:T(8,128)(2,1)S(1)}, bf16[128,1024]{1,0:T(8,128)(2,1)S(1)}, u32[]{:S(2)}, u32[]{:S(2)}) collective-permute-start(bf16[128,1024]{1,0:T(8,128)(2,1)S(1)} %copy-done.1), channel_id=1, source_target_pairs={{0,2},{1,3},{2,0},{3,1},{4,6},{5,7},{6,4},{7,5},{8,10},{9,11},{10,... | collective-permute-start | bytes 786440 | tf_op jit(solution)/shard_map/ppermute | solution.py:168
  9.2 16.0 %collective-permute-start.4 = (bf16[128,1024]{1,0:T(8,128)(2,1)S(1)}, bf16[128,1024]{1,0:T(8,128)(2,1)S(1)}, u32[]{:S(2)}, u32[]{:S(2)}) collective-permute-start(bf16[128,1024]{1,0:T(8,128)(2,1)S(1)} %copy-done.1), channel_id=1, source_target_pairs={{0,4},{1,5},{2,6},{3,7},{4,0},{5,1},{6,2},{7,3},{8,12},{9,13},{10,... | collective-permute-start | bytes 786440 | tf_op jit(solution)/shard_map/ppermute | solution.py:168
  12.6 12.6 %collective-permute-start.2 = (bf16[720,128]{1,0:T(8,128)(2,1)S(1)}, bf16[720,128]{1,0:T(8,128)(2,1)S(1)}, u32[]{:S(2)}, u32[]{:S(2)}) collective-permute-start(bf16[720,128]{1,0:T(8,128)(2,1)S(1)} %collective-permute-done.1.refs_3_), channel_id=1, source_target_pairs={{0,8},{8,0},{16,24},{24,16},{1,9},{9,1},{17,25},{25,17},{2,10},{10... | collective-permute-start | bytes 552968 | tf_op jit(solution)/shard_map/ppermute | solution.py:168
  14.7 11.1 %collective-permute-start.6 = (bf16[1376,128]{1,0:T(8,128)(2,1)S(1)}, bf16[1376,128]{1,0:T(8,128)(2,1)S(1)}, u32[]{:S(2)}, u32[]{:S(2)}) collective-permute-start(bf16[1376,128]{1,0:T(8,128)(2,1)S(1)} %get-tuple-element.28), channel_id=1, source_target_pairs={{0,4},{1,5},{2,6},{3,7},{4,0},{5,1},{6,2},{7,3},{8,12},{9,13},{10,... | collective-permute-start | bytes 1056776 | tf_op jit(solution)/shard_map/ppermute | solution.py:168
  25.2 6.0 %collective-permute-start.5 = (bf16[328,1024]{1,0:T(8,128)(2,1)S(1)}, bf16[328,1024]{1,0:T(8,128)(2,1)S(1)}, u32[]{:S(2)}, u32[]{:S(2)}) collective-permute-start(bf16[328,1024]{1,0:T(8,128)(2,1)S(1)} %copy-done.2), channel_id=1, source_target_pairs={{0,1},{1,0},{2,3},{3,2},{4,5},{5,4},{6,7},{7,6},{8,9},{9,8},{10,11... | collective-permute-start | bytes 2015240 | tf_op jit(solution)/shard_map/ppermute | solution.py:168
  25.3 2.6 %collective-permute-start.7 = (bf16[1376,128]{1,0:T(8,128)(2,1)S(1)}, bf16[1376,128]{1,0:T(8,128)(2,1)S(1)}, u32[]{:S(2)}, u32[]{:S(2)}) collective-permute-start(bf16[1376,128]{1,0:T(8,128)(2,1)S(1)} %get-tuple-element.26.refs_0_), channel_id=1, source_target_pairs={{0,1},{1,0},{2,3},{3,2},{4,5},{5,4},{6,7},{7,6},{8,9},{9,8},{10,11... | collective-permute-start | bytes 1056776 | tf_op jit(solution)/shard_map/ppermute | solution.py:168
  25.8 5.4 %collective-permute-start.9 = (bf16[1376,128]{1,0:T(8,128)(2,1)S(1)}, bf16[1376,128]{1,0:T(8,128)(2,1)S(1)}, u32[]{:S(2)}, u32[]{:S(2)}) collective-permute-start(bf16[1376,128]{1,0:T(8,128)(2,1)S(1)} %collective-permute-done.6.refs_2_), channel_id=1, source_target_pairs={{0,1},{1,0},{2,3},{3,2},{4,5},{5,4},{6,7},{7,6},{8,9},{9,8},{10,11... | collective-permute-start | bytes 1056776 | tf_op jit(solution)/shard_map/ppermute | solution.py:168
  25.9 5.3 %collective-permute-start.8 = (bf16[1376,128]{1,0:T(8,128)(2,1)S(1)}, bf16[1376,128]{1,0:T(8,128)(2,1)S(1)}, u32[]{:S(2)}, u32[]{:S(2)}) collective-permute-start(bf16[1376,128]{1,0:T(8,128)(2,1)S(1)} %collective-permute-done.refs_1_), channel_id=1, source_target_pairs={{0,1},{1,0},{2,3},{3,2},{4,5},{5,4},{6,7},{7,6},{8,9},{9,8},{10,11... | collective-permute-start | bytes 1056776 | tf_op jit(solution)/shard_map/ppermute | solution.py:168
  26.3 2.9 %collective-permute-start.10 = (bf16[720,128]{1,0:T(8,128)(2,1)S(1)}, bf16[720,128]{1,0:T(8,128)(2,1)S(1)}, u32[]{:S(2)}, u32[]{:S(2)}) collective-permute-start(bf16[720,128]{1,0:T(8,128)(2,1)S(1)} %collective-permute-done.1.refs_3_), channel_id=1, source_target_pairs={{0,1},{1,0},{2,3},{3,2},{4,5},{5,4},{6,7},{7,6},{8,9},{9,8},{10,11... | collective-permute-start | bytes 552968 | tf_op jit(solution)/shard_map/ppermute | solution.py:168
  27.9 2.8 %collective-permute-start.11 = (bf16[720,128]{1,0:T(8,128)(2,1)S(1)}, bf16[720,128]{1,0:T(8,128)(2,1)S(1)}, u32[]{:S(2)}, u32[]{:S(2)}) collective-permute-start(bf16[720,128]{1,0:T(8,128)(2,1)S(1)} %collective-permute-done.2.refs_4_), channel_id=1, source_target_pairs={{0,1},{1,0},{2,3},{3,2},{4,5},{5,4},{6,7},{7,6},{8,9},{9,8},{10,11... | collective-permute-start | bytes 552968 | tf_op jit(solution)/shard_map/ppermute | solution.py:168
  28.1 4.0 %copy-start.4 = (f32[1024]{0:T(1024)S(1)}, f32[1024]{0:T(1024)}, u32[]{:S(2)}) copy-start(f32[1024]{0:T(1024)} %param.10) | copy-start | bytes 12292
  29.2 7.9 %collective-permute-start.13 = (bf16[64,1024]{1,0:T(8,128)(2,1)S(1)}, bf16[64,1024]{1,0:T(8,128)(2,1)S(1)}, u32[]{:S(2)}, u32[]{:S(2)}) collective-permute-start(bf16[64,1024]{1,0:T(8,128)(2,1)S(1)} %slice.6), channel_id=1, source_target_pairs={{0,2},{1,3},{2,0},{3,1},{4,6},{5,7},{6,4},{7,5},{8,10},{9,11},{10,... | collective-permute-start | bytes 393224 | tf_op jit(solution)/shard_map/ppermute | solution.py:168
  30.7 6.3 %collective-permute-start.14 = (bf16[64,1024]{1,0:T(8,128)(2,1)S(1)}, bf16[64,1024]{1,0:T(8,128)(2,1)S(1)}, u32[]{:S(2)}, u32[]{:S(2)}) collective-permute-start(bf16[64,1024]{1,0:T(8,128)(2,1)S(1)} %slice.7), channel_id=1, source_target_pairs={{0,4},{1,5},{2,6},{3,7},{4,0},{5,1},{6,2},{7,3},{8,12},{9,13},{10,... | collective-permute-start | bytes 393224 | tf_op jit(solution)/shard_map/ppermute | solution.py:168
  33.5 9.0 %collective-permute-start.12 = (bf16[128,1024]{1,0:T(8,128)(2,1)S(1)}, bf16[128,1024]{1,0:T(8,128)(2,1)S(1)}, u32[]{:S(2)}, u32[]{:S(2)}) collective-permute-start(bf16[128,1024]{1,0:T(8,128)(2,1)S(1)} %shard_map.106), channel_id=1, source_target_pairs={{0,2},{1,3},{2,0},{3,1},{4,6},{5,7},{6,4},{7,5},{8,10},{9,11},{10,... | collective-permute-start | bytes 786440 | tf_op jit(solution)/shard_map/ppermute | solution.py:168
  35.3 13.4 %collective-permute-start.16 = (bf16[128,1024]{1,0:T(8,128)(2,1)S(1)}, bf16[128,1024]{1,0:T(8,128)(2,1)S(1)}, u32[]{:S(2)}, u32[]{:S(2)}) collective-permute-start(bf16[128,1024]{1,0:T(8,128)(2,1)S(1)} %shard_map.109), channel_id=1, source_target_pairs={{0,4},{1,5},{2,6},{3,7},{4,0},{5,1},{6,2},{7,3},{8,12},{9,13},{10,... | collective-permute-start | bytes 786440 | tf_op jit(solution)/shard_map/ppermute | solution.py:168
  38.4 10.2 %copy-start.3 = (bf16[1024,128]{1,0:T(8,128)(2,1)S(1)}, bf16[1024,128]{1,0:T(8,128)(2,1)}, u32[]{:S(2)}) copy-start(bf16[1024,128]{1,0:T(8,128)(2,1)} %proj_ref.1) | copy-start | bytes 786436
  38.4 10.2 %copy-start.6 = (f32[1024]{0:T(1024)S(1)}, f32[1024]{0:T(1024)}, u32[]{:S(2)}) copy-start(f32[1024]{0:T(1024)} %param.13) | copy-start | bytes 12292
  38.5 10.2 %copy-start.8 = (s32[1,4]{1,0:T(1,128)S(1)}, s32[1,4]{1,0:T(1,128)}, u32[]{:S(2)}) copy-start(s32[1,4]{1,0:T(1,128)} %lengths_ref.1) | copy-start | bytes 52
  38.5 10.2 %collective-permute-start.15 = (bf16[128,1024]{1,0:T(8,128)(2,1)S(1)}, bf16[128,1024]{1,0:T(8,128)(2,1)S(1)}, u32[]{:S(2)}, u32[]{:S(2)}) collective-permute-start(bf16[128,1024]{1,0:T(8,128)(2,1)S(1)} %shard_map.108), channel_id=1, source_target_pairs={{0,6},{1,7},{2,4},{3,5},{4,2},{5,3},{6,0},{7,1},{8,14},{9,15},{10,... | collective-permute-start | bytes 786440 | tf_op jit(solution)/shard_map/ppermute | solution.py:168
  43.9 25.5 %copy-start.7 = (s32[2,100]{1,0:T(2,128)S(1)}, s32[2,100]{1,0:T(2,128)}, u32[]{:S(2)}) copy-start(s32[2,100]{1,0:T(2,128)} %cand_ref.1) | copy-start | bytes 2404
  50.4 4.4 %collective-permute-start.17 = (bf16[144,128]{1,0:T(8,128)(2,1)S(1)}, bf16[144,128]{1,0:T(8,128)(2,1)S(1)}, u32[]{:S(2)}, u32[]{:S(2)}) collective-permute-start(bf16[144,128]{1,0:T(8,128)(2,1)S(1)} %get-tuple-element.39.refs_0_), channel_id=1, source_target_pairs={{0,8},{8,0},{16,24},{24,16},{1,9},{9,1},{17,25},{25,17},{2,10},{10... | collective-permute-start | bytes 110600 | tf_op jit(solution)/shard_map/ppermute | solution.py:168
  52.0 5.6 %collective-permute-start.18 = (bf16[144,128]{1,0:T(8,128)(2,1)S(1)}, bf16[144,128]{1,0:T(8,128)(2,1)S(1)}, u32[]{:S(2)}, u32[]{:S(2)}) collective-permute-start(bf16[144,128]{1,0:T(8,128)(2,1)S(1)} %get-tuple-element.39.refs_0_), channel_id=1, source_target_pairs={{0,16},{8,24},{16,0},{24,8},{1,17},{9,25},{17,1},{25,9},{2,18},{10... | collective-permute-start | bytes 110600 | tf_op jit(solution)/shard_map/ppermute | solution.py:168
  54.6 5.8 %collective-permute-start.19 = (bf16[144,128]{1,0:T(8,128)(2,1)S(1)}, bf16[144,128]{1,0:T(8,128)(2,1)S(1)}, u32[]{:S(2)}, u32[]{:S(2)}) collective-permute-start(bf16[144,128]{1,0:T(8,128)(2,1)S(1)} %get-tuple-element.39.refs_0_), channel_id=1, source_target_pairs={{0,24},{8,16},{16,8},{24,0},{1,25},{9,17},{17,9},{25,1},{2,26},{10... | collective-permute-start | bytes 110600 | tf_op jit(solution)/shard_map/ppermute | solution.py:168

commit v8 on v3

--- a/solution.py
+++ b/solution.py
@@ -69,6 +69,11 @@
     out_ref[...] = jnp.dot(hidden, wo_part[...], preferred_element_type=jnp.float32).astype(
         out_ref.dtype
     )
+
+
+def far_order(groups):
+    masks = list(range(1, groups))
+    return masks[2:] + masks[:1] + masks[1:2]
 
 
 def finish_kernel(chips, lengths_ref, tokens_ref, gain_ref, proj_ref, own_ref, *refs):
@@ -91,7 +96,7 @@
         high = low + lengths_ref[0, doc]
         inside.append((spot >= low) & (spot < high))
         low = high
-    for far, block in enumerate(queries):
+    for far, block in zip([0, *far_order(len(queries))], queries):
         for start in range(0, block.shape[0], 128):
             similar = dot_nt(vectors, block[start : start + 128, :])
             best = [
@@ -196,7 +201,7 @@
             compiler_params=params,
         )(norm_gain.reshape(1, -1), *weights, tokens[step])
     arrived = [swap(partial[step], 2 * step) for step in range(1, chips)]
-    queries = [plane] + [swap(plane, mask, "group") for mask in range(1, groups)]
+    queries = [plane] + [swap(plane, mask, "group") for mask in far_order(groups)]
 
     docs = doc_lengths.shape[1]
     vectors, best = pl.pallas_call(

time: 66.9 us -> 63.6 us (0.951)
  blocking collectives: 12.4 us -> 10 us
  waiting for transfers between devices: 22.7 us -> 20.5 us
  starting transfers between devices: 19.3 us -> 20.6 us
    all_to_all x1, blocking collectives: 12.4 us -> 10 us  [body(): lax.all_to_all(best, ('group', 'dev'), split_axis=0, concat_axis=0, tiled...]
    ppermute x17, waiting for transfers between devices: 22.7 us -> 20.5 us  [swap(): return lax.ppermute(values, axis, [(i, i ^ mask) for i in range(size)])]
    ppermute x17, starting transfers between devices: 19.3 us -> 20.6 us  [swap(): return lax.ppermute(values, axis, [(i, i ^ mask) for i in range(size)])]
  transfers between devices with their start and end apart: 17 -> 17, of which waited for: 6 -> 7; matrix products, arithmetic and copies ran while one was open for 0% -> 0% of each run, Pallas kernels for 10% -> 11%
where the time goes in v8:
time: 63.6 us; the launch traced here: 63.3 us
  starting transfers between devices  20.6 us (32%)
  waiting for transfers between devices  20.5 us (32%)
  blocking collectives  10 us (16%)
  Pallas kernels  9.39 us (15%)
  local copies, waits for them, and re-layouts  2.08 us (3%)
  between operations  0.75 us (1%)
    ppermute x17, starting transfers between devices, swap(): return lax.ppermute(values, axis, [(i, i ^ mask) for i in range(size)])  20.6 us
    ppermute x17, waiting for transfers between devices, swap(): return lax.ppermute(values, axis, [(i, i ^ mask) for i in range(size)])  20.5 us
    all_to_all x1, blocking collectives, body(): lax.all_to_all(best, ('group', 'dev'), split_axis=0, concat_axis=0, tiled...  10 us
    pallas_call x4, Pallas kernels, body(): pl.pallas_call(ffn_kernel, out_shape=jax.ShapeDtypeStruct((rows, width),...  5.52 us
    unnamed x18, local copies, waits for them, and re-layouts  2.08 us
    pallas_call x1, Pallas kernels, body(): pl.pallas_call(functools.partial(finish_kernel, chips), out_shape=[jax.Sh...  1.85 us
  transfers between devices with their start and end apart: 17, of which 7 were waited for; matrix products, arithmetic and copies ran while one was open for 0% of the time, Pallas kernels for 11%

profile of v8, /device:TPU:0, one launch (start us, length us, event | category | flops | bytes accessed | tf_op | source)
XLA Modules:
  0.0 63.3 jit_solution(4959121608356965971)
XLA Ops:
  0.6 3.0 %collective-permute-start.2 = (bf16[128,1024]{1,0:T(8,128)(2,1)}, bf16[128,1024]{1,0:T(8,128)(2,1)S(1)}, u32[]{:S(2)}, u32[]{:S(2)}) collective-permute-start(bf16[128,1024]{1,0:T(8,128)(2,1)} %tokens_ref.3), channel_id=1, source_target_pairs={{0,2},{1,3},{2,0},{3,1},{4,6},{5,7},{6,4},{7,5},{8,10},{9,11},{10,... | collective-permute-start | bytes 786440 | tf_op jit(solution)/shard_map/ppermute | solution.py:153
  3.6 1.5 %collective-permute-start.3 = (bf16[128,1024]{1,0:T(8,128)(2,1)}, bf16[128,1024]{1,0:T(8,128)(2,1)S(1)}, u32[]{:S(2)}, u32[]{:S(2)}) collective-permute-start(bf16[128,1024]{1,0:T(8,128)(2,1)} %tokens_ref.3), channel_id=1, source_target_pairs={{0,4},{1,5},{2,6},{3,7},{4,0},{5,1},{6,2},{7,3},{8,12},{9,13},{10,... | collective-permute-start | bytes 786440 | tf_op jit(solution)/shard_map/ppermute | solution.py:153
  5.2 1.3 %copy-done = bf16[128,5248]{1,0:T(8,128)(2,1)S(1)} copy-done((bf16[128,5248]{1,0:T(8,128)(2,1)S(1)}, bf16[128,5248]{1,0:T(8,128)(2,1)}, u32[]{:S(2)}) %copy-start) | copy-done | bytes 1343512
  6.5 0.7 %copy-done.5 = bf16[2,32,128]{2,1,0:T(8,128)(2,1)S(1)} copy-done((bf16[2,32,128]{2,1,0:T(8,128)(2,1)S(1)}, bf16[2,32,128]{2,1,0:T(8,128)(2,1)}, u32[]{:S(2)}) %copy-start.5) | copy-done | bytes 16408
  7.2 0.5 shard_map.104
  7.7 0.6 collective-permute-start.1
  8.3 0.1 collective-permute-start.4
  8.4 2.9 %collective-permute-start.5 = (bf16[1376,128]{1,0:T(8,128)(2,1)S(1)}, bf16[1376,128]{1,0:T(8,128)(2,1)S(1)}, u32[]{:S(2)}, u32[]{:S(2)}) collective-permute-start(bf16[1376,128]{1,0:T(8,128)(2,1)S(1)} %get-tuple-element.19), channel_id=1, source_target_pairs={{0,6},{1,7},{2,4},{3,5},{4,2},{5,3},{6,0},{7,1},{8,14},{9,15},{10,... | collective-permute-start | bytes 1056776 | tf_op jit(solution)/shard_map/ppermute | solution.py:153
  11.3 1.8 %collective-permute-done.3.tokens_ref = bf16[128,1024]{1,0:T(8,128)(2,1)S(1)} collective-permute-done((bf16[128,1024]{1,0:T(8,128)(2,1)}, bf16[128,1024]{1,0:T(8,128)(2,1)S(1)}, u32[]{:S(2)}, u32[]{:S(2)}) %collective-permute-start.3) | collective-permute-done | bytes 262176 | tf_op jit(solution)/shard_map/ppermute | solution.py:153
  13.1 5.9 %collective-permute-done.1.refs_1_ = bf16[1376,128]{1,0:T(8,128)(2,1)S(1)} collective-permute-done((bf16[1376,128]{1,0:T(8,128)(2,1)S(1)}, bf16[1376,128]{1,0:T(8,128)(2,1)S(1)}, u32[]{:S(2)}, u32[]{:S(2)}) %collective-permute-start.1) | collective-permute-done | bytes 352288 | tf_op jit(solution)/shard_map/ppermute | solution.py:153
  18.9 7.8 %collective-permute-done.4.refs_2_ = bf16[1376,128]{1,0:T(8,128)(2,1)S(1)} collective-permute-done((bf16[1376,128]{1,0:T(8,128)(2,1)S(1)}, bf16[1376,128]{1,0:T(8,128)(2,1)S(1)}, u32[]{:S(2)}, u32[]{:S(2)}) %collective-permute-start.4) | collective-permute-done | bytes 352288 | tf_op jit(solution)/shard_map/ppermute | solution.py:153
  26.7 0.5 collective-permute-start.9
  27.2 1.5 %collective-permute-start.10 = (bf16[128,1024]{1,0:T(8,128)(2,1)S(1)}, bf16[128,1024]{1,0:T(8,128)(2,1)S(1)}, u32[]{:S(2)}, u32[]{:S(2)}) collective-permute-start(bf16[128,1024]{1,0:T(8,128)(2,1)S(1)} %copy-done.1), channel_id=1, source_target_pairs={{0,6},{1,7},{2,4},{3,5},{4,2},{5,3},{6,0},{7,1},{8,14},{9,15},{10,... | collective-permute-start | bytes 786440 | tf_op jit(solution)/shard_map/ppermute | solution.py:153
  28.7 0.1 collective-permute-done.9.refs_7_
  28.9 0.9 %shard_map.105 = (bf16[656,1024]{1,0:T(8,128)(2,1)S(1)}, bf16[656,1024]{1,0:T(8,128)(2,1)S(1)}, bf16[656,1024]{1,0:T(8,128)(2,1)S(1)}, bf16[512,128]{1,0:T(8,128)(2,1)S(1)}) custom-call(bf16[328,1024]{1,0:T(8,128)(2,1)S(1)} %copy-done.2, bf16[328,1024]{1,0:T(8,128)(2,1)S(1)} %collective-permute-done.wo_other, ...), custom_call_target="tpu_custom_call" | custom-call | tf_op jit(solution)/shard_map/pallas_call | solution.py:172
  29.8 1.4 %shard_map.109 = bf16[128,1024]{1,0:T(8,128)(2,1)S(1)} custom-call(f32[1,1024]{1,0:T(1,128)S(1)} %bitcast.5, bf16[656,1024]{1,0:T(8,128)(2,1)S(1)} %get-tuple-element.20.gelu_w, bf16[656,1024]{1,0:T(8,128)(2,1)S(1)} %get-tuple-element.21.gate_w, bf16[656,1024]{1,0:T(8,128)(2,1)S(1)} %get-tuple-element.22.wo_part, ...), custom_call_target="tpu_custom_call" | custom-call | tf_op jit(solution)/shard_map/pallas_call | solution.py:196
  31.1 1.4 %collective-permute-start.13 = (bf16[128,1024]{1,0:T(8,128)(2,1)S(1)}, bf16[128,1024]{1,0:T(8,128)(2,1)S(1)}, u32[]{:S(2)}, u32[]{:S(2)}) collective-permute-start(bf16[128,1024]{1,0:T(8,128)(2,1)S(1)} %shard_map.109), channel_id=1, source_target_pairs={{0,2},{1,3},{2,0},{3,1},{4,6},{5,7},{6,4},{7,5},{8,10},{9,11},{10,... | collective-permute-start | bytes 786440 | tf_op jit(solution)/shard_map/ppermute | solution.py:153
  32.6 1.4 %shard_map.108 = bf16[128,1024]{1,0:T(8,128)(2,1)S(1)} custom-call(f32[1,1024]{1,0:T(1,128)S(1)} %bitcast.6, bf16[656,1024]{1,0:T(8,128)(2,1)S(1)} %get-tuple-element.20.gelu_w, bf16[656,1024]{1,0:T(8,128)(2,1)S(1)} %get-tuple-element.21.gate_w, bf16[656,1024]{1,0:T(8,128)(2,1)S(1)} %get-tuple-element.22.wo_part, ...), custom_call_target="tpu_custom_call" | custom-call | tf_op jit(solution)/shard_map/pallas_call | solution.py:196
  34.0 3.7 %collective-permute-start.14 = (bf16[512,128]{1,0:T(8,128)(2,1)S(1)}, bf16[512,128]{1,0:T(8,128)(2,1)S(1)}, u32[]{:S(2)}, u32[]{:S(2)}) collective-permute-start(bf16[512,128]{1,0:T(8,128)(2,1)S(1)} %get-tuple-element.25.refs_3_), channel_id=1, source_target_pairs={{0,24},{8,16},{16,8},{24,0},{1,25},{9,17},{17,9},{25,1},{2,26},{10... | collective-permute-start | bytes 393224 | tf_op jit(solution)/shard_map/ppermute | solution.py:153
  37.6 0.7 %collective-permute-start.12 = (bf16[128,1024]{1,0:T(8,128)(2,1)S(1)}, bf16[128,1024]{1,0:T(8,128)(2,1)S(1)}, u32[]{:S(2)}, u32[]{:S(2)}) collective-permute-start(bf16[128,1024]{1,0:T(8,128)(2,1)S(1)} %shard_map.108), channel_id=1, source_target_pairs={{0,4},{1,5},{2,6},{3,7},{4,0},{5,1},{6,2},{7,3},{8,12},{9,13},{10,... | collective-permute-start | bytes 786440 | tf_op jit(solution)/shard_map/ppermute | solution.py:153
  38.3 1.4 %shard_map.107 = bf16[128,1024]{1,0:T(8,128)(2,1)S(1)} custom-call(f32[1,1024]{1,0:T(1,128)S(1)} %bitcast.7, bf16[656,1024]{1,0:T(8,128)(2,1)S(1)} %get-tuple-element.20.gelu_w, bf16[656,1024]{1,0:T(8,128)(2,1)S(1)} %get-tuple-element.21.gate_w, bf16[656,1024]{1,0:T(8,128)(2,1)S(1)} %get-tuple-element.22.wo_part, ...), custom_call_target="tpu_custom_call" | custom-call | tf_op jit(solution)/shard_map/pallas_call | solution.py:196
  39.7 0.0 copy-start.8
  39.7 1.5 %collective-permute-start.11 = (bf16[128,1024]{1,0:T(8,128)(2,1)S(1)}, bf16[128,1024]{1,0:T(8,128)(2,1)S(1)}, u32[]{:S(2)}, u32[]{:S(2)}) collective-permute-start(bf16[128,1024]{1,0:T(8,128)(2,1)S(1)} %shard_map.107), channel_id=1, source_target_pairs={{0,6},{1,7},{2,4},{3,5},{4,2},{5,3},{6,0},{7,1},{8,14},{9,15},{10,... | collective-permute-start | bytes 786440 | tf_op jit(solution)/shard_map/ppermute | solution.py:153
  41.2 0.6 collective-permute-start.15
  41.9 2.6 %collective-permute-start.16 = (bf16[512,128]{1,0:T(8,128)(2,1)S(1)}, bf16[512,128]{1,0:T(8,128)(2,1)S(1)}, u32[]{:S(2)}, u32[]{:S(2)}) collective-permute-start(bf16[512,128]{1,0:T(8,128)(2,1)S(1)} %get-tuple-element.25.refs_3_), channel_id=1, source_target_pairs={{0,16},{8,24},{16,0},{24,8},{1,17},{9,25},{17,1},{25,9},{2,18},{10... | collective-permute-start | bytes 393224 | tf_op jit(solution)/shard_map/ppermute | solution.py:153
  44.4 1.4 %shard_map.106.own_ref = f32[128,1024]{1,0:T(8,128)S(1)} custom-call(f32[1,1024]{1,0:T(1,128)S(1)} %bitcast.8, bf16[656,1024]{1,0:T(8,128)(2,1)S(1)} %get-tuple-element.20.gelu_w, bf16[656,1024]{1,0:T(8,128)(2,1)S(1)} %get-tuple-element.21.gate_w, bf16[656,1024]{1,0:T(8,128)(2,1)S(1)} %get-tuple-element.22.wo_part, bf16[128,1024]{1,0:T(8,128)(2,1)S(1)} %copy-done.1), custom_call_target="tpu_custom_call" | custom-call | tf_op jit(solution)/shard_map/pallas_call | solution.py:196
  45.8 2.0 %collective-permute-done.15.refs_5_ = bf16[512,128]{1,0:T(8,128)(2,1)S(1)} collective-permute-done((bf16[512,128]{1,0:T(8,128)(2,1)S(1)}, bf16[512,128]{1,0:T(8,128)(2,1)S(1)}, u32[]{:S(2)}, u32[]{:S(2)}) %collective-permute-start.15) | collective-permute-done | bytes 131104 | tf_op jit(solution)/shard_map/ppermute | solution.py:153
  47.8 2.1 %collective-permute-done.16.refs_6_ = bf16[512,128]{1,0:T(8,128)(2,1)S(1)} collective-permute-done((bf16[512,128]{1,0:T(8,128)(2,1)S(1)}, bf16[512,128]{1,0:T(8,128)(2,1)S(1)}, u32[]{:S(2)}, u32[]{:S(2)}) %collective-permute-start.16) | collective-permute-done | bytes 131104 | tf_op jit(solution)/shard_map/ppermute | solution.py:153
  49.9 0.9 %collective-permute-done.12.refs_1_ = bf16[128,1024]{1,0:T(8,128)(2,1)S(1)} collective-permute-done((bf16[128,1024]{1,0:T(8,128)(2,1)S(1)}, bf16[128,1024]{1,0:T(8,128)(2,1)S(1)}, u32[]{:S(2)}, u32[]{:S(2)}) %collective-permute-start.12) | collective-permute-done | bytes 262176 | tf_op jit(solution)/shard_map/ppermute | solution.py:153
  50.7 1.9 %shard_map.110 = (bf16[128,128]{1,0:T(8,128)(2,1)}, bf16[32,4,128]{2,1,0:T(4,128)(2,1)S(1)}) custom-call(s32[1,4]{1,0:T(1,128)S(1)} %copy-done.8, bf16[128,1024]{1,0:T(8,128)(2,1)S(1)} %copy-done.1, f32[1,1024]{1,0:T(1,128)S(1)} %bitcast.10, bf16[1024,128]{1,0:T(8,128)(2,1)S(1)} %copy-done.3, f32[128,1024]{1,0:T(8,128)S(1)} %shard_map.106.own_ref, ...), custom_call_target="tpu_custom_call" | custom-call | tf_op jit(solution)/shard_map/pallas_call | solution.py:207
  52.6 10.0 %all_to_all.5 = bf16[32,4,128]{2,1,0:T(4,128)(2,1)S(1)} all-to-all(bf16[32,4,128]{2,1,0:T(4,128)(2,1)S(1)} %get-tuple-element.27), channel_id=1, replica_groups=mesh['group'=4,'dev'=8] {'group','dev'}, dimensions={0} | all-to-all | bytes 65536 | tf_op jit(solution)/shard_map/all_to_all | solution.py:225
  62.6 0.7 %shard_map.111 = f32[2,100]{1,0:T(2,128)} custom-call(s32[2,100]{1,0:T(2,128)S(1)} %copy-done.7, bf16[4,8,4,128]{3,2,1,0:T(4,128)(2,1)S(1)} %bitcast.4), custom_call_target="tpu_custom_call" | custom-call | tf_op jit(solution)/shard_map/pallas_call | solution.py:226
  (29 shorter events, 0.1 us)
Async XLA Ops:
  0.6 10.6 %collective-permute-start.2 = (bf16[128,1024]{1,0:T(8,128)(2,1)}, bf16[128,1024]{1,0:T(8,128)(2,1)S(1)}, u32[]{:S(2)}, u32[]{:S(2)}) collective-permute-start(bf16[128,1024]{1,0:T(8,128)(2,1)} %tokens_ref.3), channel_id=1, source_target_pairs={{0,2},{1,3},{2,0},{3,1},{4,6},{5,7},{6,4},{7,5},{8,10},{9,11},{10,... | collective-permute-start | bytes 786440 | tf_op jit(solution)/shard_map/ppermute | solution.py:153
  3.6 9.4 %collective-permute-start.3 = (bf16[128,1024]{1,0:T(8,128)(2,1)}, bf16[128,1024]{1,0:T(8,128)(2,1)S(1)}, u32[]{:S(2)}, u32[]{:S(2)}) collective-permute-start(bf16[128,1024]{1,0:T(8,128)(2,1)} %tokens_ref.3), channel_id=1, source_target_pairs={{0,4},{1,5},{2,6},{3,7},{4,0},{5,1},{6,2},{7,3},{8,12},{9,13},{10,... | collective-permute-start | bytes 786440 | tf_op jit(solution)/shard_map/ppermute | solution.py:153
  5.2 1.3 %copy-start = (bf16[128,5248]{1,0:T(8,128)(2,1)S(1)}, bf16[128,5248]{1,0:T(8,128)(2,1)}, u32[]{:S(2)}) copy-start(bf16[128,5248]{1,0:T(8,128)(2,1)} %wi_ref.1) | copy-start | bytes 4030468
  6.5 0.7 %copy-start.5 = (bf16[2,32,128]{2,1,0:T(8,128)(2,1)S(1)}, bf16[2,32,128]{2,1,0:T(8,128)(2,1)}, u32[]{:S(2)}) copy-start(bf16[2,32,128]{2,1,0:T(8,128)(2,1)} %param.15) | copy-start | bytes 49156
  7.2 4.1 %copy-start.2 = (bf16[328,1024]{1,0:T(8,128)(2,1)S(1)}, bf16[328,1024]{1,0:T(8,128)(2,1)}, u32[]{:S(2)}) copy-start(bf16[328,1024]{1,0:T(8,128)(2,1)} %wo_mine.1) | copy-start | bytes 2015236
  7.2 20.0 %copy-start.1 = (bf16[128,1024]{1,0:T(8,128)(2,1)S(1)}, bf16[128,1024]{1,0:T(8,128)(2,1)}, u32[]{:S(2)}) copy-start(bf16[128,1024]{1,0:T(8,128)(2,1)} %tokens_ref.3) | copy-start | bytes 786436
  7.7 11.2 %collective-permute-start.1 = (bf16[1376,128]{1,0:T(8,128)(2,1)S(1)}, bf16[1376,128]{1,0:T(8,128)(2,1)S(1)}, u32[]{:S(2)}, u32[]{:S(2)}) collective-permute-start(bf16[1376,128]{1,0:T(8,128)(2,1)S(1)} %get-tuple-element.16), channel_id=1, source_target_pairs={{0,2},{1,3},{2,0},{3,1},{4,6},{5,7},{6,4},{7,5},{8,10},{9,11},{10,... | collective-permute-start | bytes 1056776 | tf_op jit(solution)/shard_map/ppermute | solution.py:153
  8.3 18.4 %collective-permute-start.4 = (bf16[1376,128]{1,0:T(8,128)(2,1)S(1)}, bf16[1376,128]{1,0:T(8,128)(2,1)S(1)}, u32[]{:S(2)}, u32[]{:S(2)}) collective-permute-start(bf16[1376,128]{1,0:T(8,128)(2,1)S(1)} %get-tuple-element.18), channel_id=1, source_target_pairs={{0,4},{1,5},{2,6},{3,7},{4,0},{5,1},{6,2},{7,3},{8,12},{9,13},{10,... | collective-permute-start | bytes 1056776 | tf_op jit(solution)/shard_map/ppermute | solution.py:153
  8.4 18.4 %collective-permute-start.5 = (bf16[1376,128]{1,0:T(8,128)(2,1)S(1)}, bf16[1376,128]{1,0:T(8,128)(2,1)S(1)}, u32[]{:S(2)}, u32[]{:S(2)}) collective-permute-start(bf16[1376,128]{1,0:T(8,128)(2,1)S(1)} %get-tuple-element.19), channel_id=1, source_target_pairs={{0,6},{1,7},{2,4},{3,5},{4,2},{5,3},{6,0},{7,1},{8,14},{9,15},{10,... | collective-permute-start | bytes 1056776 | tf_op jit(solution)/shard_map/ppermute | solution.py:153
  11.3 17.5 %collective-permute-start = (bf16[328,1024]{1,0:T(8,128)(2,1)S(1)}, bf16[328,1024]{1,0:T(8,128)(2,1)S(1)}, u32[]{:S(2)}, u32[]{:S(2)}) collective-permute-start(bf16[328,1024]{1,0:T(8,128)(2,1)S(1)} %copy-done.2), channel_id=1, source_target_pairs={{0,1},{1,0},{2,3},{3,2},{4,5},{5,4},{6,7},{7,6},{8,9},{9,8},{10,11... | collective-permute-start | bytes 2015240 | tf_op jit(solution)/shard_map/ppermute | solution.py:153
  13.1 16.7 %copy-start.4 = (f32[1024]{0:T(1024)S(1)}, f32[1024]{0:T(1024)}, u32[]{:S(2)}) copy-start(f32[1024]{0:T(1024)} %param.10) | copy-start | bytes 12292
  13.1 14.1 %collective-permute-start.6 = (bf16[1376,128]{1,0:T(8,128)(2,1)S(1)}, bf16[1376,128]{1,0:T(8,128)(2,1)S(1)}, u32[]{:S(2)}, u32[]{:S(2)}) collective-permute-start(bf16[1376,128]{1,0:T(8,128)(2,1)S(1)} %get-tuple-element.15.refs_0_), channel_id=1, source_target_pairs={{0,1},{1,0},{2,3},{3,2},{4,5},{5,4},{6,7},{7,6},{8,9},{9,8},{10,11... | collective-permute-start | bytes 1056776 | tf_op jit(solution)/shard_map/ppermute | solution.py:153
  18.9 9.8 %collective-permute-start.7 = (bf16[1376,128]{1,0:T(8,128)(2,1)S(1)}, bf16[1376,128]{1,0:T(8,128)(2,1)S(1)}, u32[]{:S(2)}, u32[]{:S(2)}) collective-permute-start(bf16[1376,128]{1,0:T(8,128)(2,1)S(1)} %collective-permute-done.1.refs_1_), channel_id=1, source_target_pairs={{0,1},{1,0},{2,3},{3,2},{4,5},{5,4},{6,7},{7,6},{8,9},{9,8},{10,11... | collective-permute-start | bytes 1056776 | tf_op jit(solution)/shard_map/ppermute | solution.py:153
  26.7 2.0 %collective-permute-start.8 = (bf16[1376,128]{1,0:T(8,128)(2,1)S(1)}, bf16[1376,128]{1,0:T(8,128)(2,1)S(1)}, u32[]{:S(2)}, u32[]{:S(2)}) collective-permute-start(bf16[1376,128]{1,0:T(8,128)(2,1)S(1)} %collective-permute-done.4.refs_2_), channel_id=1, source_target_pairs={{0,1},{1,0},{2,3},{3,2},{4,5},{5,4},{6,7},{7,6},{8,9},{9,8},{10,11... | collective-permute-start | bytes 1056776 | tf_op jit(solution)/shard_map/ppermute | solution.py:153
  26.7 2.2 %collective-permute-start.9 = (bf16[1376,128]{1,0:T(8,128)(2,1)S(1)}, bf16[1376,128]{1,0:T(8,128)(2,1)S(1)}, u32[]{:S(2)}, u32[]{:S(2)}) collective-permute-start(bf16[1376,128]{1,0:T(8,128)(2,1)S(1)} %collective-permute-done.5.refs_3_), channel_id=1, source_target_pairs={{0,1},{1,0},{2,3},{3,2},{4,5},{5,4},{6,7},{7,6},{8,9},{9,8},{10,11... | collective-permute-start | bytes 1056776 | tf_op jit(solution)/shard_map/ppermute | solution.py:153
  27.2 11.1 %collective-permute-start.10 = (bf16[128,1024]{1,0:T(8,128)(2,1)S(1)}, bf16[128,1024]{1,0:T(8,128)(2,1)S(1)}, u32[]{:S(2)}, u32[]{:S(2)}) collective-permute-start(bf16[128,1024]{1,0:T(8,128)(2,1)S(1)} %copy-done.1), channel_id=1, source_target_pairs={{0,6},{1,7},{2,4},{3,5},{4,2},{5,3},{6,0},{7,1},{8,14},{9,15},{10,... | collective-permute-start | bytes 786440 | tf_op jit(solution)/shard_map/ppermute | solution.py:153
  31.1 18.7 %collective-permute-start.13 = (bf16[128,1024]{1,0:T(8,128)(2,1)S(1)}, bf16[128,1024]{1,0:T(8,128)(2,1)S(1)}, u32[]{:S(2)}, u32[]{:S(2)}) collective-permute-start(bf16[128,1024]{1,0:T(8,128)(2,1)S(1)} %shard_map.109), channel_id=1, source_target_pairs={{0,2},{1,3},{2,0},{3,1},{4,6},{5,7},{6,4},{7,5},{8,10},{9,11},{10,... | collective-permute-start | bytes 786440 | tf_op jit(solution)/shard_map/ppermute | solution.py:153
  34.0 7.9 %collective-permute-start.14 = (bf16[512,128]{1,0:T(8,128)(2,1)S(1)}, bf16[512,128]{1,0:T(8,128)(2,1)S(1)}, u32[]{:S(2)}, u32[]{:S(2)}) collective-permute-start(bf16[512,128]{1,0:T(8,128)(2,1)S(1)} %get-tuple-element.25.refs_3_), channel_id=1, source_target_pairs={{0,24},{8,16},{16,8},{24,0},{1,25},{9,17},{17,9},{25,1},{2,26},{10... | collective-permute-start | bytes 393224 | tf_op jit(solution)/shard_map/ppermute | solution.py:153
  37.6 13.1 %collective-permute-start.12 = (bf16[128,1024]{1,0:T(8,128)(2,1)S(1)}, bf16[128,1024]{1,0:T(8,128)(2,1)S(1)}, u32[]{:S(2)}, u32[]{:S(2)}) collective-permute-start(bf16[128,1024]{1,0:T(8,128)(2,1)S(1)} %shard_map.108), channel_id=1, source_target_pairs={{0,4},{1,5},{2,6},{3,7},{4,0},{5,1},{6,2},{7,3},{8,12},{9,13},{10,... | collective-permute-start | bytes 786440 | tf_op jit(solution)/shard_map/ppermute | solution.py:153
  39.7 11.0 %copy-start.3 = (bf16[1024,128]{1,0:T(8,128)(2,1)S(1)}, bf16[1024,128]{1,0:T(8,128)(2,1)}, u32[]{:S(2)}) copy-start(bf16[1024,128]{1,0:T(8,128)(2,1)} %proj_ref.1) | copy-start | bytes 786436
  39.7 11.0 %copy-start.6 = (f32[1024]{0:T(1024)S(1)}, f32[1024]{0:T(1024)}, u32[]{:S(2)}) copy-start(f32[1024]{0:T(1024)} %param.13) | copy-start | bytes 12292
  39.7 11.0 %copy-start.8 = (s32[1,4]{1,0:T(1,128)S(1)}, s32[1,4]{1,0:T(1,128)}, u32[]{:S(2)}) copy-start(s32[1,4]{1,0:T(1,128)} %lengths_ref.1) | copy-start | bytes 52
  39.7 11.0 %collective-permute-start.11 = (bf16[128,1024]{1,0:T(8,128)(2,1)S(1)}, bf16[128,1024]{1,0:T(8,128)(2,1)S(1)}, u32[]{:S(2)}, u32[]{:S(2)}) collective-permute-start(bf16[128,1024]{1,0:T(8,128)(2,1)S(1)} %shard_map.107), channel_id=1, source_target_pairs={{0,6},{1,7},{2,4},{3,5},{4,2},{5,3},{6,0},{7,1},{8,14},{9,15},{10,... | collective-permute-start | bytes 786440 | tf_op jit(solution)/shard_map/ppermute | solution.py:153
  41.2 6.6 %collective-permute-start.15 = (bf16[512,128]{1,0:T(8,128)(2,1)S(1)}, bf16[512,128]{1,0:T(8,128)(2,1)S(1)}, u32[]{:S(2)}, u32[]{:S(2)}) collective-permute-start(bf16[512,128]{1,0:T(8,128)(2,1)S(1)} %get-tuple-element.25.refs_3_), channel_id=1, source_target_pairs={{0,8},{8,0},{16,24},{24,16},{1,9},{9,1},{17,25},{25,17},{2,10},{10... | collective-permute-start | bytes 393224 | tf_op jit(solution)/shard_map/ppermute | solution.py:153
  41.9 8.0 %collective-permute-start.16 = (bf16[512,128]{1,0:T(8,128)(2,1)S(1)}, bf16[512,128]{1,0:T(8,128)(2,1)S(1)}, u32[]{:S(2)}, u32[]{:S(2)}) collective-permute-start(bf16[512,128]{1,0:T(8,128)(2,1)S(1)} %get-tuple-element.25.refs_3_), channel_id=1, source_target_pairs={{0,16},{8,24},{16,0},{24,8},{1,17},{9,25},{17,1},{25,9},{2,18},{10... | collective-permute-start | bytes 393224 | tf_op jit(solution)/shard_map/ppermute | solution.py:153
  45.8 16.8 %copy-start.7 = (s32[2,100]{1,0:T(2,128)S(1)}, s32[2,100]{1,0:T(2,128)}, u32[]{:S(2)}) copy-start(s32[2,100]{1,0:T(2,128)} %cand_ref.1) | copy-start | bytes 2404

commit v9 on v5

--- a/solution.py
+++ b/solution.py
@@ -72,15 +72,19 @@
             queries[pl.ds(pl.multiple_of(at * own, own), own), :] = blocks[step][last : last + own]
 
 
-def ffn_kernel(gain_ref, gelu_w, gate_w, wo_part, *refs):
-    tokens, out_ref = jnp.concatenate([ref[...] for ref in refs[:-1]], axis=0), refs[-1]
-    normed = norm_rows(tokens.astype(jnp.float32), gain_ref[...])
+def ffn_kernel(gain_ref, gelu_w, gate_w, wo_part, tokens_ref, out_ref):
+    normed = norm_rows(tokens_ref[...].astype(jnp.float32), gain_ref[...])
     first = dot_nt(normed, gelu_w[...])
     second = dot_nt(normed, gate_w[...])
     hidden = (0.5 * first * (1.0 + lax.erf(first * 0.7071067811865476)) * second).astype(jnp.bfloat16)
     out_ref[...] = jnp.dot(hidden, wo_part[...], preferred_element_type=jnp.float32).astype(
         out_ref.dtype
     )
+
+
+def far_order(groups):
+    masks = list(range(1, groups))
+    return masks[2:] + masks[:1] + masks[1:2]
 
 
 def finish_kernel(chips, lengths_ref, tokens_ref, gain_ref, proj_ref, own_ref, *refs):
@@ -103,7 +107,7 @@
         high = low + lengths_ref[0, doc]
         inside.append((spot >= low) & (spot < high))
         low = high
-    for far, block in enumerate(queries):
+    for far, block in zip([0, *far_order(len(queries))], queries):
         for start in range(0, block.shape[0], 128):
             similar = dot_nt(vectors, block[start : start + 128, :])
             best = [
@@ -162,7 +166,7 @@
     per_query, query_len, vector_dim = query_vectors.shape
     query_own = query_vectors.reshape(-1, vector_dim)
     wo_other = swap(wo_weight, 1)
-    near = [corpus_tokens] + [swap(corpus_tokens, 2 * step) for step in (1, 2)]
+    tokens = [corpus_tokens] + [swap(corpus_tokens, 2 * step) for step in range(1, chips)]
     if wi_weight.shape[0] == 128 and part % 16 == 0 and chips == 4 and groups % 2 == 0:
         own = query_own.shape[0]
         pieces = pl.pallas_call(
@@ -178,9 +182,9 @@
         )(wi_weight, query_own)
         mine = [pieces[0]] + [swap(pieces[step], 2 * step) for step in range(1, chips)]
         mine.append(swap(mine[3], 1, "group"))
-        mine[1], near[1], near[2] = lax.optimization_barrier((mine[1], near[1], near[2]))
-        far = [swap(near[2][: rows // 2], 2), swap(near[1][rows // 2 :], 4)]
-        tokens = [[each] for each in near] + [far]
+        mine[1], mine[4], tokens[1], tokens[2] = lax.optimization_barrier(
+            (mine[1], mine[4], tokens[1], tokens[2])
+        )
         other = [swap(piece, 1) for piece in mine]
         *weights, plane = pl.pallas_call(
             functools.partial(join_kernel, chips),
@@ -203,23 +207,18 @@
             [jnp.where(even, wo_weight, wo_other), jnp.where(even, wo_other, wo_weight)], axis=0
         )
         weights = [columns[:, 0].T, columns[:, 1].T, wo_part]
-        tokens = [[each] for each in near]
-        tokens += [[swap(corpus_tokens, 2 * step)] for step in range(3, chips)]
         plane = lax.all_gather(query_own, "dev", axis=0, tiled=True)
-    partial, arrived = [None] * chips, [None] * chips
+    partial = [None] * chips
     for step in list(range(1, chips)) + [0]:
-        if step == 0:
-            arrived[1], tokens[0][0] = lax.optimization_barrier((arrived[1], tokens[0][0]))
         partial[step] = pl.pallas_call(
             ffn_kernel,
             out_shape=jax.ShapeDtypeStruct((rows, width), jnp.bfloat16 if step else jnp.float32),
-            in_specs=[vmem] * (4 + len(tokens[step])),
+            in_specs=[vmem] * 5,
             out_specs=vmem,
             compiler_params=params,
-        )(norm_gain.reshape(1, -1), *weights, *tokens[step])
-        if step:
-            arrived[step] = swap(partial[step], 2 * step)
-    queries = [plane] + [swap(plane, mask, "group") for mask in range(1, groups)]
+        )(norm_gain.reshape(1, -1), *weights, tokens[step])
+    arrived = [swap(partial[step], 2 * step) for step in range(1, chips)]
+    queries = [plane] + [swap(plane, mask, "group") for mask in far_order(groups)]
 
     docs = doc_lengths.shape[1]
     vectors, best = pl.pallas_call(
@@ -237,7 +236,7 @@
         final_gain.reshape(1, -1),
         proj_weight,
         partial[0],
-        *arrived[:0:-1],
+        *arrived[::-1],
         *queries,
     )
     met = lax.all_to_all(best, ("group", "dev"), split_axis=0, concat_axis=0, tiled=True)

time: 72.7 us -> 64.7 us (0.89)
  waiting for transfers between devices: 25.6 us -> 19.8 us
  starting transfers between devices: 23.6 us -> 22.2 us
    ppermute x20 -> x19, waiting for transfers between devices: 25.6 us -> 19.8 us  [swap(): return lax.ppermute(values, axis, [(i, i ^ mask) for i in range(size)])]
    ppermute x20 -> x19, starting transfers between devices: 23.6 us -> 22.2 us  [swap(): return lax.ppermute(values, axis, [(i, i ^ mask) for i in range(size)])]
  transfers between devices with their start and end apart: 20 -> 19, of which waited for: 6 -> 7; matrix products, arithmetic and copies ran while one was open for 0% -> 0% of each run, Pallas kernels for 9% -> 11%
where the time goes in v9:
time: 64.7 us; the launch traced here: 64.5 us
  starting transfers between devices  22.2 us (34%)
  waiting for transfers between devices  19.8 us (31%)
  blocking collectives  10.3 us (16%)
  Pallas kernels  9.39 us (15%)
  local copies, waits for them, and re-layouts  2.08 us (3%)
  between operations  0.76 us (1%)
    ppermute x19, starting transfers between devices, swap(): return lax.ppermute(values, axis, [(i, i ^ mask) for i in range(size)])  22.2 us
    ppermute x19, waiting for transfers between devices, swap(): return lax.ppermute(values, axis, [(i, i ^ mask) for i in range(size)])  19.8 us
    all_to_all x1, blocking collectives, body(): lax.all_to_all(best, ('group', 'dev'), split_axis=0, concat_axis=0, tiled...  10.3 us
    pallas_call x4, Pallas kernels, body(): pl.pallas_call(ffn_kernel, out_shape=jax.ShapeDtypeStruct((rows, width),...  5.51 us
    unnamed x18, local copies, waits for them, and re-layouts  2.08 us
    pallas_call x1, Pallas kernels, body(): pl.pallas_call(functools.partial(finish_kernel, chips), out_shape=[jax.Sh...  1.85 us
  transfers between devices with their start and end apart: 19, of which 7 were waited for; matrix products, arithmetic and copies ran while one was open for 0% of the time, Pallas kernels for 11%

profile of v9, /device:TPU:0, one launch (start us, length us, event | category | flops | bytes accessed | tf_op | source)
XLA Modules:
  0.0 64.5 jit_solution(15349249177925312200)
XLA Ops:
  0.6 3.0 %collective-permute-start.4 = (bf16[128,1024]{1,0:T(8,128)(2,1)}, bf16[128,1024]{1,0:T(8,128)(2,1)S(1)}, u32[]{:S(2)}, u32[]{:S(2)}) collective-permute-start(bf16[128,1024]{1,0:T(8,128)(2,1)} %tokens_ref.3), channel_id=1, source_target_pairs={{0,2},{1,3},{2,0},{3,1},{4,6},{5,7},{6,4},{7,5},{8,10},{9,11},{10,... | collective-permute-start | bytes 786440 | tf_op jit(solution)/shard_map/ppermute | solution.py:164
  3.6 1.3 %copy-done = bf16[128,5248]{1,0:T(8,128)(2,1)S(1)} copy-done((bf16[128,5248]{1,0:T(8,128)(2,1)S(1)}, bf16[128,5248]{1,0:T(8,128)(2,1)}, u32[]{:S(2)}) %copy-start) | copy-done | bytes 1343512
  5.0 0.7 %copy-done.5 = bf16[2,32,128]{2,1,0:T(8,128)(2,1)S(1)} copy-done((bf16[2,32,128]{2,1,0:T(8,128)(2,1)S(1)}, bf16[2,32,128]{2,1,0:T(8,128)(2,1)}, u32[]{:S(2)}) %copy-start.5) | copy-done | bytes 16408
  5.7 0.5 shard_map.104
  6.2 1.6 %collective-permute-start.2 = (bf16[720,128]{1,0:T(8,128)(2,1)S(1)}, bf16[720,128]{1,0:T(8,128)(2,1)S(1)}, u32[]{:S(2)}, u32[]{:S(2)}) collective-permute-start(bf16[720,128]{1,0:T(8,128)(2,1)S(1)} %get-tuple-element.18), channel_id=1, source_target_pairs={{0,6},{1,7},{2,4},{3,5},{4,2},{5,3},{6,0},{7,1},{8,14},{9,15},{10,... | collective-permute-start | bytes 552968 | tf_op jit(solution)/shard_map/ppermute | solution.py:164
  7.7 0.4 collective-permute-start.5
  8.2 1.6 %collective-permute-start.1 = (bf16[1376,128]{1,0:T(8,128)(2,1)S(1)}, bf16[1376,128]{1,0:T(8,128)(2,1)S(1)}, u32[]{:S(2)}, u32[]{:S(2)}) collective-permute-start(bf16[1376,128]{1,0:T(8,128)(2,1)S(1)} %get-tuple-element.17), channel_id=1, source_target_pairs={{0,2},{1,3},{2,0},{3,1},{4,6},{5,7},{6,4},{7,5},{8,10},{9,11},{10,... | collective-permute-start | bytes 1056776 | tf_op jit(solution)/shard_map/ppermute | solution.py:164
  9.7 1.5 %collective-permute-start.6 = (bf16[1376,128]{1,0:T(8,128)(2,1)S(1)}, bf16[1376,128]{1,0:T(8,128)(2,1)S(1)}, u32[]{:S(2)}, u32[]{:S(2)}) collective-permute-start(bf16[1376,128]{1,0:T(8,128)(2,1)S(1)} %get-tuple-element.20), channel_id=1, source_target_pairs={{0,4},{1,5},{2,6},{3,7},{4,0},{5,1},{6,2},{7,3},{8,12},{9,13},{10,... | collective-permute-start | bytes 1056776 | tf_op jit(solution)/shard_map/ppermute | solution.py:164
  11.3 5.2 %collective-permute-done.2.refs_3_ = bf16[720,128]{1,0:T(8,128)(2,1)S(1)} collective-permute-done((bf16[720,128]{1,0:T(8,128)(2,1)S(1)}, bf16[720,128]{1,0:T(8,128)(2,1)S(1)}, u32[]{:S(2)}, u32[]{:S(2)}) %collective-permute-start.2) | collective-permute-done | bytes 184352 | tf_op jit(solution)/shard_map/ppermute | solution.py:164
  16.5 0.5 collective-permute-start.7
  17.0 3.4 %collective-permute-done.5.tokens_ref = bf16[128,1024]{1,0:T(8,128)(2,1)S(1)} collective-permute-done((bf16[128,1024]{1,0:T(8,128)(2,1)S(1)}, bf16[128,1024]{1,0:T(8,128)(2,1)S(1)}, u32[]{:S(2)}, u32[]{:S(2)}) %collective-permute-start.5) | collective-permute-done | bytes 262176 | tf_op jit(solution)/shard_map/ppermute | solution.py:164
  20.4 1.6 %collective-permute-start.3 = (bf16[720,128]{1,0:T(8,128)(2,1)S(1)}, bf16[720,128]{1,0:T(8,128)(2,1)S(1)}, u32[]{:S(2)}, u32[]{:S(2)}) collective-permute-start(bf16[720,128]{1,0:T(8,128)(2,1)S(1)} %collective-permute-done.2.refs_3_), channel_id=1, source_target_pairs={{0,8},{8,0},{16,24},{24,16},{1,9},{9,1},{17,25},{25,17},{2,10},{10... | collective-permute-start | bytes 552968 | tf_op jit(solution)/shard_map/ppermute | solution.py:164
  22.0 4.8 %collective-permute-done.6.refs_2_ = bf16[1376,128]{1,0:T(8,128)(2,1)S(1)} collective-permute-done((bf16[1376,128]{1,0:T(8,128)(2,1)S(1)}, bf16[1376,128]{1,0:T(8,128)(2,1)S(1)}, u32[]{:S(2)}, u32[]{:S(2)}) %collective-permute-start.6) | collective-permute-done | bytes 352288 | tf_op jit(solution)/shard_map/ppermute | solution.py:164
  26.7 0.5 collective-permute-start.8
  27.2 1.4 %collective-permute-start.12 = (bf16[128,1024]{1,0:T(8,128)(2,1)S(1)}, bf16[128,1024]{1,0:T(8,128)(2,1)S(1)}, u32[]{:S(2)}, u32[]{:S(2)}) collective-permute-start(bf16[128,1024]{1,0:T(8,128)(2,1)S(1)} %copy-done.1), channel_id=1, source_target_pairs={{0,6},{1,7},{2,4},{3,5},{4,2},{5,3},{6,0},{7,1},{8,14},{9,15},{10,... | collective-permute-start | bytes 786440 | tf_op jit(solution)/shard_map/ppermute | solution.py:164
  28.7 1.4 %collective-permute-done.11.refs_9_ = bf16[720,128]{1,0:T(8,128)(2,1)S(1)} collective-permute-done((bf16[720,128]{1,0:T(8,128)(2,1)S(1)}, bf16[720,128]{1,0:T(8,128)(2,1)S(1)}, u32[]{:S(2)}, u32[]{:S(2)}) %collective-permute-start.11) | collective-permute-done | bytes 184352 | tf_op jit(solution)/shard_map/ppermute | solution.py:164
  30.1 0.9 %shard_map.105 = (bf16[656,1024]{1,0:T(8,128)(2,1)S(1)}, bf16[656,1024]{1,0:T(8,128)(2,1)S(1)}, bf16[656,1024]{1,0:T(8,128)(2,1)S(1)}, bf16[512,128]{1,0:T(8,128)(2,1)S(1)}) custom-call(bf16[328,1024]{1,0:T(8,128)(2,1)S(1)} %copy-done.2, bf16[328,1024]{1,0:T(8,128)(2,1)S(1)} %collective-permute-done.wo_other, ...), custom_call_target="tpu_custom_call" | custom-call | tf_op jit(solution)/shard_map/pallas_call | solution.py:189
  31.0 1.4 %shard_map.109 = bf16[128,1024]{1,0:T(8,128)(2,1)S(1)} custom-call(f32[1,1024]{1,0:T(1,128)S(1)} %bitcast.5, bf16[656,1024]{1,0:T(8,128)(2,1)S(1)} %get-tuple-element.22.gelu_w, bf16[656,1024]{1,0:T(8,128)(2,1)S(1)} %get-tuple-element.23.gate_w, bf16[656,1024]{1,0:T(8,128)(2,1)S(1)} %get-tuple-element.24.wo_part, ...), custom_call_target="tpu_custom_call" | custom-call | tf_op jit(solution)/shard_map/pallas_call | solution.py:213
  32.4 0.8 %collective-permute-start.15 = (bf16[128,1024]{1,0:T(8,128)(2,1)S(1)}, bf16[128,1024]{1,0:T(8,128)(2,1)S(1)}, u32[]{:S(2)}, u32[]{:S(2)}) collective-permute-start(bf16[128,1024]{1,0:T(8,128)(2,1)S(1)} %shard_map.109), channel_id=1, source_target_pairs={{0,2},{1,3},{2,0},{3,1},{4,6},{5,7},{6,4},{7,5},{8,10},{9,11},{10,... | collective-permute-start | bytes 786440 | tf_op jit(solution)/shard_map/ppermute | solution.py:164
  33.2 1.4 %shard_map.108 = bf16[128,1024]{1,0:T(8,128)(2,1)S(1)} custom-call(f32[1,1024]{1,0:T(1,128)S(1)} %bitcast.6, bf16[656,1024]{1,0:T(8,128)(2,1)S(1)} %get-tuple-element.22.gelu_w, bf16[656,1024]{1,0:T(8,128)(2,1)S(1)} %get-tuple-element.23.gate_w, bf16[656,1024]{1,0:T(8,128)(2,1)S(1)} %get-tuple-element.24.wo_part, ...), custom_call_target="tpu_custom_call" | custom-call | tf_op jit(solution)/shard_map/pallas_call | solution.py:213
  34.6 3.7 %collective-permute-start.16 = (bf16[512,128]{1,0:T(8,128)(2,1)S(1)}, bf16[512,128]{1,0:T(8,128)(2,1)S(1)}, u32[]{:S(2)}, u32[]{:S(2)}) collective-permute-start(bf16[512,128]{1,0:T(8,128)(2,1)S(1)} %get-tuple-element.27.refs_3_), channel_id=1, source_target_pairs={{0,24},{8,16},{16,8},{24,0},{1,25},{9,17},{17,9},{25,1},{2,26},{10... | collective-permute-start | bytes 393224 | tf_op jit(solution)/shard_map/ppermute | solution.py:164
  38.2 1.3 %collective-permute-start.14 = (bf16[128,1024]{1,0:T(8,128)(2,1)S(1)}, bf16[128,1024]{1,0:T(8,128)(2,1)S(1)}, u32[]{:S(2)}, u32[]{:S(2)}) collective-permute-start(bf16[128,1024]{1,0:T(8,128)(2,1)S(1)} %shard_map.108), channel_id=1, source_target_pairs={{0,4},{1,5},{2,6},{3,7},{4,0},{5,1},{6,2},{7,3},{8,12},{9,13},{10,... | collective-permute-start | bytes 786440 | tf_op jit(solution)/shard_map/ppermute | solution.py:164
  39.6 1.4 %shard_map.107 = bf16[128,1024]{1,0:T(8,128)(2,1)S(1)} custom-call(f32[1,1024]{1,0:T(1,128)S(1)} %bitcast.7, bf16[656,1024]{1,0:T(8,128)(2,1)S(1)} %get-tuple-element.22.gelu_w, bf16[656,1024]{1,0:T(8,128)(2,1)S(1)} %get-tuple-element.23.gate_w, bf16[656,1024]{1,0:T(8,128)(2,1)S(1)} %get-tuple-element.24.wo_part, ...), custom_call_target="tpu_custom_call" | custom-call | tf_op jit(solution)/shard_map/pallas_call | solution.py:213
  41.0 1.5 %collective-permute-start.13 = (bf16[128,1024]{1,0:T(8,128)(2,1)S(1)}, bf16[128,1024]{1,0:T(8,128)(2,1)S(1)}, u32[]{:S(2)}, u32[]{:S(2)}) collective-permute-start(bf16[128,1024]{1,0:T(8,128)(2,1)S(1)} %shard_map.107), channel_id=1, source_target_pairs={{0,6},{1,7},{2,4},{3,5},{4,2},{5,3},{6,0},{7,1},{8,14},{9,15},{10,... | collective-permute-start | bytes 786440 | tf_op jit(solution)/shard_map/ppermute | solution.py:164
  42.5 2.8 %collective-permute-start.18 = (bf16[512,128]{1,0:T(8,128)(2,1)S(1)}, bf16[512,128]{1,0:T(8,128)(2,1)S(1)}, u32[]{:S(2)}, u32[]{:S(2)}) collective-permute-start(bf16[512,128]{1,0:T(8,128)(2,1)S(1)} %get-tuple-element.27.refs_3_), channel_id=1, source_target_pairs={{0,16},{8,24},{16,0},{24,8},{1,17},{9,25},{17,1},{25,9},{2,18},{10... | collective-permute-start | bytes 393224 | tf_op jit(solution)/shard_map/ppermute | solution.py:164
  45.3 1.4 %shard_map.106.own_ref = f32[128,1024]{1,0:T(8,128)S(1)} custom-call(f32[1,1024]{1,0:T(1,128)S(1)} %bitcast.8, bf16[656,1024]{1,0:T(8,128)(2,1)S(1)} %get-tuple-element.22.gelu_w, bf16[656,1024]{1,0:T(8,128)(2,1)S(1)} %get-tuple-element.23.gate_w, bf16[656,1024]{1,0:T(8,128)(2,1)S(1)} %get-tuple-element.24.wo_part, bf16[128,1024]{1,0:T(8,128)(2,1)S(1)} %copy-done.1), custom_call_target="tpu_custom_call" | custom-call | tf_op jit(solution)/shard_map/pallas_call | solution.py:213
  46.7 2.2 %collective-permute-done.17.refs_5_ = bf16[512,128]{1,0:T(8,128)(2,1)S(1)} collective-permute-done((bf16[512,128]{1,0:T(8,128)(2,1)S(1)}, bf16[512,128]{1,0:T(8,128)(2,1)S(1)}, u32[]{:S(2)}, u32[]{:S(2)}) %collective-permute-start.17) | collective-permute-done | bytes 131104 | tf_op jit(solution)/shard_map/ppermute | solution.py:164
  48.9 2.0 %collective-permute-done.18.refs_6_ = bf16[512,128]{1,0:T(8,128)(2,1)S(1)} collective-permute-done((bf16[512,128]{1,0:T(8,128)(2,1)S(1)}, bf16[512,128]{1,0:T(8,128)(2,1)S(1)}, u32[]{:S(2)}, u32[]{:S(2)}) %collective-permute-start.18) | collective-permute-done | bytes 131104 | tf_op jit(solution)/shard_map/ppermute | solution.py:164
  50.9 0.8 %collective-permute-done.14.refs_1_ = bf16[128,1024]{1,0:T(8,128)(2,1)S(1)} collective-permute-done((bf16[128,1024]{1,0:T(8,128)(2,1)S(1)}, bf16[128,1024]{1,0:T(8,128)(2,1)S(1)}, u32[]{:S(2)}, u32[]{:S(2)}) %collective-permute-start.14) | collective-permute-done | bytes 262176 | tf_op jit(solution)/shard_map/ppermute | solution.py:164
  51.7 1.9 %shard_map.110 = (bf16[128,128]{1,0:T(8,128)(2,1)}, bf16[32,4,128]{2,1,0:T(4,128)(2,1)S(1)}) custom-call(s32[1,4]{1,0:T(1,128)S(1)} %copy-done.8, bf16[128,1024]{1,0:T(8,128)(2,1)S(1)} %copy-done.1, f32[1,1024]{1,0:T(1,128)S(1)} %bitcast.10, bf16[1024,128]{1,0:T(8,128)(2,1)S(1)} %copy-done.3, f32[128,1024]{1,0:T(8,128)S(1)} %shard_map.106.own_ref, ...), custom_call_target="tpu_custom_call" | custom-call | tf_op jit(solution)/shard_map/pallas_call | solution.py:224
  53.5 10.3 %all_to_all.5 = bf16[32,4,128]{2,1,0:T(4,128)(2,1)S(1)} all-to-all(bf16[32,4,128]{2,1,0:T(4,128)(2,1)S(1)} %get-tuple-element.29), channel_id=1, replica_groups=mesh['group'=4,'dev'=8] {'group','dev'}, dimensions={0} | all-to-all | bytes 65536 | tf_op jit(solution)/shard_map/all_to_all | solution.py:242
  63.8 0.7 %shard_map.111 = f32[2,100]{1,0:T(2,128)} custom-call(s32[2,100]{1,0:T(2,128)S(1)} %copy-done.7, bf16[4,8,4,128]{3,2,1,0:T(4,128)(2,1)S(1)} %bitcast.4), custom_call_target="tpu_custom_call" | custom-call | tf_op jit(solution)/shard_map/pallas_call | solution.py:243
  (33 shorter events, 0.1 us)
Async XLA Ops:
  0.6 15.9 %collective-permute-start.4 = (bf16[128,1024]{1,0:T(8,128)(2,1)}, bf16[128,1024]{1,0:T(8,128)(2,1)S(1)}, u32[]{:S(2)}, u32[]{:S(2)}) collective-permute-start(bf16[128,1024]{1,0:T(8,128)(2,1)} %tokens_ref.3), channel_id=1, source_target_pairs={{0,2},{1,3},{2,0},{3,1},{4,6},{5,7},{6,4},{7,5},{8,10},{9,11},{10,... | collective-permute-start | bytes 786440 | tf_op jit(solution)/shard_map/ppermute | solution.py:164
  3.6 1.3 %copy-start = (bf16[128,5248]{1,0:T(8,128)(2,1)S(1)}, bf16[128,5248]{1,0:T(8,128)(2,1)}, u32[]{:S(2)}) copy-start(bf16[128,5248]{1,0:T(8,128)(2,1)} %wi_ref.1) | copy-start | bytes 4030468
  5.0 0.7 %copy-start.5 = (bf16[2,32,128]{2,1,0:T(8,128)(2,1)S(1)}, bf16[2,32,128]{2,1,0:T(8,128)(2,1)}, u32[]{:S(2)}) copy-start(bf16[2,32,128]{2,1,0:T(8,128)(2,1)} %param.15) | copy-start | bytes 49156
  5.7 2.1 %copy-start.1 = (bf16[128,1024]{1,0:T(8,128)(2,1)S(1)}, bf16[128,1024]{1,0:T(8,128)(2,1)}, u32[]{:S(2)}) copy-start(bf16[128,1024]{1,0:T(8,128)(2,1)} %tokens_ref.3) | copy-start | bytes 786436
  5.7 10.8 %copy-start.2 = (bf16[328,1024]{1,0:T(8,128)(2,1)S(1)}, bf16[328,1024]{1,0:T(8,128)(2,1)}, u32[]{:S(2)}) copy-start(bf16[328,1024]{1,0:T(8,128)(2,1)} %wo_mine.1) | copy-start | bytes 2015236
  6.2 10.3 %collective-permute-start.2 = (bf16[720,128]{1,0:T(8,128)(2,1)S(1)}, bf16[720,128]{1,0:T(8,128)(2,1)S(1)}, u32[]{:S(2)}, u32[]{:S(2)}) collective-permute-start(bf16[720,128]{1,0:T(8,128)(2,1)S(1)} %get-tuple-element.18), channel_id=1, source_target_pairs={{0,6},{1,7},{2,4},{3,5},{4,2},{5,3},{6,0},{7,1},{8,14},{9,15},{10,... | collective-permute-start | bytes 552968 | tf_op jit(solution)/shard_map/ppermute | solution.py:164
  7.7 12.6 %collective-permute-start.5 = (bf16[128,1024]{1,0:T(8,128)(2,1)S(1)}, bf16[128,1024]{1,0:T(8,128)(2,1)S(1)}, u32[]{:S(2)}, u32[]{:S(2)}) collective-permute-start(bf16[128,1024]{1,0:T(8,128)(2,1)S(1)} %copy-done.1), channel_id=1, source_target_pairs={{0,4},{1,5},{2,6},{3,7},{4,0},{5,1},{6,2},{7,3},{8,12},{9,13},{10,... | collective-permute-start | bytes 786440 | tf_op jit(solution)/shard_map/ppermute | solution.py:164
  8.2 13.8 %collective-permute-start.1 = (bf16[1376,128]{1,0:T(8,128)(2,1)S(1)}, bf16[1376,128]{1,0:T(8,128)(2,1)S(1)}, u32[]{:S(2)}, u32[]{:S(2)}) collective-permute-start(bf16[1376,128]{1,0:T(8,128)(2,1)S(1)} %get-tuple-element.17), channel_id=1, source_target_pairs={{0,2},{1,3},{2,0},{3,1},{4,6},{5,7},{6,4},{7,5},{8,10},{9,11},{10,... | collective-permute-start | bytes 1056776 | tf_op jit(solution)/shard_map/ppermute | solution.py:164
  9.7 17.0 %collective-permute-start.6 = (bf16[1376,128]{1,0:T(8,128)(2,1)S(1)}, bf16[1376,128]{1,0:T(8,128)(2,1)S(1)}, u32[]{:S(2)}, u32[]{:S(2)}) collective-permute-start(bf16[1376,128]{1,0:T(8,128)(2,1)S(1)} %get-tuple-element.20), channel_id=1, source_target_pairs={{0,4},{1,5},{2,6},{3,7},{4,0},{5,1},{6,2},{7,3},{8,12},{9,13},{10,... | collective-permute-start | bytes 1056776 | tf_op jit(solution)/shard_map/ppermute | solution.py:164
  16.5 13.6 %collective-permute-start = (bf16[328,1024]{1,0:T(8,128)(2,1)S(1)}, bf16[328,1024]{1,0:T(8,128)(2,1)S(1)}, u32[]{:S(2)}, u32[]{:S(2)}) collective-permute-start(bf16[328,1024]{1,0:T(8,128)(2,1)S(1)} %copy-done.2), channel_id=1, source_target_pairs={{0,1},{1,0},{2,3},{3,2},{4,5},{5,4},{6,7},{7,6},{8,9},{9,8},{10,11... | collective-permute-start | bytes 2015240 | tf_op jit(solution)/shard_map/ppermute | solution.py:164
  16.5 14.5 %copy-start.4 = (f32[1024]{0:T(1024)S(1)}, f32[1024]{0:T(1024)}, u32[]{:S(2)}) copy-start(f32[1024]{0:T(1024)} %param.10) | copy-start | bytes 12292
  16.5 10.7 %collective-permute-start.7 = (bf16[1376,128]{1,0:T(8,128)(2,1)S(1)}, bf16[1376,128]{1,0:T(8,128)(2,1)S(1)}, u32[]{:S(2)}, u32[]{:S(2)}) collective-permute-start(bf16[1376,128]{1,0:T(8,128)(2,1)S(1)} %get-tuple-element.16.refs_0_), channel_id=1, source_target_pairs={{0,1},{1,0},{2,3},{3,2},{4,5},{5,4},{6,7},{7,6},{8,9},{9,8},{10,11... | collective-permute-start | bytes 1056776 | tf_op jit(solution)/shard_map/ppermute | solution.py:164
  20.4 6.3 %collective-permute-start.3 = (bf16[720,128]{1,0:T(8,128)(2,1)S(1)}, bf16[720,128]{1,0:T(8,128)(2,1)S(1)}, u32[]{:S(2)}, u32[]{:S(2)}) collective-permute-start(bf16[720,128]{1,0:T(8,128)(2,1)S(1)} %collective-permute-done.2.refs_3_), channel_id=1, source_target_pairs={{0,8},{8,0},{16,24},{24,16},{1,9},{9,1},{17,25},{25,17},{2,10},{10... | collective-permute-start | bytes 552968 | tf_op jit(solution)/shard_map/ppermute | solution.py:164
  22.0 6.7 %collective-permute-start.10 = (bf16[720,128]{1,0:T(8,128)(2,1)S(1)}, bf16[720,128]{1,0:T(8,128)(2,1)S(1)}, u32[]{:S(2)}, u32[]{:S(2)}) collective-permute-start(bf16[720,128]{1,0:T(8,128)(2,1)S(1)} %collective-permute-done.2.refs_3_), channel_id=1, source_target_pairs={{0,1},{1,0},{2,3},{3,2},{4,5},{5,4},{6,7},{7,6},{8,9},{9,8},{10,11... | collective-permute-start | bytes 552968 | tf_op jit(solution)/shard_map/ppermute | solution.py:164
  26.7 3.4 %collective-permute-start.9 = (bf16[1376,128]{1,0:T(8,128)(2,1)S(1)}, bf16[1376,128]{1,0:T(8,128)(2,1)S(1)}, u32[]{:S(2)}, u32[]{:S(2)}) collective-permute-start(bf16[1376,128]{1,0:T(8,128)(2,1)S(1)} %collective-permute-done.6.refs_2_), channel_id=1, source_target_pairs={{0,1},{1,0},{2,3},{3,2},{4,5},{5,4},{6,7},{7,6},{8,9},{9,8},{10,11... | collective-permute-start | bytes 1056776 | tf_op jit(solution)/shard_map/ppermute | solution.py:164
  26.7 3.4 %collective-permute-start.8 = (bf16[1376,128]{1,0:T(8,128)(2,1)S(1)}, bf16[1376,128]{1,0:T(8,128)(2,1)S(1)}, u32[]{:S(2)}, u32[]{:S(2)}) collective-permute-start(bf16[1376,128]{1,0:T(8,128)(2,1)S(1)} %collective-permute-done.1.refs_1_), channel_id=1, source_target_pairs={{0,1},{1,0},{2,3},{3,2},{4,5},{5,4},{6,7},{7,6},{8,9},{9,8},{10,11... | collective-permute-start | bytes 1056776 | tf_op jit(solution)/shard_map/ppermute | solution.py:164
  27.2 12.3 %collective-permute-start.12 = (bf16[128,1024]{1,0:T(8,128)(2,1)S(1)}, bf16[128,1024]{1,0:T(8,128)(2,1)S(1)}, u32[]{:S(2)}, u32[]{:S(2)}) collective-permute-start(bf16[128,1024]{1,0:T(8,128)(2,1)S(1)} %copy-done.1), channel_id=1, source_target_pairs={{0,6},{1,7},{2,4},{3,5},{4,2},{5,3},{6,0},{7,1},{8,14},{9,15},{10,... | collective-permute-start | bytes 786440 | tf_op jit(solution)/shard_map/ppermute | solution.py:164
  28.7 1.4 %collective-permute-start.11 = (bf16[720,128]{1,0:T(8,128)(2,1)S(1)}, bf16[720,128]{1,0:T(8,128)(2,1)S(1)}, u32[]{:S(2)}, u32[]{:S(2)}) collective-permute-start(bf16[720,128]{1,0:T(8,128)(2,1)S(1)} %collective-permute-done.3.refs_4_), channel_id=1, source_target_pairs={{0,1},{1,0},{2,3},{3,2},{4,5},{5,4},{6,7},{7,6},{8,9},{9,8},{10,11... | collective-permute-start | bytes 552968 | tf_op jit(solution)/shard_map/ppermute | solution.py:164
  32.4 18.5 %collective-permute-start.15 = (bf16[128,1024]{1,0:T(8,128)(2,1)S(1)}, bf16[128,1024]{1,0:T(8,128)(2,1)S(1)}, u32[]{:S(2)}, u32[]{:S(2)}) collective-permute-start(bf16[128,1024]{1,0:T(8,128)(2,1)S(1)} %shard_map.109), channel_id=1, source_target_pairs={{0,2},{1,3},{2,0},{3,1},{4,6},{5,7},{6,4},{7,5},{8,10},{9,11},{10,... | collective-permute-start | bytes 786440 | tf_op jit(solution)/shard_map/ppermute | solution.py:164
  34.6 7.9 %collective-permute-start.16 = (bf16[512,128]{1,0:T(8,128)(2,1)S(1)}, bf16[512,128]{1,0:T(8,128)(2,1)S(1)}, u32[]{:S(2)}, u32[]{:S(2)}) collective-permute-start(bf16[512,128]{1,0:T(8,128)(2,1)S(1)} %get-tuple-element.27.refs_3_), channel_id=1, source_target_pairs={{0,24},{8,16},{16,8},{24,0},{1,25},{9,17},{17,9},{25,1},{2,26},{10... | collective-permute-start | bytes 393224 | tf_op jit(solution)/shard_map/ppermute | solution.py:164
  38.2 13.4 %collective-permute-start.14 = (bf16[128,1024]{1,0:T(8,128)(2,1)S(1)}, bf16[128,1024]{1,0:T(8,128)(2,1)S(1)}, u32[]{:S(2)}, u32[]{:S(2)}) collective-permute-start(bf16[128,1024]{1,0:T(8,128)(2,1)S(1)} %shard_map.108), channel_id=1, source_target_pairs={{0,4},{1,5},{2,6},{3,7},{4,0},{5,1},{6,2},{7,3},{8,12},{9,13},{10,... | collective-permute-start | bytes 786440 | tf_op jit(solution)/shard_map/ppermute | solution.py:164
  41.0 10.7 %copy-start.3 = (bf16[1024,128]{1,0:T(8,128)(2,1)S(1)}, bf16[1024,128]{1,0:T(8,128)(2,1)}, u32[]{:S(2)}) copy-start(bf16[1024,128]{1,0:T(8,128)(2,1)} %proj_ref.1) | copy-start | bytes 786436
  41.0 10.7 %copy-start.6 = (f32[1024]{0:T(1024)S(1)}, f32[1024]{0:T(1024)}, u32[]{:S(2)}) copy-start(f32[1024]{0:T(1024)} %param.13) | copy-start | bytes 12292
  41.0 10.7 %copy-start.8 = (s32[1,4]{1,0:T(1,128)S(1)}, s32[1,4]{1,0:T(1,128)}, u32[]{:S(2)}) copy-start(s32[1,4]{1,0:T(1,128)} %lengths_ref.1) | copy-start | bytes 52
  41.0 10.7 %collective-permute-start.13 = (bf16[128,1024]{1,0:T(8,128)(2,1)S(1)}, bf16[128,1024]{1,0:T(8,128)(2,1)S(1)}, u32[]{:S(2)}, u32[]{:S(2)}) collective-permute-start(bf16[128,1024]{1,0:T(8,128)(2,1)S(1)} %shard_map.107), channel_id=1, source_target_pairs={{0,6},{1,7},{2,4},{3,5},{4,2},{5,3},{6,0},{7,1},{8,14},{9,15},{10,... | collective-permute-start | bytes 786440 | tf_op jit(solution)/shard_map/ppermute | solution.py:164
  42.5 6.4 %collective-permute-start.17 = (bf16[512,128]{1,0:T(8,128)(2,1)S(1)}, bf16[512,128]{1,0:T(8,128)(2,1)S(1)}, u32[]{:S(2)}, u32[]{:S(2)}) collective-permute-start(bf16[512,128]{1,0:T(8,128)(2,1)S(1)} %get-tuple-element.27.refs_3_), channel_id=1, source_target_pairs={{0,8},{8,0},{16,24},{24,16},{1,9},{9,1},{17,25},{25,17},{2,10},{10... | collective-permute-start | bytes 393224 | tf_op jit(solution)/shard_map/ppermute | solution.py:164
  42.5 8.4 %collective-permute-start.18 = (bf16[512,128]{1,0:T(8,128)(2,1)S(1)}, bf16[512,128]{1,0:T(8,128)(2,1)S(1)}, u32[]{:S(2)}, u32[]{:S(2)}) collective-permute-start(bf16[512,128]{1,0:T(8,128)(2,1)S(1)} %get-tuple-element.27.refs_3_), channel_id=1, source_target_pairs={{0,16},{8,24},{16,0},{24,8},{1,17},{9,25},{17,1},{25,9},{2,18},{10... | collective-permute-start | bytes 393224 | tf_op jit(solution)/shard_map/ppermute | solution.py:164
  46.7 17.1 %copy-start.7 = (s32[2,100]{1,0:T(2,128)S(1)}, s32[2,100]{1,0:T(2,128)}, u32[]{:S(2)}) copy-start(s32[2,100]{1,0:T(2,128)} %cand_ref.1) | copy-start | bytes 2404

commit v10 on v9

--- a/solution.py
+++ b/solution.py
@@ -181,9 +181,10 @@
             compiler_params=params,
         )(wi_weight, query_own)
         mine = [pieces[0]] + [swap(pieces[step], 2 * step) for step in range(1, chips)]
+        mine[3], tokens[1], tokens[2] = lax.optimization_barrier((mine[3], tokens[1], tokens[2]))
         mine.append(swap(mine[3], 1, "group"))
-        mine[1], mine[4], tokens[1], tokens[2] = lax.optimization_barrier(
-            (mine[1], mine[4], tokens[1], tokens[2])
+        mine[0], mine[1], mine[4], tokens[1], tokens[2] = lax.optimization_barrier(
+            (mine[0], mine[1], mine[4], tokens[1], tokens[2])
         )
         other = [swap(piece, 1) for piece in mine]
         *weights, plane = pl.pallas_call(

time: 64.7 us -> 61.1 us (0.944)
  waiting for transfers between devices: 19.8 us -> 15.7 us
  starting transfers between devices: 22.2 us -> 23.6 us
  blocking collectives: 10.3 us -> 9.33 us
    ppermute x19, waiting for transfers between devices: 19.8 us -> 15.7 us  [swap(): return lax.ppermute(values, axis, [(i, i ^ mask) for i in range(size)])]
    ppermute x19, starting transfers between devices: 22.2 us -> 23.6 us  [swap(): return lax.ppermute(values, axis, [(i, i ^ mask) for i in range(size)])]
    all_to_all x1, blocking collectives: 10.3 us -> 9.33 us  [body(): lax.all_to_all(best, ('group', 'dev'), split_axis=0, concat_axis=0, tiled...]
where the time goes in v10:
time: 61.1 us; the launch traced here: 60.8 us
  starting transfers between devices  23.6 us (39%)
  waiting for transfers between devices  15.7 us (26%)
  Pallas kernels  9.39 us (15%)
  blocking collectives  9.33 us (15%)
  local copies, waits for them, and re-layouts  2.08 us (3%)
  between operations  0.77 us (1%)
    ppermute x19, starting transfers between devices, swap(): return lax.ppermute(values, axis, [(i, i ^ mask) for i in range(size)])  23.6 us
    ppermute x19, waiting for transfers between devices, swap(): return lax.ppermute(values, axis, [(i, i ^ mask) for i in range(size)])  15.7 us
    all_to_all x1, blocking collectives, body(): lax.all_to_all(best, ('group', 'dev'), split_axis=0, concat_axis=0, tiled...  9.33 us
    pallas_call x4, Pallas kernels, body(): pl.pallas_call(ffn_kernel, out_shape=jax.ShapeDtypeStruct((rows, width),...  5.51 us
    unnamed x18, local copies, waits for them, and re-layouts  2.08 us
    pallas_call x1, Pallas kernels, body(): pl.pallas_call(functools.partial(finish_kernel, chips), out_shape=[jax.Sh...  1.85 us
  transfers between devices with their start and end apart: 19, of which 7 were waited for; matrix products, arithmetic and copies ran while one was open for 0% of the time, Pallas kernels for 11%

profile of v10, /device:TPU:0, one launch (start us, length us, event | category | flops | bytes accessed | tf_op | source)
XLA Modules:
  0.0 60.8 jit_solution(14504554547679853400)
XLA Ops:
  0.6 3.0 %collective-permute-start.3 = (bf16[128,1024]{1,0:T(8,128)(2,1)}, bf16[128,1024]{1,0:T(8,128)(2,1)S(1)}, u32[]{:S(2)}, u32[]{:S(2)}) collective-permute-start(bf16[128,1024]{1,0:T(8,128)(2,1)} %tokens_ref.3), channel_id=1, source_target_pairs={{0,2},{1,3},{2,0},{3,1},{4,6},{5,7},{6,4},{7,5},{8,10},{9,11},{10,... | collective-permute-start | bytes 786440 | tf_op jit(solution)/shard_map/ppermute | solution.py:164
  3.6 1.5 %collective-permute-start.4 = (bf16[128,1024]{1,0:T(8,128)(2,1)}, bf16[128,1024]{1,0:T(8,128)(2,1)S(1)}, u32[]{:S(2)}, u32[]{:S(2)}) collective-permute-start(bf16[128,1024]{1,0:T(8,128)(2,1)} %tokens_ref.3), channel_id=1, source_target_pairs={{0,4},{1,5},{2,6},{3,7},{4,0},{5,1},{6,2},{7,3},{8,12},{9,13},{10,... | collective-permute-start | bytes 786440 | tf_op jit(solution)/shard_map/ppermute | solution.py:164
  5.2 1.3 %copy-done = bf16[128,5248]{1,0:T(8,128)(2,1)S(1)} copy-done((bf16[128,5248]{1,0:T(8,128)(2,1)S(1)}, bf16[128,5248]{1,0:T(8,128)(2,1)}, u32[]{:S(2)}) %copy-start) | copy-done | bytes 1343512
  6.5 0.7 %copy-done.5 = bf16[2,32,128]{2,1,0:T(8,128)(2,1)S(1)} copy-done((bf16[2,32,128]{2,1,0:T(8,128)(2,1)S(1)}, bf16[2,32,128]{2,1,0:T(8,128)(2,1)}, u32[]{:S(2)}) %copy-start.5) | copy-done | bytes 16408
  7.2 0.5 shard_map.104
  7.8 1.9 %collective-permute-start.1 = (bf16[1376,128]{1,0:T(8,128)(2,1)S(1)}, bf16[1376,128]{1,0:T(8,128)(2,1)S(1)}, u32[]{:S(2)}, u32[]{:S(2)}) collective-permute-start(bf16[1376,128]{1,0:T(8,128)(2,1)S(1)} %get-tuple-element.21), channel_id=1, source_target_pairs={{0,2},{1,3},{2,0},{3,1},{4,6},{5,7},{6,4},{7,5},{8,10},{9,11},{10,... | collective-permute-start | bytes 1056776 | tf_op jit(solution)/shard_map/ppermute | solution.py:164
  9.7 1.5 %collective-permute-start.6 = (bf16[1376,128]{1,0:T(8,128)(2,1)S(1)}, bf16[1376,128]{1,0:T(8,128)(2,1)S(1)}, u32[]{:S(2)}, u32[]{:S(2)}) collective-permute-start(bf16[1376,128]{1,0:T(8,128)(2,1)S(1)} %get-tuple-element.28), channel_id=1, source_target_pairs={{0,4},{1,5},{2,6},{3,7},{4,0},{5,1},{6,2},{7,3},{8,12},{9,13},{10,... | collective-permute-start | bytes 1056776 | tf_op jit(solution)/shard_map/ppermute | solution.py:164
  11.2 5.0 %collective-permute-done.2.refs_3_ = bf16[720,128]{1,0:T(8,128)(2,1)S(1)} collective-permute-done((bf16[720,128]{1,0:T(8,128)(2,1)S(1)}, bf16[720,128]{1,0:T(8,128)(2,1)S(1)}, u32[]{:S(2)}, u32[]{:S(2)}) %collective-permute-start.2) | collective-permute-done | bytes 184352 | tf_op jit(solution)/shard_map/ppermute | solution.py:164
  16.3 1.6 %collective-permute-start.5 = (bf16[720,128]{1,0:T(8,128)(2,1)S(1)}, bf16[720,128]{1,0:T(8,128)(2,1)S(1)}, u32[]{:S(2)}, u32[]{:S(2)}) collective-permute-start(bf16[720,128]{1,0:T(8,128)(2,1)S(1)} %collective-permute-done.2.refs_3_), channel_id=1, source_target_pairs={{0,8},{8,0},{16,24},{24,16},{1,9},{9,1},{17,25},{25,17},{2,10},{10... | collective-permute-start | bytes 552968 | tf_op jit(solution)/shard_map/ppermute | solution.py:164
  18.1 3.6 %collective-permute-done.1.refs_1_ = bf16[1376,128]{1,0:T(8,128)(2,1)S(1)} collective-permute-done((bf16[1376,128]{1,0:T(8,128)(2,1)S(1)}, bf16[1376,128]{1,0:T(8,128)(2,1)S(1)}, u32[]{:S(2)}, u32[]{:S(2)}) %collective-permute-start.1) | collective-permute-done | bytes 352288 | tf_op jit(solution)/shard_map/ppermute | solution.py:164
  21.7 1.7 %collective-permute-done.5.refs_4_ = bf16[720,128]{1,0:T(8,128)(2,1)S(1)} collective-permute-done((bf16[720,128]{1,0:T(8,128)(2,1)S(1)}, bf16[720,128]{1,0:T(8,128)(2,1)S(1)}, u32[]{:S(2)}, u32[]{:S(2)}) %collective-permute-start.5) | collective-permute-done | bytes 184352 | tf_op jit(solution)/shard_map/ppermute | solution.py:164
  23.4 0.5 collective-permute-start.9
  23.9 0.4 collective-permute-start.8
  24.4 0.4 collective-permute-done.11.refs_9_
  24.8 1.7 %collective-permute-start.12 = (bf16[128,1024]{1,0:T(8,128)(2,1)S(1)}, bf16[128,1024]{1,0:T(8,128)(2,1)S(1)}, u32[]{:S(2)}, u32[]{:S(2)}) collective-permute-start(bf16[128,1024]{1,0:T(8,128)(2,1)S(1)} %copy-done.1), channel_id=1, source_target_pairs={{0,6},{1,7},{2,4},{3,5},{4,2},{5,3},{6,0},{7,1},{8,14},{9,15},{10,... | collective-permute-start | bytes 786440 | tf_op jit(solution)/shard_map/ppermute | solution.py:164
  26.5 0.9 %shard_map.105 = (bf16[656,1024]{1,0:T(8,128)(2,1)S(1)}, bf16[656,1024]{1,0:T(8,128)(2,1)S(1)}, bf16[656,1024]{1,0:T(8,128)(2,1)S(1)}, bf16[512,128]{1,0:T(8,128)(2,1)S(1)}) custom-call(bf16[328,1024]{1,0:T(8,128)(2,1)S(1)} %copy-done.2, bf16[328,1024]{1,0:T(8,128)(2,1)S(1)} %collective-permute-done.wo_other, ...), custom_call_target="tpu_custom_call" | custom-call | tf_op jit(solution)/shard_map/pallas_call | solution.py:190
  27.4 1.4 %shard_map.109 = bf16[128,1024]{1,0:T(8,128)(2,1)S(1)} custom-call(f32[1,1024]{1,0:T(1,128)S(1)} %bitcast.5, bf16[656,1024]{1,0:T(8,128)(2,1)S(1)} %get-tuple-element.30.gelu_w, bf16[656,1024]{1,0:T(8,128)(2,1)S(1)} %get-tuple-element.31.gate_w, bf16[656,1024]{1,0:T(8,128)(2,1)S(1)} %get-tuple-element.32.wo_part, ...), custom_call_target="tpu_custom_call" | custom-call | tf_op jit(solution)/shard_map/pallas_call | solution.py:214
  28.8 1.6 %collective-permute-start.15 = (bf16[128,1024]{1,0:T(8,128)(2,1)S(1)}, bf16[128,1024]{1,0:T(8,128)(2,1)S(1)}, u32[]{:S(2)}, u32[]{:S(2)}) collective-permute-start(bf16[128,1024]{1,0:T(8,128)(2,1)S(1)} %shard_map.109), channel_id=1, source_target_pairs={{0,2},{1,3},{2,0},{3,1},{4,6},{5,7},{6,4},{7,5},{8,10},{9,11},{10,... | collective-permute-start | bytes 786440 | tf_op jit(solution)/shard_map/ppermute | solution.py:164
  30.3 1.4 %shard_map.108 = bf16[128,1024]{1,0:T(8,128)(2,1)S(1)} custom-call(f32[1,1024]{1,0:T(1,128)S(1)} %bitcast.6, bf16[656,1024]{1,0:T(8,128)(2,1)S(1)} %get-tuple-element.30.gelu_w, bf16[656,1024]{1,0:T(8,128)(2,1)S(1)} %get-tuple-element.31.gate_w, bf16[656,1024]{1,0:T(8,128)(2,1)S(1)} %get-tuple-element.32.wo_part, ...), custom_call_target="tpu_custom_call" | custom-call | tf_op jit(solution)/shard_map/pallas_call | solution.py:214
  31.7 3.7 %collective-permute-start.16 = (bf16[512,128]{1,0:T(8,128)(2,1)S(1)}, bf16[512,128]{1,0:T(8,128)(2,1)S(1)}, u32[]{:S(2)}, u32[]{:S(2)}) collective-permute-start(bf16[512,128]{1,0:T(8,128)(2,1)S(1)} %get-tuple-element.35.refs_3_), channel_id=1, source_target_pairs={{0,24},{8,16},{16,8},{24,0},{1,25},{9,17},{17,9},{25,1},{2,26},{10... | collective-permute-start | bytes 393224 | tf_op jit(solution)/shard_map/ppermute | solution.py:164
  35.4 0.5 collective-permute-start.14
  35.9 1.4 %shard_map.107 = bf16[128,1024]{1,0:T(8,128)(2,1)S(1)} custom-call(f32[1,1024]{1,0:T(1,128)S(1)} %bitcast.7, bf16[656,1024]{1,0:T(8,128)(2,1)S(1)} %get-tuple-element.30.gelu_w, bf16[656,1024]{1,0:T(8,128)(2,1)S(1)} %get-tuple-element.31.gate_w, bf16[656,1024]{1,0:T(8,128)(2,1)S(1)} %get-tuple-element.32.wo_part, ...), custom_call_target="tpu_custom_call" | custom-call | tf_op jit(solution)/shard_map/pallas_call | solution.py:214
  37.3 1.5 %collective-permute-start.13 = (bf16[128,1024]{1,0:T(8,128)(2,1)S(1)}, bf16[128,1024]{1,0:T(8,128)(2,1)S(1)}, u32[]{:S(2)}, u32[]{:S(2)}) collective-permute-start(bf16[128,1024]{1,0:T(8,128)(2,1)S(1)} %shard_map.107), channel_id=1, source_target_pairs={{0,6},{1,7},{2,4},{3,5},{4,2},{5,3},{6,0},{7,1},{8,14},{9,15},{10,... | collective-permute-start | bytes 786440 | tf_op jit(solution)/shard_map/ppermute | solution.py:164
  38.8 0.7 %collective-permute-start.17 = (bf16[512,128]{1,0:T(8,128)(2,1)S(1)}, bf16[512,128]{1,0:T(8,128)(2,1)S(1)}, u32[]{:S(2)}, u32[]{:S(2)}) collective-permute-start(bf16[512,128]{1,0:T(8,128)(2,1)S(1)} %get-tuple-element.35.refs_3_), channel_id=1, source_target_pairs={{0,8},{8,0},{16,24},{24,16},{1,9},{9,1},{17,25},{25,17},{2,10},{10... | collective-permute-start | bytes 393224 | tf_op jit(solution)/shard_map/ppermute | solution.py:164
  39.6 3.0 %collective-permute-start.18 = (bf16[512,128]{1,0:T(8,128)(2,1)S(1)}, bf16[512,128]{1,0:T(8,128)(2,1)S(1)}, u32[]{:S(2)}, u32[]{:S(2)}) collective-permute-start(bf16[512,128]{1,0:T(8,128)(2,1)S(1)} %get-tuple-element.35.refs_3_), channel_id=1, source_target_pairs={{0,16},{8,24},{16,0},{24,8},{1,17},{9,25},{17,1},{25,9},{2,18},{10... | collective-permute-start | bytes 393224 | tf_op jit(solution)/shard_map/ppermute | solution.py:164
  42.6 1.4 %shard_map.106.own_ref = f32[128,1024]{1,0:T(8,128)S(1)} custom-call(f32[1,1024]{1,0:T(1,128)S(1)} %bitcast.8, bf16[656,1024]{1,0:T(8,128)(2,1)S(1)} %get-tuple-element.30.gelu_w, bf16[656,1024]{1,0:T(8,128)(2,1)S(1)} %get-tuple-element.31.gate_w, bf16[656,1024]{1,0:T(8,128)(2,1)S(1)} %get-tuple-element.32.wo_part, bf16[128,1024]{1,0:T(8,128)(2,1)S(1)} %copy-done.1), custom_call_target="tpu_custom_call" | custom-call | tf_op jit(solution)/shard_map/pallas_call | solution.py:214
  44.0 1.1 %collective-permute-done.17.refs_5_ = bf16[512,128]{1,0:T(8,128)(2,1)S(1)} collective-permute-done((bf16[512,128]{1,0:T(8,128)(2,1)S(1)}, bf16[512,128]{1,0:T(8,128)(2,1)S(1)}, u32[]{:S(2)}, u32[]{:S(2)}) %collective-permute-start.17) | collective-permute-done | bytes 131104 | tf_op jit(solution)/shard_map/ppermute | solution.py:164
  45.1 3.0 %collective-permute-done.18.refs_6_ = bf16[512,128]{1,0:T(8,128)(2,1)S(1)} collective-permute-done((bf16[512,128]{1,0:T(8,128)(2,1)S(1)}, bf16[512,128]{1,0:T(8,128)(2,1)S(1)}, u32[]{:S(2)}, u32[]{:S(2)}) %collective-permute-start.18) | collective-permute-done | bytes 131104 | tf_op jit(solution)/shard_map/ppermute | solution.py:164
  48.1 0.8 %collective-permute-done.14.refs_1_ = bf16[128,1024]{1,0:T(8,128)(2,1)S(1)} collective-permute-done((bf16[128,1024]{1,0:T(8,128)(2,1)S(1)}, bf16[128,1024]{1,0:T(8,128)(2,1)S(1)}, u32[]{:S(2)}, u32[]{:S(2)}) %collective-permute-start.14) | collective-permute-done | bytes 262176 | tf_op jit(solution)/shard_map/ppermute | solution.py:164
  48.9 1.9 %shard_map.110 = (bf16[128,128]{1,0:T(8,128)(2,1)}, bf16[32,4,128]{2,1,0:T(4,128)(2,1)S(1)}) custom-call(s32[1,4]{1,0:T(1,128)S(1)} %copy-done.8, bf16[128,1024]{1,0:T(8,128)(2,1)S(1)} %copy-done.1, f32[1,1024]{1,0:T(1,128)S(1)} %bitcast.10, bf16[1024,128]{1,0:T(8,128)(2,1)S(1)} %copy-done.3, f32[128,1024]{1,0:T(8,128)S(1)} %shard_map.106.own_ref, ...), custom_call_target="tpu_custom_call" | custom-call | tf_op jit(solution)/shard_map/pallas_call | solution.py:225
  50.8 9.3 %all_to_all.5 = bf16[32,4,128]{2,1,0:T(4,128)(2,1)S(1)} all-to-all(bf16[32,4,128]{2,1,0:T(4,128)(2,1)S(1)} %get-tuple-element.37), channel_id=1, replica_groups=mesh['group'=4,'dev'=8] {'group','dev'}, dimensions={0} | all-to-all | bytes 65536 | tf_op jit(solution)/shard_map/all_to_all | solution.py:243
  60.1 0.7 %shard_map.111 = f32[2,100]{1,0:T(2,128)} custom-call(s32[2,100]{1,0:T(2,128)S(1)} %copy-done.7, bf16[4,8,4,128]{3,2,1,0:T(4,128)(2,1)S(1)} %bitcast.4), custom_call_target="tpu_custom_call" | custom-call | tf_op jit(solution)/shard_map/pallas_call | solution.py:244
  (33 shorter events, 0.4 us)
Async XLA Ops:
  0.6 15.7 %collective-permute-start.3 = (bf16[128,1024]{1,0:T(8,128)(2,1)}, bf16[128,1024]{1,0:T(8,128)(2,1)S(1)}, u32[]{:S(2)}, u32[]{:S(2)}) collective-permute-start(bf16[128,1024]{1,0:T(8,128)(2,1)} %tokens_ref.3), channel_id=1, source_target_pairs={{0,2},{1,3},{2,0},{3,1},{4,6},{5,7},{6,4},{7,5},{8,10},{9,11},{10,... | collective-permute-start | bytes 786440 | tf_op jit(solution)/shard_map/ppermute | solution.py:164
  3.6 12.7 %collective-permute-start.4 = (bf16[128,1024]{1,0:T(8,128)(2,1)}, bf16[128,1024]{1,0:T(8,128)(2,1)S(1)}, u32[]{:S(2)}, u32[]{:S(2)}) collective-permute-start(bf16[128,1024]{1,0:T(8,128)(2,1)} %tokens_ref.3), channel_id=1, source_target_pairs={{0,4},{1,5},{2,6},{3,7},{4,0},{5,1},{6,2},{7,3},{8,12},{9,13},{10,... | collective-permute-start | bytes 786440 | tf_op jit(solution)/shard_map/ppermute | solution.py:164
  5.2 1.3 %copy-start = (bf16[128,5248]{1,0:T(8,128)(2,1)S(1)}, bf16[128,5248]{1,0:T(8,128)(2,1)}, u32[]{:S(2)}) copy-start(bf16[128,5248]{1,0:T(8,128)(2,1)} %wi_ref.1) | copy-start | bytes 4030468
  6.5 0.7 %copy-start.5 = (bf16[2,32,128]{2,1,0:T(8,128)(2,1)S(1)}, bf16[2,32,128]{2,1,0:T(8,128)(2,1)}, u32[]{:S(2)}) copy-start(bf16[2,32,128]{2,1,0:T(8,128)(2,1)} %param.15) | copy-start | bytes 49156
  7.2 9.1 %copy-start.2 = (bf16[328,1024]{1,0:T(8,128)(2,1)S(1)}, bf16[328,1024]{1,0:T(8,128)(2,1)}, u32[]{:S(2)}) copy-start(bf16[328,1024]{1,0:T(8,128)(2,1)} %wo_mine.1) | copy-start | bytes 2015236
  7.2 17.6 %copy-start.1 = (bf16[128,1024]{1,0:T(8,128)(2,1)S(1)}, bf16[128,1024]{1,0:T(8,128)(2,1)}, u32[]{:S(2)}) copy-start(bf16[128,1024]{1,0:T(8,128)(2,1)} %tokens_ref.3) | copy-start | bytes 786436
  7.7 8.6 %collective-permute-start.2 = (bf16[720,128]{1,0:T(8,128)(2,1)S(1)}, bf16[720,128]{1,0:T(8,128)(2,1)S(1)}, u32[]{:S(2)}, u32[]{:S(2)}) collective-permute-start(bf16[720,128]{1,0:T(8,128)(2,1)S(1)} %get-tuple-element.22), channel_id=1, source_target_pairs={{0,6},{1,7},{2,4},{3,5},{4,2},{5,3},{6,0},{7,1},{8,14},{9,15},{10,... | collective-permute-start | bytes 552968 | tf_op jit(solution)/shard_map/ppermute | solution.py:164
  7.8 13.9 %collective-permute-start.1 = (bf16[1376,128]{1,0:T(8,128)(2,1)S(1)}, bf16[1376,128]{1,0:T(8,128)(2,1)S(1)}, u32[]{:S(2)}, u32[]{:S(2)}) collective-permute-start(bf16[1376,128]{1,0:T(8,128)(2,1)S(1)} %get-tuple-element.21), channel_id=1, source_target_pairs={{0,2},{1,3},{2,0},{3,1},{4,6},{5,7},{6,4},{7,5},{8,10},{9,11},{10,... | collective-permute-start | bytes 1056776 | tf_op jit(solution)/shard_map/ppermute | solution.py:164
  9.7 13.6 %collective-permute-start.6 = (bf16[1376,128]{1,0:T(8,128)(2,1)S(1)}, bf16[1376,128]{1,0:T(8,128)(2,1)S(1)}, u32[]{:S(2)}, u32[]{:S(2)}) collective-permute-start(bf16[1376,128]{1,0:T(8,128)(2,1)S(1)} %get-tuple-element.28), channel_id=1, source_target_pairs={{0,4},{1,5},{2,6},{3,7},{4,0},{5,1},{6,2},{7,3},{8,12},{9,13},{10,... | collective-permute-start | bytes 1056776 | tf_op jit(solution)/shard_map/ppermute | solution.py:164
  16.3 10.2 %collective-permute-start = (bf16[328,1024]{1,0:T(8,128)(2,1)S(1)}, bf16[328,1024]{1,0:T(8,128)(2,1)S(1)}, u32[]{:S(2)}, u32[]{:S(2)}) collective-permute-start(bf16[328,1024]{1,0:T(8,128)(2,1)S(1)} %copy-done.2), channel_id=1, source_target_pairs={{0,1},{1,0},{2,3},{3,2},{4,5},{5,4},{6,7},{7,6},{8,9},{9,8},{10,11... | collective-permute-start | bytes 2015240 | tf_op jit(solution)/shard_map/ppermute | solution.py:164
  16.3 7.1 %collective-permute-start.5 = (bf16[720,128]{1,0:T(8,128)(2,1)S(1)}, bf16[720,128]{1,0:T(8,128)(2,1)S(1)}, u32[]{:S(2)}, u32[]{:S(2)}) collective-permute-start(bf16[720,128]{1,0:T(8,128)(2,1)S(1)} %collective-permute-done.2.refs_3_), channel_id=1, source_target_pairs={{0,8},{8,0},{16,24},{24,16},{1,9},{9,1},{17,25},{25,17},{2,10},{10... | collective-permute-start | bytes 552968 | tf_op jit(solution)/shard_map/ppermute | solution.py:164
  17.9 6.0 %collective-permute-start.10 = (bf16[720,128]{1,0:T(8,128)(2,1)S(1)}, bf16[720,128]{1,0:T(8,128)(2,1)S(1)}, u32[]{:S(2)}, u32[]{:S(2)}) collective-permute-start(bf16[720,128]{1,0:T(8,128)(2,1)S(1)} %collective-permute-done.2.refs_3_), channel_id=1, source_target_pairs={{0,1},{1,0},{2,3},{3,2},{4,5},{5,4},{6,7},{7,6},{8,9},{9,8},{10,11... | collective-permute-start | bytes 552968 | tf_op jit(solution)/shard_map/ppermute | solution.py:164
  23.4 4.0 %copy-start.4 = (f32[1024]{0:T(1024)S(1)}, f32[1024]{0:T(1024)}, u32[]{:S(2)}) copy-start(f32[1024]{0:T(1024)} %param.10) | copy-start | bytes 12292
  23.4 1.4 %collective-permute-start.11 = (bf16[720,128]{1,0:T(8,128)(2,1)S(1)}, bf16[720,128]{1,0:T(8,128)(2,1)S(1)}, u32[]{:S(2)}, u32[]{:S(2)}) collective-permute-start(bf16[720,128]{1,0:T(8,128)(2,1)S(1)} %collective-permute-done.5.refs_4_), channel_id=1, source_target_pairs={{0,1},{1,0},{2,3},{3,2},{4,5},{5,4},{6,7},{7,6},{8,9},{9,8},{10,11... | collective-permute-start | bytes 552968 | tf_op jit(solution)/shard_map/ppermute | solution.py:164
  23.4 3.1 %collective-permute-start.9 = (bf16[1376,128]{1,0:T(8,128)(2,1)S(1)}, bf16[1376,128]{1,0:T(8,128)(2,1)S(1)}, u32[]{:S(2)}, u32[]{:S(2)}) collective-permute-start(bf16[1376,128]{1,0:T(8,128)(2,1)S(1)} %collective-permute-done.6.refs_2_), channel_id=1, source_target_pairs={{0,1},{1,0},{2,3},{3,2},{4,5},{5,4},{6,7},{7,6},{8,9},{9,8},{10,11... | collective-permute-start | bytes 1056776 | tf_op jit(solution)/shard_map/ppermute | solution.py:164
  23.9 2.6 %collective-permute-start.7 = (bf16[1376,128]{1,0:T(8,128)(2,1)S(1)}, bf16[1376,128]{1,0:T(8,128)(2,1)S(1)}, u32[]{:S(2)}, u32[]{:S(2)}) collective-permute-start(bf16[1376,128]{1,0:T(8,128)(2,1)S(1)} %get-tuple-element.26.refs_0_), channel_id=1, source_target_pairs={{0,1},{1,0},{2,3},{3,2},{4,5},{5,4},{6,7},{7,6},{8,9},{9,8},{10,11... | collective-permute-start | bytes 1056776 | tf_op jit(solution)/shard_map/ppermute | solution.py:164
  23.9 2.5 %collective-permute-start.8 = (bf16[1376,128]{1,0:T(8,128)(2,1)S(1)}, bf16[1376,128]{1,0:T(8,128)(2,1)S(1)}, u32[]{:S(2)}, u32[]{:S(2)}) collective-permute-start(bf16[1376,128]{1,0:T(8,128)(2,1)S(1)} %collective-permute-done.1.refs_1_), channel_id=1, source_target_pairs={{0,1},{1,0},{2,3},{3,2},{4,5},{5,4},{6,7},{7,6},{8,9},{9,8},{10,11... | collective-permute-start | bytes 1056776 | tf_op jit(solution)/shard_map/ppermute | solution.py:164
  24.8 11.1 %collective-permute-start.12 = (bf16[128,1024]{1,0:T(8,128)(2,1)S(1)}, bf16[128,1024]{1,0:T(8,128)(2,1)S(1)}, u32[]{:S(2)}, u32[]{:S(2)}) collective-permute-start(bf16[128,1024]{1,0:T(8,128)(2,1)S(1)} %copy-done.1), channel_id=1, source_target_pairs={{0,6},{1,7},{2,4},{3,5},{4,2},{5,3},{6,0},{7,1},{8,14},{9,15},{10,... | collective-permute-start | bytes 786440 | tf_op jit(solution)/shard_map/ppermute | solution.py:164
  28.8 19.3 %collective-permute-start.15 = (bf16[128,1024]{1,0:T(8,128)(2,1)S(1)}, bf16[128,1024]{1,0:T(8,128)(2,1)S(1)}, u32[]{:S(2)}, u32[]{:S(2)}) collective-permute-start(bf16[128,1024]{1,0:T(8,128)(2,1)S(1)} %shard_map.109), channel_id=1, source_target_pairs={{0,2},{1,3},{2,0},{3,1},{4,6},{5,7},{6,4},{7,5},{8,10},{9,11},{10,... | collective-permute-start | bytes 786440 | tf_op jit(solution)/shard_map/ppermute | solution.py:164
  31.7 7.8 %collective-permute-start.16 = (bf16[512,128]{1,0:T(8,128)(2,1)S(1)}, bf16[512,128]{1,0:T(8,128)(2,1)S(1)}, u32[]{:S(2)}, u32[]{:S(2)}) collective-permute-start(bf16[512,128]{1,0:T(8,128)(2,1)S(1)} %get-tuple-element.35.refs_3_), channel_id=1, source_target_pairs={{0,24},{8,16},{16,8},{24,0},{1,25},{9,17},{17,9},{25,1},{2,26},{10... | collective-permute-start | bytes 393224 | tf_op jit(solution)/shard_map/ppermute | solution.py:164
  35.4 13.5 %collective-permute-start.14 = (bf16[128,1024]{1,0:T(8,128)(2,1)S(1)}, bf16[128,1024]{1,0:T(8,128)(2,1)S(1)}, u32[]{:S(2)}, u32[]{:S(2)}) collective-permute-start(bf16[128,1024]{1,0:T(8,128)(2,1)S(1)} %shard_map.108), channel_id=1, source_target_pairs={{0,4},{1,5},{2,6},{3,7},{4,0},{5,1},{6,2},{7,3},{8,12},{9,13},{10,... | collective-permute-start | bytes 786440 | tf_op jit(solution)/shard_map/ppermute | solution.py:164
  37.3 11.6 %copy-start.3 = (bf16[1024,128]{1,0:T(8,128)(2,1)S(1)}, bf16[1024,128]{1,0:T(8,128)(2,1)}, u32[]{:S(2)}) copy-start(bf16[1024,128]{1,0:T(8,128)(2,1)} %proj_ref.1) | copy-start | bytes 786436
  37.3 11.6 %copy-start.6 = (f32[1024]{0:T(1024)S(1)}, f32[1024]{0:T(1024)}, u32[]{:S(2)}) copy-start(f32[1024]{0:T(1024)} %param.13) | copy-start | bytes 12292
  37.3 11.6 %copy-start.8 = (s32[1,4]{1,0:T(1,128)S(1)}, s32[1,4]{1,0:T(1,128)}, u32[]{:S(2)}) copy-start(s32[1,4]{1,0:T(1,128)} %lengths_ref.1) | copy-start | bytes 52
  37.3 11.6 %collective-permute-start.13 = (bf16[128,1024]{1,0:T(8,128)(2,1)S(1)}, bf16[128,1024]{1,0:T(8,128)(2,1)S(1)}, u32[]{:S(2)}, u32[]{:S(2)}) collective-permute-start(bf16[128,1024]{1,0:T(8,128)(2,1)S(1)} %shard_map.107), channel_id=1, source_target_pairs={{0,6},{1,7},{2,4},{3,5},{4,2},{5,3},{6,0},{7,1},{8,14},{9,15},{10,... | collective-permute-start | bytes 786440 | tf_op jit(solution)/shard_map/ppermute | solution.py:164
  38.8 6.2 %collective-permute-start.17 = (bf16[512,128]{1,0:T(8,128)(2,1)S(1)}, bf16[512,128]{1,0:T(8,128)(2,1)S(1)}, u32[]{:S(2)}, u32[]{:S(2)}) collective-permute-start(bf16[512,128]{1,0:T(8,128)(2,1)S(1)} %get-tuple-element.35.refs_3_), channel_id=1, source_target_pairs={{0,8},{8,0},{16,24},{24,16},{1,9},{9,1},{17,25},{25,17},{2,10},{10... | collective-permute-start | bytes 393224 | tf_op jit(solution)/shard_map/ppermute | solution.py:164
  39.6 8.5 %collective-permute-start.18 = (bf16[512,128]{1,0:T(8,128)(2,1)S(1)}, bf16[512,128]{1,0:T(8,128)(2,1)S(1)}, u32[]{:S(2)}, u32[]{:S(2)}) collective-permute-start(bf16[512,128]{1,0:T(8,128)(2,1)S(1)} %get-tuple-element.35.refs_3_), channel_id=1, source_target_pairs={{0,16},{8,24},{16,0},{24,8},{1,17},{9,25},{17,1},{25,9},{2,18},{10... | collective-permute-start | bytes 393224 | tf_op jit(solution)/shard_map/ppermute | solution.py:164
  44.0 16.2 %copy-start.7 = (s32[2,100]{1,0:T(2,128)S(1)}, s32[2,100]{1,0:T(2,128)}, u32[]{:S(2)}) copy-start(s32[2,100]{1,0:T(2,128)} %cand_ref.1) | copy-start | bytes 2404

commit v11 on v10

--- a/solution.py
+++ b/solution.py
@@ -84,7 +84,7 @@
 
 def far_order(groups):
     masks = list(range(1, groups))
-    return masks[2:] + masks[:1] + masks[1:2]
+    return masks[1:2] + masks[:1] + masks[2:]
 
 
 def finish_kernel(chips, lengths_ref, tokens_ref, gain_ref, proj_ref, own_ref, *refs):

time: 61.1 us -> 62.3 us (1.020)
  blocking collectives: 9.33 us -> 11.3 us
  waiting for transfers between devices: 15.7 us -> 14.5 us
    all_to_all x1, blocking collectives: 9.33 us -> 11.3 us  [body(): lax.all_to_all(best, ('group', 'dev'), split_axis=0, concat_axis=0, tiled...]
    ppermute x19, waiting for transfers between devices: 15.7 us -> 14.5 us  [swap(): return lax.ppermute(values, axis, [(i, i ^ mask) for i in range(size)])]
  transfers between devices with their start and end apart: 19 -> 19, of which waited for: 7 -> 6; matrix products, arithmetic and copies ran while one was open for 0% -> 0% of each run, Pallas kernels for 11% -> 11%
where the time goes in v11:
time: 62.3 us; the launch traced here: 62.1 us
  starting transfers between devices  24.1 us (39%)
  waiting for transfers between devices  14.5 us (23%)
  blocking collectives  11.3 us (18%)
  Pallas kernels  9.38 us (15%)
  local copies, waits for them, and re-layouts  2.08 us (3%)
  between operations  0.79 us (1%)
    ppermute x19, starting transfers between devices, swap(): return lax.ppermute(values, axis, [(i, i ^ mask) for i in range(size)])  24.1 us
    ppermute x19, waiting for transfers between devices, swap(): return lax.ppermute(values, axis, [(i, i ^ mask) for i in range(size)])  14.5 us
    all_to_all x1, blocking collectives, body(): lax.all_to_all(best, ('group', 'dev'), split_axis=0, concat_axis=0, tiled...  11.3 us
    pallas_call x4, Pallas kernels, body(): pl.pallas_call(ffn_kernel, out_shape=jax.ShapeDtypeStruct((rows, width),...  5.49 us
    unnamed x18, local copies, waits for them, and re-layouts  2.08 us
    pallas_call x1, Pallas kernels, body(): pl.pallas_call(functools.partial(finish_kernel, chips), out_shape=[jax.Sh...  1.85 us
  transfers between devices with their start and end apart: 19, of which 6 were waited for; matrix products, arithmetic and copies ran while one was open for 0% of the time, Pallas kernels for 11%

profile of v11, /device:TPU:0, one launch (start us, length us, event | category | flops | bytes accessed | tf_op | source)
XLA Modules:
  0.0 62.1 jit_solution(13073319142376079147)
XLA Ops:
  0.6 3.0 %collective-permute-start.3 = (bf16[128,1024]{1,0:T(8,128)(2,1)}, bf16[128,1024]{1,0:T(8,128)(2,1)S(1)}, u32[]{:S(2)}, u32[]{:S(2)}) collective-permute-start(bf16[128,1024]{1,0:T(8,128)(2,1)} %tokens_ref.3), channel_id=1, source_target_pairs={{0,2},{1,3},{2,0},{3,1},{4,6},{5,7},{6,4},{7,5},{8,10},{9,11},{10,... | collective-permute-start | bytes 786440 | tf_op jit(solution)/shard_map/ppermute | solution.py:164
  3.6 1.5 %collective-permute-start.4 = (bf16[128,1024]{1,0:T(8,128)(2,1)}, bf16[128,1024]{1,0:T(8,128)(2,1)S(1)}, u32[]{:S(2)}, u32[]{:S(2)}) collective-permute-start(bf16[128,1024]{1,0:T(8,128)(2,1)} %tokens_ref.3), channel_id=1, source_target_pairs={{0,4},{1,5},{2,6},{3,7},{4,0},{5,1},{6,2},{7,3},{8,12},{9,13},{10,... | collective-permute-start | bytes 786440 | tf_op jit(solution)/shard_map/ppermute | solution.py:164
  5.2 1.3 %copy-done = bf16[128,5248]{1,0:T(8,128)(2,1)S(1)} copy-done((bf16[128,5248]{1,0:T(8,128)(2,1)S(1)}, bf16[128,5248]{1,0:T(8,128)(2,1)}, u32[]{:S(2)}) %copy-start) | copy-done | bytes 1343512
  6.5 0.7 %copy-done.5 = bf16[2,32,128]{2,1,0:T(8,128)(2,1)S(1)} copy-done((bf16[2,32,128]{2,1,0:T(8,128)(2,1)S(1)}, bf16[2,32,128]{2,1,0:T(8,128)(2,1)}, u32[]{:S(2)}) %copy-start.5) | copy-done | bytes 16408
  7.2 0.5 shard_map.104
  7.8 1.9 %collective-permute-start.1 = (bf16[1376,128]{1,0:T(8,128)(2,1)S(1)}, bf16[1376,128]{1,0:T(8,128)(2,1)S(1)}, u32[]{:S(2)}, u32[]{:S(2)}) collective-permute-start(bf16[1376,128]{1,0:T(8,128)(2,1)S(1)} %get-tuple-element.21), channel_id=1, source_target_pairs={{0,2},{1,3},{2,0},{3,1},{4,6},{5,7},{6,4},{7,5},{8,10},{9,11},{10,... | collective-permute-start | bytes 1056776 | tf_op jit(solution)/shard_map/ppermute | solution.py:164
  9.7 1.5 %collective-permute-start.6 = (bf16[1376,128]{1,0:T(8,128)(2,1)S(1)}, bf16[1376,128]{1,0:T(8,128)(2,1)S(1)}, u32[]{:S(2)}, u32[]{:S(2)}) collective-permute-start(bf16[1376,128]{1,0:T(8,128)(2,1)S(1)} %get-tuple-element.28), channel_id=1, source_target_pairs={{0,4},{1,5},{2,6},{3,7},{4,0},{5,1},{6,2},{7,3},{8,12},{9,13},{10,... | collective-permute-start | bytes 1056776 | tf_op jit(solution)/shard_map/ppermute | solution.py:164
  11.2 5.0 %collective-permute-done.2.refs_3_ = bf16[720,128]{1,0:T(8,128)(2,1)S(1)} collective-permute-done((bf16[720,128]{1,0:T(8,128)(2,1)S(1)}, bf16[720,128]{1,0:T(8,128)(2,1)S(1)}, u32[]{:S(2)}, u32[]{:S(2)}) %collective-permute-start.2) | collective-permute-done | bytes 184352 | tf_op jit(solution)/shard_map/ppermute | solution.py:164
  16.3 1.6 %collective-permute-start.5 = (bf16[720,128]{1,0:T(8,128)(2,1)S(1)}, bf16[720,128]{1,0:T(8,128)(2,1)S(1)}, u32[]{:S(2)}, u32[]{:S(2)}) collective-permute-start(bf16[720,128]{1,0:T(8,128)(2,1)S(1)} %collective-permute-done.2.refs_3_), channel_id=1, source_target_pairs={{0,8},{8,0},{16,24},{24,16},{1,9},{9,1},{17,25},{25,17},{2,10},{10... | collective-permute-start | bytes 552968 | tf_op jit(solution)/shard_map/ppermute | solution.py:164
  17.9 0.2 collective-permute-start.10
  18.1 3.6 %collective-permute-done.1.refs_1_ = bf16[1376,128]{1,0:T(8,128)(2,1)S(1)} collective-permute-done((bf16[1376,128]{1,0:T(8,128)(2,1)S(1)}, bf16[1376,128]{1,0:T(8,128)(2,1)S(1)}, u32[]{:S(2)}, u32[]{:S(2)}) %collective-permute-start.1) | collective-permute-done | bytes 352288 | tf_op jit(solution)/shard_map/ppermute | solution.py:164
  21.7 1.7 %collective-permute-done.5.refs_4_ = bf16[720,128]{1,0:T(8,128)(2,1)S(1)} collective-permute-done((bf16[720,128]{1,0:T(8,128)(2,1)S(1)}, bf16[720,128]{1,0:T(8,128)(2,1)S(1)}, u32[]{:S(2)}, u32[]{:S(2)}) %collective-permute-start.5) | collective-permute-done | bytes 184352 | tf_op jit(solution)/shard_map/ppermute | solution.py:164
  23.4 0.5 collective-permute-start.9
  23.9 0.4 collective-permute-start.8
  24.4 0.4 collective-permute-done.11.refs_9_
  24.8 1.7 %collective-permute-start.12 = (bf16[128,1024]{1,0:T(8,128)(2,1)S(1)}, bf16[128,1024]{1,0:T(8,128)(2,1)S(1)}, u32[]{:S(2)}, u32[]{:S(2)}) collective-permute-start(bf16[128,1024]{1,0:T(8,128)(2,1)S(1)} %copy-done.1), channel_id=1, source_target_pairs={{0,6},{1,7},{2,4},{3,5},{4,2},{5,3},{6,0},{7,1},{8,14},{9,15},{10,... | collective-permute-start | bytes 786440 | tf_op jit(solution)/shard_map/ppermute | solution.py:164
  26.5 0.9 %shard_map.105 = (bf16[656,1024]{1,0:T(8,128)(2,1)S(1)}, bf16[656,1024]{1,0:T(8,128)(2,1)S(1)}, bf16[656,1024]{1,0:T(8,128)(2,1)S(1)}, bf16[512,128]{1,0:T(8,128)(2,1)S(1)}) custom-call(bf16[328,1024]{1,0:T(8,128)(2,1)S(1)} %copy-done.2, bf16[328,1024]{1,0:T(8,128)(2,1)S(1)} %collective-permute-done.wo_other, ...), custom_call_target="tpu_custom_call" | custom-call | tf_op jit(solution)/shard_map/pallas_call | solution.py:190
  27.4 1.4 %shard_map.109 = bf16[128,1024]{1,0:T(8,128)(2,1)S(1)} custom-call(f32[1,1024]{1,0:T(1,128)S(1)} %bitcast.5, bf16[656,1024]{1,0:T(8,128)(2,1)S(1)} %get-tuple-element.30.gelu_w, bf16[656,1024]{1,0:T(8,128)(2,1)S(1)} %get-tuple-element.31.gate_w, bf16[656,1024]{1,0:T(8,128)(2,1)S(1)} %get-tuple-element.32.wo_part, ...), custom_call_target="tpu_custom_call" | custom-call | tf_op jit(solution)/shard_map/pallas_call | solution.py:214
  28.8 1.6 %collective-permute-start.15 = (bf16[128,1024]{1,0:T(8,128)(2,1)S(1)}, bf16[128,1024]{1,0:T(8,128)(2,1)S(1)}, u32[]{:S(2)}, u32[]{:S(2)}) collective-permute-start(bf16[128,1024]{1,0:T(8,128)(2,1)S(1)} %shard_map.109), channel_id=1, source_target_pairs={{0,2},{1,3},{2,0},{3,1},{4,6},{5,7},{6,4},{7,5},{8,10},{9,11},{10,... | collective-permute-start | bytes 786440 | tf_op jit(solution)/shard_map/ppermute | solution.py:164
  30.3 1.4 %shard_map.108 = bf16[128,1024]{1,0:T(8,128)(2,1)S(1)} custom-call(f32[1,1024]{1,0:T(1,128)S(1)} %bitcast.6, bf16[656,1024]{1,0:T(8,128)(2,1)S(1)} %get-tuple-element.30.gelu_w, bf16[656,1024]{1,0:T(8,128)(2,1)S(1)} %get-tuple-element.31.gate_w, bf16[656,1024]{1,0:T(8,128)(2,1)S(1)} %get-tuple-element.32.wo_part, ...), custom_call_target="tpu_custom_call" | custom-call | tf_op jit(solution)/shard_map/pallas_call | solution.py:214
  31.7 2.7 %collective-permute-start.16 = (bf16[512,128]{1,0:T(8,128)(2,1)S(1)}, bf16[512,128]{1,0:T(8,128)(2,1)S(1)}, u32[]{:S(2)}, u32[]{:S(2)}) collective-permute-start(bf16[512,128]{1,0:T(8,128)(2,1)S(1)} %get-tuple-element.35.refs_3_), channel_id=1, source_target_pairs={{0,16},{8,24},{16,0},{24,8},{1,17},{9,25},{17,1},{25,9},{2,18},{10... | collective-permute-start | bytes 393224 | tf_op jit(solution)/shard_map/ppermute | solution.py:164
  34.4 0.5 collective-permute-start.14
  34.9 1.4 %shard_map.107 = bf16[128,1024]{1,0:T(8,128)(2,1)S(1)} custom-call(f32[1,1024]{1,0:T(1,128)S(1)} %bitcast.7, bf16[656,1024]{1,0:T(8,128)(2,1)S(1)} %get-tuple-element.30.gelu_w, bf16[656,1024]{1,0:T(8,128)(2,1)S(1)} %get-tuple-element.31.gate_w, bf16[656,1024]{1,0:T(8,128)(2,1)S(1)} %get-tuple-element.32.wo_part, ...), custom_call_target="tpu_custom_call" | custom-call | tf_op jit(solution)/shard_map/pallas_call | solution.py:214
  36.3 1.7 %collective-permute-start.13 = (bf16[128,1024]{1,0:T(8,128)(2,1)S(1)}, bf16[128,1024]{1,0:T(8,128)(2,1)S(1)}, u32[]{:S(2)}, u32[]{:S(2)}) collective-permute-start(bf16[128,1024]{1,0:T(8,128)(2,1)S(1)} %shard_map.107), channel_id=1, source_target_pairs={{0,6},{1,7},{2,4},{3,5},{4,2},{5,3},{6,0},{7,1},{8,14},{9,15},{10,... | collective-permute-start | bytes 786440 | tf_op jit(solution)/shard_map/ppermute | solution.py:164
  38.0 1.6 %collective-permute-start.17 = (bf16[512,128]{1,0:T(8,128)(2,1)S(1)}, bf16[512,128]{1,0:T(8,128)(2,1)S(1)}, u32[]{:S(2)}, u32[]{:S(2)}) collective-permute-start(bf16[512,128]{1,0:T(8,128)(2,1)S(1)} %get-tuple-element.35.refs_3_), channel_id=1, source_target_pairs={{0,8},{8,0},{16,24},{24,16},{1,9},{9,1},{17,25},{25,17},{2,10},{10... | collective-permute-start | bytes 393224 | tf_op jit(solution)/shard_map/ppermute | solution.py:164
  39.6 1.4 %collective-permute-done.16.refs_4_ = bf16[512,128]{1,0:T(8,128)(2,1)S(1)} collective-permute-done((bf16[512,128]{1,0:T(8,128)(2,1)S(1)}, bf16[512,128]{1,0:T(8,128)(2,1)S(1)}, u32[]{:S(2)}, u32[]{:S(2)}) %collective-permute-start.16) | collective-permute-done | bytes 131104 | tf_op jit(solution)/shard_map/ppermute | solution.py:164
  41.0 3.5 %collective-permute-start.18 = (bf16[512,128]{1,0:T(8,128)(2,1)S(1)}, bf16[512,128]{1,0:T(8,128)(2,1)S(1)}, u32[]{:S(2)}, u32[]{:S(2)}) collective-permute-start(bf16[512,128]{1,0:T(8,128)(2,1)S(1)} %get-tuple-element.35.refs_3_), channel_id=1, source_target_pairs={{0,24},{8,16},{16,8},{24,0},{1,25},{9,17},{17,9},{25,1},{2,26},{10... | collective-permute-start | bytes 393224 | tf_op jit(solution)/shard_map/ppermute | solution.py:164
  44.5 1.4 %shard_map.106.own_ref = f32[128,1024]{1,0:T(8,128)S(1)} custom-call(f32[1,1024]{1,0:T(1,128)S(1)} %bitcast.8, bf16[656,1024]{1,0:T(8,128)(2,1)S(1)} %get-tuple-element.30.gelu_w, bf16[656,1024]{1,0:T(8,128)(2,1)S(1)} %get-tuple-element.31.gate_w, bf16[656,1024]{1,0:T(8,128)(2,1)S(1)} %get-tuple-element.32.wo_part, bf16[128,1024]{1,0:T(8,128)(2,1)S(1)} %copy-done.1), custom_call_target="tpu_custom_call" | custom-call | tf_op jit(solution)/shard_map/pallas_call | solution.py:214
  45.9 2.3 %collective-permute-done.18.refs_6_ = bf16[512,128]{1,0:T(8,128)(2,1)S(1)} collective-permute-done((bf16[512,128]{1,0:T(8,128)(2,1)S(1)}, bf16[512,128]{1,0:T(8,128)(2,1)S(1)}, u32[]{:S(2)}, u32[]{:S(2)}) %collective-permute-start.18) | collective-permute-done | bytes 131104 | tf_op jit(solution)/shard_map/ppermute | solution.py:164
  48.2 1.9 %shard_map.110 = (bf16[128,128]{1,0:T(8,128)(2,1)}, bf16[32,4,128]{2,1,0:T(4,128)(2,1)S(1)}) custom-call(s32[1,4]{1,0:T(1,128)S(1)} %copy-done.8, bf16[128,1024]{1,0:T(8,128)(2,1)S(1)} %copy-done.1, f32[1,1024]{1,0:T(1,128)S(1)} %bitcast.10, bf16[1024,128]{1,0:T(8,128)(2,1)S(1)} %copy-done.3, f32[128,1024]{1,0:T(8,128)S(1)} %shard_map.106.own_ref, ...), custom_call_target="tpu_custom_call" | custom-call | tf_op jit(solution)/shard_map/pallas_call | solution.py:225
  50.1 11.3 %all_to_all.5 = bf16[32,4,128]{2,1,0:T(4,128)(2,1)S(1)} all-to-all(bf16[32,4,128]{2,1,0:T(4,128)(2,1)S(1)} %get-tuple-element.37), channel_id=1, replica_groups=mesh['group'=4,'dev'=8] {'group','dev'}, dimensions={0} | all-to-all | bytes 65536 | tf_op jit(solution)/shard_map/all_to_all | solution.py:243
  61.4 0.7 %shard_map.111 = f32[2,100]{1,0:T(2,128)} custom-call(s32[2,100]{1,0:T(2,128)S(1)} %copy-done.7, bf16[4,8,4,128]{3,2,1,0:T(4,128)(2,1)S(1)} %bitcast.4), custom_call_target="tpu_custom_call" | custom-call | tf_op jit(solution)/shard_map/pallas_call | solution.py:244
  (33 shorter events, 0.2 us)
Async XLA Ops:
  0.6 15.7 %collective-permute-start.3 = (bf16[128,1024]{1,0:T(8,128)(2,1)}, bf16[128,1024]{1,0:T(8,128)(2,1)S(1)}, u32[]{:S(2)}, u32[]{:S(2)}) collective-permute-start(bf16[128,1024]{1,0:T(8,128)(2,1)} %tokens_ref.3), channel_id=1, source_target_pairs={{0,2},{1,3},{2,0},{3,1},{4,6},{5,7},{6,4},{7,5},{8,10},{9,11},{10,... | collective-permute-start | bytes 786440 | tf_op jit(solution)/shard_map/ppermute | solution.py:164
  3.6 12.7 %collective-permute-start.4 = (bf16[128,1024]{1,0:T(8,128)(2,1)}, bf16[128,1024]{1,0:T(8,128)(2,1)S(1)}, u32[]{:S(2)}, u32[]{:S(2)}) collective-permute-start(bf16[128,1024]{1,0:T(8,128)(2,1)} %tokens_ref.3), channel_id=1, source_target_pairs={{0,4},{1,5},{2,6},{3,7},{4,0},{5,1},{6,2},{7,3},{8,12},{9,13},{10,... | collective-permute-start | bytes 786440 | tf_op jit(solution)/shard_map/ppermute | solution.py:164
  5.2 1.3 %copy-start = (bf16[128,5248]{1,0:T(8,128)(2,1)S(1)}, bf16[128,5248]{1,0:T(8,128)(2,1)}, u32[]{:S(2)}) copy-start(bf16[128,5248]{1,0:T(8,128)(2,1)} %wi_ref.1) | copy-start | bytes 4030468
  6.5 0.7 %copy-start.5 = (bf16[2,32,128]{2,1,0:T(8,128)(2,1)S(1)}, bf16[2,32,128]{2,1,0:T(8,128)(2,1)}, u32[]{:S(2)}) copy-start(bf16[2,32,128]{2,1,0:T(8,128)(2,1)} %param.15) | copy-start | bytes 49156
  7.2 9.1 %copy-start.2 = (bf16[328,1024]{1,0:T(8,128)(2,1)S(1)}, bf16[328,1024]{1,0:T(8,128)(2,1)}, u32[]{:S(2)}) copy-start(bf16[328,1024]{1,0:T(8,128)(2,1)} %wo_mine.1) | copy-start | bytes 2015236
  7.2 17.6 %copy-start.1 = (bf16[128,1024]{1,0:T(8,128)(2,1)S(1)}, bf16[128,1024]{1,0:T(8,128)(2,1)}, u32[]{:S(2)}) copy-start(bf16[128,1024]{1,0:T(8,128)(2,1)} %tokens_ref.3) | copy-start | bytes 786436
  7.7 8.6 %collective-permute-start.2 = (bf16[720,128]{1,0:T(8,128)(2,1)S(1)}, bf16[720,128]{1,0:T(8,128)(2,1)S(1)}, u32[]{:S(2)}, u32[]{:S(2)}) collective-permute-start(bf16[720,128]{1,0:T(8,128)(2,1)S(1)} %get-tuple-element.22), channel_id=1, source_target_pairs={{0,6},{1,7},{2,4},{3,5},{4,2},{5,3},{6,0},{7,1},{8,14},{9,15},{10,... | collective-permute-start | bytes 552968 | tf_op jit(solution)/shard_map/ppermute | solution.py:164
  7.8 13.9 %collective-permute-start.1 = (bf16[1376,128]{1,0:T(8,128)(2,1)S(1)}, bf16[1376,128]{1,0:T(8,128)(2,1)S(1)}, u32[]{:S(2)}, u32[]{:S(2)}) collective-permute-start(bf16[1376,128]{1,0:T(8,128)(2,1)S(1)} %get-tuple-element.21), channel_id=1, source_target_pairs={{0,2},{1,3},{2,0},{3,1},{4,6},{5,7},{6,4},{7,5},{8,10},{9,11},{10,... | collective-permute-start | bytes 1056776 | tf_op jit(solution)/shard_map/ppermute | solution.py:164
  9.7 13.6 %collective-permute-start.6 = (bf16[1376,128]{1,0:T(8,128)(2,1)S(1)}, bf16[1376,128]{1,0:T(8,128)(2,1)S(1)}, u32[]{:S(2)}, u32[]{:S(2)}) collective-permute-start(bf16[1376,128]{1,0:T(8,128)(2,1)S(1)} %get-tuple-element.28), channel_id=1, source_target_pairs={{0,4},{1,5},{2,6},{3,7},{4,0},{5,1},{6,2},{7,3},{8,12},{9,13},{10,... | collective-permute-start | bytes 1056776 | tf_op jit(solution)/shard_map/ppermute | solution.py:164
  16.3 10.2 %collective-permute-start = (bf16[328,1024]{1,0:T(8,128)(2,1)S(1)}, bf16[328,1024]{1,0:T(8,128)(2,1)S(1)}, u32[]{:S(2)}, u32[]{:S(2)}) collective-permute-start(bf16[328,1024]{1,0:T(8,128)(2,1)S(1)} %copy-done.2), channel_id=1, source_target_pairs={{0,1},{1,0},{2,3},{3,2},{4,5},{5,4},{6,7},{7,6},{8,9},{9,8},{10,11... | collective-permute-start | bytes 2015240 | tf_op jit(solution)/shard_map/ppermute | solution.py:164
  16.3 7.1 %collective-permute-start.5 = (bf16[720,128]{1,0:T(8,128)(2,1)S(1)}, bf16[720,128]{1,0:T(8,128)(2,1)S(1)}, u32[]{:S(2)}, u32[]{:S(2)}) collective-permute-start(bf16[720,128]{1,0:T(8,128)(2,1)S(1)} %collective-permute-done.2.refs_3_), channel_id=1, source_target_pairs={{0,8},{8,0},{16,24},{24,16},{1,9},{9,1},{17,25},{25,17},{2,10},{10... | collective-permute-start | bytes 552968 | tf_op jit(solution)/shard_map/ppermute | solution.py:164
  17.9 6.0 %collective-permute-start.10 = (bf16[720,128]{1,0:T(8,128)(2,1)S(1)}, bf16[720,128]{1,0:T(8,128)(2,1)S(1)}, u32[]{:S(2)}, u32[]{:S(2)}) collective-permute-start(bf16[720,128]{1,0:T(8,128)(2,1)S(1)} %collective-permute-done.2.refs_3_), channel_id=1, source_target_pairs={{0,1},{1,0},{2,3},{3,2},{4,5},{5,4},{6,7},{7,6},{8,9},{9,8},{10,11... | collective-permute-start | bytes 552968 | tf_op jit(solution)/shard_map/ppermute | solution.py:164
  23.4 4.0 %copy-start.4 = (f32[1024]{0:T(1024)S(1)}, f32[1024]{0:T(1024)}, u32[]{:S(2)}) copy-start(f32[1024]{0:T(1024)} %param.10) | copy-start | bytes 12292
  23.4 1.4 %collective-permute-start.11 = (bf16[720,128]{1,0:T(8,128)(2,1)S(1)}, bf16[720,128]{1,0:T(8,128)(2,1)S(1)}, u32[]{:S(2)}, u32[]{:S(2)}) collective-permute-start(bf16[720,128]{1,0:T(8,128)(2,1)S(1)} %collective-permute-done.5.refs_4_), channel_id=1, source_target_pairs={{0,1},{1,0},{2,3},{3,2},{4,5},{5,4},{6,7},{7,6},{8,9},{9,8},{10,11... | collective-permute-start | bytes 552968 | tf_op jit(solution)/shard_map/ppermute | solution.py:164
  23.4 3.1 %collective-permute-start.9 = (bf16[1376,128]{1,0:T(8,128)(2,1)S(1)}, bf16[1376,128]{1,0:T(8,128)(2,1)S(1)}, u32[]{:S(2)}, u32[]{:S(2)}) collective-permute-start(bf16[1376,128]{1,0:T(8,128)(2,1)S(1)} %collective-permute-done.6.refs_2_), channel_id=1, source_target_pairs={{0,1},{1,0},{2,3},{3,2},{4,5},{5,4},{6,7},{7,6},{8,9},{9,8},{10,11... | collective-permute-start | bytes 1056776 | tf_op jit(solution)/shard_map/ppermute | solution.py:164
  23.9 2.6 %collective-permute-start.7 = (bf16[1376,128]{1,0:T(8,128)(2,1)S(1)}, bf16[1376,128]{1,0:T(8,128)(2,1)S(1)}, u32[]{:S(2)}, u32[]{:S(2)}) collective-permute-start(bf16[1376,128]{1,0:T(8,128)(2,1)S(1)} %get-tuple-element.26.refs_0_), channel_id=1, source_target_pairs={{0,1},{1,0},{2,3},{3,2},{4,5},{5,4},{6,7},{7,6},{8,9},{9,8},{10,11... | collective-permute-start | bytes 1056776 | tf_op jit(solution)/shard_map/ppermute | solution.py:164
  23.9 2.5 %collective-permute-start.8 = (bf16[1376,128]{1,0:T(8,128)(2,1)S(1)}, bf16[1376,128]{1,0:T(8,128)(2,1)S(1)}, u32[]{:S(2)}, u32[]{:S(2)}) collective-permute-start(bf16[1376,128]{1,0:T(8,128)(2,1)S(1)} %collective-permute-done.1.refs_1_), channel_id=1, source_target_pairs={{0,1},{1,0},{2,3},{3,2},{4,5},{5,4},{6,7},{7,6},{8,9},{9,8},{10,11... | collective-permute-start | bytes 1056776 | tf_op jit(solution)/shard_map/ppermute | solution.py:164
  24.8 10.1 %collective-permute-start.12 = (bf16[128,1024]{1,0:T(8,128)(2,1)S(1)}, bf16[128,1024]{1,0:T(8,128)(2,1)S(1)}, u32[]{:S(2)}, u32[]{:S(2)}) collective-permute-start(bf16[128,1024]{1,0:T(8,128)(2,1)S(1)} %copy-done.1), channel_id=1, source_target_pairs={{0,6},{1,7},{2,4},{3,5},{4,2},{5,3},{6,0},{7,1},{8,14},{9,15},{10,... | collective-permute-start | bytes 786440 | tf_op jit(solution)/shard_map/ppermute | solution.py:164
  28.8 19.4 %collective-permute-start.15 = (bf16[128,1024]{1,0:T(8,128)(2,1)S(1)}, bf16[128,1024]{1,0:T(8,128)(2,1)S(1)}, u32[]{:S(2)}, u32[]{:S(2)}) collective-permute-start(bf16[128,1024]{1,0:T(8,128)(2,1)S(1)} %shard_map.109), channel_id=1, source_target_pairs={{0,2},{1,3},{2,0},{3,1},{4,6},{5,7},{6,4},{7,5},{8,10},{9,11},{10,... | collective-permute-start | bytes 786440 | tf_op jit(solution)/shard_map/ppermute | solution.py:164
  31.7 9.3 %collective-permute-start.16 = (bf16[512,128]{1,0:T(8,128)(2,1)S(1)}, bf16[512,128]{1,0:T(8,128)(2,1)S(1)}, u32[]{:S(2)}, u32[]{:S(2)}) collective-permute-start(bf16[512,128]{1,0:T(8,128)(2,1)S(1)} %get-tuple-element.35.refs_3_), channel_id=1, source_target_pairs={{0,16},{8,24},{16,0},{24,8},{1,17},{9,25},{17,1},{25,9},{2,18},{10... | collective-permute-start | bytes 393224 | tf_op jit(solution)/shard_map/ppermute | solution.py:164
  34.4 13.8 %collective-permute-start.14 = (bf16[128,1024]{1,0:T(8,128)(2,1)S(1)}, bf16[128,1024]{1,0:T(8,128)(2,1)S(1)}, u32[]{:S(2)}, u32[]{:S(2)}) collective-permute-start(bf16[128,1024]{1,0:T(8,128)(2,1)S(1)} %shard_map.108), channel_id=1, source_target_pairs={{0,4},{1,5},{2,6},{3,7},{4,0},{5,1},{6,2},{7,3},{8,12},{9,13},{10,... | collective-permute-start | bytes 786440 | tf_op jit(solution)/shard_map/ppermute | solution.py:164
  36.3 11.9 %copy-start.3 = (bf16[1024,128]{1,0:T(8,128)(2,1)S(1)}, bf16[1024,128]{1,0:T(8,128)(2,1)}, u32[]{:S(2)}) copy-start(bf16[1024,128]{1,0:T(8,128)(2,1)} %proj_ref.1) | copy-start | bytes 786436
  36.3 11.9 %copy-start.6 = (f32[1024]{0:T(1024)S(1)}, f32[1024]{0:T(1024)}, u32[]{:S(2)}) copy-start(f32[1024]{0:T(1024)} %param.13) | copy-start | bytes 12292
  36.3 11.9 %copy-start.8 = (s32[1,4]{1,0:T(1,128)S(1)}, s32[1,4]{1,0:T(1,128)}, u32[]{:S(2)}) copy-start(s32[1,4]{1,0:T(1,128)} %lengths_ref.1) | copy-start | bytes 52
  36.3 11.9 %collective-permute-start.13 = (bf16[128,1024]{1,0:T(8,128)(2,1)S(1)}, bf16[128,1024]{1,0:T(8,128)(2,1)S(1)}, u32[]{:S(2)}, u32[]{:S(2)}) collective-permute-start(bf16[128,1024]{1,0:T(8,128)(2,1)S(1)} %shard_map.107), channel_id=1, source_target_pairs={{0,6},{1,7},{2,4},{3,5},{4,2},{5,3},{6,0},{7,1},{8,14},{9,15},{10,... | collective-permute-start | bytes 786440 | tf_op jit(solution)/shard_map/ppermute | solution.py:164
  38.0 7.9 %collective-permute-start.17 = (bf16[512,128]{1,0:T(8,128)(2,1)S(1)}, bf16[512,128]{1,0:T(8,128)(2,1)S(1)}, u32[]{:S(2)}, u32[]{:S(2)}) collective-permute-start(bf16[512,128]{1,0:T(8,128)(2,1)S(1)} %get-tuple-element.35.refs_3_), channel_id=1, source_target_pairs={{0,8},{8,0},{16,24},{24,16},{1,9},{9,1},{17,25},{25,17},{2,10},{10... | collective-permute-start | bytes 393224 | tf_op jit(solution)/shard_map/ppermute | solution.py:164
  41.0 7.2 %collective-permute-start.18 = (bf16[512,128]{1,0:T(8,128)(2,1)S(1)}, bf16[512,128]{1,0:T(8,128)(2,1)S(1)}, u32[]{:S(2)}, u32[]{:S(2)}) collective-permute-start(bf16[512,128]{1,0:T(8,128)(2,1)S(1)} %get-tuple-element.35.refs_3_), channel_id=1, source_target_pairs={{0,24},{8,16},{16,8},{24,0},{1,25},{9,17},{17,9},{25,1},{2,26},{10... | collective-permute-start | bytes 393224 | tf_op jit(solution)/shard_map/ppermute | solution.py:164
  45.8 15.6 %copy-start.7 = (s32[2,100]{1,0:T(2,128)S(1)}, s32[2,100]{1,0:T(2,128)}, u32[]{:S(2)}) copy-start(s32[2,100]{1,0:T(2,128)} %cand_ref.1) | copy-start | bytes 2404
